TPU v7x, 32 devices: a whole 2x2x4 slice. The times are simulated.
32 devices in a mesh: tm: 4 (over z), space: 8 (over y, x, core).
Axes of the slice: x: 2, y: 2, z: 4, core: 2. Of those that a mesh axis runs over, the one named last changes fastest.
Arguments:
- probes: bfloat16 [192, 128, 1024], P('tm', 'space'), may hold values from -6 to 6
- local_links: int32 [128, 4], P('space'), may hold values from 0 to 15
- remote_links: int32 [128, 2], P('space'), may hold values from 0 to 15
- shared_blocks: int32 [8, 2], P('space'), may hold values from 0 to 15, as said below
- slab_days: int32 [4], P('tm'), may hold values from 1 to 48, 120 in all
- local_coupling: bfloat16 [128, 4, 64, 64], P('space'), may hold values from -0.3125 to 0.3125
- remote_coupling: bfloat16 [128, 2, 64, 64], P('space'), may hold values from -0.3125 to 0.3125
- block_inverse: bfloat16 [128, 64, 64], P('space'), may hold values from -0.0546875 to 0.0546875
- retention: float32 [192, 8192], P('tm', 'space'), as said below
Outputs:
- variance: float32 [192, 8192], P('tm', 'space')
Inputs may be any that keep to these rules, and one draw needn't show every extreme that they name: `shared_blocks`: each group's 2 numbers differ, and each list holds the group's last local block. `retention`: share of a node's state carried from one day to the next.
All inputs are finite; a program needn't handle non-finite values. No bound on the sum of `slab_days` on one device may be relied on, other than what follows from the above.
Results may differ from a plain program's by a relative error of at most 0.0028.
Values may be sent and summed in bfloat16 or wider, within the bound.
No kernel may reach another device: no remote copies, remote signals or barrier semaphores. Data moves between devices by JAX's collectives and lax.ppermute only.
A program may use at most 192 MiB of HBM per device.

v0:
```python
import functools

import jax
import jax.numpy as jnp
from jax import lax
from jax.experimental import pallas as pl
from jax.experimental.pallas import tpu as pltpu
from jax.sharding import PartitionSpec as P

LANES = 128
VMEM_LIMIT = 56 * 1024 * 1024
TURNED = (((1,), (1,)), ((), ()))


def permutation(size, probes, start, width):
    total = size * probes
    column = lax.broadcasted_iota(jnp.int32, (total, width), 1) + start
    origin = (column % size) * probes + column // size
    row = lax.broadcasted_iota(jnp.int32, (total, width), 0)
    return (row == origin).astype(jnp.float32).astype(jnp.bfloat16)


def doubled(weight, size):
    wide = weight.astype(jnp.float32)
    return jnp.concatenate([wide, pltpu.roll(wide, size, 1)], axis=0).astype(jnp.bfloat16)


def outgoing_kernel(dims, shared_ref, z_ref, outgoing_ref):
    days, blocks, size, probes = dims
    count = outgoing_ref.shape[0]
    z = z_ref[...].reshape(days * blocks, size * probes)
    row = lax.broadcasted_iota(jnp.int32, (days, days * blocks), 0)
    column = lax.broadcasted_iota(jnp.int32, (days, days * blocks), 1)
    picks = [
        (column == row * blocks + shared_ref[0, m]).astype(jnp.float32).astype(jnp.bfloat16) for m in range(count)
    ]
    picked = jnp.dot(jnp.concatenate(picks, axis=0), z, preferred_element_type=jnp.float32).astype(jnp.bfloat16)
    step = 2 * LANES
    for start in range(0, size * probes, step):
        moved = jnp.dot(picked, permutation(size, probes, start, step), preferred_element_type=jnp.float32)
        moved = moved.astype(jnp.bfloat16)
        for half in range(2):
            pair = start // LANES + half
            for m in range(count):
                outgoing_ref[m, pl.ds(pair * days, days), :] = moved[
                    m * days : (m + 1) * days, half * LANES : (half + 1) * LANES
                ]


def local_kernel(
    dims, links_ref, days_ref, z_ref, weight_ref, retention_ref, running_ref, moved_ref, retain_ref, product_ref, stage, turned
):
    days, blocks, size, probes = dims
    pairs = size * probes // LANES
    count = links_ref.shape[1]
    z = z_ref[...].reshape(days * blocks, size * probes)
    step = 2 * LANES
    for start in range(0, size * probes, step):
        moved = jnp.dot(z, permutation(size, probes, start, step), preferred_element_type=jnp.float32)
        for half in range(2):
            pair = start // LANES + half
            stage[pair] = moved[:, half * LANES : (half + 1) * LANES]
            moved_ref[pair] = moved[:, half * LANES : (half + 1) * LANES].astype(jnp.bfloat16)
    for block in range(blocks):
        for pair in range(pairs):
            rows = stage[pair, pl.ds(block, days, stride=blocks), :]
            turned[block, pl.ds(pair * days, days), :] = rows.astype(jnp.bfloat16)
    for block in range(blocks):
        near = jnp.concatenate([turned[links_ref[block, k]] for k in range(count)], axis=1)
        weight = jnp.concatenate([doubled(weight_ref[block, k], size) for k in range(count)], axis=1)
        total = lax.dot_general(near, weight, TURNED, preferred_element_type=jnp.float32)
        running_ref[block] = turned[block].astype(jnp.float32) - total
    observed = days_ref[0]
    product = jnp.ones((blocks, LANES), jnp.float32)
    for day in range(days):
        factor = retention_ref[pl.ds(day * blocks, blocks), :]
        factor = jnp.where(day < observed, factor, 1.0)
        retain_ref[day] = factor
        product = product * factor
    product_ref[...] = product


def forward_kernel(
    dims, links_ref, days_ref, running_ref, remote_ref, weight_ref, inverse_ref, retain_ref, product_ref,
    forcing_ref, message_ref,
):
    days, blocks, size, probes = dims
    pairs = size * probes // LANES
    count = links_ref.shape[1]
    for block in range(blocks):
        far = jnp.concatenate([remote_ref[links_ref[block, k]] for k in range(count)], axis=1)
        weight = jnp.concatenate([doubled(weight_ref[block, k], size) for k in range(count)], axis=1)
        total = lax.dot_general(far, weight, TURNED, preferred_element_type=jnp.float32)
        source = (running_ref[block] - total).astype(jnp.bfloat16)
        inverse = doubled(inverse_ref[block], size)
        drive = lax.dot_general(source, inverse, TURNED, preferred_element_type=jnp.float32)
        for pair in range(pairs):
            forcing_ref[pair, pl.ds(block, days, stride=blocks), :] = drive[pair * days : (pair + 1) * days]
    observed = days_ref[0]
    states = [jnp.zeros((blocks, LANES), jnp.float32)] * pairs
    for day in range(days):
        factor = retain_ref[day]
        rows = pl.ds(day * blocks, blocks)
        for pair in range(pairs):
            drive = jnp.where(day < observed, forcing_ref[pair, rows, :], 0.0)
            states[pair] = factor * states[pair] + drive
    for pair in range(pairs):
        message_ref[pair] = states[pair]
    message_ref[pairs] = product_ref[...]


def carried(pairs, message_refs):
    carries = [message_refs[-1][pair] for pair in range(pairs)]
    for ref in reversed(message_refs[:-1]):
        factor = ref[pairs]
        carries = [ref[pair] + factor * carries[pair] for pair in range(pairs)]
    return carries


def adjoint_kernel(dims, hops, days_ref, forcing_ref, retain_ref, product_ref, inverse_ref, *rest):
    days, blocks, size, probes = dims
    pairs = size * probes // LANES
    message_refs = rest[:hops]
    adjoint_ref, message_ref, stage = rest[hops:]
    observed = days_ref[0]
    states = carried(pairs, message_refs)
    for day in range(days):
        factor = retain_ref[day]
        rows = pl.ds(day * blocks, blocks)
        for pair in range(pairs):
            drive = jnp.where(day < observed, forcing_ref[pair, rows, :], 0.0)
            states[pair] = factor * states[pair] + drive
            stage[pair, rows, :] = states[pair]
    for block in range(blocks):
        stored = jnp.concatenate(
            [stage[pair, pl.ds(block, days, stride=blocks), :].astype(jnp.bfloat16) for pair in range(pairs)], axis=0
        )
        inverse = doubled(inverse_ref[block], size)
        adjoint = jnp.dot(stored, inverse, preferred_element_type=jnp.float32)
        for pair in range(pairs):
            adjoint_ref[pair, pl.ds(block, days, stride=blocks), :] = adjoint[pair * days : (pair + 1) * days]
    carries = [jnp.zeros((blocks, LANES), jnp.float32)] * pairs
    for day in reversed(range(days)):
        factor = retain_ref[day]
        rows = pl.ds(day * blocks, blocks)
        for pair in range(pairs):
            value = jnp.where(day < observed, adjoint_ref[pair, rows, :], 0.0)
            carries[pair] = factor * (value + carries[pair])
    for pair in range(pairs):
        message_ref[pair] = carries[pair]
    message_ref[pairs] = product_ref[...]


def variance_kernel(dims, hops, days_ref, adjoint_ref, retain_ref, moved_ref, *rest):
    days, blocks, size, probes = dims
    pairs = size * probes // LANES
    message_refs = rest[:hops]
    out_ref, stage = rest[hops:]
    observed = days_ref[0]
    carries = carried(pairs, message_refs)
    for day in reversed(range(days)):
        factor = retain_ref[day]
        rows = pl.ds(day * blocks, blocks)
        total = None
        for pair in range(pairs):
            smoothed = jnp.where(day < observed, adjoint_ref[pair, rows, :], 0.0) + carries[pair]
            carries[pair] = factor * smoothed
            term = smoothed * moved_ref[pair, rows, :].astype(jnp.float32)
            total = term if total is None else total + term
        stage[rows, :] = total
    lane = lax.broadcasted_iota(jnp.int32, (days, LANES), 1)
    for block in range(0, blocks, 2):
        both = [stage[pl.ds(block + half, days, stride=blocks), :] for half in range(2)]
        both = [value + pltpu.roll(value, size, 1) for value in both]
        out_ref[:, pl.ds(block * size, LANES)] = jnp.where(lane < size, both[0], both[1]) * (1.0 / probes)


def call(kernel, outs, scratch, flops, moved, scalars, *operands):
    in_specs = [
        pl.BlockSpec(memory_space=pltpu.SMEM if i < scalars else pltpu.VMEM) for i in range(len(operands))
    ]
    return pl.pallas_call(
        kernel,
        out_shape=[jax.ShapeDtypeStruct(shape, kind) for shape, kind in outs],
        in_specs=in_specs,
        out_specs=[pl.BlockSpec(memory_space=pltpu.VMEM) for _ in outs],
        scratch_shapes=scratch,
        compiler_params=pltpu.CompilerParams(vmem_limit_bytes=VMEM_LIMIT),
        cost_estimate=pl.CostEstimate(flops=flops, bytes_accessed=moved, transcendentals=0),
    )(*operands)


def shifted(block, axis, distance):
    count = lax.axis_size(axis)
    route = [(i, i + distance) for i in range(count) if 0 <= i + distance < count]
    return lax.ppermute(block, axis, route)


def local(
    probes,
    local_links,
    remote_links,
    shared_blocks,
    slab_days,
    local_coupling,
    remote_coupling,
    block_inverse,
    retention,
):
    days, blocks, width = probes.shape
    size = block_inverse.shape[1]
    dims = (days, blocks, size, width // size)
    pairs = width // LANES
    f32, bf16 = jnp.float32, jnp.bfloat16
    bound = shared_blocks.shape[1]
    tm_count = lax.axis_size("tm")
    hops = tm_count - 1
    rows = days * blocks
    padded = lambda weight: jnp.pad(weight, [(0, 0)] * (weight.ndim - 1) + [(0, LANES - size)])
    retention_rows = retention.reshape(rows, size)
    retention_rows = jnp.concatenate([retention_rows, retention_rows], axis=1)
    inverse = padded(block_inverse)

    (outgoing,) = call(
        functools.partial(outgoing_kernel, dims),
        [((bound, pairs * days, LANES), bf16)],
        [], 10**7, 4 * 10**6, 1, shared_blocks, probes,
    )
    remote = lax.all_gather(outgoing, "space", axis=0, tiled=True)
    running, moved, retain, product = call(
        functools.partial(local_kernel, dims),
        [
            ((blocks, pairs * days, LANES), f32),
            ((pairs, rows, LANES), bf16),
            ((days, blocks, LANES), f32),
            ((blocks, LANES), f32),
        ],
        [pltpu.VMEM((pairs, rows, LANES), f32), pltpu.VMEM((blocks, pairs * days, LANES), bf16)],
        10**9, 10**7, 2, local_links, slab_days, probes, padded(local_coupling), retention_rows,
    )
    message_shape = ((pairs + 1, blocks, LANES), f32)
    forcing, message = call(
        functools.partial(forward_kernel, dims),
        [((pairs, rows, LANES), f32), message_shape],
        [], 10**9, 10**7, 2,
        remote_links, slab_days, running, remote, padded(remote_coupling), inverse, retain, product,
    )
    received = [shifted(message, "tm", distance) for distance in range(1, tm_count)]
    adjoint, message = call(
        functools.partial(adjoint_kernel, dims, hops),
        [((pairs, rows, LANES), f32), message_shape],
        [pltpu.VMEM((pairs, rows, LANES), f32)], 10**9, 10**7, 1,
        slab_days, forcing, retain, product, inverse, *received,
    )
    received = [shifted(message, "tm", -distance) for distance in range(1, tm_count)]
    (variance,) = call(
        functools.partial(variance_kernel, dims, hops),
        [((days, blocks * size), f32)],
        [pltpu.VMEM((rows, LANES), f32)], 10**9, 10**7, 1,
        slab_days, adjoint, retain, moved, *received,
    )
    return variance


def solution(mesh):
    placed = (
        P("tm", "space", None),
        P("space", None),
        P("space", None),
        P("space", None),
        P("tm"),
        P("space", None, None, None),
        P("space", None, None, None),
        P("space", None, None),
        P("tm", "space"),
    )
    return jax.shard_map(
        local, mesh=mesh, in_specs=placed, out_specs=P("tm", "space"), check_vma=False
    )
```

profile of v0, /device:TPU:0, one launch (start us, length us, event | category | flops | bytes accessed | tf_op | source)
XLA Modules:
  0.0 87.9 jit_solution(16364240112333126132)
XLA Ops:
  6.5 0.0 copy-start.1
  6.5 0.0 copy-start
  6.5 0.0 all-gather.2.cloned.1.call-start
  6.5 3.0 %shard_map.92 = bf16[2,384,128]{2,1,0:T(8,128)(2,1)} custom-call(s32[1,2]{1,0:T(1,128)} %shared_ref.1, bf16[48,16,1024]{2,1,0:T(8,128)(2,1)} %z_ref.3), custom_call_target="tpu_custom_call" | custom-call | flops 10000000 | bytes 4000000 | tf_op jit(solution)/shard_map/pallas_call | solution.py:182
  9.5 0.0 all-gather.2.cloned.1.call-update
  10.2 1.4 %copy.14.links_ref = s32[16,4]{1,0:T(8,128)} copy(s32[16,4]{0,1:T(4,128)} %param.10) | data formatting | bytes 512 | tf_op args[1]
  11.6 1.3 %copy.15.links_ref = s32[16,2]{1,0:T(8,128)} copy(s32[16,2]{0,1:T(2,128)} %param.11) | data formatting | bytes 256 | tf_op args[2]
  12.9 1.0 %reshape.3 = f32[768,64]{1,0:T(8,128)S(1)} reshape(f32[48,1024]{1,0:T(8,128)} %param.17) | data formatting | bytes 393216 | tf_op jit(solution)/shard_map/reshape | solution.py:220
  14.0 1.7 %pad.14.inverse_ref = bf16[16,64,128]{2,1,0:T(8,128)(2,1)} pad(bf16[16,64,64]{2,1,0:T(8,128)(2,1)} %param.16, bf16[]{:T(256)} %constant.2.clone.1), padding=0_0x0_0x0_64 | pad | bytes 393218 | tf_op jit(solution)/shard_map/jit(_pad)/pad | solution.py:219
  15.7 0.0 copy-done.1
  15.7 0.9 %pad.13.weight_ref = bf16[16,2,64,128]{3,2,1,0:T(8,128)(2,1)} pad(bf16[16,2,64,64]{3,2,1,0:T(8,128)(2,1)S(1)} %copy-done.1, bf16[]{:T(256)} %constant.2.clone.1), padding=0_0x0_0x0_0x0_64 | pad | bytes 786434 | tf_op jit(solution)/shard_map/jit(_pad)/pad | solution.py:219
  16.6 0.0 copy-done
  16.6 1.3 %pad.12.weight_ref = bf16[16,4,64,128]{3,2,1,0:T(8,128)(2,1)} pad(bf16[16,4,64,64]{3,2,1,0:T(8,128)(2,1)S(1)} %copy-done, bf16[]{:T(256)} %constant.2.clone.1), padding=0_0x0_0x0_0x0_64 | pad | bytes 1572866 | tf_op jit(solution)/shard_map/jit(_pad)/pad | solution.py:219
  18.0 0.9 %pad_maximum_fusion.retention_ref = f32[768,128]{1,0:T(8,128)} fusion(f32[768,64]{1,0:T(8,128)S(1)} %reshape.3), kind=kLoop, calls=%fused_computation | loop fusion | flops 98304 | bytes 589824 | tf_op jit(solution)/shard_map/concatenate | solution.py:221
  18.9 8.0 %shard_map.91 = (f32[16,384,128]{2,1,0:T(8,128)}, bf16[8,768,128]{2,1,0:T(8,128)(2,1)}, f32[48,16,128]{2,1,0:T(8,128)}, f32[16,128]{1,0:T(8,128)}) custom-call(s32[16,4]{1,0:T(8,128)} %copy.14.links_ref, s32[1]{0:T(128)S(6)} %copy.16.days_ref, bf16[48,16,1024]{2,1,0:T(8,128)(2,1)} %z_ref.3, bf16[16,4,64,128]{3,2,1,0:T(8,128)(2,1)} %pad.12.weight_ref, ...), custom_call_target="tpu_custom_call" | custom-call | flops 1000000000 | bytes 10000000 | tf_op jit(solution)/shard_map/pallas_call | solution.py:182
  26.9 11.2 %all-gather.2.cloned.1.call-done.remote_ref = bf16[16,384,128]{2,1,0:T(8,128)(2,1)} async-done(((bf16[2,384,128]{2,1,0:T(8,128)(2,1)}), bf16[16,384,128]{2,1,0:T(8,128)(2,1)}) %all-gather.2.cloned.1.call-update) | async-done | bytes 1572880 | tf_op jit(solution)/shard_map/all_gather | solution.py:229
  38.1 8.5 %shard_map.93 = (f32[8,768,128]{2,1,0:T(8,128)}, f32[9,16,128]{2,1,0:T(8,128)}) custom-call(s32[16,2]{1,0:T(8,128)} %copy.15.links_ref, s32[1]{0:T(128)S(6)} %copy.16.days_ref, f32[16,384,128]{2,1,0:T(8,128)} %get-tuple-element.13.running_ref, bf16[16,384,128]{2,1,0:T(8,128)(2,1)} %all-gather.2.cloned.1.call-done.remote_ref, ...), custom_call_target="tpu_custom_call" | custom-call | flops 1000000000 | bytes 10000000 | tf_op jit(solution)/shard_map/pallas_call | solution.py:182
  46.6 5.2 %collective-permute-start.2 = (f32[9,16,128]{2,1,0:T(8,128)}, f32[9,16,128]{2,1,0:T(8,128)S(1)}, u32[]{:S(2)}, u32[]{:S(2)}) collective-permute-start(f32[9,16,128]{2,1,0:T(8,128)} %get-tuple-element.17), channel_id=1, source_target_pairs={{0,24},{1,25},{2,26},{3,27},{4,28},{5,29},{6,30},{7,31}} | collective-permute-start | bytes 221192 | tf_op jit(solution)/shard_map/ppermute | solution.py:196
  51.8 1.3 %collective-permute-start.1 = (f32[9,16,128]{2,1,0:T(8,128)}, f32[9,16,128]{2,1,0:T(8,128)S(1)}, u32[]{:S(2)}, u32[]{:S(2)}) collective-permute-start(f32[9,16,128]{2,1,0:T(8,128)} %get-tuple-element.17), channel_id=1, source_target_pairs={{0,16},{8,24},{1,17},{9,25},{2,18},{10,26},{3,19},{11,27},{4,20},{... | collective-permute-start | bytes 221192 | tf_op jit(solution)/shard_map/ppermute | solution.py:196
  53.1 2.5 %collective-permute-start = (f32[9,16,128]{2,1,0:T(8,128)}, f32[9,16,128]{2,1,0:T(8,128)S(1)}, u32[]{:S(2)}, u32[]{:S(2)}) collective-permute-start(f32[9,16,128]{2,1,0:T(8,128)} %get-tuple-element.17), channel_id=1, source_target_pairs={{0,8},{8,16},{16,24},{1,9},{9,17},{17,25},{2,10},{10,18},{18,26},{... | collective-permute-start | bytes 221192 | tf_op jit(solution)/shard_map/ppermute | solution.py:196
  55.6 0.0 collective-permute-done.2.rest_2_
  55.6 0.0 copy-start.2
  55.6 0.1 collective-permute-done.1.rest_1_
  55.7 0.0 copy-start.4
  55.7 2.2 %collective-permute-done.rest_0_ = f32[9,16,128]{2,1,0:T(8,128)S(1)} collective-permute-done((f32[9,16,128]{2,1,0:T(8,128)}, f32[9,16,128]{2,1,0:T(8,128)S(1)}, u32[]{:S(2)}, u32[]{:S(2)}) %collective-permute-start) | collective-permute-done | bytes 73760 | tf_op jit(solution)/shard_map/ppermute | solution.py:196
  57.9 0.0 copy-start.6
  57.9 0.0 copy-done.2
  57.9 0.0 copy-done.4
  57.9 0.6 copy-done.6
  58.5 6.4 %shard_map.94 = (f32[8,768,128]{2,1,0:T(8,128)}, f32[9,16,128]{2,1,0:T(8,128)}) custom-call(s32[1]{0:T(128)S(6)} %copy.16.days_ref, f32[8,768,128]{2,1,0:T(8,128)} %get-tuple-element.16.forcing_ref, f32[48,16,128]{2,1,0:T(8,128)} %get-tuple-element.14.retain_ref, f32[16,128]{1,0:T(8,128)} %get-tuple-element.15.product_ref, ...), custom_call_target="tpu_custom_call" | custom-call | flops 1000000000 | bytes 10000000 | tf_op jit(solution)/shard_map/pallas_call | solution.py:182
  65.0 1.3 %collective-permute-start.5 = (f32[9,16,128]{2,1,0:T(8,128)}, f32[9,16,128]{2,1,0:T(8,128)S(1)}, u32[]{:S(2)}, u32[]{:S(2)}) collective-permute-start(f32[9,16,128]{2,1,0:T(8,128)} %get-tuple-element.20), channel_id=1, source_target_pairs={{24,0},{25,1},{26,2},{27,3},{28,4},{29,5},{30,6},{31,7}} | collective-permute-start | bytes 221192 | tf_op jit(solution)/shard_map/ppermute | solution.py:196
  66.2 1.3 %collective-permute-start.4 = (f32[9,16,128]{2,1,0:T(8,128)}, f32[9,16,128]{2,1,0:T(8,128)S(1)}, u32[]{:S(2)}, u32[]{:S(2)}) collective-permute-start(f32[9,16,128]{2,1,0:T(8,128)} %get-tuple-element.20), channel_id=1, source_target_pairs={{16,0},{24,8},{17,1},{25,9},{18,2},{26,10},{19,3},{27,11},{20,4},{... | collective-permute-start | bytes 221192 | tf_op jit(solution)/shard_map/ppermute | solution.py:196
  67.5 1.3 %collective-permute-start.3 = (f32[9,16,128]{2,1,0:T(8,128)}, f32[9,16,128]{2,1,0:T(8,128)S(1)}, u32[]{:S(2)}, u32[]{:S(2)}) collective-permute-start(f32[9,16,128]{2,1,0:T(8,128)} %get-tuple-element.20), channel_id=1, source_target_pairs={{8,0},{16,8},{24,16},{9,1},{17,9},{25,17},{10,2},{18,10},{26,18},{... | collective-permute-start | bytes 221192 | tf_op jit(solution)/shard_map/ppermute | solution.py:196
  68.8 4.6 %collective-permute-done.5.rest_2_ = f32[9,16,128]{2,1,0:T(8,128)S(1)} collective-permute-done((f32[9,16,128]{2,1,0:T(8,128)}, f32[9,16,128]{2,1,0:T(8,128)S(1)}, u32[]{:S(2)}, u32[]{:S(2)}) %collective-permute-start.5) | collective-permute-done | bytes 73760 | tf_op jit(solution)/shard_map/ppermute | solution.py:196
  73.4 0.0 copy-start.3
  73.4 3.0 %collective-permute-done.4.rest_1_ = f32[9,16,128]{2,1,0:T(8,128)S(1)} collective-permute-done((f32[9,16,128]{2,1,0:T(8,128)}, f32[9,16,128]{2,1,0:T(8,128)S(1)}, u32[]{:S(2)}, u32[]{:S(2)}) %collective-permute-start.4) | collective-permute-done | bytes 73760 | tf_op jit(solution)/shard_map/ppermute | solution.py:196
  76.4 0.0 copy-start.5
  76.5 0.0 collective-permute-done.3.rest_0_
  76.5 0.0 copy-start.7
  76.5 0.0 copy-done.3
  76.5 0.6 copy-done.5
  77.1 0.0 copy-done.7
  77.1 3.9 %shard_map.95 = f32[48,1024]{1,0:T(8,128)} custom-call(s32[1]{0:T(128)S(6)} %copy.16.days_ref, f32[8,768,128]{2,1,0:T(8,128)} %get-tuple-element.18.adjoint_ref, f32[48,16,128]{2,1,0:T(8,128)} %get-tuple-element.14.retain_ref, bf16[8,768,128]{2,1,0:T(8,128)(2,1)} %get-tuple-element.19.moved_ref, f32[9,16,128]{2,1,0:T(8,128)} %copy-done.7, ...), custom_call_target="tpu_custom_call" | custom-call | flops 1000000000 | bytes 10000000 | tf_op jit(solution)/shard_map/pallas_call | solution.py:182
Async XLA Ops:
  6.5 9.2 %copy-start.1 = (bf16[16,2,64,64]{3,2,1,0:T(8,128)(2,1)S(1)}, bf16[16,2,64,64]{3,2,1,0:T(8,128)(2,1)}, u32[]{:S(2)}) copy-start(bf16[16,2,64,64]{3,2,1,0:T(8,128)(2,1)} %param.15) | copy-start | bytes 786436
  6.5 10.1 %copy-start = (bf16[16,4,64,64]{3,2,1,0:T(8,128)(2,1)S(1)}, bf16[16,4,64,64]{3,2,1,0:T(8,128)(2,1)}, u32[]{:S(2)}) copy-start(bf16[16,4,64,64]{3,2,1,0:T(8,128)(2,1)} %param.14) | copy-start | bytes 1572868
  6.5 31.6 %all-gather.2.cloned.1.call-start = ((), (), s32[]{:S(2)}) async-start(), calls=%async_computation | async-start | bytes 1769472 | tf_op jit(solution)/shard_map/all_gather | solution.py:229
  46.6 9.0 %collective-permute-start.2 = (f32[9,16,128]{2,1,0:T(8,128)}, f32[9,16,128]{2,1,0:T(8,128)S(1)}, u32[]{:S(2)}, u32[]{:S(2)}) collective-permute-start(f32[9,16,128]{2,1,0:T(8,128)} %get-tuple-element.17), channel_id=1, source_target_pairs={{0,24},{1,25},{2,26},{3,27},{4,28},{5,29},{6,30},{7,31}} | collective-permute-start | bytes 221192 | tf_op jit(solution)/shard_map/ppermute | solution.py:196
  51.8 3.9 %collective-permute-start.1 = (f32[9,16,128]{2,1,0:T(8,128)}, f32[9,16,128]{2,1,0:T(8,128)S(1)}, u32[]{:S(2)}, u32[]{:S(2)}) collective-permute-start(f32[9,16,128]{2,1,0:T(8,128)} %get-tuple-element.17), channel_id=1, source_target_pairs={{0,16},{8,24},{1,17},{9,25},{2,18},{10,26},{3,19},{11,27},{4,20},{... | collective-permute-start | bytes 221192 | tf_op jit(solution)/shard_map/ppermute | solution.py:196
  53.1 4.8 %collective-permute-start = (f32[9,16,128]{2,1,0:T(8,128)}, f32[9,16,128]{2,1,0:T(8,128)S(1)}, u32[]{:S(2)}, u32[]{:S(2)}) collective-permute-start(f32[9,16,128]{2,1,0:T(8,128)} %get-tuple-element.17), channel_id=1, source_target_pairs={{0,8},{8,16},{16,24},{1,9},{9,17},{17,25},{2,10},{10,18},{18,26},{... | collective-permute-start | bytes 221192 | tf_op jit(solution)/shard_map/ppermute | solution.py:196
  55.6 2.3 %copy-start.2 = (f32[9,16,128]{2,1,0:T(8,128)}, f32[9,16,128]{2,1,0:T(8,128)S(1)}, u32[]{:S(2)}) copy-start(f32[9,16,128]{2,1,0:T(8,128)S(1)} %collective-permute-done.2.rest_2_) | copy-start | bytes 221188
  55.7 2.2 %copy-start.4 = (f32[9,16,128]{2,1,0:T(8,128)}, f32[9,16,128]{2,1,0:T(8,128)S(1)}, u32[]{:S(2)}) copy-start(f32[9,16,128]{2,1,0:T(8,128)S(1)} %collective-permute-done.1.rest_1_) | copy-start | bytes 221188
  57.9 0.6 copy-start.6
  65.0 8.5 %collective-permute-start.5 = (f32[9,16,128]{2,1,0:T(8,128)}, f32[9,16,128]{2,1,0:T(8,128)S(1)}, u32[]{:S(2)}, u32[]{:S(2)}) collective-permute-start(f32[9,16,128]{2,1,0:T(8,128)} %get-tuple-element.20), channel_id=1, source_target_pairs={{24,0},{25,1},{26,2},{27,3},{28,4},{29,5},{30,6},{31,7}} | collective-permute-start | bytes 221192 | tf_op jit(solution)/shard_map/ppermute | solution.py:196
  66.2 10.2 %collective-permute-start.4 = (f32[9,16,128]{2,1,0:T(8,128)}, f32[9,16,128]{2,1,0:T(8,128)S(1)}, u32[]{:S(2)}, u32[]{:S(2)}) collective-permute-start(f32[9,16,128]{2,1,0:T(8,128)} %get-tuple-element.20), channel_id=1, source_target_pairs={{16,0},{24,8},{17,1},{25,9},{18,2},{26,10},{19,3},{27,11},{20,4},{... | collective-permute-start | bytes 221192 | tf_op jit(solution)/shard_map/ppermute | solution.py:196
  67.5 8.9 %collective-permute-start.3 = (f32[9,16,128]{2,1,0:T(8,128)}, f32[9,16,128]{2,1,0:T(8,128)S(1)}, u32[]{:S(2)}, u32[]{:S(2)}) collective-permute-start(f32[9,16,128]{2,1,0:T(8,128)} %get-tuple-element.20), channel_id=1, source_target_pairs={{8,0},{16,8},{24,16},{9,1},{17,9},{25,17},{10,2},{18,10},{26,18},{... | collective-permute-start | bytes 221192 | tf_op jit(solution)/shard_map/ppermute | solution.py:196
  73.4 3.0 %copy-start.3 = (f32[9,16,128]{2,1,0:T(8,128)}, f32[9,16,128]{2,1,0:T(8,128)S(1)}, u32[]{:S(2)}) copy-start(f32[9,16,128]{2,1,0:T(8,128)S(1)} %collective-permute-done.5.rest_2_) | copy-start | bytes 221188
  76.4 0.7 copy-start.5
  76.5 0.7 copy-start.7
Sparse Core Ops, SparseCore 0:
  9.7 28.3 all-gather.1
where the time goes:
time: 88.2 us; the launch traced here: 87.9 us
  Pallas kernels  29.8 us (34%)
  waiting for transfers between devices  21.1 us (24%)
  between operations  14.1 us (16%)
  starting transfers between devices  12.9 us (15%)
  local copies, waits for them, and re-layouts  9.05 us (10%)
  other arithmetic  0.93 us (1%)
    pallas_call x5, Pallas kernels, call(): pl.pallas_call(kernel, out_shape=[jax.ShapeDtypeStruct(shape, kind) for s...  29.8 us
    ppermute x6, starting transfers between devices, shifted(): return lax.ppermute(block, axis, route)  12.8 us
    all_gather x1, waiting for transfers between devices, local(): remote = lax.all_gather(outgoing, 'space', axis=0, tiled=True)  11.2 us
    ppermute x6, waiting for transfers between devices, shifted(): return lax.ppermute(block, axis, route)  9.87 us
    pad x3, local copies, waits for them, and re-layouts, local(): jnp.pad(weight, [(0, 0)] * (weight.ndim - 1) + [(0, LANES - size)])  4.02 us
    unnamed x18, local copies, waits for them, and re-layouts  3.99 us
  transfers between devices with their start and end apart: 7, of which 5 were waited for; matrix products, arithmetic and copies ran while one was open for 10% of the time, Pallas kernels for 9%

commit v1 on v0

v1 whole, which is shorter than its diff:
```python
import functools

import jax
import jax.numpy as jnp
from jax import lax
from jax.experimental import pallas as pl
from jax.experimental.pallas import tpu as pltpu
from jax.sharding import PartitionSpec as P

LANES = 128
VMEM_LIMIT = 20 * 1024 * 1024
CHUNKS = 2
TURNED = (((1,), (1,)), ((), ()))


def permutation(size, probes, start, width):
    total = size * probes
    column = lax.broadcasted_iota(jnp.int32, (total, width), 1) + start
    origin = (column % size) * probes + column // size
    row = lax.broadcasted_iota(jnp.int32, (total, width), 0)
    return (row == origin).astype(jnp.float32).astype(jnp.bfloat16)


def doubled(weight):
    zero = jnp.zeros_like(weight)
    return jnp.concatenate(
        [jnp.concatenate([weight, zero], axis=1), jnp.concatenate([zero, weight], axis=1)], axis=0
    )


def outgoing_kernel(dims, shared_ref, z_ref, *outgoing_refs):
    days, blocks, size, probes = dims
    count = outgoing_refs[0].shape[0]
    per_chunk = size * probes // LANES // len(outgoing_refs)
    z = z_ref[...].reshape(days * blocks, size * probes)
    row = lax.broadcasted_iota(jnp.int32, (days, days * blocks), 0)
    column = lax.broadcasted_iota(jnp.int32, (days, days * blocks), 1)
    picks = [
        (column == row * blocks + shared_ref[0, m]).astype(jnp.float32).astype(jnp.bfloat16) for m in range(count)
    ]
    picked = jnp.dot(jnp.concatenate(picks, axis=0), z, preferred_element_type=jnp.float32).astype(jnp.bfloat16)
    step = 2 * LANES
    for start in range(0, size * probes, step):
        moved = jnp.dot(picked, permutation(size, probes, start, step), preferred_element_type=jnp.float32)
        moved = moved.astype(jnp.bfloat16)
        for half in range(2):
            pair = start // LANES + half
            for m in range(count):
                outgoing_refs[pair // per_chunk][m, pl.ds(pair % per_chunk * days, days), :] = moved[
                    m * days : (m + 1) * days, half * LANES : (half + 1) * LANES
                ]


def local_kernel(
    dims, chunks, links_ref, days_ref, z_ref, weight_ref, remote_weight_ref, inverse_ref, retention_ref, *rest
):
    days, blocks, size, probes = dims
    pairs = size * probes // LANES
    per_chunk = pairs // chunks
    running_refs, moved_refs = rest[:chunks], rest[chunks : 2 * chunks]
    retain_ref, product_ref, remote_doubled_ref, inverse_doubled_ref, stage, turned = rest[2 * chunks :]
    count = links_ref.shape[0]
    z = z_ref[...].reshape(days * blocks, size * probes)
    step = 2 * LANES
    for start in range(0, size * probes, step):
        moved = jnp.dot(z, permutation(size, probes, start, step), preferred_element_type=jnp.float32)
        for half in range(2):
            pair = start // LANES + half
            tile = moved[:, half * LANES : (half + 1) * LANES]
            stage[pair] = tile
            moved_refs[pair // per_chunk][pair % per_chunk] = tile.astype(jnp.bfloat16)
    for block in range(blocks):
        for pair in range(pairs):
            rows = stage[pair, pl.ds(block, days, stride=blocks), :]
            turned[block, pl.ds(pair * days, days), :] = rows.astype(jnp.bfloat16)
    for block in range(blocks):
        near = jnp.concatenate([turned[links_ref[k, block]] for k in range(count)], axis=1)
        weight = jnp.concatenate([doubled(weight_ref[block, k]) for k in range(count)], axis=1)
        total = lax.dot_general(near, weight, TURNED, preferred_element_type=jnp.float32)
        running = turned[block].astype(jnp.float32) - total
        for chunk in range(chunks):
            part = per_chunk * days
            running_refs[chunk][block] = running[chunk * part : (chunk + 1) * part]
        remote_doubled_ref[block] = jnp.concatenate(
            [doubled(remote_weight_ref[block, k]) for k in range(remote_weight_ref.shape[1])], axis=1
        )
        inverse_doubled_ref[block] = doubled(inverse_ref[block])
    observed = days_ref[0]
    shape = (days, LANES)
    first = lax.broadcasted_iota(jnp.int32, shape, 1) < size
    seen = lax.broadcasted_iota(jnp.int32, shape, 0) < observed
    for block in range(0, blocks, 2):
        factor = jnp.where(seen, retention_ref[:, pl.ds(block * size, LANES)], 1.0)
        other = pltpu.roll(factor, size, 1)
        retain_ref[pl.ds(block, days, stride=blocks), :] = jnp.where(first, factor, other)
        retain_ref[pl.ds(block + 1, days, stride=blocks), :] = jnp.where(first, other, factor)
    product = jnp.ones((blocks, LANES), jnp.float32)
    for day in range(days):
        product = product * retain_ref[pl.ds(day * blocks, blocks), :]
    high = product.astype(jnp.bfloat16)
    product_ref[0] = high
    product_ref[1] = (product - high.astype(jnp.float32)).astype(jnp.bfloat16)


def forward_kernel(
    dims, links_ref, days_ref, running_ref, remote_ref, weight_ref, inverse_ref, retain_ref, product_ref,
    forcing_ref, message_ref,
):
    days, blocks, size, probes = dims
    pairs = forcing_ref.shape[0]
    count = links_ref.shape[0]
    seen = lax.broadcasted_iota(jnp.int32, (days, LANES), 0) < days_ref[0]
    for block in range(blocks):
        far = jnp.concatenate([remote_ref[links_ref[k, block]] for k in range(count)], axis=1)
        total = lax.dot_general(far, weight_ref[block], TURNED, preferred_element_type=jnp.float32)
        source = (running_ref[block] - total).astype(jnp.bfloat16)
        drive = lax.dot_general(source, inverse_ref[block], TURNED, preferred_element_type=jnp.float32)
        for pair in range(pairs):
            forcing_ref[pair, pl.ds(block, days, stride=blocks), :] = jnp.where(
                seen, drive[pair * days : (pair + 1) * days], 0.0
            )
    states = [jnp.zeros((blocks, LANES), jnp.float32)] * pairs
    for day in range(days):
        rows = pl.ds(day * blocks, blocks)
        factor = retain_ref[rows, :]
        for pair in range(pairs):
            states[pair] = factor * states[pair] + forcing_ref[pair, rows, :]
    leave(message_ref, states, product_ref)


def leave(message_ref, values, product_ref):
    for pair, value in enumerate(values):
        message_ref[pair] = value.astype(jnp.bfloat16)
    message_ref[len(values)] = product_ref[0]
    message_ref[len(values) + 1] = product_ref[1]


def carried(pairs, message_refs):
    carries = [message_refs[-1][pair].astype(jnp.float32) for pair in range(pairs)]
    for ref in reversed(message_refs[:-1]):
        factor = ref[pairs].astype(jnp.float32) + ref[pairs + 1].astype(jnp.float32)
        carries = [ref[pair].astype(jnp.float32) + factor * carries[pair] for pair in range(pairs)]
    return carries


def adjoint_kernel(dims, hops, days_ref, forcing_ref, retain_ref, product_ref, inverse_ref, *rest):
    days, blocks, size, probes = dims
    pairs = forcing_ref.shape[0]
    message_refs = rest[:hops]
    adjoint_ref, message_ref, stage = rest[hops:]
    seen = lax.broadcasted_iota(jnp.int32, (days, LANES), 0) < days_ref[0]
    states = carried(pairs, message_refs)
    for day in range(days):
        rows = pl.ds(day * blocks, blocks)
        factor = retain_ref[rows, :]
        for pair in range(pairs):
            states[pair] = factor * states[pair] + forcing_ref[pair, rows, :]
            stage[pair, rows, :] = states[pair]
    for block in range(blocks):
        stored = jnp.concatenate(
            [stage[pair, pl.ds(block, days, stride=blocks), :].astype(jnp.bfloat16) for pair in range(pairs)], axis=0
        )
        adjoint = jnp.dot(stored, inverse_ref[block], preferred_element_type=jnp.float32)
        for pair in range(pairs):
            adjoint_ref[pair, pl.ds(block, days, stride=blocks), :] = jnp.where(
                seen, adjoint[pair * days : (pair + 1) * days], 0.0
            )
    carries = [jnp.zeros((blocks, LANES), jnp.float32)] * pairs
    for day in reversed(range(days)):
        rows = pl.ds(day * blocks, blocks)
        factor = retain_ref[rows, :]
        for pair in range(pairs):
            carries[pair] = factor * (adjoint_ref[pair, rows, :] + carries[pair])
    leave(message_ref, carries, product_ref)


def variance_kernel(dims, hops, last, first, adjoint_ref, retain_ref, moved_ref, *rest):
    days, blocks, size, probes = dims
    pairs = adjoint_ref.shape[0]
    message_refs = rest[:hops]
    rest = rest[hops:]
    if not first:
        partial_ref, rest = rest[0], rest[1:]
    out_ref = rest[0]
    stage = rest[1] if last else out_ref
    carries = carried(pairs, message_refs)
    for day in reversed(range(days)):
        rows = pl.ds(day * blocks, blocks)
        factor = retain_ref[rows, :]
        total = None if first else partial_ref[rows, :]
        for pair in range(pairs):
            smoothed = adjoint_ref[pair, rows, :] + carries[pair]
            carries[pair] = factor * smoothed
            term = smoothed * moved_ref[pair, rows, :].astype(jnp.float32)
            total = term if total is None else total + term
        stage[rows, :] = total
    if last:
        lane = lax.broadcasted_iota(jnp.int32, (days, LANES), 1)
        for block in range(0, blocks, 2):
            both = [stage[pl.ds(block + half, days, stride=blocks), :] for half in range(2)]
            both = [value + pltpu.roll(value, size, 1) for value in both]
            out_ref[:, pl.ds(block * size, LANES)] = jnp.where(lane < size, both[0], both[1]) * (1.0 / probes)


def call(kernel, outs, scratch, flops, moved, scalars, *operands):
    in_specs = [
        pl.BlockSpec(memory_space=pltpu.SMEM if i < scalars else pltpu.VMEM) for i in range(len(operands))
    ]
    return pl.pallas_call(
        kernel,
        out_shape=[jax.ShapeDtypeStruct(shape, kind) for shape, kind in outs],
        in_specs=in_specs,
        out_specs=[pl.BlockSpec(memory_space=pltpu.VMEM) for _ in outs],
        scratch_shapes=scratch,
        compiler_params=pltpu.CompilerParams(vmem_limit_bytes=VMEM_LIMIT),
        cost_estimate=pl.CostEstimate(flops=flops, bytes_accessed=moved, transcendentals=0),
    )(*operands)


def shifted(block, axis, distance):
    count = lax.axis_size(axis)
    route = [(i, i + distance) for i in range(count) if 0 <= i + distance < count]
    return lax.ppermute(block, axis, route)


def local(
    probes,
    local_links,
    remote_links,
    shared_blocks,
    slab_days,
    local_coupling,
    remote_coupling,
    block_inverse,
    retention,
):
    days, blocks, width = probes.shape
    size = block_inverse.shape[1]
    dims = (days, blocks, size, width // size)
    pairs = width // LANES
    per_chunk = pairs // CHUNKS
    f32, bf16 = jnp.float32, jnp.bfloat16
    bound = shared_blocks.shape[1]
    far = remote_links.shape[1]
    tm_count = lax.axis_size("tm")
    hops = tm_count - 1
    rows = days * blocks
    near_table, far_table = local_links.T, remote_links.T

    outgoing = call(
        functools.partial(outgoing_kernel, dims),
        [((bound, per_chunk * days, LANES), bf16)] * CHUNKS,
        [], 10**9, 4 * 10**6, 1, shared_blocks, probes,
    )
    remote = [lax.all_gather(part, "space", axis=0, tiled=True) for part in outgoing]
    results = call(
        functools.partial(local_kernel, dims, CHUNKS),
        [((blocks, per_chunk * days, LANES), f32)] * CHUNKS
        + [((per_chunk, rows, LANES), bf16)] * CHUNKS
        + [
            ((rows, LANES), f32),
            ((2, blocks, LANES), bf16),
            ((blocks, LANES, far * LANES), bf16),
            ((blocks, LANES, LANES), bf16),
        ],
        [pltpu.VMEM((pairs, rows, LANES), f32), pltpu.VMEM((blocks, pairs * days, LANES), bf16)],
        10**10, 10**7, 2,
        near_table, slab_days, probes, local_coupling, remote_coupling, block_inverse, retention,
    )
    running, moved = results[:CHUNKS], results[CHUNKS : 2 * CHUNKS]
    retain, product, remote_weight, inverse = results[2 * CHUNKS :]
    message_shape = ((per_chunk + 2, blocks, LANES), bf16)
    partial = None
    for chunk in range(CHUNKS):
        forcing, message = call(
            functools.partial(forward_kernel, dims),
            [((per_chunk, rows, LANES), f32), message_shape],
            [], 10**10 // CHUNKS, 10**7 // CHUNKS, 2,
            far_table, slab_days, running[chunk], remote[chunk], remote_weight, inverse, retain, product,
        )
        received = [shifted(message, "tm", distance) for distance in range(1, tm_count)]
        adjoint, message = call(
            functools.partial(adjoint_kernel, dims, hops),
            [((per_chunk, rows, LANES), f32), message_shape],
            [pltpu.VMEM((per_chunk, rows, LANES), f32)], 10**10 // CHUNKS, 10**7 // CHUNKS, 1,
            slab_days, forcing, retain, product, inverse, *received,
        )
        received = [shifted(message, "tm", -distance) for distance in range(1, tm_count)]
        first, last = chunk == 0, chunk == CHUNKS - 1
        (partial,) = call(
            functools.partial(variance_kernel, dims, hops, last, first),
            [((days, blocks * size), f32) if last else ((rows, LANES), f32)],
            [pltpu.VMEM((rows, LANES), f32)] if last else [], 10**10 // CHUNKS, 10**7 // CHUNKS, 0,
            adjoint, retain, moved[chunk], *received, *([] if first else [partial]),
        )
    return partial


def solution(mesh):
    placed = (
        P("tm", "space", None),
        P("space", None),
        P("space", None),
        P("space", None),
        P("tm"),
        P("space", None, None, None),
        P("space", None, None, None),
        P("space", None, None),
        P("tm", "space"),
    )
    return jax.shard_map(
        local, mesh=mesh, in_specs=placed, out_specs=P("tm", "space"), check_vma=False
    )
```

time: 88.2 us -> 71.9 us (0.82)
  blocking collectives: 0 us -> 22.3 us
  waiting for transfers between devices: 21.1 us -> 7.74 us
  between operations: 14.1 us -> 0.91 us
  Pallas kernels: 29.8 us -> 17.6 us
  starting transfers between devices: 12.9 us -> 20.9 us
  local copies, waits for them, and re-layouts: 9.05 us -> 2.09 us
  other arithmetic: 0.93 us -> 0 us
    all_gather x0 -> x2, blocking collectives: none -> 22.3 us  [local(): lax.all_gather(part, 'space', axis=0, tiled=True)]
    pallas_call x5 -> x8, Pallas kernels: 29.8 us -> 17.6 us  [call(): pl.pallas_call(kernel, out_shape=[jax.ShapeDtypeStruct(shape, kind) for s...]
    all_gather x1 -> x0, waiting for transfers between devices: 11.2 us -> none  [local(): remote = lax.all_gather(outgoing, 'space', axis=0, tiled=True)]
    ppermute x6 -> x12, starting transfers between devices: 12.8 us -> 20.9 us  [shifted(): return lax.ppermute(block, axis, route)]
    pad x3 -> x0, local copies, waits for them, and re-layouts: 4.02 us -> none  [local(): jnp.pad(weight, [(0, 0)] * (weight.ndim - 1) + [(0, LANES - size)])]
    ppermute x6 -> x12, waiting for transfers between devices: 9.87 us -> 7.74 us  [shifted(): return lax.ppermute(block, axis, route)]
    unnamed x18, local copies, waits for them, and re-layouts: 3.99 us -> 2.09 us
    reshape x1 -> x0, local copies, waits for them, and re-layouts: 1.04 us -> none  [local(): retention_rows = retention.reshape(rows, size)]
  transfers between devices with their start and end apart: 7 -> 12, of which waited for: 5 -> 3; matrix products, arithmetic and copies ran while one was open for 10% -> 0% of each run, Pallas kernels for 9% -> 9%
where the time goes in v1:
time: 71.9 us; the launch traced here: 71.5 us
  blocking collectives  22.3 us (31%)
  starting transfers between devices  20.9 us (29%)
  Pallas kernels  17.6 us (24%)
  waiting for transfers between devices  7.74 us (11%)
  local copies, waits for them, and re-layouts  2.09 us (3%)
  between operations  0.91 us (1%)
    all_gather x2, blocking collectives, local(): lax.all_gather(part, 'space', axis=0, tiled=True)  22.3 us
    ppermute x12, starting transfers between devices, shifted(): return lax.ppermute(block, axis, route)  20.9 us
    pallas_call x8, Pallas kernels, call(): pl.pallas_call(kernel, out_shape=[jax.ShapeDtypeStruct(shape, kind) for s...  17.6 us
    ppermute x12, waiting for transfers between devices, shifted(): return lax.ppermute(block, axis, route)  7.74 us
    unnamed x18, local copies, waits for them, and re-layouts  2.09 us
  transfers between devices with their start and end apart: 12, of which 3 were waited for; matrix products, arithmetic and copies ran while one was open for 0% of the time, Pallas kernels for 9%

profile of v1, /device:TPU:0, one launch (start us, length us, event | category | flops | bytes accessed | tf_op | source)
XLA Modules:
  0.0 71.5 jit_solution(6687082530093794562)
XLA Ops:
  0.7 0.0 copy-start
  0.7 1.4 %copy-done = bf16[48,16,1024]{2,1,0:T(8,128)(2,1)S(1)} copy-done((bf16[48,16,1024]{2,1,0:T(8,128)(2,1)S(1)}, bf16[48,16,1024]{2,1,0:T(8,128)(2,1)}, u32[]{:S(2)}) %copy-start) | copy-done | bytes 1572888
  2.1 0.0 copy-start.8
  2.1 0.7 copy-done.8
  2.7 0.0 copy-start.1
  2.7 0.0 copy-start.2
  2.7 0.0 copy-start.3
  2.7 0.0 copy-start.4
  2.7 0.0 copy-start.5
  2.7 0.0 copy-start.6
  2.7 1.3 %shard_map.92 = (bf16[2,192,128]{2,1,0:T(8,128)(2,1)S(1)}, bf16[2,192,128]{2,1,0:T(8,128)(2,1)S(1)}) custom-call(s32[1,2]{1,0:T(1,128)S(1)} %copy-done.8, bf16[48,16,1024]{2,1,0:T(8,128)(2,1)S(1)} %copy-done), custom_call_target="tpu_custom_call" | custom-call | flops 1000000000 | bytes 4000000 | tf_op jit(solution)/shard_map/pallas_call | solution.py:209
  4.1 11.9 %all_gather.7.remote_ref = bf16[16,192,128]{2,1,0:T(8,128)(2,1)S(1)} all-gather(bf16[2,192,128]{2,1,0:T(8,128)(2,1)S(1)} %get-tuple-element.35), channel_id=1, replica_groups=mesh['tm'=4,'space'=8] {'space'}, dimensions={0}, use_global_device_ids=true | all-gather | bytes 884736 | tf_op jit(solution)/shard_map/all_gather | solution.py:255
  15.9 0.0 copy-done.1
  15.9 0.0 copy-done.2
  15.9 0.0 copy-done.3
  15.9 0.0 copy-done.4
  15.9 0.0 copy-done.5
  16.0 0.0 copy-done.6
  16.0 0.0 copy-start.7
  16.0 5.0 %shard_map.91 = (f32[16,192,128]{2,1,0:T(8,128)S(1)}, f32[16,192,128]{2,1,0:T(8,128)S(1)}, bf16[4,768,128]{2,1,0:T(8,128)(2,1)S(1)}, bf16[4,768,128]{2,1,0:T(8,1...) custom-call(s32[4,16]{1,0:T(4,128)S(1)} %bitcast.2, ...), custom_call_target="tpu_custom_call" | custom-call | flops 10000000000 | bytes 10000000 | tf_op jit(solution)/shard_map/pallas_call | solution.py:209
  20.9 0.0 copy-done.7
  21.0 3.5 %shard_map.95 = (f32[4,768,128]{2,1,0:T(8,128)S(1)}, bf16[6,16,128]{2,1,0:T(8,128)(2,1)S(1)}) custom-call(s32[2,16]{1,0:T(2,128)S(1)} %bitcast.3, s32[1]{0:T(128)S(6)} %copy.10.days_ref, f32[16,192,128]{2,1,0:T(8,128)S(1)} %get-tuple-element.34.running_ref, bf16[16,192,128]{2,1,0:T(8,128)(2,1)S(1)} %all_gather.7.remote_ref, ...), custom_call_target="tpu_custom_call" | custom-call | flops 5000000000 | bytes 5000000 | tf_op jit(solution)/shard_map/pallas_call | solution.py:209
  24.5 3.5 %collective-permute-start.6 = (bf16[6,16,128]{2,1,0:T(8,128)(2,1)S(1)}, bf16[6,16,128]{2,1,0:T(8,128)(2,1)S(1)}, u32[]{:S(2)}, u32[]{:S(2)}) collective-permute-start(bf16[6,16,128]{2,1,0:T(8,128)(2,1)S(1)} %get-tuple-element.37), channel_id=1, source_target_pairs={{0,8},{8,16},{16,24},{1,9},{9,17},{17,25},{2,10},{10,18},{18,26},{... | collective-permute-start | bytes 73736 | tf_op jit(solution)/shard_map/ppermute | solution.py:223
  28.0 4.5 %collective-permute-start.7 = (bf16[6,16,128]{2,1,0:T(8,128)(2,1)S(1)}, bf16[6,16,128]{2,1,0:T(8,128)(2,1)S(1)}, u32[]{:S(2)}, u32[]{:S(2)}) collective-permute-start(bf16[6,16,128]{2,1,0:T(8,128)(2,1)S(1)} %get-tuple-element.37), channel_id=1, source_target_pairs={{0,16},{8,24},{1,17},{9,25},{2,18},{10,26},{3,19},{11,27},{4,20},{... | collective-permute-start | bytes 73736 | tf_op jit(solution)/shard_map/ppermute | solution.py:223
  32.5 1.3 %collective-permute-start.8 = (bf16[6,16,128]{2,1,0:T(8,128)(2,1)S(1)}, bf16[6,16,128]{2,1,0:T(8,128)(2,1)S(1)}, u32[]{:S(2)}, u32[]{:S(2)}) collective-permute-start(bf16[6,16,128]{2,1,0:T(8,128)(2,1)S(1)} %get-tuple-element.37), channel_id=1, source_target_pairs={{0,24},{1,25},{2,26},{3,27},{4,28},{5,29},{6,30},{7,31}} | collective-permute-start | bytes 73736 | tf_op jit(solution)/shard_map/ppermute | solution.py:223
  33.8 10.4 %all_gather.6.remote_ref = bf16[16,192,128]{2,1,0:T(8,128)(2,1)S(1)} all-gather(bf16[2,192,128]{2,1,0:T(8,128)(2,1)S(1)} %get-tuple-element.24), channel_id=1, replica_groups=mesh['tm'=4,'space'=8] {'space'}, dimensions={0}, use_global_device_ids=true | all-gather | bytes 884736 | tf_op jit(solution)/shard_map/all_gather | solution.py:255
  44.2 3.5 %shard_map.93 = (f32[4,768,128]{2,1,0:T(8,128)S(1)}, bf16[6,16,128]{2,1,0:T(8,128)(2,1)S(1)}) custom-call(s32[2,16]{1,0:T(2,128)S(1)} %bitcast.4, s32[1]{0:T(128)S(6)} %copy.10.days_ref, f32[16,192,128]{2,1,0:T(8,128)S(1)} %get-tuple-element.23.running_ref, bf16[16,192,128]{2,1,0:T(8,128)(2,1)S(1)} %all_gather.6.remote_ref, ...), custom_call_target="tpu_custom_call" | custom-call | flops 5000000000 | bytes 5000000 | tf_op jit(solution)/shard_map/pallas_call | solution.py:209
  47.7 1.3 %collective-permute-start = (bf16[6,16,128]{2,1,0:T(8,128)(2,1)S(1)}, bf16[6,16,128]{2,1,0:T(8,128)(2,1)S(1)}, u32[]{:S(2)}, u32[]{:S(2)}) collective-permute-start(bf16[6,16,128]{2,1,0:T(8,128)(2,1)S(1)} %get-tuple-element.30), channel_id=1, source_target_pairs={{0,8},{8,16},{16,24},{1,9},{9,17},{17,25},{2,10},{10,18},{18,26},{... | collective-permute-start | bytes 73736 | tf_op jit(solution)/shard_map/ppermute | solution.py:223
  49.0 1.3 %collective-permute-start.1 = (bf16[6,16,128]{2,1,0:T(8,128)(2,1)S(1)}, bf16[6,16,128]{2,1,0:T(8,128)(2,1)S(1)}, u32[]{:S(2)}, u32[]{:S(2)}) collective-permute-start(bf16[6,16,128]{2,1,0:T(8,128)(2,1)S(1)} %get-tuple-element.30), channel_id=1, source_target_pairs={{0,16},{8,24},{1,17},{9,25},{2,18},{10,26},{3,19},{11,27},{4,20},{... | collective-permute-start | bytes 73736 | tf_op jit(solution)/shard_map/ppermute | solution.py:223
  50.3 0.0 collective-permute-done.6.rest_0_
  50.3 1.3 %collective-permute-start.2 = (bf16[6,16,128]{2,1,0:T(8,128)(2,1)S(1)}, bf16[6,16,128]{2,1,0:T(8,128)(2,1)S(1)}, u32[]{:S(2)}, u32[]{:S(2)}) collective-permute-start(bf16[6,16,128]{2,1,0:T(8,128)(2,1)S(1)} %get-tuple-element.30), channel_id=1, source_target_pairs={{0,24},{1,25},{2,26},{3,27},{4,28},{5,29},{6,30},{7,31}} | collective-permute-start | bytes 73736 | tf_op jit(solution)/shard_map/ppermute | solution.py:223
  51.6 0.0 collective-permute-done.7.rest_1_
  51.7 0.0 collective-permute-done.8.rest_2_
  51.7 1.4 %shard_map.96 = (f32[4,768,128]{2,1,0:T(8,128)S(1)}, bf16[6,16,128]{2,1,0:T(8,128)(2,1)S(1)}) custom-call(s32[1]{0:T(128)S(6)} %copy.10.days_ref, f32[4,768,128]{2,1,0:T(8,128)S(1)} %get-tuple-element.36.forcing_ref, f32[768,128]{1,0:T(8,128)S(1)} %get-tuple-element.27.retain_ref, bf16[2,16,128]{2,1,0:T(8,128)(2,1)S(1)} %get-tuple-element.28.product_ref, ...), custom_call_target="tpu_custom_call" | custom-call | flops 5000000000 | bytes 5000000 | tf_op jit(solution)/shard_map/pallas_call | solution.py:209
  53.1 1.3 %collective-permute-start.10 = (bf16[6,16,128]{2,1,0:T(8,128)(2,1)S(1)}, bf16[6,16,128]{2,1,0:T(8,128)(2,1)S(1)}, u32[]{:S(2)}, u32[]{:S(2)}) collective-permute-start(bf16[6,16,128]{2,1,0:T(8,128)(2,1)S(1)} %get-tuple-element.40), channel_id=1, source_target_pairs={{16,0},{24,8},{17,1},{25,9},{18,2},{26,10},{19,3},{27,11},{20,4},{... | collective-permute-start | bytes 73736 | tf_op jit(solution)/shard_map/ppermute | solution.py:223
  54.4 1.3 %collective-permute-start.11 = (bf16[6,16,128]{2,1,0:T(8,128)(2,1)S(1)}, bf16[6,16,128]{2,1,0:T(8,128)(2,1)S(1)}, u32[]{:S(2)}, u32[]{:S(2)}) collective-permute-start(bf16[6,16,128]{2,1,0:T(8,128)(2,1)S(1)} %get-tuple-element.40), channel_id=1, source_target_pairs={{24,0},{25,1},{26,2},{27,3},{28,4},{29,5},{30,6},{31,7}} | collective-permute-start | bytes 73736 | tf_op jit(solution)/shard_map/ppermute | solution.py:223
  55.7 0.0 collective-permute-done.rest_0_
  55.7 1.3 %collective-permute-start.9 = (bf16[6,16,128]{2,1,0:T(8,128)(2,1)S(1)}, bf16[6,16,128]{2,1,0:T(8,128)(2,1)S(1)}, u32[]{:S(2)}, u32[]{:S(2)}) collective-permute-start(bf16[6,16,128]{2,1,0:T(8,128)(2,1)S(1)} %get-tuple-element.40), channel_id=1, source_target_pairs={{8,0},{16,8},{24,16},{9,1},{17,9},{25,17},{10,2},{18,10},{26,18},{... | collective-permute-start | bytes 73736 | tf_op jit(solution)/shard_map/ppermute | solution.py:223
  57.0 0.0 collective-permute-done.1.rest_1_
  57.0 0.0 collective-permute-done.2.rest_2_
  57.0 1.4 %shard_map.94 = (f32[4,768,128]{2,1,0:T(8,128)S(1)}, bf16[6,16,128]{2,1,0:T(8,128)(2,1)S(1)}) custom-call(s32[1]{0:T(128)S(6)} %copy.10.days_ref, f32[4,768,128]{2,1,0:T(8,128)S(1)} %get-tuple-element.29.forcing_ref, f32[768,128]{1,0:T(8,128)S(1)} %get-tuple-element.27.retain_ref, bf16[2,16,128]{2,1,0:T(8,128)(2,1)S(1)} %get-tuple-element.28.product_ref, ...), custom_call_target="tpu_custom_call" | custom-call | flops 5000000000 | bytes 5000000 | tf_op jit(solution)/shard_map/pallas_call | solution.py:209
  58.4 1.3 %collective-permute-start.3 = (bf16[6,16,128]{2,1,0:T(8,128)(2,1)S(1)}, bf16[6,16,128]{2,1,0:T(8,128)(2,1)S(1)}, u32[]{:S(2)}, u32[]{:S(2)}) collective-permute-start(bf16[6,16,128]{2,1,0:T(8,128)(2,1)S(1)} %get-tuple-element.33), channel_id=1, source_target_pairs={{8,0},{16,8},{24,16},{9,1},{17,9},{25,17},{10,2},{18,10},{26,18},{... | collective-permute-start | bytes 73736 | tf_op jit(solution)/shard_map/ppermute | solution.py:223
  59.7 1.3 %collective-permute-start.4 = (bf16[6,16,128]{2,1,0:T(8,128)(2,1)S(1)}, bf16[6,16,128]{2,1,0:T(8,128)(2,1)S(1)}, u32[]{:S(2)}, u32[]{:S(2)}) collective-permute-start(bf16[6,16,128]{2,1,0:T(8,128)(2,1)S(1)} %get-tuple-element.33), channel_id=1, source_target_pairs={{16,0},{24,8},{17,1},{25,9},{18,2},{26,10},{19,3},{27,11},{20,4},{... | collective-permute-start | bytes 73736 | tf_op jit(solution)/shard_map/ppermute | solution.py:223
  61.0 0.0 collective-permute-done.10.rest_1_
  61.0 1.3 %collective-permute-start.5 = (bf16[6,16,128]{2,1,0:T(8,128)(2,1)S(1)}, bf16[6,16,128]{2,1,0:T(8,128)(2,1)S(1)}, u32[]{:S(2)}, u32[]{:S(2)}) collective-permute-start(bf16[6,16,128]{2,1,0:T(8,128)(2,1)S(1)} %get-tuple-element.33), channel_id=1, source_target_pairs={{24,0},{25,1},{26,2},{27,3},{28,4},{29,5},{30,6},{31,7}} | collective-permute-start | bytes 73736 | tf_op jit(solution)/shard_map/ppermute | solution.py:223
  62.3 0.0 collective-permute-done.11.rest_2_
  62.3 0.0 collective-permute-done.9.rest_0_
  62.3 0.3 shard_map.97.rest_3_
  62.6 2.1 %collective-permute-done.3.rest_0_ = bf16[6,16,128]{2,1,0:T(8,128)(2,1)S(1)} collective-permute-done((bf16[6,16,128]{2,1,0:T(8,128)(2,1)S(1)}, bf16[6,16,128]{2,1,0:T(8,128)(2,1)S(1)}, u32[]{:S(2)}, u32[]{:S(2)}) %collective-permute-start.3) | collective-permute-done | bytes 24608 | tf_op jit(solution)/shard_map/ppermute | solution.py:223
  64.8 2.8 %collective-permute-done.4.rest_1_ = bf16[6,16,128]{2,1,0:T(8,128)(2,1)S(1)} collective-permute-done((bf16[6,16,128]{2,1,0:T(8,128)(2,1)S(1)}, bf16[6,16,128]{2,1,0:T(8,128)(2,1)S(1)}, u32[]{:S(2)}, u32[]{:S(2)}) %collective-permute-start.4) | collective-permute-done | bytes 24608 | tf_op jit(solution)/shard_map/ppermute | solution.py:223
  67.5 2.8 %collective-permute-done.5.rest_2_ = bf16[6,16,128]{2,1,0:T(8,128)(2,1)S(1)} collective-permute-done((bf16[6,16,128]{2,1,0:T(8,128)(2,1)S(1)}, bf16[6,16,128]{2,1,0:T(8,128)(2,1)S(1)}, u32[]{:S(2)}, u32[]{:S(2)}) %collective-permute-start.5) | collective-permute-done | bytes 24608 | tf_op jit(solution)/shard_map/ppermute | solution.py:223
  70.4 1.1 %shard_map.98 = f32[48,1024]{1,0:T(8,128)} custom-call(f32[4,768,128]{2,1,0:T(8,128)S(1)} %get-tuple-element.31.adjoint_ref, f32[768,128]{1,0:T(8,128)S(1)} %get-tuple-element.27.retain_ref, bf16[4,768,128]{2,1,0:T(8,128)(2,1)S(1)} %get-tuple-element.32.moved_ref, bf16[6,16,128]{2,1,0:T(8,128)(2,1)S(1)} %collective-permute-done.3.rest_0_, ...), custom_call_target="tpu_custom_call" | custom-call | flops 5000000000 | bytes 5000000 | tf_op jit(solution)/shard_map/pallas_call | solution.py:209
Async XLA Ops:
  0.7 1.4 %copy-start = (bf16[48,16,1024]{2,1,0:T(8,128)(2,1)S(1)}, bf16[48,16,1024]{2,1,0:T(8,128)(2,1)}, u32[]{:S(2)}) copy-start(bf16[48,16,1024]{2,1,0:T(8,128)(2,1)} %z_ref.3) | copy-start | bytes 4718596
  2.1 0.7 copy-start.8
  2.7 13.2 %copy-start.1 = (bf16[48,16,1024]{2,1,0:T(8,128)(2,1)S(1)}, bf16[48,16,1024]{2,1,0:T(8,128)(2,1)}, u32[]{:S(2)}) copy-start(bf16[48,16,1024]{2,1,0:T(8,128)(2,1)} %z_ref.3) | copy-start | bytes 4718596
  2.7 13.2 %copy-start.2 = (bf16[16,4,64,64]{3,2,1,0:T(8,128)(2,1)S(1)}, bf16[16,4,64,64]{3,2,1,0:T(8,128)(2,1)}, u32[]{:S(2)}) copy-start(bf16[16,4,64,64]{3,2,1,0:T(8,128)(2,1)} %weight_ref.1) | copy-start | bytes 1572868
  2.7 13.2 %copy-start.3 = (bf16[16,2,64,64]{3,2,1,0:T(8,128)(2,1)S(1)}, bf16[16,2,64,64]{3,2,1,0:T(8,128)(2,1)}, u32[]{:S(2)}) copy-start(bf16[16,2,64,64]{3,2,1,0:T(8,128)(2,1)} %remote_weight_ref.1) | copy-start | bytes 786436
  2.7 13.2 %copy-start.4 = (bf16[16,64,64]{2,1,0:T(8,128)(2,1)S(1)}, bf16[16,64,64]{2,1,0:T(8,128)(2,1)}, u32[]{:S(2)}) copy-start(bf16[16,64,64]{2,1,0:T(8,128)(2,1)} %inverse_ref.1) | copy-start | bytes 393220
  2.7 13.2 %copy-start.5 = (f32[48,1024]{1,0:T(8,128)S(1)}, f32[48,1024]{1,0:T(8,128)}, u32[]{:S(2)}) copy-start(f32[48,1024]{1,0:T(8,128)} %retention_ref.1) | copy-start | bytes 589828
  2.7 13.2 %copy-start.6 = (s32[16,4]{0,1:T(4,128)S(1)}, s32[16,4]{0,1:T(4,128)}, u32[]{:S(2)}) copy-start(s32[16,4]{0,1:T(4,128)} %param.10) | copy-start | bytes 772
  16.0 5.0 %copy-start.7 = (s32[16,2]{0,1:T(2,128)S(1)}, s32[16,2]{0,1:T(2,128)}, u32[]{:S(2)}) copy-start(s32[16,2]{0,1:T(2,128)} %param.11) | copy-start | bytes 388
  24.5 25.8 %collective-permute-start.6 = (bf16[6,16,128]{2,1,0:T(8,128)(2,1)S(1)}, bf16[6,16,128]{2,1,0:T(8,128)(2,1)S(1)}, u32[]{:S(2)}, u32[]{:S(2)}) collective-permute-start(bf16[6,16,128]{2,1,0:T(8,128)(2,1)S(1)} %get-tuple-element.37), channel_id=1, source_target_pairs={{0,8},{8,16},{16,24},{1,9},{9,17},{17,25},{2,10},{10,18},{18,26},{... | collective-permute-start | bytes 73736 | tf_op jit(solution)/shard_map/ppermute | solution.py:223
  28.0 23.6 %collective-permute-start.7 = (bf16[6,16,128]{2,1,0:T(8,128)(2,1)S(1)}, bf16[6,16,128]{2,1,0:T(8,128)(2,1)S(1)}, u32[]{:S(2)}, u32[]{:S(2)}) collective-permute-start(bf16[6,16,128]{2,1,0:T(8,128)(2,1)S(1)} %get-tuple-element.37), channel_id=1, source_target_pairs={{0,16},{8,24},{1,17},{9,25},{2,18},{10,26},{3,19},{11,27},{4,20},{... | collective-permute-start | bytes 73736 | tf_op jit(solution)/shard_map/ppermute | solution.py:223
  32.5 19.1 %collective-permute-start.8 = (bf16[6,16,128]{2,1,0:T(8,128)(2,1)S(1)}, bf16[6,16,128]{2,1,0:T(8,128)(2,1)S(1)}, u32[]{:S(2)}, u32[]{:S(2)}) collective-permute-start(bf16[6,16,128]{2,1,0:T(8,128)(2,1)S(1)} %get-tuple-element.37), channel_id=1, source_target_pairs={{0,24},{1,25},{2,26},{3,27},{4,28},{5,29},{6,30},{7,31}} | collective-permute-start | bytes 73736 | tf_op jit(solution)/shard_map/ppermute | solution.py:223
  47.7 8.0 %collective-permute-start = (bf16[6,16,128]{2,1,0:T(8,128)(2,1)S(1)}, bf16[6,16,128]{2,1,0:T(8,128)(2,1)S(1)}, u32[]{:S(2)}, u32[]{:S(2)}) collective-permute-start(bf16[6,16,128]{2,1,0:T(8,128)(2,1)S(1)} %get-tuple-element.30), channel_id=1, source_target_pairs={{0,8},{8,16},{16,24},{1,9},{9,17},{17,25},{2,10},{10,18},{18,26},{... | collective-permute-start | bytes 73736 | tf_op jit(solution)/shard_map/ppermute | solution.py:223
  49.0 8.0 %collective-permute-start.1 = (bf16[6,16,128]{2,1,0:T(8,128)(2,1)S(1)}, bf16[6,16,128]{2,1,0:T(8,128)(2,1)S(1)}, u32[]{:S(2)}, u32[]{:S(2)}) collective-permute-start(bf16[6,16,128]{2,1,0:T(8,128)(2,1)S(1)} %get-tuple-element.30), channel_id=1, source_target_pairs={{0,16},{8,24},{1,17},{9,25},{2,18},{10,26},{3,19},{11,27},{4,20},{... | collective-permute-start | bytes 73736 | tf_op jit(solution)/shard_map/ppermute | solution.py:223
  50.3 6.7 %collective-permute-start.2 = (bf16[6,16,128]{2,1,0:T(8,128)(2,1)S(1)}, bf16[6,16,128]{2,1,0:T(8,128)(2,1)S(1)}, u32[]{:S(2)}, u32[]{:S(2)}) collective-permute-start(bf16[6,16,128]{2,1,0:T(8,128)(2,1)S(1)} %get-tuple-element.30), channel_id=1, source_target_pairs={{0,24},{1,25},{2,26},{3,27},{4,28},{5,29},{6,30},{7,31}} | collective-permute-start | bytes 73736 | tf_op jit(solution)/shard_map/ppermute | solution.py:223
  53.1 7.9 %collective-permute-start.10 = (bf16[6,16,128]{2,1,0:T(8,128)(2,1)S(1)}, bf16[6,16,128]{2,1,0:T(8,128)(2,1)S(1)}, u32[]{:S(2)}, u32[]{:S(2)}) collective-permute-start(bf16[6,16,128]{2,1,0:T(8,128)(2,1)S(1)} %get-tuple-element.40), channel_id=1, source_target_pairs={{16,0},{24,8},{17,1},{25,9},{18,2},{26,10},{19,3},{27,11},{20,4},{... | collective-permute-start | bytes 73736 | tf_op jit(solution)/shard_map/ppermute | solution.py:223
  54.4 7.9 %collective-permute-start.11 = (bf16[6,16,128]{2,1,0:T(8,128)(2,1)S(1)}, bf16[6,16,128]{2,1,0:T(8,128)(2,1)S(1)}, u32[]{:S(2)}, u32[]{:S(2)}) collective-permute-start(bf16[6,16,128]{2,1,0:T(8,128)(2,1)S(1)} %get-tuple-element.40), channel_id=1, source_target_pairs={{24,0},{25,1},{26,2},{27,3},{28,4},{29,5},{30,6},{31,7}} | collective-permute-start | bytes 73736 | tf_op jit(solution)/shard_map/ppermute | solution.py:223
  55.7 6.6 %collective-permute-start.9 = (bf16[6,16,128]{2,1,0:T(8,128)(2,1)S(1)}, bf16[6,16,128]{2,1,0:T(8,128)(2,1)S(1)}, u32[]{:S(2)}, u32[]{:S(2)}) collective-permute-start(bf16[6,16,128]{2,1,0:T(8,128)(2,1)S(1)} %get-tuple-element.40), channel_id=1, source_target_pairs={{8,0},{16,8},{24,16},{9,1},{17,9},{25,17},{10,2},{18,10},{26,18},{... | collective-permute-start | bytes 73736 | tf_op jit(solution)/shard_map/ppermute | solution.py:223
  58.4 6.3 %collective-permute-start.3 = (bf16[6,16,128]{2,1,0:T(8,128)(2,1)S(1)}, bf16[6,16,128]{2,1,0:T(8,128)(2,1)S(1)}, u32[]{:S(2)}, u32[]{:S(2)}) collective-permute-start(bf16[6,16,128]{2,1,0:T(8,128)(2,1)S(1)} %get-tuple-element.33), channel_id=1, source_target_pairs={{8,0},{16,8},{24,16},{9,1},{17,9},{25,17},{10,2},{18,10},{26,18},{... | collective-permute-start | bytes 73736 | tf_op jit(solution)/shard_map/ppermute | solution.py:223
  59.7 7.8 %collective-permute-start.4 = (bf16[6,16,128]{2,1,0:T(8,128)(2,1)S(1)}, bf16[6,16,128]{2,1,0:T(8,128)(2,1)S(1)}, u32[]{:S(2)}, u32[]{:S(2)}) collective-permute-start(bf16[6,16,128]{2,1,0:T(8,128)(2,1)S(1)} %get-tuple-element.33), channel_id=1, source_target_pairs={{16,0},{24,8},{17,1},{25,9},{18,2},{26,10},{19,3},{27,11},{20,4},{... | collective-permute-start | bytes 73736 | tf_op jit(solution)/shard_map/ppermute | solution.py:223
  61.0 9.3 %collective-permute-start.5 = (bf16[6,16,128]{2,1,0:T(8,128)(2,1)S(1)}, bf16[6,16,128]{2,1,0:T(8,128)(2,1)S(1)}, u32[]{:S(2)}, u32[]{:S(2)}) collective-permute-start(bf16[6,16,128]{2,1,0:T(8,128)(2,1)S(1)} %get-tuple-element.33), channel_id=1, source_target_pairs={{24,0},{25,1},{26,2},{27,3},{28,4},{29,5},{30,6},{31,7}} | collective-permute-start | bytes 73736 | tf_op jit(solution)/shard_map/ppermute | solution.py:223

commit v2 on v1

v2 whole, which is shorter than its diff:
```python
import functools

import jax
import jax.numpy as jnp
from jax import lax
from jax.experimental import pallas as pl
from jax.experimental.pallas import tpu as pltpu
from jax.sharding import PartitionSpec as P

LANES = 128
VMEM_LIMIT = 20 * 1024 * 1024
TURNED = (((1,), (1,)), ((), ()))


def permutation(size, probes, start, width):
    total = size * probes
    column = lax.broadcasted_iota(jnp.int32, (total, width), 1) + start
    origin = (column % size) * probes + column // size
    row = lax.broadcasted_iota(jnp.int32, (total, width), 0)
    return (row == origin).astype(jnp.float32).astype(jnp.bfloat16)


def doubled(weight):
    zero = jnp.zeros_like(weight)
    return jnp.concatenate(
        [jnp.concatenate([weight, zero], axis=1), jnp.concatenate([zero, weight], axis=1)], axis=0
    )


def outgoing_kernel(dims, shared_ref, z_ref, outgoing_ref):
    days, blocks, size, probes = dims
    count = outgoing_ref.shape[0]
    z = z_ref[...].reshape(days * blocks, size * probes)
    row = lax.broadcasted_iota(jnp.int32, (days, days * blocks), 0)
    column = lax.broadcasted_iota(jnp.int32, (days, days * blocks), 1)
    picks = [
        (column == row * blocks + shared_ref[0, m]).astype(jnp.float32).astype(jnp.bfloat16) for m in range(count)
    ]
    picked = jnp.dot(jnp.concatenate(picks, axis=0), z, preferred_element_type=jnp.float32).astype(jnp.bfloat16)
    step = 2 * LANES
    for start in range(0, size * probes, step):
        moved = jnp.dot(picked, permutation(size, probes, start, step), preferred_element_type=jnp.float32)
        moved = moved.astype(jnp.bfloat16)
        for half in range(2):
            pair = start // LANES + half
            for m in range(count):
                outgoing_ref[m, pl.ds(pair * days, days), :] = moved[
                    m * days : (m + 1) * days, half * LANES : (half + 1) * LANES
                ]


def local_kernel(
    dims, links_ref, days_ref, z_ref, weight_ref, remote_weight_ref, inverse_ref, retention_ref,
    running_ref, moved_ref, retain_ref, product_ref, remote_doubled_ref, inverse_doubled_ref, stage, turned,
):
    days, blocks, size, probes = dims
    pairs = size * probes // LANES
    count = links_ref.shape[0]
    z = z_ref[...].reshape(days * blocks, size * probes)
    step = 2 * LANES
    for start in range(0, size * probes, step):
        moved = jnp.dot(z, permutation(size, probes, start, step), preferred_element_type=jnp.float32)
        for half in range(2):
            pair = start // LANES + half
            tile = moved[:, half * LANES : (half + 1) * LANES]
            stage[pair] = tile
            moved_ref[pair] = tile.astype(jnp.bfloat16)
    for block in range(blocks):
        for pair in range(pairs):
            rows = stage[pair, pl.ds(block, days, stride=blocks), :]
            turned[block, pl.ds(pair * days, days), :] = rows.astype(jnp.bfloat16)
    for block in range(blocks):
        near = jnp.concatenate([turned[links_ref[k, block]] for k in range(count)], axis=1)
        weight = jnp.concatenate([doubled(weight_ref[block, k]) for k in range(count)], axis=1)
        total = lax.dot_general(near, weight, TURNED, preferred_element_type=jnp.float32)
        running_ref[block] = turned[block].astype(jnp.float32) - total
        remote_doubled_ref[block] = jnp.concatenate(
            [doubled(remote_weight_ref[block, k]) for k in range(remote_weight_ref.shape[1])], axis=1
        )
        inverse_doubled_ref[block] = doubled(inverse_ref[block])
    observed = days_ref[0]
    shape = (days, LANES)
    first = lax.broadcasted_iota(jnp.int32, shape, 1) < size
    seen = lax.broadcasted_iota(jnp.int32, shape, 0) < observed
    for block in range(0, blocks, 2):
        factor = jnp.where(seen, retention_ref[:, pl.ds(block * size, LANES)], 1.0)
        other = pltpu.roll(factor, size, 1)
        retain_ref[pl.ds(block, days, stride=blocks), :] = jnp.where(first, factor, other)
        retain_ref[pl.ds(block + 1, days, stride=blocks), :] = jnp.where(first, other, factor)
    product = jnp.ones((blocks, LANES), jnp.float32)
    for day in range(days):
        product = product * retain_ref[pl.ds(day * blocks, blocks), :]
    high = product.astype(jnp.bfloat16)
    product_ref[0] = high
    product_ref[1] = (product - high.astype(jnp.float32)).astype(jnp.bfloat16)


def assemble_kernel(*refs):
    *piece_refs, product_ref, out_ref = refs
    count = piece_refs[0].shape[0]
    for i, ref in enumerate(piece_refs):
        out_ref[pl.ds(i * count, count)] = ref[...]


def forward_kernel(
    dims, links_ref, days_ref, running_ref, same_ref, other_ref, weight_ref, inverse_ref, retain_ref, product_ref,
    forcing_ref, message_ref, remote,
):
    days, blocks, size, probes = dims
    pairs = forcing_ref.shape[0]
    count = links_ref.shape[0]
    held = same_ref.shape[0]
    bound = 2 * held // lax.axis_size("space")
    me = lax.axis_index("space")
    remote[pl.ds(0, held)] = same_ref[...]
    remote[pl.ds(held, held)] = other_ref[...]
    seen = lax.broadcasted_iota(jnp.int32, (days, LANES), 0) < days_ref[0]
    for block in range(blocks):
        places = []
        for k in range(count):
            link = links_ref[k, block]
            distance = (link // bound) ^ me
            places.append((distance % 2) * held + (distance // 2) * bound + link % bound)
        far = jnp.concatenate([remote[place] for place in places], axis=1)
        total = lax.dot_general(far, weight_ref[block], TURNED, preferred_element_type=jnp.float32)
        source = (running_ref[block] - total).astype(jnp.bfloat16)
        drive = lax.dot_general(source, inverse_ref[block], TURNED, preferred_element_type=jnp.float32)
        for pair in range(pairs):
            forcing_ref[pair, pl.ds(block, days, stride=blocks), :] = jnp.where(
                seen, drive[pair * days : (pair + 1) * days], 0.0
            )
    states = [jnp.zeros((blocks, LANES), jnp.float32)] * pairs
    for day in range(days):
        rows = pl.ds(day * blocks, blocks)
        factor = retain_ref[rows, :]
        for pair in range(pairs):
            states[pair] = factor * states[pair] + forcing_ref[pair, rows, :]
    leave(message_ref, states, product_ref)


def leave(message_ref, values, product_ref):
    for pair, value in enumerate(values):
        message_ref[pair] = value.astype(jnp.bfloat16)
    message_ref[len(values)] = product_ref[0]
    message_ref[len(values) + 1] = product_ref[1]


def carried(pairs, messages_ref, backward):
    me, count = lax.axis_index("tm"), messages_ref.shape[0]
    order = reversed(range(1, count)) if backward else range(count - 1)
    carries = [jnp.zeros(messages_ref.shape[2:], jnp.float32)] * pairs
    for slab in order:
        valid = slab > me if backward else slab < me
        factor = messages_ref[slab, pairs].astype(jnp.float32) + messages_ref[slab, pairs + 1].astype(jnp.float32)
        for pair in range(pairs):
            update = messages_ref[slab, pair].astype(jnp.float32) + factor * carries[pair]
            carries[pair] = jnp.where(valid, update, carries[pair])
    return carries


def adjoint_kernel(
    dims, days_ref, forcing_ref, retain_ref, product_ref, inverse_ref, messages_ref, adjoint_ref, message_ref, stage
):
    days, blocks, size, probes = dims
    pairs = forcing_ref.shape[0]
    seen = lax.broadcasted_iota(jnp.int32, (days, LANES), 0) < days_ref[0]
    states = carried(pairs, messages_ref, False)
    for day in range(days):
        rows = pl.ds(day * blocks, blocks)
        factor = retain_ref[rows, :]
        for pair in range(pairs):
            states[pair] = factor * states[pair] + forcing_ref[pair, rows, :]
            stage[pair, rows, :] = states[pair]
    for block in range(blocks):
        stored = jnp.concatenate(
            [stage[pair, pl.ds(block, days, stride=blocks), :].astype(jnp.bfloat16) for pair in range(pairs)], axis=0
        )
        adjoint = jnp.dot(stored, inverse_ref[block], preferred_element_type=jnp.float32)
        for pair in range(pairs):
            adjoint_ref[pair, pl.ds(block, days, stride=blocks), :] = jnp.where(
                seen, adjoint[pair * days : (pair + 1) * days], 0.0
            )
    carries = [jnp.zeros((blocks, LANES), jnp.float32)] * pairs
    for day in reversed(range(days)):
        rows = pl.ds(day * blocks, blocks)
        factor = retain_ref[rows, :]
        for pair in range(pairs):
            carries[pair] = factor * (adjoint_ref[pair, rows, :] + carries[pair])
    leave(message_ref, carries, product_ref)


def variance_kernel(dims, adjoint_ref, retain_ref, moved_ref, messages_ref, out_ref, stage):
    days, blocks, size, probes = dims
    pairs = adjoint_ref.shape[0]
    carries = carried(pairs, messages_ref, True)
    for day in reversed(range(days)):
        rows = pl.ds(day * blocks, blocks)
        factor = retain_ref[rows, :]
        total = None
        for pair in range(pairs):
            smoothed = adjoint_ref[pair, rows, :] + carries[pair]
            carries[pair] = factor * smoothed
            term = smoothed * moved_ref[pair, rows, :].astype(jnp.float32)
            total = term if total is None else total + term
        stage[rows, :] = total
    lane = lax.broadcasted_iota(jnp.int32, (days, LANES), 1)
    for block in range(0, blocks, 2):
        both = [stage[pl.ds(block + half, days, stride=blocks), :] for half in range(2)]
        both = [value + pltpu.roll(value, size, 1) for value in both]
        out_ref[:, pl.ds(block * size, LANES)] = jnp.where(lane < size, both[0], both[1]) * (1.0 / probes)


def call(kernel, outs, scratch, flops, moved, scalars, *operands):
    in_specs = [
        pl.BlockSpec(memory_space=pltpu.SMEM if i < scalars else pltpu.VMEM) for i in range(len(operands))
    ]
    return pl.pallas_call(
        kernel,
        out_shape=[jax.ShapeDtypeStruct(shape, kind) for shape, kind in outs],
        in_specs=in_specs,
        out_specs=[pl.BlockSpec(memory_space=pltpu.VMEM) for _ in outs],
        scratch_shapes=scratch,
        compiler_params=pltpu.CompilerParams(vmem_limit_bytes=VMEM_LIMIT),
        cost_estimate=pl.CostEstimate(flops=flops, bytes_accessed=moved, transcendentals=0),
    )(*operands)


def crossed(block, axis, bits):
    return lax.ppermute(block, axis, [(i, i ^ bits) for i in range(lax.axis_size(axis))])


def local(
    probes,
    local_links,
    remote_links,
    shared_blocks,
    slab_days,
    local_coupling,
    remote_coupling,
    block_inverse,
    retention,
):
    days, blocks, width = probes.shape
    size = block_inverse.shape[1]
    dims = (days, blocks, size, width // size)
    pairs = width // LANES
    f32, bf16 = jnp.float32, jnp.bfloat16
    bound = shared_blocks.shape[1]
    far = remote_links.shape[1]
    rows = days * blocks
    groups = lax.axis_size("space")
    held = groups // 2 * bound
    near_table, far_table = local_links.T, remote_links.T
    big = ((pairs, rows, LANES), f32)

    (outgoing,) = call(
        functools.partial(outgoing_kernel, dims),
        [((bound, pairs * days, LANES), bf16)],
        [], 10**9, 4 * 10**6, 1, shared_blocks, probes,
    )
    pieces = {bits: crossed(outgoing, "space", bits) for bits in range(groups - 2, 0, -2)}
    running, moved, retain, product, remote_weight, inverse = call(
        functools.partial(local_kernel, dims),
        [
            ((blocks, pairs * days, LANES), f32),
            ((pairs, rows, LANES), bf16),
            ((rows, LANES), f32),
            ((2, blocks, LANES), bf16),
            ((blocks, LANES, far * LANES), bf16),
            ((blocks, LANES, LANES), bf16),
        ],
        [pltpu.VMEM(*big), pltpu.VMEM((blocks, pairs * days, LANES), bf16)],
        10**10, 10**7, 2,
        near_table, slab_days, probes, local_coupling, remote_coupling, block_inverse, retention,
    )
    (same,) = call(
        assemble_kernel,
        [((held, pairs * days, LANES), bf16)],
        [], 0, 10**6, 0, outgoing, *[pieces[bits] for bits in range(2, groups, 2)], product,
    )
    other = crossed(same, "space", 1)
    message_shape = ((pairs + 2, blocks, LANES), bf16)
    forcing, message = call(
        functools.partial(forward_kernel, dims),
        [big, message_shape],
        [pltpu.VMEM((2 * held, pairs * days, LANES), bf16)], 10**10, 10**7, 2,
        far_table, slab_days, running, same, other, remote_weight, inverse, retain, product,
    )
    messages = lax.all_gather(message, "tm", axis=0)
    adjoint, message = call(
        functools.partial(adjoint_kernel, dims),
        [big, message_shape],
        [pltpu.VMEM(*big)], 10**10, 10**7, 1,
        slab_days, forcing, retain, product, inverse, messages,
    )
    messages = lax.all_gather(message, "tm", axis=0)
    (variance,) = call(
        functools.partial(variance_kernel, dims),
        [((days, blocks * size), f32)],
        [pltpu.VMEM((rows, LANES), f32)], 10**10, 10**7, 0,
        adjoint, retain, moved, messages,
    )
    return variance


def solution(mesh):
    placed = (
        P("tm", "space", None),
        P("space", None),
        P("space", None),
        P("space", None),
        P("tm"),
        P("space", None, None, None),
        P("space", None, None, None),
        P("space", None, None),
        P("tm", "space"),
    )
    return jax.shard_map(
        local, mesh=mesh, in_specs=placed, out_specs=P("tm", "space"), check_vma=False
    )
```

time: 71.9 us -> 55.3 us (0.77)
  starting transfers between devices: 20.9 us -> 4.67 us
  blocking collectives: 22.3 us -> 27.4 us
  Pallas kernels: 17.6 us -> 14.9 us
  waiting for transfers between devices: 7.74 us -> 5.35 us
    ppermute x12 -> x4, starting transfers between devices: 20.9 us -> 4.67 us  [crossed(): lax.ppermute(block, axis, [(i, i ^ bits) for i in range(lax.axis_size(axi...]
    all_gather x2, blocking collectives: 22.3 us -> 27.4 us  [local(): messages = lax.all_gather(message, 'tm', axis=0)]
    pallas_call x8 -> x6, Pallas kernels: 17.6 us -> 14.9 us  [call(): pl.pallas_call(kernel, out_shape=[jax.ShapeDtypeStruct(shape, kind) for s...]
    ppermute x12 -> x4, waiting for transfers between devices: 7.74 us -> 5.35 us  [crossed(): lax.ppermute(block, axis, [(i, i ^ bits) for i in range(lax.axis_size(axi...]
  transfers between devices with their start and end apart: 12 -> 4, of which waited for: 3 -> 3; matrix products, arithmetic and copies ran while one was open for 0% -> 0% of each run, Pallas kernels for 9% -> 9%
where the time goes in v2:
time: 55.3 us; the launch traced here: 55.2 us
  blocking collectives  27.4 us (50%)
  Pallas kernels  14.9 us (27%)
  waiting for transfers between devices  5.35 us (10%)
  starting transfers between devices  4.67 us (8%)
  local copies, waits for them, and re-layouts  2.09 us (4%)
  between operations  0.77 us (1%)
    all_gather x2, blocking collectives, local(): messages = lax.all_gather(message, 'tm', axis=0)  27.4 us
    pallas_call x6, Pallas kernels, call(): pl.pallas_call(kernel, out_shape=[jax.ShapeDtypeStruct(shape, kind) for s...  14.9 us
    ppermute x4, waiting for transfers between devices, crossed(): lax.ppermute(block, axis, [(i, i ^ bits) for i in range(lax.axis_size(axi...  5.35 us
    ppermute x4, starting transfers between devices, crossed(): lax.ppermute(block, axis, [(i, i ^ bits) for i in range(lax.axis_size(axi...  4.67 us
    unnamed x18, local copies, waits for them, and re-layouts  2.09 us
  transfers between devices with their start and end apart: 4, of which 3 were waited for; matrix products, arithmetic and copies ran while one was open for 0% of the time, Pallas kernels for 9%

profile of v2, /device:TPU:0, one launch (start us, length us, event | category | flops | bytes accessed | tf_op | source)
XLA Modules:
  0.0 55.2 jit_solution(12986589017968776483)
XLA Ops:
  0.0 0.0 copy-start
  0.0 1.4 %copy-done = bf16[48,16,1024]{2,1,0:T(8,128)(2,1)S(1)} copy-done((bf16[48,16,1024]{2,1,0:T(8,128)(2,1)S(1)}, bf16[48,16,1024]{2,1,0:T(8,128)(2,1)}, u32[]{:S(2)}) %copy-start) | copy-done | bytes 1572888
  1.4 0.0 copy-start.8
  1.4 0.7 %copy-done.8 = s32[1,2]{1,0:T(1,128)S(1)} copy-done((s32[1,2]{1,0:T(1,128)S(1)}, s32[1,2]{1,0:T(1,128)}, u32[]{:S(2)}) %copy-start.8) | copy-done | bytes 32
  2.1 0.0 copy-start.1
  2.1 0.0 copy-start.2
  2.1 0.0 copy-start.3
  2.1 0.0 copy-start.4
  2.1 0.0 copy-start.5
  2.1 0.0 copy-start.6
  2.1 1.3 %shard_map.92.refs_0_ = bf16[2,384,128]{2,1,0:T(8,128)(2,1)S(1)} custom-call(s32[1,2]{1,0:T(1,128)S(1)} %copy-done.8, bf16[48,16,1024]{2,1,0:T(8,128)(2,1)S(1)} %copy-done), custom_call_target="tpu_custom_call" | custom-call | flops 1000000000 | bytes 4000000 | tf_op jit(solution)/shard_map/pallas_call | solution.py:217
  3.4 4.0 %collective-permute-start.2 = (bf16[2,384,128]{2,1,0:T(8,128)(2,1)S(1)}, bf16[2,384,128]{2,1,0:T(8,128)(2,1)S(1)}, u32[]{:S(2)}, u32[]{:S(2)}) collective-permute-start(bf16[2,384,128]{2,1,0:T(8,128)(2,1)S(1)} %shard_map.92.refs_0_), channel_id=1, source_target_pairs={{0,6},{1,7},{2,4},{3,5},{4,2},{5,3},{6,0},{7,1},{8,14},{9,15},{10,... | collective-permute-start | bytes 589832 | tf_op jit(solution)/shard_map/ppermute | solution.py:229
  7.4 0.5 collective-permute-start.1
  7.9 0.1 collective-permute-start
  8.7 0.0 copy-done.1
  8.7 0.0 copy-done.2
  8.7 0.0 copy-done.3
  8.7 0.0 copy-done.4
  8.7 0.0 copy-done.5
  8.7 0.0 copy-done.6
  8.7 0.0 copy-start.7
  8.7 4.9 %shard_map.91 = (f32[16,384,128]{2,1,0:T(8,128)S(1)}, bf16[8,768,128]{2,1,0:T(8,128)(2,1)S(1)}, f32[768,128]{1,0:T(8,128)S(1)}, bf16[2,16,128]{2,1,0:T(8,128)(2,...) custom-call(s32[4,16]{1,0:T(4,128)S(1)} %bitcast.6, s32[1]{0:T(128)S(6)} %copy.10.days_ref, ...), custom_call_target="tpu_custom_call" | custom-call | flops 10000000000 | bytes 10000000 | tf_op jit(solution)/shard_map/pallas_call | solution.py:217
  13.7 0.0 collective-permute-done.2.refs_3_
  13.7 2.8 %collective-permute-done.1.refs_2_ = bf16[2,384,128]{2,1,0:T(8,128)(2,1)S(1)} collective-permute-done((bf16[2,384,128]{2,1,0:T(8,128)(2,1)S(1)}, bf16[2,384,128]{2,1,0:T(8,128)(2,1)S(1)}, u32[]{:S(2)}, u32[]{:S(2)}) %collective-permute-start.1) | collective-permute-done | bytes 196640 | tf_op jit(solution)/shard_map/ppermute | solution.py:229
  16.5 0.3 collective-permute-done.refs_1_
  16.8 0.1 shard_map.93.same_ref
  16.8 0.1 collective-permute-start.3
  16.9 2.3 %collective-permute-done.3.other_ref = bf16[8,384,128]{2,1,0:T(8,128)(2,1)S(1)} collective-permute-done((bf16[8,384,128]{2,1,0:T(8,128)(2,1)S(1)}, bf16[8,384,128]{2,1,0:T(8,128)(2,1)S(1)}, u32[]{:S(2)}, u32[]{:S(2)}) %collective-permute-start.3) | collective-permute-done | bytes 786464 | tf_op jit(solution)/shard_map/ppermute | solution.py:229
  19.2 0.0 copy-done.7
  19.2 4.6 %shard_map.94 = (f32[8,768,128]{2,1,0:T(8,128)S(1)}, bf16[10,16,128]{2,1,0:T(8,128)(2,1)S(1)}) custom-call(s32[2,16]{1,0:T(2,128)S(1)} %bitcast.7, s32[1]{0:T(128)S(6)} %copy.10.days_ref, f32[16,384,128]{2,1,0:T(8,128)S(1)} %get-tuple-element.15.running_ref, bf16[8,384,128]{2,1,0:T(8,128)(2,1)S(1)} %shard_map.93.same_ref, ...), custom_call_target="tpu_custom_call" | custom-call | flops 10000000000 | bytes 10000000 | tf_op jit(solution)/shard_map/pallas_call | solution.py:217
  23.8 13.7 %all-gather = bf16[40,16,128]{2,1,0:T(8,128)(2,1)S(1)} all-gather(bf16[10,16,128]{2,1,0:T(8,128)(2,1)S(1)} %get-tuple-element.21), channel_id=2, replica_groups=mesh['tm'=4,'space'=8] {'tm'}, dimensions={0}, use_global_device_ids=true | all-gather | bytes 204800 | tf_op jit(solution)/shard_map/all_gather | solution.py:289
  37.5 2.6 %shard_map.95 = (f32[8,768,128]{2,1,0:T(8,128)S(1)}, bf16[10,16,128]{2,1,0:T(8,128)(2,1)S(1)}) custom-call(s32[1]{0:T(128)S(6)} %copy.10.days_ref, f32[8,768,128]{2,1,0:T(8,128)S(1)} %get-tuple-element.20.forcing_ref, f32[768,128]{1,0:T(8,128)S(1)} %get-tuple-element.19.retain_ref, bf16[2,16,128]{2,1,0:T(8,128)(2,1)S(1)} %get-tuple-element.16.refs_4_.product_ref, ...), custom_call_target="tpu_custom_call" | custom-call | flops 10000000000 | bytes 10000000 | tf_op jit(solution)/shard_map/pallas_call | solution.py:217
  40.1 13.7 %all-gather.1 = bf16[40,16,128]{2,1,0:T(8,128)(2,1)S(1)} all-gather(bf16[10,16,128]{2,1,0:T(8,128)(2,1)S(1)} %get-tuple-element.24), channel_id=3, replica_groups=mesh['tm'=4,'space'=8] {'tm'}, dimensions={0}, use_global_device_ids=true | all-gather | bytes 204800 | tf_op jit(solution)/shard_map/all_gather | solution.py:296
  53.8 1.4 %shard_map.96 = f32[48,1024]{1,0:T(8,128)} custom-call(f32[8,768,128]{2,1,0:T(8,128)S(1)} %get-tuple-element.22.adjoint_ref, f32[768,128]{1,0:T(8,128)S(1)} %get-tuple-element.19.retain_ref, bf16[8,768,128]{2,1,0:T(8,128)(2,1)S(1)} %get-tuple-element.23.moved_ref, bf16[4,10,16,128]{3,2,1,0:T(8,128)(2,1)S(1)} %bitcast.5), custom_call_target="tpu_custom_call" | custom-call | flops 10000000000 | bytes 10000000 | tf_op jit(solution)/shard_map/pallas_call | solution.py:217
Async XLA Ops:
  0.0 1.4 %copy-start = (bf16[48,16,1024]{2,1,0:T(8,128)(2,1)S(1)}, bf16[48,16,1024]{2,1,0:T(8,128)(2,1)}, u32[]{:S(2)}) copy-start(bf16[48,16,1024]{2,1,0:T(8,128)(2,1)} %z_ref.3) | copy-start | bytes 4718596
  1.4 0.7 %copy-start.8 = (s32[1,2]{1,0:T(1,128)S(1)}, s32[1,2]{1,0:T(1,128)}, u32[]{:S(2)}) copy-start(s32[1,2]{1,0:T(1,128)} %shared_ref.1) | copy-start | bytes 28
  2.1 6.6 %copy-start.1 = (bf16[48,16,1024]{2,1,0:T(8,128)(2,1)S(1)}, bf16[48,16,1024]{2,1,0:T(8,128)(2,1)}, u32[]{:S(2)}) copy-start(bf16[48,16,1024]{2,1,0:T(8,128)(2,1)} %z_ref.3) | copy-start | bytes 4718596
  2.1 6.6 %copy-start.2 = (bf16[16,4,64,64]{3,2,1,0:T(8,128)(2,1)S(1)}, bf16[16,4,64,64]{3,2,1,0:T(8,128)(2,1)}, u32[]{:S(2)}) copy-start(bf16[16,4,64,64]{3,2,1,0:T(8,128)(2,1)} %weight_ref.1) | copy-start | bytes 1572868
  2.1 6.6 %copy-start.3 = (bf16[16,2,64,64]{3,2,1,0:T(8,128)(2,1)S(1)}, bf16[16,2,64,64]{3,2,1,0:T(8,128)(2,1)}, u32[]{:S(2)}) copy-start(bf16[16,2,64,64]{3,2,1,0:T(8,128)(2,1)} %remote_weight_ref.1) | copy-start | bytes 786436
  2.1 6.6 %copy-start.4 = (bf16[16,64,64]{2,1,0:T(8,128)(2,1)S(1)}, bf16[16,64,64]{2,1,0:T(8,128)(2,1)}, u32[]{:S(2)}) copy-start(bf16[16,64,64]{2,1,0:T(8,128)(2,1)} %inverse_ref.1) | copy-start | bytes 393220
  2.1 6.6 %copy-start.5 = (f32[48,1024]{1,0:T(8,128)S(1)}, f32[48,1024]{1,0:T(8,128)}, u32[]{:S(2)}) copy-start(f32[48,1024]{1,0:T(8,128)} %retention_ref.1) | copy-start | bytes 589828
  2.1 6.6 %copy-start.6 = (s32[16,4]{0,1:T(4,128)S(1)}, s32[16,4]{0,1:T(4,128)}, u32[]{:S(2)}) copy-start(s32[16,4]{0,1:T(4,128)} %param.10) | copy-start | bytes 772
  3.4 10.3 %collective-permute-start.2 = (bf16[2,384,128]{2,1,0:T(8,128)(2,1)S(1)}, bf16[2,384,128]{2,1,0:T(8,128)(2,1)S(1)}, u32[]{:S(2)}, u32[]{:S(2)}) collective-permute-start(bf16[2,384,128]{2,1,0:T(8,128)(2,1)S(1)} %shard_map.92.refs_0_), channel_id=1, source_target_pairs={{0,6},{1,7},{2,4},{3,5},{4,2},{5,3},{6,0},{7,1},{8,14},{9,15},{10,... | collective-permute-start | bytes 589832 | tf_op jit(solution)/shard_map/ppermute | solution.py:229
  7.4 9.1 %collective-permute-start.1 = (bf16[2,384,128]{2,1,0:T(8,128)(2,1)S(1)}, bf16[2,384,128]{2,1,0:T(8,128)(2,1)S(1)}, u32[]{:S(2)}, u32[]{:S(2)}) collective-permute-start(bf16[2,384,128]{2,1,0:T(8,128)(2,1)S(1)} %shard_map.92.refs_0_), channel_id=1, source_target_pairs={{0,4},{1,5},{2,6},{3,7},{4,0},{5,1},{6,2},{7,3},{8,12},{9,13},{10,... | collective-permute-start | bytes 589832 | tf_op jit(solution)/shard_map/ppermute | solution.py:229
  7.9 8.9 %collective-permute-start = (bf16[2,384,128]{2,1,0:T(8,128)(2,1)S(1)}, bf16[2,384,128]{2,1,0:T(8,128)(2,1)S(1)}, u32[]{:S(2)}, u32[]{:S(2)}) collective-permute-start(bf16[2,384,128]{2,1,0:T(8,128)(2,1)S(1)} %shard_map.92.refs_0_), channel_id=1, source_target_pairs={{0,2},{1,3},{2,0},{3,1},{4,6},{5,7},{6,4},{7,5},{8,10},{9,11},{10,... | collective-permute-start | bytes 589832 | tf_op jit(solution)/shard_map/ppermute | solution.py:229
  8.7 10.5 %copy-start.7 = (s32[16,2]{0,1:T(2,128)S(1)}, s32[16,2]{0,1:T(2,128)}, u32[]{:S(2)}) copy-start(s32[16,2]{0,1:T(2,128)} %param.11) | copy-start | bytes 388
  16.8 2.4 %collective-permute-start.3 = (bf16[8,384,128]{2,1,0:T(8,128)(2,1)S(1)}, bf16[8,384,128]{2,1,0:T(8,128)(2,1)S(1)}, u32[]{:S(2)}, u32[]{:S(2)}) collective-permute-start(bf16[8,384,128]{2,1,0:T(8,128)(2,1)S(1)} %shard_map.93.same_ref), channel_id=1, source_target_pairs={{0,1},{1,0},{2,3},{3,2},{4,5},{5,4},{6,7},{7,6},{8,9},{9,8},{10,11... | collective-permute-start | bytes 2359304 | tf_op jit(solution)/shard_map/ppermute | solution.py:229

commit v3 on v2

--- a/solution.py
+++ b/solution.py
@@ -27,22 +27,33 @@
     )
 
 
-def outgoing_kernel(dims, shared_ref, z_ref, outgoing_ref):
+def outgoing_kernel(dims, shared_ref, z_hbm, outgoing_ref, z_ref, arrived):
     days, blocks, size, probes = dims
     count = outgoing_ref.shape[0]
-    z = z_ref[...].reshape(days * blocks, size * probes)
-    row = lax.broadcasted_iota(jnp.int32, (days, days * blocks), 0)
-    column = lax.broadcasted_iota(jnp.int32, (days, days * blocks), 1)
-    picks = [
-        (column == row * blocks + shared_ref[0, m]).astype(jnp.float32).astype(jnp.bfloat16) for m in range(count)
+    part = 8
+    copies = [
+        pltpu.make_async_copy(z_hbm.at[pl.ds(i * part, part)], z_ref.at[pl.ds(i * part, part)], arrived.at[i])
+        for i in range(days // part)
     ]
-    picked = jnp.dot(jnp.concatenate(picks, axis=0), z, preferred_element_type=jnp.float32).astype(jnp.bfloat16)
+    for copy in copies:
+        copy.start()
     step = 2 * LANES
-    for start in range(0, size * probes, step):
-        moved = jnp.dot(picked, permutation(size, probes, start, step), preferred_element_type=jnp.float32)
-        moved = moved.astype(jnp.bfloat16)
+    moves = [permutation(size, probes, start, step) for start in range(0, size * probes, step)]
+    row = lax.broadcasted_iota(jnp.int32, (part, part * blocks), 0)
+    column = lax.broadcasted_iota(jnp.int32, (part, part * blocks), 1)
+    picks = [(column == row * blocks + shared_ref[0, m]).astype(jnp.float32) for m in range(count)]
+    pick = jnp.concatenate(picks, axis=0).astype(jnp.bfloat16)
+    picked = []
+    for i, copy in enumerate(copies):
+        copy.wait()
+        z = z_ref[pl.ds(i * part, part)].reshape(part * blocks, size * probes)
+        picked.append(jnp.dot(pick, z, preferred_element_type=jnp.float32))
+    picked = jnp.concatenate([rows[m * part : (m + 1) * part] for m in range(count) for rows in picked], axis=0)
+    picked = picked.astype(jnp.bfloat16)
+    for i, move in enumerate(moves):
+        moved = jnp.dot(picked, move, preferred_element_type=jnp.float32).astype(jnp.bfloat16)
         for half in range(2):
-            pair = start // LANES + half
+            pair = i * 2 + half
             for m in range(count):
                 outgoing_ref[m, pl.ds(pair * days, days), :] = moved[
                     m * days : (m + 1) * days, half * LANES : (half + 1) * LANES
@@ -135,36 +146,41 @@
         factor = retain_ref[rows, :]
         for pair in range(pairs):
             states[pair] = factor * states[pair] + forcing_ref[pair, rows, :]
-    leave(message_ref, states, product_ref)
-
-
-def leave(message_ref, values, product_ref):
+    leave(message_ref, states)
+    message_ref[pairs] = product_ref[0]
+    message_ref[pairs + 1] = product_ref[1]
+
+
+def leave(message_ref, values):
     for pair, value in enumerate(values):
         message_ref[pair] = value.astype(jnp.bfloat16)
-    message_ref[len(values)] = product_ref[0]
-    message_ref[len(values) + 1] = product_ref[1]
-
-
-def carried(pairs, messages_ref, backward):
-    me, count = lax.axis_index("tm"), messages_ref.shape[0]
-    order = reversed(range(1, count)) if backward else range(count - 1)
-    carries = [jnp.zeros(messages_ref.shape[2:], jnp.float32)] * pairs
-    for slab in order:
+
+
+def collect(piece_refs, inbox):
+    me = lax.axis_index("tm")
+    for k, ref in enumerate(piece_refs):
+        inbox[me ^ (k + 1)] = ref[...]
+
+
+def carried(pairs, inbox, products, backward):
+    me, count = lax.axis_index("tm"), inbox.shape[0]
+    carries = [jnp.zeros(inbox.shape[2:], jnp.float32)] * pairs
+    for slab in range(count - 1, 0, -1) if backward else range(count - 1):
         valid = slab > me if backward else slab < me
-        factor = messages_ref[slab, pairs].astype(jnp.float32) + messages_ref[slab, pairs + 1].astype(jnp.float32)
-        for pair in range(pairs):
-            update = messages_ref[slab, pair].astype(jnp.float32) + factor * carries[pair]
+        factor = products[slab, pairs].astype(jnp.float32) + products[slab, pairs + 1].astype(jnp.float32)
+        for pair in range(pairs):
+            update = inbox[slab, pair].astype(jnp.float32) + factor * carries[pair]
             carries[pair] = jnp.where(valid, update, carries[pair])
     return carries
 
 
-def adjoint_kernel(
-    dims, days_ref, forcing_ref, retain_ref, product_ref, inverse_ref, messages_ref, adjoint_ref, message_ref, stage
-):
+def adjoint_kernel(dims, hops, days_ref, forcing_ref, retain_ref, inverse_ref, *rest):
     days, blocks, size, probes = dims
     pairs = forcing_ref.shape[0]
+    adjoint_ref, message_ref, stage, inbox = rest[hops:]
+    collect(rest[:hops], inbox)
     seen = lax.broadcasted_iota(jnp.int32, (days, LANES), 0) < days_ref[0]
-    states = carried(pairs, messages_ref, False)
+    states = carried(pairs, inbox, inbox, False)
     for day in range(days):
         rows = pl.ds(day * blocks, blocks)
         factor = retain_ref[rows, :]
@@ -186,13 +202,16 @@
         factor = retain_ref[rows, :]
         for pair in range(pairs):
             carries[pair] = factor * (adjoint_ref[pair, rows, :] + carries[pair])
-    leave(message_ref, carries, product_ref)
-
-
-def variance_kernel(dims, adjoint_ref, retain_ref, moved_ref, messages_ref, out_ref, stage):
+    leave(message_ref, carries)
+
+
+def variance_kernel(dims, hops, adjoint_ref, retain_ref, moved_ref, *rest):
     days, blocks, size, probes = dims
     pairs = adjoint_ref.shape[0]
-    carries = carried(pairs, messages_ref, True)
+    out_ref, stage, inbox, products = rest[2 * hops :]
+    collect(rest[:hops], inbox)
+    collect(rest[hops : 2 * hops], products)
+    carries = carried(pairs, inbox, products, True)
     for day in reversed(range(days)):
         rows = pl.ds(day * blocks, blocks)
         factor = retain_ref[rows, :]
@@ -210,9 +229,10 @@
         out_ref[:, pl.ds(block * size, LANES)] = jnp.where(lane < size, both[0], both[1]) * (1.0 / probes)
 
 
-def call(kernel, outs, scratch, flops, moved, scalars, *operands):
+def call(kernel, outs, scratch, flops, moved, scalars, *operands, apart=(), limit=VMEM_LIMIT):
     in_specs = [
-        pl.BlockSpec(memory_space=pltpu.SMEM if i < scalars else pltpu.VMEM) for i in range(len(operands))
+        pl.BlockSpec(memory_space=pltpu.SMEM if i < scalars else pl.ANY if i in apart else pltpu.VMEM)
+        for i in range(len(operands))
     ]
     return pl.pallas_call(
         kernel,
@@ -220,7 +240,7 @@
         in_specs=in_specs,
         out_specs=[pl.BlockSpec(memory_space=pltpu.VMEM) for _ in outs],
         scratch_shapes=scratch,
-        compiler_params=pltpu.CompilerParams(vmem_limit_bytes=VMEM_LIMIT),
+        compiler_params=pltpu.CompilerParams(vmem_limit_bytes=limit),
         cost_estimate=pl.CostEstimate(flops=flops, bytes_accessed=moved, transcendentals=0),
     )(*operands)
 
@@ -256,7 +276,8 @@
     (outgoing,) = call(
         functools.partial(outgoing_kernel, dims),
         [((bound, pairs * days, LANES), bf16)],
-        [], 10**9, 4 * 10**6, 1, shared_blocks, probes,
+        [pltpu.VMEM(probes.shape, bf16), pltpu.SemaphoreType.DMA((days // 8,))], 10**9, 4 * 10**6, 1,
+        shared_blocks, probes, apart=(1,), limit=56 * 1024 * 1024,
     )
     pieces = {bits: crossed(outgoing, "space", bits) for bits in range(groups - 2, 0, -2)}
     running, moved, retain, product, remote_weight, inverse = call(
@@ -279,26 +300,29 @@
         [], 0, 10**6, 0, outgoing, *[pieces[bits] for bits in range(2, groups, 2)], product,
     )
     other = crossed(same, "space", 1)
-    message_shape = ((pairs + 2, blocks, LANES), bf16)
+    slabs = lax.axis_size("tm")
+    hops = slabs - 1
+    exchange = lambda message: [crossed(message, "tm", bits) for bits in range(hops, 0, -1)][::-1]
+    inbox = pltpu.VMEM((slabs, pairs + 2, blocks, LANES), bf16)
     forcing, message = call(
         functools.partial(forward_kernel, dims),
-        [big, message_shape],
+        [big, ((pairs + 2, blocks, LANES), bf16)],
         [pltpu.VMEM((2 * held, pairs * days, LANES), bf16)], 10**10, 10**7, 2,
         far_table, slab_days, running, same, other, remote_weight, inverse, retain, product,
     )
-    messages = lax.all_gather(message, "tm", axis=0)
+    ends = exchange(message)
     adjoint, message = call(
-        functools.partial(adjoint_kernel, dims),
-        [big, message_shape],
-        [pltpu.VMEM(*big)], 10**10, 10**7, 1,
-        slab_days, forcing, retain, product, inverse, messages,
-    )
-    messages = lax.all_gather(message, "tm", axis=0)
+        functools.partial(adjoint_kernel, dims, hops),
+        [big, ((pairs, blocks, LANES), bf16)],
+        [pltpu.VMEM(*big), inbox], 10**10, 10**7, 1,
+        slab_days, forcing, retain, inverse, *ends,
+    )
+    starts = exchange(message)
     (variance,) = call(
-        functools.partial(variance_kernel, dims),
+        functools.partial(variance_kernel, dims, hops),
         [((days, blocks * size), f32)],
-        [pltpu.VMEM((rows, LANES), f32)], 10**10, 10**7, 0,
-        adjoint, retain, moved, messages,
+        [pltpu.VMEM((rows, LANES), f32), pltpu.VMEM((slabs, pairs, blocks, LANES), bf16), inbox], 10**10, 10**7, 0,
+        adjoint, retain, moved, *starts, *ends,
     )
     return variance
 

time: 55.3 us -> 44.6 us (0.81)
  blocking collectives: 27.4 us -> 0 us
  starting transfers between devices: 4.67 us -> 13.6 us
  waiting for transfers between devices: 5.35 us -> 12.3 us
  Pallas kernels: 14.9 us -> 17.7 us
  local copies, waits for them, and re-layouts: 2.09 us -> 0.04 us
    all_gather x2 -> x0, blocking collectives: 27.4 us -> none  [local(): messages = lax.all_gather(message, 'tm', axis=0)]
    ppermute x4 -> x10, starting transfers between devices: 4.67 us -> 13.6 us  [crossed(): lax.ppermute(block, axis, [(i, i ^ bits) for i in range(lax.axis_size(axi...]
    ppermute x4 -> x10, waiting for transfers between devices: 5.35 us -> 12.3 us  [crossed(): lax.ppermute(block, axis, [(i, i ^ bits) for i in range(lax.axis_size(axi...]
    pallas_call x6, Pallas kernels: 14.9 us -> 17.7 us  [call(): pl.pallas_call(kernel, out_shape=[jax.ShapeDtypeStruct(shape, kind) for s...]
    unnamed x18 -> x16, local copies, waits for them, and re-layouts: 2.09 us -> 0.04 us
  transfers between devices with their start and end apart: 4 -> 10, of which waited for: 3 -> 7; matrix products, arithmetic and copies ran while one was open for 0% -> 0% of each run, Pallas kernels for 9% -> 11%
where the time goes in v3:
time: 44.6 us; the launch traced here: 44.4 us
  Pallas kernels  17.7 us (40%)
  starting transfers between devices  13.6 us (30%)
  waiting for transfers between devices  12.3 us (28%)
  between operations  0.78 us (2%)
    pallas_call x6, Pallas kernels, call(): pl.pallas_call(kernel, out_shape=[jax.ShapeDtypeStruct(shape, kind) for s...  17.7 us
    ppermute x10, starting transfers between devices, crossed(): lax.ppermute(block, axis, [(i, i ^ bits) for i in range(lax.axis_size(axi...  13.6 us
    ppermute x10, waiting for transfers between devices, crossed(): lax.ppermute(block, axis, [(i, i ^ bits) for i in range(lax.axis_size(axi...  12.3 us
  transfers between devices with their start and end apart: 10, of which 7 were waited for; matrix products, arithmetic and copies ran while one was open for 0% of the time, Pallas kernels for 11%

profile of v3, /device:TPU:0, one launch (start us, length us, event | category | flops | bytes accessed | tf_op | source)
XLA Modules:
  0.0 44.4 jit_solution(4406614913426670571)
XLA Ops:
  0.0 0.0 copy-start.1
  0.0 0.0 copy-start.5
  0.0 0.0 copy-start.4
  0.0 0.0 copy-start.3
  0.0 0.0 copy-start.2
  0.0 0.0 copy-start.6
  0.0 4.1 %shard_map.92.refs_0_ = bf16[2,384,128]{2,1,0:T(8,128)(2,1)} custom-call(s32[1,2]{1,0:T(1,128)} %shared_ref.1, bf16[48,16,1024]{2,1,0:T(8,128)(2,1)} %z_hbm.1), custom_call_target="tpu_custom_call" | custom-call | flops 1000000000 | bytes 4000000 | tf_op jit(solution)/shard_map/pallas_call | solution.py:237
  4.1 4.0 %collective-permute-start.2 = (bf16[2,384,128]{2,1,0:T(8,128)(2,1)}, bf16[2,384,128]{2,1,0:T(8,128)(2,1)S(1)}, u32[]{:S(2)}, u32[]{:S(2)}) collective-permute-start(bf16[2,384,128]{2,1,0:T(8,128)(2,1)} %shard_map.92.refs_0_), channel_id=1, source_target_pairs={{0,6},{1,7},{2,4},{3,5},{4,2},{5,3},{6,0},{7,1},{8,14},{9,15},{10,... | collective-permute-start | bytes 589832 | tf_op jit(solution)/shard_map/ppermute | solution.py:249
  8.1 0.5 %collective-permute-start.1 = (bf16[2,384,128]{2,1,0:T(8,128)(2,1)}, bf16[2,384,128]{2,1,0:T(8,128)(2,1)S(1)}, u32[]{:S(2)}, u32[]{:S(2)}) collective-permute-start(bf16[2,384,128]{2,1,0:T(8,128)(2,1)} %shard_map.92.refs_0_), channel_id=1, source_target_pairs={{0,4},{1,5},{2,6},{3,7},{4,0},{5,1},{6,2},{7,3},{8,12},{9,13},{10,... | collective-permute-start | bytes 589832 | tf_op jit(solution)/shard_map/ppermute | solution.py:249
  8.6 0.1 collective-permute-start
  9.4 0.0 copy-done.1
  9.4 0.0 copy-done.5
  9.4 0.0 copy-done.4
  9.4 0.0 copy-done.3
  9.4 0.0 copy-done.2
  9.4 0.0 copy-done.6
  9.4 0.0 copy-start
  9.4 0.0 copy-start.7
  9.4 4.9 %shard_map.91 = (f32[16,384,128]{2,1,0:T(8,128)S(1)}, bf16[8,768,128]{2,1,0:T(8,128)(2,1)S(1)}, f32[768,128]{1,0:T(8,128)S(1)}, bf16[2,16,128]{2,1,0:T(8,128)(2,...) custom-call(s32[4,16]{1,0:T(4,128)S(1)} %bitcast.2, s32[1]{0:T(128)S(6)} %copy.10.days_ref, ...), custom_call_target="tpu_custom_call" | custom-call | flops 10000000000 | bytes 10000000 | tf_op jit(solution)/shard_map/pallas_call | solution.py:237
  14.4 0.0 collective-permute-done.2.refs_3_
  14.4 3.0 %collective-permute-done.1.refs_2_ = bf16[2,384,128]{2,1,0:T(8,128)(2,1)S(1)} collective-permute-done((bf16[2,384,128]{2,1,0:T(8,128)(2,1)}, bf16[2,384,128]{2,1,0:T(8,128)(2,1)S(1)}, u32[]{:S(2)}, u32[]{:S(2)}) %collective-permute-start.1) | collective-permute-done | bytes 196640 | tf_op jit(solution)/shard_map/ppermute | solution.py:249
  17.4 0.3 collective-permute-done.refs_1_
  17.7 0.0 copy-done
  17.7 0.1 shard_map.93.same_ref
  17.7 0.1 collective-permute-start.3
  17.8 2.3 %collective-permute-done.3.other_ref = bf16[8,384,128]{2,1,0:T(8,128)(2,1)S(1)} collective-permute-done((bf16[8,384,128]{2,1,0:T(8,128)(2,1)S(1)}, bf16[8,384,128]{2,1,0:T(8,128)(2,1)S(1)}, u32[]{:S(2)}, u32[]{:S(2)}) %collective-permute-start.3) | collective-permute-done | bytes 786464 | tf_op jit(solution)/shard_map/ppermute | solution.py:249
  20.1 0.0 copy-done.7
  20.1 4.6 %shard_map.94 = (f32[8,768,128]{2,1,0:T(8,128)S(1)}, bf16[10,16,128]{2,1,0:T(8,128)(2,1)S(1)}) custom-call(s32[2,16]{1,0:T(2,128)S(1)} %bitcast.3, s32[1]{0:T(128)S(6)} %copy.10.days_ref, f32[16,384,128]{2,1,0:T(8,128)S(1)} %get-tuple-element.15.running_ref, bf16[8,384,128]{2,1,0:T(8,128)(2,1)S(1)} %shard_map.93.same_ref, ...), custom_call_target="tpu_custom_call" | custom-call | flops 10000000000 | bytes 10000000 | tf_op jit(solution)/shard_map/pallas_call | solution.py:237
  24.7 3.7 %collective-permute-start.6 = (bf16[10,16,128]{2,1,0:T(8,128)(2,1)S(1)}, bf16[10,16,128]{2,1,0:T(8,128)(2,1)S(1)}, u32[]{:S(2)}, u32[]{:S(2)}) collective-permute-start(bf16[10,16,128]{2,1,0:T(8,128)(2,1)S(1)} %get-tuple-element.21), channel_id=1, source_target_pairs={{0,24},{8,16},{16,8},{24,0},{1,25},{9,17},{17,9},{25,1},{2,26},{10... | collective-permute-start | bytes 122888 | tf_op jit(solution)/shard_map/ppermute | solution.py:249
  28.4 0.0 collective-permute-start.5
  28.4 0.8 %collective-permute-start.4 = (bf16[10,16,128]{2,1,0:T(8,128)(2,1)S(1)}, bf16[10,16,128]{2,1,0:T(8,128)(2,1)S(1)}, u32[]{:S(2)}, u32[]{:S(2)}) collective-permute-start(bf16[10,16,128]{2,1,0:T(8,128)(2,1)S(1)} %get-tuple-element.21), channel_id=1, source_target_pairs={{0,8},{8,0},{16,24},{24,16},{1,9},{9,1},{17,25},{25,17},{2,10},{10... | collective-permute-start | bytes 122888 | tf_op jit(solution)/shard_map/ppermute | solution.py:249
  29.2 1.5 %collective-permute-done.6.rest_2_.rest_5_ = bf16[10,16,128]{2,1,0:T(8,128)(2,1)S(1)} collective-permute-done((bf16[10,16,128]{2,1,0:T(8,128)(2,1)S(1)}, bf16[10,16,128]{2,1,0:T(8,128)(2,1)S(1)}, u32[]{:S(2)}, u32[]{:S(2)}) %collective-permute-start.6) | collective-permute-done | bytes 40992 | tf_op jit(solution)/shard_map/ppermute | solution.py:249
  30.6 2.7 %collective-permute-done.5.rest_1_.rest_4_ = bf16[10,16,128]{2,1,0:T(8,128)(2,1)S(1)} collective-permute-done((bf16[10,16,128]{2,1,0:T(8,128)(2,1)S(1)}, bf16[10,16,128]{2,1,0:T(8,128)(2,1)S(1)}, u32[]{:S(2)}, u32[]{:S(2)}) %collective-permute-start.5) | collective-permute-done | bytes 40992 | tf_op jit(solution)/shard_map/ppermute | solution.py:249
  33.3 0.0 collective-permute-done.4.rest_0_.rest_3_
  33.3 2.6 %shard_map.95 = (f32[8,768,128]{2,1,0:T(8,128)S(1)}, bf16[8,16,128]{2,1,0:T(8,128)(2,1)S(1)}) custom-call(s32[1]{0:T(128)S(6)} %copy.10.days_ref, f32[8,768,128]{2,1,0:T(8,128)S(1)} %get-tuple-element.20.forcing_ref, f32[768,128]{1,0:T(8,128)S(1)} %get-tuple-element.19.retain_ref, bf16[16,128,128]{2,1,0:T(8,128)(2,1)S(1)} %get-tuple-element.18.inverse_ref, ...), custom_call_target="tpu_custom_call" | custom-call | flops 10000000000 | bytes 10000000 | tf_op jit(solution)/shard_map/pallas_call | solution.py:237
  35.9 1.9 %collective-permute-start.9 = (bf16[8,16,128]{2,1,0:T(8,128)(2,1)S(1)}, bf16[8,16,128]{2,1,0:T(8,128)(2,1)S(1)}, u32[]{:S(2)}, u32[]{:S(2)}) collective-permute-start(bf16[8,16,128]{2,1,0:T(8,128)(2,1)S(1)} %get-tuple-element.24), channel_id=1, source_target_pairs={{0,24},{8,16},{16,8},{24,0},{1,25},{9,17},{17,9},{25,1},{2,26},{10... | collective-permute-start | bytes 98312 | tf_op jit(solution)/shard_map/ppermute | solution.py:249
  37.7 0.3 collective-permute-start.8
  38.0 2.3 %collective-permute-start.7 = (bf16[8,16,128]{2,1,0:T(8,128)(2,1)S(1)}, bf16[8,16,128]{2,1,0:T(8,128)(2,1)S(1)}, u32[]{:S(2)}, u32[]{:S(2)}) collective-permute-start(bf16[8,16,128]{2,1,0:T(8,128)(2,1)S(1)} %get-tuple-element.24), channel_id=1, source_target_pairs={{0,8},{8,0},{16,24},{24,16},{1,9},{9,1},{17,25},{25,17},{2,10},{10... | collective-permute-start | bytes 98312 | tf_op jit(solution)/shard_map/ppermute | solution.py:249
  40.3 1.5 %collective-permute-done.9.rest_2_ = bf16[8,16,128]{2,1,0:T(8,128)(2,1)S(1)} collective-permute-done((bf16[8,16,128]{2,1,0:T(8,128)(2,1)S(1)}, bf16[8,16,128]{2,1,0:T(8,128)(2,1)S(1)}, u32[]{:S(2)}, u32[]{:S(2)}) %collective-permute-start.9) | collective-permute-done | bytes 32800 | tf_op jit(solution)/shard_map/ppermute | solution.py:249
  41.8 1.1 %collective-permute-done.8.rest_1_ = bf16[8,16,128]{2,1,0:T(8,128)(2,1)S(1)} collective-permute-done((bf16[8,16,128]{2,1,0:T(8,128)(2,1)S(1)}, bf16[8,16,128]{2,1,0:T(8,128)(2,1)S(1)}, u32[]{:S(2)}, u32[]{:S(2)}) %collective-permute-start.8) | collective-permute-done | bytes 32800 | tf_op jit(solution)/shard_map/ppermute | solution.py:249
  42.9 0.0 collective-permute-done.7.rest_0_
  42.9 1.5 %shard_map.96 = f32[48,1024]{1,0:T(8,128)} custom-call(f32[8,768,128]{2,1,0:T(8,128)S(1)} %get-tuple-element.22.adjoint_ref, f32[768,128]{1,0:T(8,128)S(1)} %get-tuple-element.19.retain_ref, bf16[8,768,128]{2,1,0:T(8,128)(2,1)S(1)} %get-tuple-element.23.moved_ref, bf16[8,16,128]{2,1,0:T(8,128)(2,1)S(1)} %collective-permute-done.7.rest_0_, ...), custom_call_target="tpu_custom_call" | custom-call | flops 10000000000 | bytes 10000000 | tf_op jit(solution)/shard_map/pallas_call | solution.py:237
Async XLA Ops:
  0.0 9.4 %copy-start.1 = (bf16[48,16,1024]{2,1,0:T(8,128)(2,1)S(1)}, bf16[48,16,1024]{2,1,0:T(8,128)(2,1)}, u32[]{:S(2)}) copy-start(bf16[48,16,1024]{2,1,0:T(8,128)(2,1)} %z_hbm.1) | copy-start | bytes 4718596
  0.0 9.4 %copy-start.5 = (f32[48,1024]{1,0:T(8,128)S(1)}, f32[48,1024]{1,0:T(8,128)}, u32[]{:S(2)}) copy-start(f32[48,1024]{1,0:T(8,128)} %retention_ref.1) | copy-start | bytes 589828
  0.0 9.4 %copy-start.4 = (bf16[16,64,64]{2,1,0:T(8,128)(2,1)S(1)}, bf16[16,64,64]{2,1,0:T(8,128)(2,1)}, u32[]{:S(2)}) copy-start(bf16[16,64,64]{2,1,0:T(8,128)(2,1)} %inverse_ref.1) | copy-start | bytes 393220
  0.0 9.4 %copy-start.3 = (bf16[16,2,64,64]{3,2,1,0:T(8,128)(2,1)S(1)}, bf16[16,2,64,64]{3,2,1,0:T(8,128)(2,1)}, u32[]{:S(2)}) copy-start(bf16[16,2,64,64]{3,2,1,0:T(8,128)(2,1)} %remote_weight_ref.1) | copy-start | bytes 786436
  0.0 9.4 %copy-start.2 = (bf16[16,4,64,64]{3,2,1,0:T(8,128)(2,1)S(1)}, bf16[16,4,64,64]{3,2,1,0:T(8,128)(2,1)}, u32[]{:S(2)}) copy-start(bf16[16,4,64,64]{3,2,1,0:T(8,128)(2,1)} %weight_ref.1) | copy-start | bytes 1572868
  0.0 9.4 %copy-start.6 = (s32[16,4]{0,1:T(4,128)S(1)}, s32[16,4]{0,1:T(4,128)}, u32[]{:S(2)}) copy-start(s32[16,4]{0,1:T(4,128)} %param.10) | copy-start | bytes 772
  4.1 10.2 %collective-permute-start.2 = (bf16[2,384,128]{2,1,0:T(8,128)(2,1)}, bf16[2,384,128]{2,1,0:T(8,128)(2,1)S(1)}, u32[]{:S(2)}, u32[]{:S(2)}) collective-permute-start(bf16[2,384,128]{2,1,0:T(8,128)(2,1)} %shard_map.92.refs_0_), channel_id=1, source_target_pairs={{0,6},{1,7},{2,4},{3,5},{4,2},{5,3},{6,0},{7,1},{8,14},{9,15},{10,... | collective-permute-start | bytes 589832 | tf_op jit(solution)/shard_map/ppermute | solution.py:249
  8.1 9.3 %collective-permute-start.1 = (bf16[2,384,128]{2,1,0:T(8,128)(2,1)}, bf16[2,384,128]{2,1,0:T(8,128)(2,1)S(1)}, u32[]{:S(2)}, u32[]{:S(2)}) collective-permute-start(bf16[2,384,128]{2,1,0:T(8,128)(2,1)} %shard_map.92.refs_0_), channel_id=1, source_target_pairs={{0,4},{1,5},{2,6},{3,7},{4,0},{5,1},{6,2},{7,3},{8,12},{9,13},{10,... | collective-permute-start | bytes 589832 | tf_op jit(solution)/shard_map/ppermute | solution.py:249
  8.6 9.1 %collective-permute-start = (bf16[2,384,128]{2,1,0:T(8,128)(2,1)}, bf16[2,384,128]{2,1,0:T(8,128)(2,1)S(1)}, u32[]{:S(2)}, u32[]{:S(2)}) collective-permute-start(bf16[2,384,128]{2,1,0:T(8,128)(2,1)} %shard_map.92.refs_0_), channel_id=1, source_target_pairs={{0,2},{1,3},{2,0},{3,1},{4,6},{5,7},{6,4},{7,5},{8,10},{9,11},{10,... | collective-permute-start | bytes 589832 | tf_op jit(solution)/shard_map/ppermute | solution.py:249
  9.4 8.3 %copy-start = (bf16[2,384,128]{2,1,0:T(8,128)(2,1)S(1)}, bf16[2,384,128]{2,1,0:T(8,128)(2,1)}, u32[]{:S(2)}) copy-start(bf16[2,384,128]{2,1,0:T(8,128)(2,1)} %shard_map.92.refs_0_) | copy-start | bytes 589828
  9.4 10.7 %copy-start.7 = (s32[16,2]{0,1:T(2,128)S(1)}, s32[16,2]{0,1:T(2,128)}, u32[]{:S(2)}) copy-start(s32[16,2]{0,1:T(2,128)} %param.11) | copy-start | bytes 388
  17.7 2.4 %collective-permute-start.3 = (bf16[8,384,128]{2,1,0:T(8,128)(2,1)S(1)}, bf16[8,384,128]{2,1,0:T(8,128)(2,1)S(1)}, u32[]{:S(2)}, u32[]{:S(2)}) collective-permute-start(bf16[8,384,128]{2,1,0:T(8,128)(2,1)S(1)} %shard_map.93.same_ref), channel_id=1, source_target_pairs={{0,1},{1,0},{2,3},{3,2},{4,5},{5,4},{6,7},{7,6},{8,9},{9,8},{10,11... | collective-permute-start | bytes 2359304 | tf_op jit(solution)/shard_map/ppermute | solution.py:249
  24.7 5.9 %collective-permute-start.6 = (bf16[10,16,128]{2,1,0:T(8,128)(2,1)S(1)}, bf16[10,16,128]{2,1,0:T(8,128)(2,1)S(1)}, u32[]{:S(2)}, u32[]{:S(2)}) collective-permute-start(bf16[10,16,128]{2,1,0:T(8,128)(2,1)S(1)} %get-tuple-element.21), channel_id=1, source_target_pairs={{0,24},{8,16},{16,8},{24,0},{1,25},{9,17},{17,9},{25,1},{2,26},{10... | collective-permute-start | bytes 122888 | tf_op jit(solution)/shard_map/ppermute | solution.py:249
  28.4 4.9 %collective-permute-start.5 = (bf16[10,16,128]{2,1,0:T(8,128)(2,1)S(1)}, bf16[10,16,128]{2,1,0:T(8,128)(2,1)S(1)}, u32[]{:S(2)}, u32[]{:S(2)}) collective-permute-start(bf16[10,16,128]{2,1,0:T(8,128)(2,1)S(1)} %get-tuple-element.21), channel_id=1, source_target_pairs={{0,16},{8,24},{16,0},{24,8},{1,17},{9,25},{17,1},{25,9},{2,18},{10... | collective-permute-start | bytes 122888 | tf_op jit(solution)/shard_map/ppermute | solution.py:249
  28.4 4.9 %collective-permute-start.4 = (bf16[10,16,128]{2,1,0:T(8,128)(2,1)S(1)}, bf16[10,16,128]{2,1,0:T(8,128)(2,1)S(1)}, u32[]{:S(2)}, u32[]{:S(2)}) collective-permute-start(bf16[10,16,128]{2,1,0:T(8,128)(2,1)S(1)} %get-tuple-element.21), channel_id=1, source_target_pairs={{0,8},{8,0},{16,24},{24,16},{1,9},{9,1},{17,25},{25,17},{2,10},{10... | collective-permute-start | bytes 122888 | tf_op jit(solution)/shard_map/ppermute | solution.py:249
  35.9 5.9 %collective-permute-start.9 = (bf16[8,16,128]{2,1,0:T(8,128)(2,1)S(1)}, bf16[8,16,128]{2,1,0:T(8,128)(2,1)S(1)}, u32[]{:S(2)}, u32[]{:S(2)}) collective-permute-start(bf16[8,16,128]{2,1,0:T(8,128)(2,1)S(1)} %get-tuple-element.24), channel_id=1, source_target_pairs={{0,24},{8,16},{16,8},{24,0},{1,25},{9,17},{17,9},{25,1},{2,26},{10... | collective-permute-start | bytes 98312 | tf_op jit(solution)/shard_map/ppermute | solution.py:249
  37.7 5.2 %collective-permute-start.8 = (bf16[8,16,128]{2,1,0:T(8,128)(2,1)S(1)}, bf16[8,16,128]{2,1,0:T(8,128)(2,1)S(1)}, u32[]{:S(2)}, u32[]{:S(2)}) collective-permute-start(bf16[8,16,128]{2,1,0:T(8,128)(2,1)S(1)} %get-tuple-element.24), channel_id=1, source_target_pairs={{0,16},{8,24},{16,0},{24,8},{1,17},{9,25},{17,1},{25,9},{2,18},{10... | collective-permute-start | bytes 98312 | tf_op jit(solution)/shard_map/ppermute | solution.py:249
  38.0 4.9 %collective-permute-start.7 = (bf16[8,16,128]{2,1,0:T(8,128)(2,1)S(1)}, bf16[8,16,128]{2,1,0:T(8,128)(2,1)S(1)}, u32[]{:S(2)}, u32[]{:S(2)}) collective-permute-start(bf16[8,16,128]{2,1,0:T(8,128)(2,1)S(1)} %get-tuple-element.24), channel_id=1, source_target_pairs={{0,8},{8,0},{16,24},{24,16},{1,9},{9,1},{17,25},{25,17},{2,10},{10... | collective-permute-start | bytes 98312 | tf_op jit(solution)/shard_map/ppermute | solution.py:249

commit v4 on v3

--- a/solution.py
+++ b/solution.py
@@ -147,19 +147,14 @@
         for pair in range(pairs):
             states[pair] = factor * states[pair] + forcing_ref[pair, rows, :]
     leave(message_ref, states)
-    message_ref[pairs] = product_ref[0]
-    message_ref[pairs + 1] = product_ref[1]
+    for slab in range(message_ref.shape[0]):
+        message_ref[slab, pl.ds(pairs, 2)] = product_ref[...]
 
 
 def leave(message_ref, values):
     for pair, value in enumerate(values):
-        message_ref[pair] = value.astype(jnp.bfloat16)
-
-
-def collect(piece_refs, inbox):
-    me = lax.axis_index("tm")
-    for k, ref in enumerate(piece_refs):
-        inbox[me ^ (k + 1)] = ref[...]
+        for slab in range(message_ref.shape[0]):
+            message_ref[slab, pair] = value.astype(jnp.bfloat16)
 
 
 def carried(pairs, inbox, products, backward):
@@ -174,11 +169,9 @@
     return carries
 
 
-def adjoint_kernel(dims, hops, days_ref, forcing_ref, retain_ref, inverse_ref, *rest):
+def adjoint_kernel(dims, days_ref, forcing_ref, retain_ref, inverse_ref, inbox, adjoint_ref, message_ref, stage):
     days, blocks, size, probes = dims
     pairs = forcing_ref.shape[0]
-    adjoint_ref, message_ref, stage, inbox = rest[hops:]
-    collect(rest[:hops], inbox)
     seen = lax.broadcasted_iota(jnp.int32, (days, LANES), 0) < days_ref[0]
     states = carried(pairs, inbox, inbox, False)
     for day in range(days):
@@ -205,12 +198,9 @@
     leave(message_ref, carries)
 
 
-def variance_kernel(dims, hops, adjoint_ref, retain_ref, moved_ref, *rest):
+def variance_kernel(dims, adjoint_ref, retain_ref, moved_ref, inbox, products, out_ref, stage):
     days, blocks, size, probes = dims
     pairs = adjoint_ref.shape[0]
-    out_ref, stage, inbox, products = rest[2 * hops :]
-    collect(rest[:hops], inbox)
-    collect(rest[hops : 2 * hops], products)
     carries = carried(pairs, inbox, products, True)
     for day in reversed(range(days)):
         rows = pl.ds(day * blocks, blocks)
@@ -277,7 +267,7 @@
         functools.partial(outgoing_kernel, dims),
         [((bound, pairs * days, LANES), bf16)],
         [pltpu.VMEM(probes.shape, bf16), pltpu.SemaphoreType.DMA((days // 8,))], 10**9, 4 * 10**6, 1,
-        shared_blocks, probes, apart=(1,), limit=56 * 1024 * 1024,
+        shared_blocks, probes, apart=(1,), limit=63 * 1024 * 1024,
     )
     pieces = {bits: crossed(outgoing, "space", bits) for bits in range(groups - 2, 0, -2)}
     running, moved, retain, product, remote_weight, inverse = call(
@@ -301,28 +291,26 @@
     )
     other = crossed(same, "space", 1)
     slabs = lax.axis_size("tm")
-    hops = slabs - 1
-    exchange = lambda message: [crossed(message, "tm", bits) for bits in range(hops, 0, -1)][::-1]
-    inbox = pltpu.VMEM((slabs, pairs + 2, blocks, LANES), bf16)
+    exchange = lambda message: lax.all_to_all(message, "tm", 0, 0)
     forcing, message = call(
         functools.partial(forward_kernel, dims),
-        [big, ((pairs + 2, blocks, LANES), bf16)],
+        [big, ((slabs, pairs + 2, blocks, LANES), bf16)],
         [pltpu.VMEM((2 * held, pairs * days, LANES), bf16)], 10**10, 10**7, 2,
         far_table, slab_days, running, same, other, remote_weight, inverse, retain, product,
     )
     ends = exchange(message)
     adjoint, message = call(
-        functools.partial(adjoint_kernel, dims, hops),
-        [big, ((pairs, blocks, LANES), bf16)],
-        [pltpu.VMEM(*big), inbox], 10**10, 10**7, 1,
-        slab_days, forcing, retain, inverse, *ends,
+        functools.partial(adjoint_kernel, dims),
+        [big, ((slabs, pairs, blocks, LANES), bf16)],
+        [pltpu.VMEM(*big)], 10**10, 10**7, 1,
+        slab_days, forcing, retain, inverse, ends,
     )
     starts = exchange(message)
     (variance,) = call(
-        functools.partial(variance_kernel, dims, hops),
+        functools.partial(variance_kernel, dims),
         [((days, blocks * size), f32)],
-        [pltpu.VMEM((rows, LANES), f32), pltpu.VMEM((slabs, pairs, blocks, LANES), bf16), inbox], 10**10, 10**7, 0,
-        adjoint, retain, moved, *starts, *ends,
+        [pltpu.VMEM((rows, LANES), f32)], 10**10, 10**7, 0,
+        adjoint, retain, moved, starts, ends,
     )
     return variance
 

time: 44.6 us -> 49.4 us (1.11)
  blocking collectives: 0 us -> 20.7 us
  waiting for transfers between devices: 12.3 us -> 2.34 us
  starting transfers between devices: 13.6 us -> 4.68 us
  local copies, waits for them, and re-layouts: 0.04 us -> 3.33 us
    all_to_all x0 -> x2, blocking collectives: none -> 20.7 us  [local(): exchange = lambda message: lax.all_to_all(message, 'tm', 0, 0)]
    ppermute x10 -> x4, waiting for transfers between devices: 12.3 us -> 2.34 us  [crossed(): lax.ppermute(block, axis, [(i, i ^ bits) for i in range(lax.axis_size(axi...]
    ppermute x10 -> x4, starting transfers between devices: 13.6 us -> 4.68 us  [crossed(): lax.ppermute(block, axis, [(i, i ^ bits) for i in range(lax.axis_size(axi...]
    unnamed x16, local copies, waits for them, and re-layouts: 0.04 us -> 3.33 us
  transfers between devices with their start and end apart: 10 -> 4, of which waited for: 7 -> 2; matrix products, arithmetic and copies ran while one was open for 0% -> 0% of each run, Pallas kernels for 11% -> 10%
where the time goes in v4:
time: 49.4 us; the launch traced here: 49.1 us
  blocking collectives  20.7 us (42%)
  Pallas kernels  17.3 us (35%)
  starting transfers between devices  4.68 us (9%)
  local copies, waits for them, and re-layouts  3.33 us (7%)
  waiting for transfers between devices  2.34 us (5%)
  between operations  0.74 us (1%)
    all_to_all x2, blocking collectives, local(): exchange = lambda message: lax.all_to_all(message, 'tm', 0, 0)  20.7 us
    pallas_call x6, Pallas kernels, call(): pl.pallas_call(kernel, out_shape=[jax.ShapeDtypeStruct(shape, kind) for s...  17.3 us
    ppermute x4, starting transfers between devices, crossed(): lax.ppermute(block, axis, [(i, i ^ bits) for i in range(lax.axis_size(axi...  4.68 us
    unnamed x16, local copies, waits for them, and re-layouts  3.33 us
    ppermute x4, waiting for transfers between devices, crossed(): lax.ppermute(block, axis, [(i, i ^ bits) for i in range(lax.axis_size(axi...  2.34 us
  transfers between devices with their start and end apart: 4, of which 2 were waited for; matrix products, arithmetic and copies ran while one was open for 0% of the time, Pallas kernels for 10%

profile of v4, /device:TPU:0, one launch (start us, length us, event | category | flops | bytes accessed | tf_op | source)
XLA Modules:
  0.0 49.1 jit_solution(11328024696842244132)
XLA Ops:
  0.0 0.0 copy-start.5
  0.0 0.0 copy-start.4
  0.0 0.0 copy-start.3
  0.0 3.8 %shard_map.92.refs_0_ = bf16[2,384,128]{2,1,0:T(8,128)(2,1)} custom-call(s32[1,2]{1,0:T(1,128)} %shared_ref.1, bf16[48,16,1024]{2,1,0:T(8,128)(2,1)} %z_hbm.1), custom_call_target="tpu_custom_call" | custom-call | flops 1000000000 | bytes 4000000 | tf_op jit(solution)/shard_map/pallas_call | solution.py:227
  3.8 4.0 %collective-permute-start.2 = (bf16[2,384,128]{2,1,0:T(8,128)(2,1)}, bf16[2,384,128]{2,1,0:T(8,128)(2,1)S(1)}, u32[]{:S(2)}, u32[]{:S(2)}) collective-permute-start(bf16[2,384,128]{2,1,0:T(8,128)(2,1)} %shard_map.92.refs_0_), channel_id=1, source_target_pairs={{0,6},{1,7},{2,4},{3,5},{4,2},{5,3},{6,0},{7,1},{8,14},{9,15},{10,... | collective-permute-start | bytes 589832 | tf_op jit(solution)/shard_map/ppermute | solution.py:239
  7.8 0.5 %collective-permute-start.1 = (bf16[2,384,128]{2,1,0:T(8,128)(2,1)}, bf16[2,384,128]{2,1,0:T(8,128)(2,1)S(1)}, u32[]{:S(2)}, u32[]{:S(2)}) collective-permute-start(bf16[2,384,128]{2,1,0:T(8,128)(2,1)} %shard_map.92.refs_0_), channel_id=1, source_target_pairs={{0,4},{1,5},{2,6},{3,7},{4,0},{5,1},{6,2},{7,3},{8,12},{9,13},{10,... | collective-permute-start | bytes 589832 | tf_op jit(solution)/shard_map/ppermute | solution.py:239
  8.3 0.1 collective-permute-start
  9.1 0.0 copy-done.5
  9.1 0.0 copy-done.4
  9.1 0.0 copy-done.3
  9.1 0.0 copy-start.1
  9.1 1.4 %copy-done.1 = bf16[48,16,1024]{2,1,0:T(8,128)(2,1)S(1)} copy-done((bf16[48,16,1024]{2,1,0:T(8,128)(2,1)S(1)}, bf16[48,16,1024]{2,1,0:T(8,128)(2,1)}, u32[]{:S(2)}) %copy-start.1) | copy-done | bytes 1572888
  10.5 0.0 copy-start.2
  10.5 1.2 %copy-done.2 = bf16[16,4,64,64]{3,2,1,0:T(8,128)(2,1)S(1)} copy-done((bf16[16,4,64,64]{3,2,1,0:T(8,128)(2,1)S(1)}, bf16[16,4,64,64]{3,2,1,0:T(8,128)(2,1)}, u32[]{:S(2)}) %copy-start.2) | copy-done | bytes 524312
  11.7 0.0 copy-start.6
  11.7 0.7 %copy-done.6 = s32[16,4]{0,1:T(4,128)S(1)} copy-done((s32[16,4]{0,1:T(4,128)S(1)}, s32[16,4]{0,1:T(4,128)}, u32[]{:S(2)}) %copy-start.6) | copy-done | bytes 280
  12.4 0.0 copy-start
  12.4 0.0 copy-start.7
  12.4 4.9 %shard_map.91 = (f32[16,384,128]{2,1,0:T(8,128)S(1)}, bf16[8,768,128]{2,1,0:T(8,128)(2,1)S(1)}, f32[768,128]{1,0:T(8,128)S(1)}, bf16[2,16,128]{2,1,0:T(8,128)(2,...) custom-call(s32[4,16]{1,0:T(4,128)S(1)} %bitcast.2, s32[1]{0:T(128)S(6)} %copy.10.days_ref, ...), custom_call_target="tpu_custom_call" | custom-call | flops 10000000000 | bytes 10000000 | tf_op jit(solution)/shard_map/pallas_call | solution.py:227
  17.3 0.0 collective-permute-done.2.refs_3_
  17.3 0.0 collective-permute-done.1.refs_2_
  17.3 0.1 collective-permute-done.refs_1_
  17.4 0.0 copy-done
  17.4 0.1 shard_map.93.same_ref
  17.4 0.1 collective-permute-start.3
  17.5 2.3 %collective-permute-done.3.other_ref = bf16[8,384,128]{2,1,0:T(8,128)(2,1)S(1)} collective-permute-done((bf16[8,384,128]{2,1,0:T(8,128)(2,1)S(1)}, bf16[8,384,128]{2,1,0:T(8,128)(2,1)S(1)}, u32[]{:S(2)}, u32[]{:S(2)}) %collective-permute-start.3) | collective-permute-done | bytes 786464 | tf_op jit(solution)/shard_map/ppermute | solution.py:239
  19.8 0.0 copy-done.7
  19.8 4.6 %shard_map.94 = (f32[8,768,128]{2,1,0:T(8,128)S(1)}, bf16[4,10,16,128]{3,2,1,0:T(8,128)(2,1)S(1)}) custom-call(s32[2,16]{1,0:T(2,128)S(1)} %bitcast.3, s32[1]{0:T(128)S(6)} %copy.10.days_ref, f32[16,384,128]{2,1,0:T(8,128)S(1)} %get-tuple-element.15.running_ref, bf16[8,384,128]{2,1,0:T(8,128)(2,1)S(1)} %shard_map.93.same_ref, ...), custom_call_target="tpu_custom_call" | custom-call | flops 10000000000 | bytes 10000000 | tf_op jit(solution)/shard_map/pallas_call | solution.py:227
  24.4 12.0 %all_to_all.10.inbox.products = bf16[4,10,16,128]{3,2,1,0:T(8,128)(2,1)S(1)} all-to-all(bf16[4,10,16,128]{3,2,1,0:T(8,128)(2,1)S(1)} %get-tuple-element.21), channel_id=1, replica_groups=mesh['tm'=4,'space'=8] {'tm'}, dimensions={0} | all-to-all | bytes 327680 | tf_op jit(solution)/shard_map/all_to_all | solution.py:294
  36.5 2.5 %shard_map.95 = (f32[8,768,128]{2,1,0:T(8,128)S(1)}, bf16[4,8,16,128]{3,2,1,0:T(8,128)(2,1)S(1)}) custom-call(s32[1]{0:T(128)S(6)} %copy.10.days_ref, f32[8,768,128]{2,1,0:T(8,128)S(1)} %get-tuple-element.20.forcing_ref, f32[768,128]{1,0:T(8,128)S(1)} %get-tuple-element.19.retain_ref, bf16[16,128,128]{2,1,0:T(8,128)(2,1)S(1)} %get-tuple-element.18.inverse_ref, ...), custom_call_target="tpu_custom_call" | custom-call | flops 10000000000 | bytes 10000000 | tf_op jit(solution)/shard_map/pallas_call | solution.py:227
  39.0 8.7 %all_to_all.11.inbox = bf16[4,8,16,128]{3,2,1,0:T(8,128)(2,1)S(1)} all-to-all(bf16[4,8,16,128]{3,2,1,0:T(8,128)(2,1)S(1)} %get-tuple-element.24), channel_id=1, replica_groups=mesh['tm'=4,'space'=8] {'tm'}, dimensions={0} | all-to-all | bytes 262144 | tf_op jit(solution)/shard_map/all_to_all | solution.py:294
  47.6 1.5 %shard_map.96 = f32[48,1024]{1,0:T(8,128)} custom-call(f32[8,768,128]{2,1,0:T(8,128)S(1)} %get-tuple-element.22.adjoint_ref, f32[768,128]{1,0:T(8,128)S(1)} %get-tuple-element.19.retain_ref, bf16[8,768,128]{2,1,0:T(8,128)(2,1)S(1)} %get-tuple-element.23.moved_ref, bf16[4,8,16,128]{3,2,1,0:T(8,128)(2,1)S(1)} %all_to_all.11.inbox, ...), custom_call_target="tpu_custom_call" | custom-call | flops 10000000000 | bytes 10000000 | tf_op jit(solution)/shard_map/pallas_call | solution.py:227
Async XLA Ops:
  0.0 9.1 %copy-start.5 = (f32[48,1024]{1,0:T(8,128)S(1)}, f32[48,1024]{1,0:T(8,128)}, u32[]{:S(2)}) copy-start(f32[48,1024]{1,0:T(8,128)} %retention_ref.1) | copy-start | bytes 589828
  0.0 9.1 %copy-start.4 = (bf16[16,64,64]{2,1,0:T(8,128)(2,1)S(1)}, bf16[16,64,64]{2,1,0:T(8,128)(2,1)}, u32[]{:S(2)}) copy-start(bf16[16,64,64]{2,1,0:T(8,128)(2,1)} %inverse_ref.1) | copy-start | bytes 393220
  0.0 9.1 %copy-start.3 = (bf16[16,2,64,64]{3,2,1,0:T(8,128)(2,1)S(1)}, bf16[16,2,64,64]{3,2,1,0:T(8,128)(2,1)}, u32[]{:S(2)}) copy-start(bf16[16,2,64,64]{3,2,1,0:T(8,128)(2,1)} %remote_weight_ref.1) | copy-start | bytes 786436
  3.8 13.5 %collective-permute-start.2 = (bf16[2,384,128]{2,1,0:T(8,128)(2,1)}, bf16[2,384,128]{2,1,0:T(8,128)(2,1)S(1)}, u32[]{:S(2)}, u32[]{:S(2)}) collective-permute-start(bf16[2,384,128]{2,1,0:T(8,128)(2,1)} %shard_map.92.refs_0_), channel_id=1, source_target_pairs={{0,6},{1,7},{2,4},{3,5},{4,2},{5,3},{6,0},{7,1},{8,14},{9,15},{10,... | collective-permute-start | bytes 589832 | tf_op jit(solution)/shard_map/ppermute | solution.py:239
  7.8 9.5 %collective-permute-start.1 = (bf16[2,384,128]{2,1,0:T(8,128)(2,1)}, bf16[2,384,128]{2,1,0:T(8,128)(2,1)S(1)}, u32[]{:S(2)}, u32[]{:S(2)}) collective-permute-start(bf16[2,384,128]{2,1,0:T(8,128)(2,1)} %shard_map.92.refs_0_), channel_id=1, source_target_pairs={{0,4},{1,5},{2,6},{3,7},{4,0},{5,1},{6,2},{7,3},{8,12},{9,13},{10,... | collective-permute-start | bytes 589832 | tf_op jit(solution)/shard_map/ppermute | solution.py:239
  8.3 9.1 %collective-permute-start = (bf16[2,384,128]{2,1,0:T(8,128)(2,1)}, bf16[2,384,128]{2,1,0:T(8,128)(2,1)S(1)}, u32[]{:S(2)}, u32[]{:S(2)}) collective-permute-start(bf16[2,384,128]{2,1,0:T(8,128)(2,1)} %shard_map.92.refs_0_), channel_id=1, source_target_pairs={{0,2},{1,3},{2,0},{3,1},{4,6},{5,7},{6,4},{7,5},{8,10},{9,11},{10,... | collective-permute-start | bytes 589832 | tf_op jit(solution)/shard_map/ppermute | solution.py:239
  9.1 1.4 %copy-start.1 = (bf16[48,16,1024]{2,1,0:T(8,128)(2,1)S(1)}, bf16[48,16,1024]{2,1,0:T(8,128)(2,1)}, u32[]{:S(2)}) copy-start(bf16[48,16,1024]{2,1,0:T(8,128)(2,1)} %z_hbm.1) | copy-start | bytes 4718596
  10.5 1.2 %copy-start.2 = (bf16[16,4,64,64]{3,2,1,0:T(8,128)(2,1)S(1)}, bf16[16,4,64,64]{3,2,1,0:T(8,128)(2,1)}, u32[]{:S(2)}) copy-start(bf16[16,4,64,64]{3,2,1,0:T(8,128)(2,1)} %weight_ref.1) | copy-start | bytes 1572868
  11.7 0.7 %copy-start.6 = (s32[16,4]{0,1:T(4,128)S(1)}, s32[16,4]{0,1:T(4,128)}, u32[]{:S(2)}) copy-start(s32[16,4]{0,1:T(4,128)} %param.10) | copy-start | bytes 772
  12.4 5.0 %copy-start = (bf16[2,384,128]{2,1,0:T(8,128)(2,1)S(1)}, bf16[2,384,128]{2,1,0:T(8,128)(2,1)}, u32[]{:S(2)}) copy-start(bf16[2,384,128]{2,1,0:T(8,128)(2,1)} %shard_map.92.refs_0_) | copy-start | bytes 589828
  12.4 7.4 %copy-start.7 = (s32[16,2]{0,1:T(2,128)S(1)}, s32[16,2]{0,1:T(2,128)}, u32[]{:S(2)}) copy-start(s32[16,2]{0,1:T(2,128)} %param.11) | copy-start | bytes 388
  17.4 2.4 %collective-permute-start.3 = (bf16[8,384,128]{2,1,0:T(8,128)(2,1)S(1)}, bf16[8,384,128]{2,1,0:T(8,128)(2,1)S(1)}, u32[]{:S(2)}, u32[]{:S(2)}) collective-permute-start(bf16[8,384,128]{2,1,0:T(8,128)(2,1)S(1)} %shard_map.93.same_ref), channel_id=1, source_target_pairs={{0,1},{1,0},{2,3},{3,2},{4,5},{5,4},{6,7},{7,6},{8,9},{9,8},{10,11... | collective-permute-start | bytes 2359304 | tf_op jit(solution)/shard_map/ppermute | solution.py:239

commit v5 on v3

--- a/solution.py
+++ b/solution.py
@@ -27,44 +27,43 @@
     )
 
 
-def outgoing_kernel(dims, shared_ref, z_hbm, outgoing_ref, z_ref, arrived):
-    days, blocks, size, probes = dims
-    count = outgoing_ref.shape[0]
-    part = 8
-    copies = [
-        pltpu.make_async_copy(z_hbm.at[pl.ds(i * part, part)], z_ref.at[pl.ds(i * part, part)], arrived.at[i])
-        for i in range(days // part)
+def locate(pair, sizes):
+    chunk = 0
+    while pair >= sizes[chunk]:
+        pair -= sizes[chunk]
+        chunk += 1
+    return chunk, pair
+
+
+def outgoing_kernel(dims, shared_ref, z_ref, *outgoing_refs):
+    days, blocks, size, probes = dims
+    count = outgoing_refs[0].shape[0]
+    z = z_ref[...].reshape(days * blocks, size * probes)
+    row = lax.broadcasted_iota(jnp.int32, (days, days * blocks), 0)
+    column = lax.broadcasted_iota(jnp.int32, (days, days * blocks), 1)
+    picks = [
+        (column == row * blocks + shared_ref[m]).astype(jnp.float32).astype(jnp.bfloat16) for m in range(count)
     ]
-    for copy in copies:
-        copy.start()
+    picked = jnp.dot(jnp.concatenate(picks, axis=0), z, preferred_element_type=jnp.float32).astype(jnp.bfloat16)
     step = 2 * LANES
-    moves = [permutation(size, probes, start, step) for start in range(0, size * probes, step)]
-    row = lax.broadcasted_iota(jnp.int32, (part, part * blocks), 0)
-    column = lax.broadcasted_iota(jnp.int32, (part, part * blocks), 1)
-    picks = [(column == row * blocks + shared_ref[0, m]).astype(jnp.float32) for m in range(count)]
-    pick = jnp.concatenate(picks, axis=0).astype(jnp.bfloat16)
-    picked = []
-    for i, copy in enumerate(copies):
-        copy.wait()
-        z = z_ref[pl.ds(i * part, part)].reshape(part * blocks, size * probes)
-        picked.append(jnp.dot(pick, z, preferred_element_type=jnp.float32))
-    picked = jnp.concatenate([rows[m * part : (m + 1) * part] for m in range(count) for rows in picked], axis=0)
-    picked = picked.astype(jnp.bfloat16)
-    for i, move in enumerate(moves):
-        moved = jnp.dot(picked, move, preferred_element_type=jnp.float32).astype(jnp.bfloat16)
+    for start in range(0, size * probes, step):
+        moved = jnp.dot(picked, permutation(size, probes, start, step), preferred_element_type=jnp.float32)
+        moved = moved.astype(jnp.bfloat16)
         for half in range(2):
-            pair = i * 2 + half
+            pair = start // LANES + half
             for m in range(count):
-                outgoing_ref[m, pl.ds(pair * days, days), :] = moved[
+                chunk, place = locate(pair, [ref.shape[1] // days for ref in outgoing_refs])
+                outgoing_refs[chunk][m, pl.ds(place * days, days), :] = moved[
                     m * days : (m + 1) * days, half * LANES : (half + 1) * LANES
                 ]
 
 
 def local_kernel(
-    dims, links_ref, days_ref, z_ref, weight_ref, remote_weight_ref, inverse_ref, retention_ref,
-    running_ref, moved_ref, retain_ref, product_ref, remote_doubled_ref, inverse_doubled_ref, stage, turned,
+    dims, chunks, links_ref, days_ref, z_ref, weight_ref, remote_weight_ref, inverse_ref, retention_ref, *rest
 ):
     days, blocks, size, probes = dims
+    running_refs, rest = rest[:chunks], rest[chunks:]
+    moved_ref, retain_ref, product_ref, remote_doubled_ref, inverse_doubled_ref, stage, turned = rest
     pairs = size * probes // LANES
     count = links_ref.shape[0]
     z = z_ref[...].reshape(days * blocks, size * probes)
@@ -84,7 +83,11 @@
         near = jnp.concatenate([turned[links_ref[k, block]] for k in range(count)], axis=1)
         weight = jnp.concatenate([doubled(weight_ref[block, k]) for k in range(count)], axis=1)
         total = lax.dot_general(near, weight, TURNED, preferred_element_type=jnp.float32)
-        running_ref[block] = turned[block].astype(jnp.float32) - total
+        running = turned[block].astype(jnp.float32) - total
+        start = 0
+        for ref in running_refs:
+            ref[block] = running[start : start + ref.shape[1]]
+            start += ref.shape[1]
         remote_doubled_ref[block] = jnp.concatenate(
             [doubled(remote_weight_ref[block, k]) for k in range(remote_weight_ref.shape[1])], axis=1
         )
@@ -101,9 +104,9 @@
     product = jnp.ones((blocks, LANES), jnp.float32)
     for day in range(days):
         product = product * retain_ref[pl.ds(day * blocks, blocks), :]
-    high = product.astype(jnp.bfloat16)
-    product_ref[0] = high
-    product_ref[1] = (product - high.astype(jnp.float32)).astype(jnp.bfloat16)
+    high = product.astype(jnp.bfloat16).astype(jnp.float32)
+    half = lax.broadcasted_iota(jnp.int32, product.shape, 1) < size
+    product_ref[...] = jnp.where(half, high, product - high).astype(jnp.bfloat16)
 
 
 def assemble_kernel(*refs):
@@ -114,7 +117,7 @@
 
 
 def forward_kernel(
-    dims, links_ref, days_ref, running_ref, same_ref, other_ref, weight_ref, inverse_ref, retain_ref, product_ref,
+    dims, start, links_ref, days_ref, running_ref, same_ref, other_ref, weight_ref, inverse_ref, retain_ref, last_ref,
     forcing_ref, message_ref, remote,
 ):
     days, blocks, size, probes = dims
@@ -146,14 +149,18 @@
         factor = retain_ref[rows, :]
         for pair in range(pairs):
             states[pair] = factor * states[pair] + forcing_ref[pair, rows, :]
-    leave(message_ref, states)
-    message_ref[pairs] = product_ref[0]
-    message_ref[pairs + 1] = product_ref[1]
-
-
-def leave(message_ref, values):
+    end = message_ref.shape[0] - 1
+    if start > 0:
+        message_ref[pl.ds(0, start)] = last_ref[pl.ds(0, start)]
+        message_ref[end] = last_ref[end]
+    else:
+        message_ref[end] = last_ref[...]
+    leave(message_ref, states, start)
+
+
+def leave(message_ref, values, start=0):
     for pair, value in enumerate(values):
-        message_ref[pair] = value.astype(jnp.bfloat16)
+        message_ref[start + pair] = value.astype(jnp.bfloat16)
 
 
 def collect(piece_refs, inbox):
@@ -167,17 +174,19 @@
     carries = [jnp.zeros(inbox.shape[2:], jnp.float32)] * pairs
     for slab in range(count - 1, 0, -1) if backward else range(count - 1):
         valid = slab > me if backward else slab < me
-        factor = products[slab, pairs].astype(jnp.float32) + products[slab, pairs + 1].astype(jnp.float32)
+        terms = products[slab, pairs].astype(jnp.float32)
+        factor = terms + pltpu.roll(terms, LANES // 2, 1)
         for pair in range(pairs):
             update = inbox[slab, pair].astype(jnp.float32) + factor * carries[pair]
             carries[pair] = jnp.where(valid, update, carries[pair])
     return carries
 
 
-def adjoint_kernel(dims, hops, days_ref, forcing_ref, retain_ref, inverse_ref, *rest):
-    days, blocks, size, probes = dims
-    pairs = forcing_ref.shape[0]
+def adjoint_kernel(dims, split, hops, days_ref, retain_ref, inverse_ref, *rest):
+    days, blocks, size, probes = dims
+    forcing_refs, rest = rest[: len(split)], rest[len(split) :]
     adjoint_ref, message_ref, stage, inbox = rest[hops:]
+    pairs = adjoint_ref.shape[0]
     collect(rest[:hops], inbox)
     seen = lax.broadcasted_iota(jnp.int32, (days, LANES), 0) < days_ref[0]
     states = carried(pairs, inbox, inbox, False)
@@ -185,7 +194,8 @@
         rows = pl.ds(day * blocks, blocks)
         factor = retain_ref[rows, :]
         for pair in range(pairs):
-            states[pair] = factor * states[pair] + forcing_ref[pair, rows, :]
+            chunk, place = locate(pair, split)
+            states[pair] = factor * states[pair] + forcing_refs[chunk][place, rows, :]
             stage[pair, rows, :] = states[pair]
     for block in range(blocks):
         stored = jnp.concatenate(
@@ -271,22 +281,23 @@
     groups = lax.axis_size("space")
     held = groups // 2 * bound
     near_table, far_table = local_links.T, remote_links.T
+    shared = jnp.maximum(shared_blocks[0], 0)
     big = ((pairs, rows, LANES), f32)
-
-    (outgoing,) = call(
+    split = (pairs - 2, 2)
+
+    outgoing = call(
         functools.partial(outgoing_kernel, dims),
-        [((bound, pairs * days, LANES), bf16)],
-        [pltpu.VMEM(probes.shape, bf16), pltpu.SemaphoreType.DMA((days // 8,))], 10**9, 4 * 10**6, 1,
-        shared_blocks, probes, apart=(1,), limit=56 * 1024 * 1024,
-    )
-    pieces = {bits: crossed(outgoing, "space", bits) for bits in range(groups - 2, 0, -2)}
-    running, moved, retain, product, remote_weight, inverse = call(
-        functools.partial(local_kernel, dims),
-        [
-            ((blocks, pairs * days, LANES), f32),
+        [((bound, part * days, LANES), bf16) for part in split],
+        [], 10**9, 4 * 10**6, 1, shared, probes,
+    )
+    pieces = [{bits: crossed(own, "space", bits) for bits in range(groups - 2, 0, -2)} for own in outgoing]
+    results = call(
+        functools.partial(local_kernel, dims, len(split)),
+        [((blocks, part * days, LANES), f32) for part in split]
+        + [
             ((pairs, rows, LANES), bf16),
             ((rows, LANES), f32),
-            ((2, blocks, LANES), bf16),
+            ((blocks, LANES), bf16),
             ((blocks, LANES, far * LANES), bf16),
             ((blocks, LANES, LANES), bf16),
         ],
@@ -294,28 +305,33 @@
         10**10, 10**7, 2,
         near_table, slab_days, probes, local_coupling, remote_coupling, block_inverse, retention,
     )
-    (same,) = call(
-        assemble_kernel,
-        [((held, pairs * days, LANES), bf16)],
-        [], 0, 10**6, 0, outgoing, *[pieces[bits] for bits in range(2, groups, 2)], product,
-    )
-    other = crossed(same, "space", 1)
+    running = results[: len(split)]
+    moved, retain, product, remote_weight, inverse = results[len(split) :]
+    same, other = [], []
+    for chunk, part in enumerate(split):
+        parts = [outgoing[chunk]] + [pieces[chunk][bits] for bits in range(2, groups, 2)]
+        (whole,) = call(assemble_kernel, [((held, part * days, LANES), bf16)], [], 0, 10**6, 0, *parts, product)
+        same.append(whole)
+        other.append(crossed(whole, "space", 1))
     slabs = lax.axis_size("tm")
     hops = slabs - 1
     exchange = lambda message: [crossed(message, "tm", bits) for bits in range(hops, 0, -1)][::-1]
-    inbox = pltpu.VMEM((slabs, pairs + 2, blocks, LANES), bf16)
-    forcing, message = call(
-        functools.partial(forward_kernel, dims),
-        [big, ((pairs + 2, blocks, LANES), bf16)],
-        [pltpu.VMEM((2 * held, pairs * days, LANES), bf16)], 10**10, 10**7, 2,
-        far_table, slab_days, running, same, other, remote_weight, inverse, retain, product,
-    )
+    inbox = pltpu.VMEM((slabs, pairs + 1, blocks, LANES), bf16)
+    message, forcing = product, []
+    for chunk, part in enumerate(split):
+        drive, message = call(
+            functools.partial(forward_kernel, dims, sum(split[:chunk])),
+            [((part, rows, LANES), f32), ((pairs + 1, blocks, LANES), bf16)],
+            [pltpu.VMEM((2 * held, part * days, LANES), bf16)], 10**8, 10**5, 2,
+            far_table, slab_days, running[chunk], same[chunk], other[chunk], remote_weight, inverse, retain, message,
+        )
+        forcing.append(drive)
     ends = exchange(message)
     adjoint, message = call(
-        functools.partial(adjoint_kernel, dims, hops),
+        functools.partial(adjoint_kernel, dims, split, hops),
         [big, ((pairs, blocks, LANES), bf16)],
         [pltpu.VMEM(*big), inbox], 10**10, 10**7, 1,
-        slab_days, forcing, retain, inverse, *ends,
+        slab_days, retain, inverse, *forcing, *ends,
     )
     starts = exchange(message)
     (variance,) = call(

time: 44.6 us -> 49.6 us (1.11)
  starting transfers between devices: 13.6 us -> 17.2 us
  local copies, waits for them, and re-layouts: 0.04 us -> 1.44 us
  Pallas kernels: 17.7 us -> 16.4 us
  other arithmetic: 0 us -> 0.66 us
  waiting for transfers between devices: 12.3 us -> 12.9 us
    ppermute x10 -> x14, starting transfers between devices: 13.6 us -> 17.2 us  [crossed(): lax.ppermute(block, axis, [(i, i ^ bits) for i in range(lax.axis_size(axi...]
    unnamed x16, local copies, waits for them, and re-layouts: 0.04 us -> 1.44 us
    pallas_call x6 -> x8, Pallas kernels: 17.7 us -> 16.4 us  [call(): pl.pallas_call(kernel, out_shape=[jax.ShapeDtypeStruct(shape, kind) for s...]
    max x0 -> x1, other arithmetic: none -> 0.66 us  [local(): shared = jnp.maximum(shared_blocks[0], 0)]
    ppermute x10 -> x14, waiting for transfers between devices: 12.3 us -> 12.9 us  [crossed(): lax.ppermute(block, axis, [(i, i ^ bits) for i in range(lax.axis_size(axi...]
  transfers between devices with their start and end apart: 10 -> 14, of which waited for: 7 -> 9; matrix products, arithmetic and copies ran while one was open for 0% -> 0% of each run, Pallas kernels for 11% -> 18%
where the time goes in v5:
time: 49.6 us; the launch traced here: 49.5 us
  starting transfers between devices  17.2 us (35%)
  Pallas kernels  16.4 us (33%)
  waiting for transfers between devices  12.9 us (26%)
  local copies, waits for them, and re-layouts  1.44 us (3%)
  between operations  0.82 us (2%)
  other arithmetic  0.66 us (1%)
    ppermute x14, starting transfers between devices, crossed(): lax.ppermute(block, axis, [(i, i ^ bits) for i in range(lax.axis_size(axi...  17.2 us
    pallas_call x8, Pallas kernels, call(): pl.pallas_call(kernel, out_shape=[jax.ShapeDtypeStruct(shape, kind) for s...  16.4 us
    ppermute x14, waiting for transfers between devices, crossed(): lax.ppermute(block, axis, [(i, i ^ bits) for i in range(lax.axis_size(axi...  12.9 us
    unnamed x16, local copies, waits for them, and re-layouts  1.44 us
  transfers between devices with their start and end apart: 14, of which 9 were waited for; matrix products, arithmetic and copies ran while one was open for 0% of the time, Pallas kernels for 18%

profile of v5, /device:TPU:0, one launch (start us, length us, event | category | flops | bytes accessed | tf_op | source)
XLA Modules:
  0.0 49.5 jit_solution(16970866934840572084)
XLA Ops:
  0.0 0.7 %maximum_bitcast_fusion.shared_ref = s32[2]{0:T(128)S(1)} fusion(s32[1,2]{1,0:T(1,128)} %param.12), kind=kLoop, calls=%fused_computation | loop fusion | flops 2 | bytes 16 | tf_op jit(solution)/shard_map/max | solution.py:284
  0.7 0.0 copy-start.1
  0.7 1.4 %copy-done.1 = bf16[48,16,1024]{2,1,0:T(8,128)(2,1)S(1)} copy-done((bf16[48,16,1024]{2,1,0:T(8,128)(2,1)S(1)}, bf16[48,16,1024]{2,1,0:T(8,128)(2,1)}, u32[]{:S(2)}) %copy-start.1) | copy-done | bytes 1572888
  2.1 0.0 copy-start.2
  2.1 0.0 copy-start.3
  2.1 0.0 copy-start.4
  2.1 0.0 copy-start.5
  2.1 0.0 copy-start.6
  2.1 0.0 copy-start.7
  2.1 1.3 %shard_map.92 = (bf16[2,288,128]{2,1,0:T(8,128)(2,1)S(1)}, bf16[2,96,128]{2,1,0:T(8,128)(2,1)S(1)}) custom-call(s32[2]{0:T(128)S(1)} %maximum_bitcast_fusion.shared_ref, bf16[48,16,1024]{2,1,0:T(8,128)(2,1)S(1)} %copy-done.1), custom_call_target="tpu_custom_call" | custom-call | flops 1000000000 | bytes 4000000 | tf_op jit(solution)/shard_map/pallas_call | solution.py:247
  3.4 3.0 %collective-permute-start = (bf16[2,288,128]{2,1,0:T(8,128)(2,1)S(1)}, bf16[2,288,128]{2,1,0:T(8,128)(2,1)S(1)}, u32[]{:S(2)}, u32[]{:S(2)}) collective-permute-start(bf16[2,288,128]{2,1,0:T(8,128)(2,1)S(1)} %get-tuple-element.23.refs_0_), channel_id=1, source_target_pairs={{0,2},{1,3},{2,0},{3,1},{4,6},{5,7},{6,4},{7,5},{8,10},{9,11},{10,... | collective-permute-start | bytes 442376 | tf_op jit(solution)/shard_map/ppermute | solution.py:259
  6.4 1.5 %collective-permute-start.1 = (bf16[2,288,128]{2,1,0:T(8,128)(2,1)S(1)}, bf16[2,288,128]{2,1,0:T(8,128)(2,1)S(1)}, u32[]{:S(2)}, u32[]{:S(2)}) collective-permute-start(bf16[2,288,128]{2,1,0:T(8,128)(2,1)S(1)} %get-tuple-element.23.refs_0_), channel_id=1, source_target_pairs={{0,4},{1,5},{2,6},{3,7},{4,0},{5,1},{6,2},{7,3},{8,12},{9,13},{10,... | collective-permute-start | bytes 442376 | tf_op jit(solution)/shard_map/ppermute | solution.py:259
  7.9 0.0 collective-permute-start.2
  8.6 0.0 copy-done.2
  8.6 0.0 copy-done.3
  8.6 0.0 copy-done.4
  8.7 0.0 copy-done.5
  8.7 0.0 copy-done.6
  8.7 0.0 copy-done.7
  8.7 0.0 copy-start
  8.7 4.9 %shard_map.91 = (f32[16,288,128]{2,1,0:T(8,128)S(1)}, f32[16,96,128]{2,1,0:T(8,128)S(1)}, bf16[8,768,128]{2,1,0:T(8,128)(2,1)S(1)}, f32[768,128]{1,0:T(8,128)S(1...) custom-call(s32[4,16]{1,0:T(4,128)S(1)} %bitcast.6, ...), custom_call_target="tpu_custom_call" | custom-call | flops 10000000000 | bytes 10000000 | tf_op jit(solution)/shard_map/pallas_call | solution.py:247
  13.6 0.0 collective-permute-done.refs_1_
  13.7 1.2 %collective-permute-done.1.refs_2_ = bf16[2,288,128]{2,1,0:T(8,128)(2,1)S(1)} collective-permute-done((bf16[2,288,128]{2,1,0:T(8,128)(2,1)S(1)}, bf16[2,288,128]{2,1,0:T(8,128)(2,1)S(1)}, u32[]{:S(2)}, u32[]{:S(2)}) %collective-permute-start.1) | collective-permute-done | bytes 147488 | tf_op jit(solution)/shard_map/ppermute | solution.py:259
  14.9 0.0 collective-permute-done.2.refs_3_
  14.9 0.1 collective-permute-start.3
  15.0 1.3 %collective-permute-start.4 = (bf16[2,96,128]{2,1,0:T(8,128)(2,1)S(1)}, bf16[2,96,128]{2,1,0:T(8,128)(2,1)S(1)}, u32[]{:S(2)}, u32[]{:S(2)}) collective-permute-start(bf16[2,96,128]{2,1,0:T(8,128)(2,1)S(1)} %get-tuple-element.28.refs_0_), channel_id=1, source_target_pairs={{0,2},{1,3},{2,0},{3,1},{4,6},{5,7},{6,4},{7,5},{8,10},{9,11},{10,... | collective-permute-start | bytes 147464 | tf_op jit(solution)/shard_map/ppermute | solution.py:259
  16.3 1.0 %collective-permute-start.5 = (bf16[2,96,128]{2,1,0:T(8,128)(2,1)S(1)}, bf16[2,96,128]{2,1,0:T(8,128)(2,1)S(1)}, u32[]{:S(2)}, u32[]{:S(2)}) collective-permute-start(bf16[2,96,128]{2,1,0:T(8,128)(2,1)S(1)} %get-tuple-element.28.refs_0_), channel_id=1, source_target_pairs={{0,4},{1,5},{2,6},{3,7},{4,0},{5,1},{6,2},{7,3},{8,12},{9,13},{10,... | collective-permute-start | bytes 147464 | tf_op jit(solution)/shard_map/ppermute | solution.py:259
  17.3 1.2 %collective-permute-start.6 = (bf16[2,96,128]{2,1,0:T(8,128)(2,1)S(1)}, bf16[2,96,128]{2,1,0:T(8,128)(2,1)S(1)}, u32[]{:S(2)}, u32[]{:S(2)}) collective-permute-start(bf16[2,96,128]{2,1,0:T(8,128)(2,1)S(1)} %get-tuple-element.28.refs_0_), channel_id=1, source_target_pairs={{0,6},{1,7},{2,4},{3,5},{4,2},{5,3},{6,0},{7,1},{8,14},{9,15},{10,... | collective-permute-start | bytes 147464 | tf_op jit(solution)/shard_map/ppermute | solution.py:259
  18.6 0.6 %collective-permute-done.4.refs_1_ = bf16[2,96,128]{2,1,0:T(8,128)(2,1)S(1)} collective-permute-done((bf16[2,96,128]{2,1,0:T(8,128)(2,1)S(1)}, bf16[2,96,128]{2,1,0:T(8,128)(2,1)S(1)}, u32[]{:S(2)}, u32[]{:S(2)}) %collective-permute-start.4) | collective-permute-done | bytes 49184 | tf_op jit(solution)/shard_map/ppermute | solution.py:259
  19.2 1.2 %collective-permute-done.5.refs_2_ = bf16[2,96,128]{2,1,0:T(8,128)(2,1)S(1)} collective-permute-done((bf16[2,96,128]{2,1,0:T(8,128)(2,1)S(1)}, bf16[2,96,128]{2,1,0:T(8,128)(2,1)S(1)}, u32[]{:S(2)}, u32[]{:S(2)}) %collective-permute-start.5) | collective-permute-done | bytes 49184 | tf_op jit(solution)/shard_map/ppermute | solution.py:259
  20.4 1.9 %collective-permute-done.6.refs_3_ = bf16[2,96,128]{2,1,0:T(8,128)(2,1)S(1)} collective-permute-done((bf16[2,96,128]{2,1,0:T(8,128)(2,1)S(1)}, bf16[2,96,128]{2,1,0:T(8,128)(2,1)S(1)}, u32[]{:S(2)}, u32[]{:S(2)}) %collective-permute-start.6) | collective-permute-done | bytes 49184 | tf_op jit(solution)/shard_map/ppermute | solution.py:259
  22.3 0.1 collective-permute-start.7
  22.4 0.0 collective-permute-done.3.other_ref
  22.4 0.0 copy-done
  22.4 4.1 %shard_map.94 = (f32[6,768,128]{2,1,0:T(8,128)S(1)}, bf16[9,16,128]{2,1,0:T(8,128)(2,1)S(1)}) custom-call(s32[2,16]{1,0:T(2,128)S(1)} %bitcast.4, s32[1]{0:T(128)S(6)} %copy.10.days_ref, f32[16,288,128]{2,1,0:T(8,128)S(1)} %get-tuple-element.22.running_ref, bf16[8,288,128]{2,1,0:T(8,128)(2,1)S(1)} %shard_map.93.same_ref, ...), custom_call_target="tpu_custom_call" | custom-call | flops 100000000 | bytes 100000 | tf_op jit(solution)/shard_map/pallas_call | solution.py:247
  26.6 0.0 collective-permute-done.7.other_ref
  26.6 1.5 %shard_map.96 = (f32[2,768,128]{2,1,0:T(8,128)S(1)}, bf16[9,16,128]{2,1,0:T(8,128)(2,1)S(1)}) custom-call(s32[2,16]{1,0:T(2,128)S(1)} %bitcast.5, s32[1]{0:T(128)S(6)} %copy.10.days_ref, f32[16,96,128]{2,1,0:T(8,128)S(1)} %get-tuple-element.27.running_ref, bf16[8,96,128]{2,1,0:T(8,128)(2,1)S(1)} %shard_map.95.same_ref, ...), custom_call_target="tpu_custom_call" | custom-call | flops 100000000 | bytes 100000 | tf_op jit(solution)/shard_map/pallas_call | solution.py:247
  28.1 3.7 %collective-permute-start.10 = (bf16[9,16,128]{2,1,0:T(8,128)(2,1)S(1)}, bf16[9,16,128]{2,1,0:T(8,128)(2,1)S(1)}, u32[]{:S(2)}, u32[]{:S(2)}) collective-permute-start(bf16[9,16,128]{2,1,0:T(8,128)(2,1)S(1)} %get-tuple-element.31), channel_id=1, source_target_pairs={{0,24},{8,16},{16,8},{24,0},{1,25},{9,17},{17,9},{25,1},{2,26},{10... | collective-permute-start | bytes 110600 | tf_op jit(solution)/shard_map/ppermute | solution.py:259
  31.8 0.0 collective-permute-start.8
  31.8 0.8 %collective-permute-start.9 = (bf16[9,16,128]{2,1,0:T(8,128)(2,1)S(1)}, bf16[9,16,128]{2,1,0:T(8,128)(2,1)S(1)}, u32[]{:S(2)}, u32[]{:S(2)}) collective-permute-start(bf16[9,16,128]{2,1,0:T(8,128)(2,1)S(1)} %get-tuple-element.31), channel_id=1, source_target_pairs={{0,16},{8,24},{16,0},{24,8},{1,17},{9,25},{17,1},{25,9},{2,18},{10... | collective-permute-start | bytes 110600 | tf_op jit(solution)/shard_map/ppermute | solution.py:259
  32.6 1.7 %collective-permute-done.10.rest_4_.rest_5_ = bf16[9,16,128]{2,1,0:T(8,128)(2,1)S(1)} collective-permute-done((bf16[9,16,128]{2,1,0:T(8,128)(2,1)S(1)}, bf16[9,16,128]{2,1,0:T(8,128)(2,1)S(1)}, u32[]{:S(2)}, u32[]{:S(2)}) %collective-permute-start.10) | collective-permute-done | bytes 36896 | tf_op jit(solution)/shard_map/ppermute | solution.py:259
  34.2 1.9 %collective-permute-done.8.rest_2_.rest_3_ = bf16[9,16,128]{2,1,0:T(8,128)(2,1)S(1)} collective-permute-done((bf16[9,16,128]{2,1,0:T(8,128)(2,1)S(1)}, bf16[9,16,128]{2,1,0:T(8,128)(2,1)S(1)}, u32[]{:S(2)}, u32[]{:S(2)}) %collective-permute-start.8) | collective-permute-done | bytes 36896 | tf_op jit(solution)/shard_map/ppermute | solution.py:259
  36.1 0.5 %collective-permute-done.9.rest_3_.rest_4_ = bf16[9,16,128]{2,1,0:T(8,128)(2,1)S(1)} collective-permute-done((bf16[9,16,128]{2,1,0:T(8,128)(2,1)S(1)}, bf16[9,16,128]{2,1,0:T(8,128)(2,1)S(1)}, u32[]{:S(2)}, u32[]{:S(2)}) %collective-permute-start.9) | collective-permute-done | bytes 36896 | tf_op jit(solution)/shard_map/ppermute | solution.py:259
  36.6 2.9 %shard_map.97 = (f32[8,768,128]{2,1,0:T(8,128)S(1)}, bf16[8,16,128]{2,1,0:T(8,128)(2,1)S(1)}) custom-call(s32[1]{0:T(128)S(6)} %copy.10.days_ref, f32[768,128]{1,0:T(8,128)S(1)} %get-tuple-element.20.retain_ref, bf16[16,128,128]{2,1,0:T(8,128)(2,1)S(1)} %get-tuple-element.21.inverse_ref, f32[6,768,128]{2,1,0:T(8,128)S(1)} %get-tuple-element.26.rest_0_, ...), custom_call_target="tpu_custom_call" | custom-call | flops 10000000000 | bytes 10000000 | tf_op jit(solution)/shard_map/pallas_call | solution.py:247
  39.5 2.1 %collective-permute-start.11 = (bf16[8,16,128]{2,1,0:T(8,128)(2,1)S(1)}, bf16[8,16,128]{2,1,0:T(8,128)(2,1)S(1)}, u32[]{:S(2)}, u32[]{:S(2)}) collective-permute-start(bf16[8,16,128]{2,1,0:T(8,128)(2,1)S(1)} %get-tuple-element.34), channel_id=1, source_target_pairs={{0,8},{8,0},{16,24},{24,16},{1,9},{9,1},{17,25},{25,17},{2,10},{10... | collective-permute-start | bytes 98312 | tf_op jit(solution)/shard_map/ppermute | solution.py:259
  41.6 0.5 %collective-permute-start.12 = (bf16[8,16,128]{2,1,0:T(8,128)(2,1)S(1)}, bf16[8,16,128]{2,1,0:T(8,128)(2,1)S(1)}, u32[]{:S(2)}, u32[]{:S(2)}) collective-permute-start(bf16[8,16,128]{2,1,0:T(8,128)(2,1)S(1)} %get-tuple-element.34), channel_id=1, source_target_pairs={{0,16},{8,24},{16,0},{24,8},{1,17},{9,25},{17,1},{25,9},{2,18},{10... | collective-permute-start | bytes 98312 | tf_op jit(solution)/shard_map/ppermute | solution.py:259
  42.2 1.9 %collective-permute-start.13 = (bf16[8,16,128]{2,1,0:T(8,128)(2,1)S(1)}, bf16[8,16,128]{2,1,0:T(8,128)(2,1)S(1)}, u32[]{:S(2)}, u32[]{:S(2)}) collective-permute-start(bf16[8,16,128]{2,1,0:T(8,128)(2,1)S(1)} %get-tuple-element.34), channel_id=1, source_target_pairs={{0,24},{8,16},{16,8},{24,0},{1,25},{9,17},{17,9},{25,1},{2,26},{10... | collective-permute-start | bytes 98312 | tf_op jit(solution)/shard_map/ppermute | solution.py:259
  44.1 0.0 collective-permute-done.11.rest_0_
  44.1 2.4 %collective-permute-done.12.rest_1_ = bf16[8,16,128]{2,1,0:T(8,128)(2,1)S(1)} collective-permute-done((bf16[8,16,128]{2,1,0:T(8,128)(2,1)S(1)}, bf16[8,16,128]{2,1,0:T(8,128)(2,1)S(1)}, u32[]{:S(2)}, u32[]{:S(2)}) %collective-permute-start.12) | collective-permute-done | bytes 32800 | tf_op jit(solution)/shard_map/ppermute | solution.py:259
  46.5 1.4 %collective-permute-done.13.rest_2_ = bf16[8,16,128]{2,1,0:T(8,128)(2,1)S(1)} collective-permute-done((bf16[8,16,128]{2,1,0:T(8,128)(2,1)S(1)}, bf16[8,16,128]{2,1,0:T(8,128)(2,1)S(1)}, u32[]{:S(2)}, u32[]{:S(2)}) %collective-permute-start.13) | collective-permute-done | bytes 32800 | tf_op jit(solution)/shard_map/ppermute | solution.py:259
  47.9 1.6 %shard_map.98 = f32[48,1024]{1,0:T(8,128)} custom-call(f32[8,768,128]{2,1,0:T(8,128)S(1)} %get-tuple-element.32.adjoint_ref, f32[768,128]{1,0:T(8,128)S(1)} %get-tuple-element.20.retain_ref, bf16[8,768,128]{2,1,0:T(8,128)(2,1)S(1)} %get-tuple-element.33.moved_ref, bf16[8,16,128]{2,1,0:T(8,128)(2,1)S(1)} %collective-permute-done.11.rest_0_, ...), custom_call_target="tpu_custom_call" | custom-call | flops 10000000000 | bytes 10000000 | tf_op jit(solution)/shard_map/pallas_call | solution.py:247
  (2 shorter events, 0.1 us)
Async XLA Ops:
  0.7 1.4 %copy-start.1 = (bf16[48,16,1024]{2,1,0:T(8,128)(2,1)S(1)}, bf16[48,16,1024]{2,1,0:T(8,128)(2,1)}, u32[]{:S(2)}) copy-start(bf16[48,16,1024]{2,1,0:T(8,128)(2,1)} %z_ref.3) | copy-start | bytes 4718596
  2.1 6.6 %copy-start.2 = (bf16[48,16,1024]{2,1,0:T(8,128)(2,1)S(1)}, bf16[48,16,1024]{2,1,0:T(8,128)(2,1)}, u32[]{:S(2)}) copy-start(bf16[48,16,1024]{2,1,0:T(8,128)(2,1)} %z_ref.3) | copy-start | bytes 4718596
  2.1 6.6 %copy-start.3 = (bf16[16,4,64,64]{3,2,1,0:T(8,128)(2,1)S(1)}, bf16[16,4,64,64]{3,2,1,0:T(8,128)(2,1)}, u32[]{:S(2)}) copy-start(bf16[16,4,64,64]{3,2,1,0:T(8,128)(2,1)} %weight_ref.1) | copy-start | bytes 1572868
  2.1 6.6 %copy-start.4 = (bf16[16,2,64,64]{3,2,1,0:T(8,128)(2,1)S(1)}, bf16[16,2,64,64]{3,2,1,0:T(8,128)(2,1)}, u32[]{:S(2)}) copy-start(bf16[16,2,64,64]{3,2,1,0:T(8,128)(2,1)} %remote_weight_ref.1) | copy-start | bytes 786436
  2.1 6.6 %copy-start.5 = (bf16[16,64,64]{2,1,0:T(8,128)(2,1)S(1)}, bf16[16,64,64]{2,1,0:T(8,128)(2,1)}, u32[]{:S(2)}) copy-start(bf16[16,64,64]{2,1,0:T(8,128)(2,1)} %inverse_ref.1) | copy-start | bytes 393220
  2.1 6.6 %copy-start.6 = (f32[48,1024]{1,0:T(8,128)S(1)}, f32[48,1024]{1,0:T(8,128)}, u32[]{:S(2)}) copy-start(f32[48,1024]{1,0:T(8,128)} %retention_ref.1) | copy-start | bytes 589828
  2.1 6.6 %copy-start.7 = (s32[16,4]{0,1:T(4,128)S(1)}, s32[16,4]{0,1:T(4,128)}, u32[]{:S(2)}) copy-start(s32[16,4]{0,1:T(4,128)} %param.10) | copy-start | bytes 772
  3.4 10.2 %collective-permute-start = (bf16[2,288,128]{2,1,0:T(8,128)(2,1)S(1)}, bf16[2,288,128]{2,1,0:T(8,128)(2,1)S(1)}, u32[]{:S(2)}, u32[]{:S(2)}) collective-permute-start(bf16[2,288,128]{2,1,0:T(8,128)(2,1)S(1)} %get-tuple-element.23.refs_0_), channel_id=1, source_target_pairs={{0,2},{1,3},{2,0},{3,1},{4,6},{5,7},{6,4},{7,5},{8,10},{9,11},{10,... | collective-permute-start | bytes 442376 | tf_op jit(solution)/shard_map/ppermute | solution.py:259
  6.4 8.5 %collective-permute-start.1 = (bf16[2,288,128]{2,1,0:T(8,128)(2,1)S(1)}, bf16[2,288,128]{2,1,0:T(8,128)(2,1)S(1)}, u32[]{:S(2)}, u32[]{:S(2)}) collective-permute-start(bf16[2,288,128]{2,1,0:T(8,128)(2,1)S(1)} %get-tuple-element.23.refs_0_), channel_id=1, source_target_pairs={{0,4},{1,5},{2,6},{3,7},{4,0},{5,1},{6,2},{7,3},{8,12},{9,13},{10,... | collective-permute-start | bytes 442376 | tf_op jit(solution)/shard_map/ppermute | solution.py:259
  7.9 7.0 %collective-permute-start.2 = (bf16[2,288,128]{2,1,0:T(8,128)(2,1)S(1)}, bf16[2,288,128]{2,1,0:T(8,128)(2,1)S(1)}, u32[]{:S(2)}, u32[]{:S(2)}) collective-permute-start(bf16[2,288,128]{2,1,0:T(8,128)(2,1)S(1)} %get-tuple-element.23.refs_0_), channel_id=1, source_target_pairs={{0,6},{1,7},{2,4},{3,5},{4,2},{5,3},{6,0},{7,1},{8,14},{9,15},{10,... | collective-permute-start | bytes 442376 | tf_op jit(solution)/shard_map/ppermute | solution.py:259
  8.7 13.8 %copy-start = (s32[16,2]{0,1:T(2,128)S(1)}, s32[16,2]{0,1:T(2,128)}, u32[]{:S(2)}) copy-start(s32[16,2]{0,1:T(2,128)} %param.11) | copy-start | bytes 388
  14.9 7.5 %collective-permute-start.3 = (bf16[8,288,128]{2,1,0:T(8,128)(2,1)S(1)}, bf16[8,288,128]{2,1,0:T(8,128)(2,1)S(1)}, u32[]{:S(2)}, u32[]{:S(2)}) collective-permute-start(bf16[8,288,128]{2,1,0:T(8,128)(2,1)S(1)} %shard_map.93.same_ref), channel_id=1, source_target_pairs={{0,1},{1,0},{2,3},{3,2},{4,5},{5,4},{6,7},{7,6},{8,9},{9,8},{10,11... | collective-permute-start | bytes 1769480 | tf_op jit(solution)/shard_map/ppermute | solution.py:259
  15.0 4.2 %collective-permute-start.4 = (bf16[2,96,128]{2,1,0:T(8,128)(2,1)S(1)}, bf16[2,96,128]{2,1,0:T(8,128)(2,1)S(1)}, u32[]{:S(2)}, u32[]{:S(2)}) collective-permute-start(bf16[2,96,128]{2,1,0:T(8,128)(2,1)S(1)} %get-tuple-element.28.refs_0_), channel_id=1, source_target_pairs={{0,2},{1,3},{2,0},{3,1},{4,6},{5,7},{6,4},{7,5},{8,10},{9,11},{10,... | collective-permute-start | bytes 147464 | tf_op jit(solution)/shard_map/ppermute | solution.py:259
  16.3 4.1 %collective-permute-start.5 = (bf16[2,96,128]{2,1,0:T(8,128)(2,1)S(1)}, bf16[2,96,128]{2,1,0:T(8,128)(2,1)S(1)}, u32[]{:S(2)}, u32[]{:S(2)}) collective-permute-start(bf16[2,96,128]{2,1,0:T(8,128)(2,1)S(1)} %get-tuple-element.28.refs_0_), channel_id=1, source_target_pairs={{0,4},{1,5},{2,6},{3,7},{4,0},{5,1},{6,2},{7,3},{8,12},{9,13},{10,... | collective-permute-start | bytes 147464 | tf_op jit(solution)/shard_map/ppermute | solution.py:259
  17.3 5.0 %collective-permute-start.6 = (bf16[2,96,128]{2,1,0:T(8,128)(2,1)S(1)}, bf16[2,96,128]{2,1,0:T(8,128)(2,1)S(1)}, u32[]{:S(2)}, u32[]{:S(2)}) collective-permute-start(bf16[2,96,128]{2,1,0:T(8,128)(2,1)S(1)} %get-tuple-element.28.refs_0_), channel_id=1, source_target_pairs={{0,6},{1,7},{2,4},{3,5},{4,2},{5,3},{6,0},{7,1},{8,14},{9,15},{10,... | collective-permute-start | bytes 147464 | tf_op jit(solution)/shard_map/ppermute | solution.py:259
  22.3 4.2 %collective-permute-start.7 = (bf16[8,96,128]{2,1,0:T(8,128)(2,1)S(1)}, bf16[8,96,128]{2,1,0:T(8,128)(2,1)S(1)}, u32[]{:S(2)}, u32[]{:S(2)}) collective-permute-start(bf16[8,96,128]{2,1,0:T(8,128)(2,1)S(1)} %shard_map.95.same_ref), channel_id=1, source_target_pairs={{0,1},{1,0},{2,3},{3,2},{4,5},{5,4},{6,7},{7,6},{8,9},{9,8},{10,11... | collective-permute-start | bytes 589832 | tf_op jit(solution)/shard_map/ppermute | solution.py:259
  28.1 6.1 %collective-permute-start.10 = (bf16[9,16,128]{2,1,0:T(8,128)(2,1)S(1)}, bf16[9,16,128]{2,1,0:T(8,128)(2,1)S(1)}, u32[]{:S(2)}, u32[]{:S(2)}) collective-permute-start(bf16[9,16,128]{2,1,0:T(8,128)(2,1)S(1)} %get-tuple-element.31), channel_id=1, source_target_pairs={{0,24},{8,16},{16,8},{24,0},{1,25},{9,17},{17,9},{25,1},{2,26},{10... | collective-permute-start | bytes 110600 | tf_op jit(solution)/shard_map/ppermute | solution.py:259
  31.8 4.4 %collective-permute-start.8 = (bf16[9,16,128]{2,1,0:T(8,128)(2,1)S(1)}, bf16[9,16,128]{2,1,0:T(8,128)(2,1)S(1)}, u32[]{:S(2)}, u32[]{:S(2)}) collective-permute-start(bf16[9,16,128]{2,1,0:T(8,128)(2,1)S(1)} %get-tuple-element.31), channel_id=1, source_target_pairs={{0,8},{8,0},{16,24},{24,16},{1,9},{9,1},{17,25},{25,17},{2,10},{10... | collective-permute-start | bytes 110600 | tf_op jit(solution)/shard_map/ppermute | solution.py:259
  31.8 4.9 %collective-permute-start.9 = (bf16[9,16,128]{2,1,0:T(8,128)(2,1)S(1)}, bf16[9,16,128]{2,1,0:T(8,128)(2,1)S(1)}, u32[]{:S(2)}, u32[]{:S(2)}) collective-permute-start(bf16[9,16,128]{2,1,0:T(8,128)(2,1)S(1)} %get-tuple-element.31), channel_id=1, source_target_pairs={{0,16},{8,24},{16,0},{24,8},{1,17},{9,25},{17,1},{25,9},{2,18},{10... | collective-permute-start | bytes 110600 | tf_op jit(solution)/shard_map/ppermute | solution.py:259
  39.5 4.5 %collective-permute-start.11 = (bf16[8,16,128]{2,1,0:T(8,128)(2,1)S(1)}, bf16[8,16,128]{2,1,0:T(8,128)(2,1)S(1)}, u32[]{:S(2)}, u32[]{:S(2)}) collective-permute-start(bf16[8,16,128]{2,1,0:T(8,128)(2,1)S(1)} %get-tuple-element.34), channel_id=1, source_target_pairs={{0,8},{8,0},{16,24},{24,16},{1,9},{9,1},{17,25},{25,17},{2,10},{10... | collective-permute-start | bytes 98312 | tf_op jit(solution)/shard_map/ppermute | solution.py:259
  41.6 4.9 %collective-permute-start.12 = (bf16[8,16,128]{2,1,0:T(8,128)(2,1)S(1)}, bf16[8,16,128]{2,1,0:T(8,128)(2,1)S(1)}, u32[]{:S(2)}, u32[]{:S(2)}) collective-permute-start(bf16[8,16,128]{2,1,0:T(8,128)(2,1)S(1)} %get-tuple-element.34), channel_id=1, source_target_pairs={{0,16},{8,24},{16,0},{24,8},{1,17},{9,25},{17,1},{25,9},{2,18},{10... | collective-permute-start | bytes 98312 | tf_op jit(solution)/shard_map/ppermute | solution.py:259
  42.2 5.7 %collective-permute-start.13 = (bf16[8,16,128]{2,1,0:T(8,128)(2,1)S(1)}, bf16[8,16,128]{2,1,0:T(8,128)(2,1)S(1)}, u32[]{:S(2)}, u32[]{:S(2)}) collective-permute-start(bf16[8,16,128]{2,1,0:T(8,128)(2,1)S(1)} %get-tuple-element.34), channel_id=1, source_target_pairs={{0,24},{8,16},{16,8},{24,0},{1,25},{9,17},{17,9},{25,1},{2,26},{10... | collective-permute-start | bytes 98312 | tf_op jit(solution)/shard_map/ppermute | solution.py:259

commit v6 on v3

--- a/solution.py
+++ b/solution.py
@@ -27,33 +27,22 @@
     )
 
 
-def outgoing_kernel(dims, shared_ref, z_hbm, outgoing_ref, z_ref, arrived):
+def outgoing_kernel(dims, shared_ref, z_ref, outgoing_ref):
     days, blocks, size, probes = dims
     count = outgoing_ref.shape[0]
-    part = 8
-    copies = [
-        pltpu.make_async_copy(z_hbm.at[pl.ds(i * part, part)], z_ref.at[pl.ds(i * part, part)], arrived.at[i])
-        for i in range(days // part)
+    z = z_ref[...].reshape(days * blocks, size * probes)
+    row = lax.broadcasted_iota(jnp.int32, (days, days * blocks), 0)
+    column = lax.broadcasted_iota(jnp.int32, (days, days * blocks), 1)
+    picks = [
+        (column == row * blocks + shared_ref[0, m]).astype(jnp.float32).astype(jnp.bfloat16) for m in range(count)
     ]
-    for copy in copies:
-        copy.start()
+    picked = jnp.dot(jnp.concatenate(picks, axis=0), z, preferred_element_type=jnp.float32).astype(jnp.bfloat16)
     step = 2 * LANES
-    moves = [permutation(size, probes, start, step) for start in range(0, size * probes, step)]
-    row = lax.broadcasted_iota(jnp.int32, (part, part * blocks), 0)
-    column = lax.broadcasted_iota(jnp.int32, (part, part * blocks), 1)
-    picks = [(column == row * blocks + shared_ref[0, m]).astype(jnp.float32) for m in range(count)]
-    pick = jnp.concatenate(picks, axis=0).astype(jnp.bfloat16)
-    picked = []
-    for i, copy in enumerate(copies):
-        copy.wait()
-        z = z_ref[pl.ds(i * part, part)].reshape(part * blocks, size * probes)
-        picked.append(jnp.dot(pick, z, preferred_element_type=jnp.float32))
-    picked = jnp.concatenate([rows[m * part : (m + 1) * part] for m in range(count) for rows in picked], axis=0)
-    picked = picked.astype(jnp.bfloat16)
-    for i, move in enumerate(moves):
-        moved = jnp.dot(picked, move, preferred_element_type=jnp.float32).astype(jnp.bfloat16)
+    for start in range(0, size * probes, step):
+        moved = jnp.dot(picked, permutation(size, probes, start, step), preferred_element_type=jnp.float32)
+        moved = moved.astype(jnp.bfloat16)
         for half in range(2):
-            pair = i * 2 + half
+            pair = start // LANES + half
             for m in range(count):
                 outgoing_ref[m, pl.ds(pair * days, days), :] = moved[
                     m * days : (m + 1) * days, half * LANES : (half + 1) * LANES
@@ -101,30 +90,28 @@
     product = jnp.ones((blocks, LANES), jnp.float32)
     for day in range(days):
         product = product * retain_ref[pl.ds(day * blocks, blocks), :]
-    high = product.astype(jnp.bfloat16)
-    product_ref[0] = high
-    product_ref[1] = (product - high.astype(jnp.float32)).astype(jnp.bfloat16)
-
-
-def assemble_kernel(*refs):
-    *piece_refs, product_ref, out_ref = refs
-    count = piece_refs[0].shape[0]
-    for i, ref in enumerate(piece_refs):
-        out_ref[pl.ds(i * count, count)] = ref[...]
+    high = product.astype(jnp.bfloat16).astype(jnp.float32)
+    half = lax.broadcasted_iota(jnp.int32, product.shape, 1) < size
+    product_ref[...] = jnp.where(half, high, product - high).astype(jnp.bfloat16)
+
+
+def pass_kernel(piece_ref, product_ref, out_ref):
+    out_ref[...] = piece_ref[...]
 
 
 def forward_kernel(
-    dims, links_ref, days_ref, running_ref, same_ref, other_ref, weight_ref, inverse_ref, retain_ref, product_ref,
-    forcing_ref, message_ref, remote,
+    dims, pieces, links_ref, days_ref, running_ref, weight_ref, inverse_ref, retain_ref, product_ref, *rest
 ):
     days, blocks, size, probes = dims
+    piece_refs = rest[: 2 * pieces]
+    forcing_ref, message_ref, remote = rest[2 * pieces :]
     pairs = forcing_ref.shape[0]
     count = links_ref.shape[0]
-    held = same_ref.shape[0]
-    bound = 2 * held // lax.axis_size("space")
+    bound = piece_refs[0].shape[0]
+    held = pieces * bound
     me = lax.axis_index("space")
-    remote[pl.ds(0, held)] = same_ref[...]
-    remote[pl.ds(held, held)] = other_ref[...]
+    for k, ref in enumerate(piece_refs):
+        remote[pl.ds(k * bound, bound)] = ref[...]
     seen = lax.broadcasted_iota(jnp.int32, (days, LANES), 0) < days_ref[0]
     for block in range(blocks):
         places = []
@@ -147,8 +134,7 @@
         for pair in range(pairs):
             states[pair] = factor * states[pair] + forcing_ref[pair, rows, :]
     leave(message_ref, states)
-    message_ref[pairs] = product_ref[0]
-    message_ref[pairs + 1] = product_ref[1]
+    message_ref[pairs] = product_ref[...]
 
 
 def leave(message_ref, values):
@@ -167,7 +153,8 @@
     carries = [jnp.zeros(inbox.shape[2:], jnp.float32)] * pairs
     for slab in range(count - 1, 0, -1) if backward else range(count - 1):
         valid = slab > me if backward else slab < me
-        factor = products[slab, pairs].astype(jnp.float32) + products[slab, pairs + 1].astype(jnp.float32)
+        terms = products[slab, pairs].astype(jnp.float32)
+        factor = terms + pltpu.roll(terms, LANES // 2, 1)
         for pair in range(pairs):
             update = inbox[slab, pair].astype(jnp.float32) + factor * carries[pair]
             carries[pair] = jnp.where(valid, update, carries[pair])
@@ -205,23 +192,38 @@
     leave(message_ref, carries)
 
 
-def variance_kernel(dims, hops, adjoint_ref, retain_ref, moved_ref, *rest):
+def own_kernel(dims, adjoint_ref, retain_ref, moved_ref, partial_ref):
     days, blocks, size, probes = dims
     pairs = adjoint_ref.shape[0]
+    carries = [jnp.zeros((blocks, LANES), jnp.float32)] * pairs
+    for day in reversed(range(days)):
+        rows = pl.ds(day * blocks, blocks)
+        factor = retain_ref[rows, :]
+        total = None
+        for pair in range(pairs):
+            smoothed = adjoint_ref[pair, rows, :] + carries[pair]
+            carries[pair] = factor * smoothed
+            term = smoothed * moved_ref[pair, rows, :].astype(jnp.float32)
+            total = term if total is None else total + term
+        partial_ref[rows, :] = total
+
+
+def variance_kernel(dims, hops, partial_ref, retain_ref, moved_ref, *rest):
+    days, blocks, size, probes = dims
+    pairs = moved_ref.shape[0]
     out_ref, stage, inbox, products = rest[2 * hops :]
     collect(rest[:hops], inbox)
     collect(rest[hops : 2 * hops], products)
     carries = carried(pairs, inbox, products, True)
+    reach = jnp.ones((blocks, LANES), jnp.float32)
     for day in reversed(range(days)):
         rows = pl.ds(day * blocks, blocks)
-        factor = retain_ref[rows, :]
         total = None
         for pair in range(pairs):
-            smoothed = adjoint_ref[pair, rows, :] + carries[pair]
-            carries[pair] = factor * smoothed
-            term = smoothed * moved_ref[pair, rows, :].astype(jnp.float32)
+            term = carries[pair] * moved_ref[pair, rows, :].astype(jnp.float32)
             total = term if total is None else total + term
-        stage[rows, :] = total
+        stage[rows, :] = partial_ref[rows, :] + reach * total
+        reach = reach * retain_ref[rows, :]
     lane = lax.broadcasted_iota(jnp.int32, (days, LANES), 1)
     for block in range(0, blocks, 2):
         both = [stage[pl.ds(block + half, days, stride=blocks), :] for half in range(2)]
@@ -276,8 +278,7 @@
     (outgoing,) = call(
         functools.partial(outgoing_kernel, dims),
         [((bound, pairs * days, LANES), bf16)],
-        [pltpu.VMEM(probes.shape, bf16), pltpu.SemaphoreType.DMA((days // 8,))], 10**9, 4 * 10**6, 1,
-        shared_blocks, probes, apart=(1,), limit=56 * 1024 * 1024,
+        [], 10**9, 4 * 10**6, 1, shared_blocks, probes, limit=63 * 1024 * 1024,
     )
     pieces = {bits: crossed(outgoing, "space", bits) for bits in range(groups - 2, 0, -2)}
     running, moved, retain, product, remote_weight, inverse = call(
@@ -286,7 +287,7 @@
             ((blocks, pairs * days, LANES), f32),
             ((pairs, rows, LANES), bf16),
             ((rows, LANES), f32),
-            ((2, blocks, LANES), bf16),
+            ((blocks, LANES), bf16),
             ((blocks, LANES, far * LANES), bf16),
             ((blocks, LANES, LANES), bf16),
         ],
@@ -294,21 +295,19 @@
         10**10, 10**7, 2,
         near_table, slab_days, probes, local_coupling, remote_coupling, block_inverse, retention,
     )
-    (same,) = call(
-        assemble_kernel,
-        [((held, pairs * days, LANES), bf16)],
-        [], 0, 10**6, 0, outgoing, *[pieces[bits] for bits in range(2, groups, 2)], product,
-    )
-    other = crossed(same, "space", 1)
+    same = [outgoing]
+    for bits in range(2, groups, 2):
+        same += call(pass_kernel, [(outgoing.shape, bf16)], [], 0, 10**5, 0, pieces[bits], product)
+    other = [crossed(piece, "space", 1) for piece in same]
     slabs = lax.axis_size("tm")
     hops = slabs - 1
     exchange = lambda message: [crossed(message, "tm", bits) for bits in range(hops, 0, -1)][::-1]
-    inbox = pltpu.VMEM((slabs, pairs + 2, blocks, LANES), bf16)
+    inbox = pltpu.VMEM((slabs, pairs + 1, blocks, LANES), bf16)
     forcing, message = call(
-        functools.partial(forward_kernel, dims),
-        [big, ((pairs + 2, blocks, LANES), bf16)],
+        functools.partial(forward_kernel, dims, len(same)),
+        [big, ((pairs + 1, blocks, LANES), bf16)],
         [pltpu.VMEM((2 * held, pairs * days, LANES), bf16)], 10**10, 10**7, 2,
-        far_table, slab_days, running, same, other, remote_weight, inverse, retain, product,
+        far_table, slab_days, running, remote_weight, inverse, retain, product, *same, *other,
     )
     ends = exchange(message)
     adjoint, message = call(
@@ -318,11 +317,14 @@
         slab_days, forcing, retain, inverse, *ends,
     )
     starts = exchange(message)
+    (partial,) = call(
+        functools.partial(own_kernel, dims), [((rows, LANES), f32)], [], 10**9, 10**6, 0, adjoint, retain, moved
+    )
     (variance,) = call(
         functools.partial(variance_kernel, dims, hops),
         [((days, blocks * size), f32)],
         [pltpu.VMEM((rows, LANES), f32), pltpu.VMEM((slabs, pairs, blocks, LANES), bf16), inbox], 10**10, 10**7, 0,
-        adjoint, retain, moved, *starts, *ends,
+        partial, retain, moved, *starts, *ends,
     )
     return variance
 

time: 44.6 us -> 43.6 us (0.978)
  waiting for transfers between devices: 12.3 us -> 8.02 us
  local copies, waits for them, and re-layouts: 0.04 us -> 3.33 us
  Pallas kernels: 17.7 us -> 17.2 us
  starting transfers between devices: 13.6 us -> 14.1 us
    ppermute x10 -> x13, waiting for transfers between devices: 12.3 us -> 8.02 us  [crossed(): lax.ppermute(block, axis, [(i, i ^ bits) for i in range(lax.axis_size(axi...]
    unnamed x16, local copies, waits for them, and re-layouts: 0.04 us -> 3.33 us
    pallas_call x6 -> x9, Pallas kernels: 17.7 us -> 17.2 us  [call(): pl.pallas_call(kernel, out_shape=[jax.ShapeDtypeStruct(shape, kind) for s...]
    ppermute x10 -> x13, starting transfers between devices: 13.6 us -> 14.1 us  [crossed(): lax.ppermute(block, axis, [(i, i ^ bits) for i in range(lax.axis_size(axi...]
  transfers between devices with their start and end apart: 10 -> 13, of which waited for: 7 -> 9; matrix products, arithmetic and copies ran while one was open for 0% -> 0% of each run, Pallas kernels for 11% -> 13%
where the time goes in v6:
time: 43.6 us; the launch traced here: 43.4 us
  Pallas kernels  17.2 us (39%)
  starting transfers between devices  14.1 us (32%)
  waiting for transfers between devices  8.02 us (18%)
  local copies, waits for them, and re-layouts  3.33 us (8%)
  between operations  0.75 us (2%)
    pallas_call x9, Pallas kernels, call(): pl.pallas_call(kernel, out_shape=[jax.ShapeDtypeStruct(shape, kind) for s...  17.2 us
    ppermute x13, starting transfers between devices, crossed(): lax.ppermute(block, axis, [(i, i ^ bits) for i in range(lax.axis_size(axi...  14.1 us
    ppermute x13, waiting for transfers between devices, crossed(): lax.ppermute(block, axis, [(i, i ^ bits) for i in range(lax.axis_size(axi...  8.02 us
    unnamed x16, local copies, waits for them, and re-layouts  3.33 us
  transfers between devices with their start and end apart: 13, of which 9 were waited for; matrix products, arithmetic and copies ran while one was open for 0% of the time, Pallas kernels for 13%

profile of v6, /device:TPU:0, one launch (start us, length us, event | category | flops | bytes accessed | tf_op | source)
XLA Modules:
  0.0 43.4 jit_solution(13751478339513029939)
XLA Ops:
  0.0 0.0 copy-start.4
  0.0 0.0 copy-start.3
  0.0 0.0 copy-start.2
  0.0 3.0 %shard_map.92.rest_0_ = bf16[2,384,128]{2,1,0:T(8,128)(2,1)} custom-call(s32[1,2]{1,0:T(1,128)} %shared_ref.1, bf16[48,16,1024]{2,1,0:T(8,128)(2,1)} %z_ref.3), custom_call_target="tpu_custom_call" | custom-call | flops 1000000000 | bytes 4000000 | tf_op jit(solution)/shard_map/pallas_call | solution.py:239
  3.0 0.5 %collective-permute-start.3 = (bf16[2,384,128]{2,1,0:T(8,128)(2,1)}, bf16[2,384,128]{2,1,0:T(8,128)(2,1)S(1)}, u32[]{:S(2)}, u32[]{:S(2)}) collective-permute-start(bf16[2,384,128]{2,1,0:T(8,128)(2,1)} %shard_map.92.rest_0_), channel_id=1, source_target_pairs={{0,1},{1,0},{2,3},{3,2},{4,5},{5,4},{6,7},{7,6},{8,9},{9,8},{10,11... | collective-permute-start | bytes 589832 | tf_op jit(solution)/shard_map/ppermute | solution.py:251
  3.4 3.4 %collective-permute-start.2 = (bf16[2,384,128]{2,1,0:T(8,128)(2,1)}, bf16[2,384,128]{2,1,0:T(8,128)(2,1)S(1)}, u32[]{:S(2)}, u32[]{:S(2)}) collective-permute-start(bf16[2,384,128]{2,1,0:T(8,128)(2,1)} %shard_map.92.rest_0_), channel_id=1, source_target_pairs={{0,6},{1,7},{2,4},{3,5},{4,2},{5,3},{6,0},{7,1},{8,14},{9,15},{10,... | collective-permute-start | bytes 589832 | tf_op jit(solution)/shard_map/ppermute | solution.py:251
  6.9 0.5 %collective-permute-start.1 = (bf16[2,384,128]{2,1,0:T(8,128)(2,1)}, bf16[2,384,128]{2,1,0:T(8,128)(2,1)S(1)}, u32[]{:S(2)}, u32[]{:S(2)}) collective-permute-start(bf16[2,384,128]{2,1,0:T(8,128)(2,1)} %shard_map.92.rest_0_), channel_id=1, source_target_pairs={{0,4},{1,5},{2,6},{3,7},{4,0},{5,1},{6,2},{7,3},{8,12},{9,13},{10,... | collective-permute-start | bytes 589832 | tf_op jit(solution)/shard_map/ppermute | solution.py:251
  7.4 0.1 collective-permute-start
  8.1 0.0 copy-done.4
  8.1 0.0 copy-done.3
  8.1 0.0 copy-done.2
  8.1 0.0 copy-start
  8.1 1.4 %copy-done = bf16[48,16,1024]{2,1,0:T(8,128)(2,1)S(1)} copy-done((bf16[48,16,1024]{2,1,0:T(8,128)(2,1)S(1)}, bf16[48,16,1024]{2,1,0:T(8,128)(2,1)}, u32[]{:S(2)}) %copy-start) | copy-done | bytes 1572888
  9.5 0.0 copy-start.1
  9.5 1.2 %copy-done.1 = bf16[16,4,64,64]{3,2,1,0:T(8,128)(2,1)S(1)} copy-done((bf16[16,4,64,64]{3,2,1,0:T(8,128)(2,1)S(1)}, bf16[16,4,64,64]{3,2,1,0:T(8,128)(2,1)}, u32[]{:S(2)}) %copy-start.1) | copy-done | bytes 524312
  10.8 0.0 copy-start.6
  10.8 0.7 %copy-done.6 = s32[16,4]{0,1:T(4,128)S(1)} copy-done((s32[16,4]{0,1:T(4,128)S(1)}, s32[16,4]{0,1:T(4,128)}, u32[]{:S(2)}) %copy-start.6) | copy-done | bytes 280
  11.4 0.0 copy-start.5
  11.4 0.0 copy-start.7
  11.4 4.9 %shard_map.91 = (f32[16,384,128]{2,1,0:T(8,128)S(1)}, bf16[8,768,128]{2,1,0:T(8,128)(2,1)S(1)}, f32[768,128]{1,0:T(8,128)S(1)}, bf16[16,128]{1,0:T(8,128)(2,1)S(...) custom-call(s32[4,16]{1,0:T(4,128)S(1)} %bitcast.2, s32[1]{0:T(128)S(6)} %copy.10.days_ref, ...), custom_call_target="tpu_custom_call" | custom-call | flops 10000000000 | bytes 10000000 | tf_op jit(solution)/shard_map/pallas_call | solution.py:239
  16.4 0.8 %collective-permute-done.piece_ref = bf16[2,384,128]{2,1,0:T(8,128)(2,1)S(1)} collective-permute-done((bf16[2,384,128]{2,1,0:T(8,128)(2,1)}, bf16[2,384,128]{2,1,0:T(8,128)(2,1)S(1)}, u32[]{:S(2)}, u32[]{:S(2)}) %collective-permute-start) | collective-permute-done | bytes 196640 | tf_op jit(solution)/shard_map/ppermute | solution.py:251
  17.2 0.1 collective-permute-start.4
  17.3 0.0 collective-permute-done.1.piece_ref
  17.3 0.5 %collective-permute-start.5 = (bf16[2,384,128]{2,1,0:T(8,128)(2,1)S(1)}, bf16[2,384,128]{2,1,0:T(8,128)(2,1)S(1)}, u32[]{:S(2)}, u32[]{:S(2)}) collective-permute-start(bf16[2,384,128]{2,1,0:T(8,128)(2,1)S(1)} %shard_map.94.rest_2_), channel_id=1, source_target_pairs={{0,1},{1,0},{2,3},{3,2},{4,5},{5,4},{6,7},{7,6},{8,9},{9,8},{10,11... | collective-permute-start | bytes 589832 | tf_op jit(solution)/shard_map/ppermute | solution.py:251
  17.8 0.0 collective-permute-done.2.piece_ref
  17.9 0.1 collective-permute-start.6
  18.0 0.0 collective-permute-done.3.rest_4_
  18.0 0.7 %collective-permute-done.4.rest_5_ = bf16[2,384,128]{2,1,0:T(8,128)(2,1)S(1)} collective-permute-done((bf16[2,384,128]{2,1,0:T(8,128)(2,1)S(1)}, bf16[2,384,128]{2,1,0:T(8,128)(2,1)S(1)}, u32[]{:S(2)}, u32[]{:S(2)}) %collective-permute-start.4) | collective-permute-done | bytes 196640 | tf_op jit(solution)/shard_map/ppermute | solution.py:251
  18.7 0.3 collective-permute-done.5.rest_6_
  19.0 0.4 collective-permute-done.6.rest_7_
  19.4 0.0 copy-done.5
  19.4 0.0 copy-done.7
  19.4 4.6 %shard_map.96 = (f32[8,768,128]{2,1,0:T(8,128)S(1)}, bf16[9,16,128]{2,1,0:T(8,128)(2,1)S(1)}) custom-call(s32[2,16]{1,0:T(2,128)S(1)} %bitcast.3, s32[1]{0:T(128)S(6)} %copy.10.days_ref, f32[16,384,128]{2,1,0:T(8,128)S(1)} %get-tuple-element.15.running_ref, bf16[16,128,256]{2,1,0:T(8,128)(2,1)S(1)} %get-tuple-element.16.weight_ref, ...), custom_call_target="tpu_custom_call" | custom-call | flops 10000000000 | bytes 10000000 | tf_op jit(solution)/shard_map/pallas_call | solution.py:239
  24.0 3.7 %collective-permute-start.9 = (bf16[9,16,128]{2,1,0:T(8,128)(2,1)S(1)}, bf16[9,16,128]{2,1,0:T(8,128)(2,1)S(1)}, u32[]{:S(2)}, u32[]{:S(2)}) collective-permute-start(bf16[9,16,128]{2,1,0:T(8,128)(2,1)S(1)} %get-tuple-element.21), channel_id=1, source_target_pairs={{0,24},{8,16},{16,8},{24,0},{1,25},{9,17},{17,9},{25,1},{2,26},{10... | collective-permute-start | bytes 110600 | tf_op jit(solution)/shard_map/ppermute | solution.py:251
  27.7 0.0 collective-permute-start.8
  27.7 0.8 %collective-permute-start.7 = (bf16[9,16,128]{2,1,0:T(8,128)(2,1)S(1)}, bf16[9,16,128]{2,1,0:T(8,128)(2,1)S(1)}, u32[]{:S(2)}, u32[]{:S(2)}) collective-permute-start(bf16[9,16,128]{2,1,0:T(8,128)(2,1)S(1)} %get-tuple-element.21), channel_id=1, source_target_pairs={{0,8},{8,0},{16,24},{24,16},{1,9},{9,1},{17,25},{25,17},{2,10},{10... | collective-permute-start | bytes 110600 | tf_op jit(solution)/shard_map/ppermute | solution.py:251
  28.4 1.4 %collective-permute-done.9.rest_2_.rest_5_ = bf16[9,16,128]{2,1,0:T(8,128)(2,1)S(1)} collective-permute-done((bf16[9,16,128]{2,1,0:T(8,128)(2,1)S(1)}, bf16[9,16,128]{2,1,0:T(8,128)(2,1)S(1)}, u32[]{:S(2)}, u32[]{:S(2)}) %collective-permute-start.9) | collective-permute-done | bytes 36896 | tf_op jit(solution)/shard_map/ppermute | solution.py:251
  29.8 2.7 %collective-permute-done.8.rest_1_.rest_4_ = bf16[9,16,128]{2,1,0:T(8,128)(2,1)S(1)} collective-permute-done((bf16[9,16,128]{2,1,0:T(8,128)(2,1)S(1)}, bf16[9,16,128]{2,1,0:T(8,128)(2,1)S(1)}, u32[]{:S(2)}, u32[]{:S(2)}) %collective-permute-start.8) | collective-permute-done | bytes 36896 | tf_op jit(solution)/shard_map/ppermute | solution.py:251
  32.5 0.0 collective-permute-done.7.rest_0_.rest_3_
  32.5 2.8 %shard_map.97 = (f32[8,768,128]{2,1,0:T(8,128)S(1)}, bf16[8,16,128]{2,1,0:T(8,128)(2,1)S(1)}) custom-call(s32[1]{0:T(128)S(6)} %copy.10.days_ref, f32[8,768,128]{2,1,0:T(8,128)S(1)} %get-tuple-element.20.forcing_ref, f32[768,128]{1,0:T(8,128)S(1)} %get-tuple-element.18.retain_ref, bf16[16,128,128]{2,1,0:T(8,128)(2,1)S(1)} %get-tuple-element.17.inverse_ref, ...), custom_call_target="tpu_custom_call" | custom-call | flops 10000000000 | bytes 10000000 | tf_op jit(solution)/shard_map/pallas_call | solution.py:239
  35.3 1.8 %collective-permute-start.12 = (bf16[8,16,128]{2,1,0:T(8,128)(2,1)S(1)}, bf16[8,16,128]{2,1,0:T(8,128)(2,1)S(1)}, u32[]{:S(2)}, u32[]{:S(2)}) collective-permute-start(bf16[8,16,128]{2,1,0:T(8,128)(2,1)S(1)} %get-tuple-element.24), channel_id=1, source_target_pairs={{0,24},{8,16},{16,8},{24,0},{1,25},{9,17},{17,9},{25,1},{2,26},{10... | collective-permute-start | bytes 98312 | tf_op jit(solution)/shard_map/ppermute | solution.py:251
  37.1 0.4 collective-permute-start.11
  37.5 2.3 %collective-permute-start.10 = (bf16[8,16,128]{2,1,0:T(8,128)(2,1)S(1)}, bf16[8,16,128]{2,1,0:T(8,128)(2,1)S(1)}, u32[]{:S(2)}, u32[]{:S(2)}) collective-permute-start(bf16[8,16,128]{2,1,0:T(8,128)(2,1)S(1)} %get-tuple-element.24), channel_id=1, source_target_pairs={{0,8},{8,0},{16,24},{24,16},{1,9},{9,1},{17,25},{25,17},{2,10},{10... | collective-permute-start | bytes 98312 | tf_op jit(solution)/shard_map/ppermute | solution.py:251
  39.8 0.5 %shard_map.98.partial_ref = f32[768,128]{1,0:T(8,128)S(1)} custom-call(f32[8,768,128]{2,1,0:T(8,128)S(1)} %get-tuple-element.22.adjoint_ref, f32[768,128]{1,0:T(8,128)S(1)} %get-tuple-element.18.retain_ref, bf16[8,768,128]{2,1,0:T(8,128)(2,1)S(1)} %get-tuple-element.23.moved_ref), custom_call_target="tpu_custom_call" | custom-call | flops 1000000000 | bytes 1000000 | tf_op jit(solution)/shard_map/pallas_call | solution.py:239
  40.3 1.0 %collective-permute-done.12.rest_2_ = bf16[8,16,128]{2,1,0:T(8,128)(2,1)S(1)} collective-permute-done((bf16[8,16,128]{2,1,0:T(8,128)(2,1)S(1)}, bf16[8,16,128]{2,1,0:T(8,128)(2,1)S(1)}, u32[]{:S(2)}, u32[]{:S(2)}) %collective-permute-start.12) | collective-permute-done | bytes 32800 | tf_op jit(solution)/shard_map/ppermute | solution.py:251
  41.2 0.7 %collective-permute-done.11.rest_1_ = bf16[8,16,128]{2,1,0:T(8,128)(2,1)S(1)} collective-permute-done((bf16[8,16,128]{2,1,0:T(8,128)(2,1)S(1)}, bf16[8,16,128]{2,1,0:T(8,128)(2,1)S(1)}, u32[]{:S(2)}, u32[]{:S(2)}) %collective-permute-start.11) | collective-permute-done | bytes 32800 | tf_op jit(solution)/shard_map/ppermute | solution.py:251
  41.9 0.1 collective-permute-done.10.rest_0_
  42.0 1.3 %shard_map.99 = f32[48,1024]{1,0:T(8,128)} custom-call(f32[768,128]{1,0:T(8,128)S(1)} %shard_map.98.partial_ref, f32[768,128]{1,0:T(8,128)S(1)} %get-tuple-element.18.retain_ref, bf16[8,768,128]{2,1,0:T(8,128)(2,1)S(1)} %get-tuple-element.23.moved_ref, bf16[8,16,128]{2,1,0:T(8,128)(2,1)S(1)} %collective-permute-done.10.rest_0_, ...), custom_call_target="tpu_custom_call" | custom-call | flops 10000000000 | bytes 10000000 | tf_op jit(solution)/shard_map/pallas_call | solution.py:239
  (3 shorter events, 0.0 us)
Async XLA Ops:
  0.0 8.1 %copy-start.4 = (f32[48,1024]{1,0:T(8,128)S(1)}, f32[48,1024]{1,0:T(8,128)}, u32[]{:S(2)}) copy-start(f32[48,1024]{1,0:T(8,128)} %retention_ref.1) | copy-start | bytes 589828
  0.0 8.1 %copy-start.3 = (bf16[16,64,64]{2,1,0:T(8,128)(2,1)S(1)}, bf16[16,64,64]{2,1,0:T(8,128)(2,1)}, u32[]{:S(2)}) copy-start(bf16[16,64,64]{2,1,0:T(8,128)(2,1)} %inverse_ref.1) | copy-start | bytes 393220
  0.0 8.1 %copy-start.2 = (bf16[16,2,64,64]{3,2,1,0:T(8,128)(2,1)S(1)}, bf16[16,2,64,64]{3,2,1,0:T(8,128)(2,1)}, u32[]{:S(2)}) copy-start(bf16[16,2,64,64]{3,2,1,0:T(8,128)(2,1)} %remote_weight_ref.1) | copy-start | bytes 786436
  3.0 15.0 %collective-permute-start.3 = (bf16[2,384,128]{2,1,0:T(8,128)(2,1)}, bf16[2,384,128]{2,1,0:T(8,128)(2,1)S(1)}, u32[]{:S(2)}, u32[]{:S(2)}) collective-permute-start(bf16[2,384,128]{2,1,0:T(8,128)(2,1)} %shard_map.92.rest_0_), channel_id=1, source_target_pairs={{0,1},{1,0},{2,3},{3,2},{4,5},{5,4},{6,7},{7,6},{8,9},{9,8},{10,11... | collective-permute-start | bytes 589832 | tf_op jit(solution)/shard_map/ppermute | solution.py:251
  3.4 14.4 %collective-permute-start.2 = (bf16[2,384,128]{2,1,0:T(8,128)(2,1)}, bf16[2,384,128]{2,1,0:T(8,128)(2,1)S(1)}, u32[]{:S(2)}, u32[]{:S(2)}) collective-permute-start(bf16[2,384,128]{2,1,0:T(8,128)(2,1)} %shard_map.92.rest_0_), channel_id=1, source_target_pairs={{0,6},{1,7},{2,4},{3,5},{4,2},{5,3},{6,0},{7,1},{8,14},{9,15},{10,... | collective-permute-start | bytes 589832 | tf_op jit(solution)/shard_map/ppermute | solution.py:251
  6.9 10.4 %collective-permute-start.1 = (bf16[2,384,128]{2,1,0:T(8,128)(2,1)}, bf16[2,384,128]{2,1,0:T(8,128)(2,1)S(1)}, u32[]{:S(2)}, u32[]{:S(2)}) collective-permute-start(bf16[2,384,128]{2,1,0:T(8,128)(2,1)} %shard_map.92.rest_0_), channel_id=1, source_target_pairs={{0,4},{1,5},{2,6},{3,7},{4,0},{5,1},{6,2},{7,3},{8,12},{9,13},{10,... | collective-permute-start | bytes 589832 | tf_op jit(solution)/shard_map/ppermute | solution.py:251
  7.4 9.8 %collective-permute-start = (bf16[2,384,128]{2,1,0:T(8,128)(2,1)}, bf16[2,384,128]{2,1,0:T(8,128)(2,1)S(1)}, u32[]{:S(2)}, u32[]{:S(2)}) collective-permute-start(bf16[2,384,128]{2,1,0:T(8,128)(2,1)} %shard_map.92.rest_0_), channel_id=1, source_target_pairs={{0,2},{1,3},{2,0},{3,1},{4,6},{5,7},{6,4},{7,5},{8,10},{9,11},{10,... | collective-permute-start | bytes 589832 | tf_op jit(solution)/shard_map/ppermute | solution.py:251
  8.1 1.4 %copy-start = (bf16[48,16,1024]{2,1,0:T(8,128)(2,1)S(1)}, bf16[48,16,1024]{2,1,0:T(8,128)(2,1)}, u32[]{:S(2)}) copy-start(bf16[48,16,1024]{2,1,0:T(8,128)(2,1)} %z_ref.3) | copy-start | bytes 4718596
  9.5 1.2 %copy-start.1 = (bf16[16,4,64,64]{3,2,1,0:T(8,128)(2,1)S(1)}, bf16[16,4,64,64]{3,2,1,0:T(8,128)(2,1)}, u32[]{:S(2)}) copy-start(bf16[16,4,64,64]{3,2,1,0:T(8,128)(2,1)} %weight_ref.1) | copy-start | bytes 1572868
  10.8 0.7 %copy-start.6 = (s32[16,4]{0,1:T(4,128)S(1)}, s32[16,4]{0,1:T(4,128)}, u32[]{:S(2)}) copy-start(s32[16,4]{0,1:T(4,128)} %param.10) | copy-start | bytes 772
  11.4 7.9 %copy-start.5 = (bf16[2,384,128]{2,1,0:T(8,128)(2,1)S(1)}, bf16[2,384,128]{2,1,0:T(8,128)(2,1)}, u32[]{:S(2)}) copy-start(bf16[2,384,128]{2,1,0:T(8,128)(2,1)} %shard_map.92.rest_0_) | copy-start | bytes 589828
  11.4 7.9 %copy-start.7 = (s32[16,2]{0,1:T(2,128)S(1)}, s32[16,2]{0,1:T(2,128)}, u32[]{:S(2)}) copy-start(s32[16,2]{0,1:T(2,128)} %param.11) | copy-start | bytes 388
  17.2 1.5 %collective-permute-start.4 = (bf16[2,384,128]{2,1,0:T(8,128)(2,1)S(1)}, bf16[2,384,128]{2,1,0:T(8,128)(2,1)S(1)}, u32[]{:S(2)}, u32[]{:S(2)}) collective-permute-start(bf16[2,384,128]{2,1,0:T(8,128)(2,1)S(1)} %shard_map.93.rest_1_), channel_id=1, source_target_pairs={{0,1},{1,0},{2,3},{3,2},{4,5},{5,4},{6,7},{7,6},{8,9},{9,8},{10,11... | collective-permute-start | bytes 589832 | tf_op jit(solution)/shard_map/ppermute | solution.py:251
  17.3 1.7 %collective-permute-start.5 = (bf16[2,384,128]{2,1,0:T(8,128)(2,1)S(1)}, bf16[2,384,128]{2,1,0:T(8,128)(2,1)S(1)}, u32[]{:S(2)}, u32[]{:S(2)}) collective-permute-start(bf16[2,384,128]{2,1,0:T(8,128)(2,1)S(1)} %shard_map.94.rest_2_), channel_id=1, source_target_pairs={{0,1},{1,0},{2,3},{3,2},{4,5},{5,4},{6,7},{7,6},{8,9},{9,8},{10,11... | collective-permute-start | bytes 589832 | tf_op jit(solution)/shard_map/ppermute | solution.py:251
  17.9 1.5 %collective-permute-start.6 = (bf16[2,384,128]{2,1,0:T(8,128)(2,1)S(1)}, bf16[2,384,128]{2,1,0:T(8,128)(2,1)S(1)}, u32[]{:S(2)}, u32[]{:S(2)}) collective-permute-start(bf16[2,384,128]{2,1,0:T(8,128)(2,1)S(1)} %shard_map.95.rest_3_), channel_id=1, source_target_pairs={{0,1},{1,0},{2,3},{3,2},{4,5},{5,4},{6,7},{7,6},{8,9},{9,8},{10,11... | collective-permute-start | bytes 589832 | tf_op jit(solution)/shard_map/ppermute | solution.py:251
  24.0 5.8 %collective-permute-start.9 = (bf16[9,16,128]{2,1,0:T(8,128)(2,1)S(1)}, bf16[9,16,128]{2,1,0:T(8,128)(2,1)S(1)}, u32[]{:S(2)}, u32[]{:S(2)}) collective-permute-start(bf16[9,16,128]{2,1,0:T(8,128)(2,1)S(1)} %get-tuple-element.21), channel_id=1, source_target_pairs={{0,24},{8,16},{16,8},{24,0},{1,25},{9,17},{17,9},{25,1},{2,26},{10... | collective-permute-start | bytes 110600 | tf_op jit(solution)/shard_map/ppermute | solution.py:251
  27.7 4.9 %collective-permute-start.8 = (bf16[9,16,128]{2,1,0:T(8,128)(2,1)S(1)}, bf16[9,16,128]{2,1,0:T(8,128)(2,1)S(1)}, u32[]{:S(2)}, u32[]{:S(2)}) collective-permute-start(bf16[9,16,128]{2,1,0:T(8,128)(2,1)S(1)} %get-tuple-element.21), channel_id=1, source_target_pairs={{0,16},{8,24},{16,0},{24,8},{1,17},{9,25},{17,1},{25,9},{2,18},{10... | collective-permute-start | bytes 110600 | tf_op jit(solution)/shard_map/ppermute | solution.py:251
  27.7 4.9 %collective-permute-start.7 = (bf16[9,16,128]{2,1,0:T(8,128)(2,1)S(1)}, bf16[9,16,128]{2,1,0:T(8,128)(2,1)S(1)}, u32[]{:S(2)}, u32[]{:S(2)}) collective-permute-start(bf16[9,16,128]{2,1,0:T(8,128)(2,1)S(1)} %get-tuple-element.21), channel_id=1, source_target_pairs={{0,8},{8,0},{16,24},{24,16},{1,9},{9,1},{17,25},{25,17},{2,10},{10... | collective-permute-start | bytes 110600 | tf_op jit(solution)/shard_map/ppermute | solution.py:251
  35.3 5.9 %collective-permute-start.12 = (bf16[8,16,128]{2,1,0:T(8,128)(2,1)S(1)}, bf16[8,16,128]{2,1,0:T(8,128)(2,1)S(1)}, u32[]{:S(2)}, u32[]{:S(2)}) collective-permute-start(bf16[8,16,128]{2,1,0:T(8,128)(2,1)S(1)} %get-tuple-element.24), channel_id=1, source_target_pairs={{0,24},{8,16},{16,8},{24,0},{1,25},{9,17},{17,9},{25,1},{2,26},{10... | collective-permute-start | bytes 98312 | tf_op jit(solution)/shard_map/ppermute | solution.py:251
  37.1 4.9 %collective-permute-start.11 = (bf16[8,16,128]{2,1,0:T(8,128)(2,1)S(1)}, bf16[8,16,128]{2,1,0:T(8,128)(2,1)S(1)}, u32[]{:S(2)}, u32[]{:S(2)}) collective-permute-start(bf16[8,16,128]{2,1,0:T(8,128)(2,1)S(1)} %get-tuple-element.24), channel_id=1, source_target_pairs={{0,16},{8,24},{16,0},{24,8},{1,17},{9,25},{17,1},{25,9},{2,18},{10... | collective-permute-start | bytes 98312 | tf_op jit(solution)/shard_map/ppermute | solution.py:251
  37.5 4.5 %collective-permute-start.10 = (bf16[8,16,128]{2,1,0:T(8,128)(2,1)S(1)}, bf16[8,16,128]{2,1,0:T(8,128)(2,1)S(1)}, u32[]{:S(2)}, u32[]{:S(2)}) collective-permute-start(bf16[8,16,128]{2,1,0:T(8,128)(2,1)S(1)} %get-tuple-element.24), channel_id=1, source_target_pairs={{0,8},{8,0},{16,24},{24,16},{1,9},{9,1},{17,25},{25,17},{2,10},{10... | collective-permute-start | bytes 98312 | tf_op jit(solution)/shard_map/ppermute | solution.py:251

commit v7 on v6

--- a/solution.py
+++ b/solution.py
@@ -27,26 +27,37 @@
     )
 
 
-def outgoing_kernel(dims, shared_ref, z_ref, outgoing_ref):
+def outgoing_kernel(dims, shared_ref, z_ref, outgoing_ref, total):
     days, blocks, size, probes = dims
     count = outgoing_ref.shape[0]
-    z = z_ref[...].reshape(days * blocks, size * probes)
+    step, width = pl.program_id(0), z_ref.shape[2]
+    z = z_ref[...].reshape(days * blocks, width)
     row = lax.broadcasted_iota(jnp.int32, (days, days * blocks), 0)
     column = lax.broadcasted_iota(jnp.int32, (days, days * blocks), 1)
     picks = [
         (column == row * blocks + shared_ref[0, m]).astype(jnp.float32).astype(jnp.bfloat16) for m in range(count)
     ]
     picked = jnp.dot(jnp.concatenate(picks, axis=0), z, preferred_element_type=jnp.float32).astype(jnp.bfloat16)
-    step = 2 * LANES
-    for start in range(0, size * probes, step):
-        moved = jnp.dot(picked, permutation(size, probes, start, step), preferred_element_type=jnp.float32)
-        moved = moved.astype(jnp.bfloat16)
-        for half in range(2):
-            pair = start // LANES + half
+    place = lax.broadcasted_iota(jnp.int32, (width, size * probes), 1)
+    origin = (place % size) * probes + place // size - step * width
+    move = (lax.broadcasted_iota(jnp.int32, (width, size * probes), 0) == origin).astype(jnp.float32)
+    moved = jnp.dot(picked, move.astype(jnp.bfloat16), preferred_element_type=jnp.float32)
+
+    @pl.when(step == 0)
+    def _():
+        total[...] = moved
+
+    @pl.when(step > 0)
+    def _():
+        total[...] += moved
+
+    @pl.when(step == pl.num_programs(0) - 1)
+    def _():
+        for pair in range(size * probes // LANES):
             for m in range(count):
-                outgoing_ref[m, pl.ds(pair * days, days), :] = moved[
-                    m * days : (m + 1) * days, half * LANES : (half + 1) * LANES
-                ]
+                outgoing_ref[m, pl.ds(pair * days, days), :] = total[
+                    pl.ds(m * days, days), pl.ds(pair * LANES, LANES)
+                ].astype(jnp.bfloat16)
 
 
 def local_kernel(
@@ -104,7 +115,7 @@
 ):
     days, blocks, size, probes = dims
     piece_refs = rest[: 2 * pieces]
-    forcing_ref, message_ref, remote = rest[2 * pieces :]
+    forcing_ref, message_ref, remote, source = rest[2 * pieces :]
     pairs = forcing_ref.shape[0]
     count = links_ref.shape[0]
     bound = piece_refs[0].shape[0]
@@ -121,8 +132,9 @@
             places.append((distance % 2) * held + (distance // 2) * bound + link % bound)
         far = jnp.concatenate([remote[place] for place in places], axis=1)
         total = lax.dot_general(far, weight_ref[block], TURNED, preferred_element_type=jnp.float32)
-        source = (running_ref[block] - total).astype(jnp.bfloat16)
-        drive = lax.dot_general(source, inverse_ref[block], TURNED, preferred_element_type=jnp.float32)
+        source[block] = (running_ref[block] - total).astype(jnp.bfloat16)
+    for block in range(blocks):
+        drive = lax.dot_general(source[block], inverse_ref[block], TURNED, preferred_element_type=jnp.float32)
         for pair in range(pairs):
             forcing_ref[pair, pl.ds(block, days, stride=blocks), :] = jnp.where(
                 seen, drive[pair * days : (pair + 1) * days], 0.0
@@ -275,11 +287,20 @@
     near_table, far_table = local_links.T, remote_links.T
     big = ((pairs, rows, LANES), f32)
 
-    (outgoing,) = call(
+    steps = 4
+    outgoing = pl.pallas_call(
         functools.partial(outgoing_kernel, dims),
-        [((bound, pairs * days, LANES), bf16)],
-        [], 10**9, 4 * 10**6, 1, shared_blocks, probes, limit=63 * 1024 * 1024,
-    )
+        out_shape=jax.ShapeDtypeStruct((bound, pairs * days, LANES), bf16),
+        grid=(steps,),
+        in_specs=[
+            pl.BlockSpec(memory_space=pltpu.SMEM),
+            pl.BlockSpec((days, blocks, width // steps), lambda step: (0, 0, step)),
+        ],
+        out_specs=pl.BlockSpec((bound, pairs * days, LANES), lambda step: (0, 0, 0)),
+        scratch_shapes=[pltpu.VMEM((bound * days, width), f32)],
+        compiler_params=pltpu.CompilerParams(vmem_limit_bytes=63 * 1024 * 1024),
+        cost_estimate=pl.CostEstimate(flops=10**9, bytes_accessed=4 * 10**6, transcendentals=0),
+    )(shared_blocks, probes)
     pieces = {bits: crossed(outgoing, "space", bits) for bits in range(groups - 2, 0, -2)}
     running, moved, retain, product, remote_weight, inverse = call(
         functools.partial(local_kernel, dims),
@@ -306,7 +327,8 @@
     forcing, message = call(
         functools.partial(forward_kernel, dims, len(same)),
         [big, ((pairs + 1, blocks, LANES), bf16)],
-        [pltpu.VMEM((2 * held, pairs * days, LANES), bf16)], 10**10, 10**7, 2,
+        [pltpu.VMEM((2 * held, pairs * days, LANES), bf16), pltpu.VMEM((blocks, pairs * days, LANES), bf16)],
+        10**10, 10**7, 2,
         far_table, slab_days, running, remote_weight, inverse, retain, product, *same, *other,
     )
     ends = exchange(message)

time: 43.6 us -> 43.4 us (level)
    pallas_call x9 -> x8, Pallas kernels: 17.2 us -> 12.6 us  [call(): pl.pallas_call(kernel, out_shape=[jax.ShapeDtypeStruct(shape, kind) for s...]
    pallas_call x0 -> x1, Pallas kernels: none -> 4.31 us  [local(): pl.pallas_call(functools.partial(outgoing_kernel, dims), out_shape=jax.Sh...]
where the time goes in v7:
time: 43.4 us; the launch traced here: 43.1 us
  Pallas kernels  16.9 us (39%)
  starting transfers between devices  14.1 us (32%)
  waiting for transfers between devices  7.96 us (18%)
  local copies, waits for them, and re-layouts  3.33 us (8%)
  between operations  0.75 us (2%)
    ppermute x13, starting transfers between devices, crossed(): lax.ppermute(block, axis, [(i, i ^ bits) for i in range(lax.axis_size(axi...  14.1 us
    pallas_call x8, Pallas kernels, call(): pl.pallas_call(kernel, out_shape=[jax.ShapeDtypeStruct(shape, kind) for s...  12.6 us
    ppermute x13, waiting for transfers between devices, crossed(): lax.ppermute(block, axis, [(i, i ^ bits) for i in range(lax.axis_size(axi...  7.96 us
    pallas_call x1, Pallas kernels, local(): pl.pallas_call(functools.partial(outgoing_kernel, dims), out_shape=jax.Sh...  4.31 us
    unnamed x16, local copies, waits for them, and re-layouts  3.33 us
  transfers between devices with their start and end apart: 13, of which 9 were waited for; matrix products, arithmetic and copies ran while one was open for 0% of the time, Pallas kernels for 13%

profile of v7, /device:TPU:0, one launch (start us, length us, event | category | flops | bytes accessed | tf_op | source)
XLA Modules:
  0.0 43.1 jit_solution(4189513105629139254)
XLA Ops:
  0.0 0.0 copy-start.4
  0.0 0.0 copy-start.3
  0.0 0.0 copy-start.2
  0.0 4.3 %shard_map.92.rest_0_ = bf16[2,384,128]{2,1,0:T(8,128)(2,1)} custom-call(s32[1,2]{1,0:T(1,128)} %shared_ref.1, bf16[48,16,1024]{2,1,0:T(8,128)(2,1)} %z_ref.3), custom_call_target="tpu_custom_call" | custom-call | flops 1000000000 | bytes 4000000 | tf_op jit(solution)/shard_map/pallas_call | solution.py:291
  4.3 0.5 %collective-permute-start.3 = (bf16[2,384,128]{2,1,0:T(8,128)(2,1)}, bf16[2,384,128]{2,1,0:T(8,128)(2,1)S(1)}, u32[]{:S(2)}, u32[]{:S(2)}) collective-permute-start(bf16[2,384,128]{2,1,0:T(8,128)(2,1)} %shard_map.92.rest_0_), channel_id=1, source_target_pairs={{0,1},{1,0},{2,3},{3,2},{4,5},{5,4},{6,7},{7,6},{8,9},{9,8},{10,11... | collective-permute-start | bytes 589832 | tf_op jit(solution)/shard_map/ppermute | solution.py:263
  4.8 3.4 %collective-permute-start.2 = (bf16[2,384,128]{2,1,0:T(8,128)(2,1)}, bf16[2,384,128]{2,1,0:T(8,128)(2,1)S(1)}, u32[]{:S(2)}, u32[]{:S(2)}) collective-permute-start(bf16[2,384,128]{2,1,0:T(8,128)(2,1)} %shard_map.92.rest_0_), channel_id=1, source_target_pairs={{0,6},{1,7},{2,4},{3,5},{4,2},{5,3},{6,0},{7,1},{8,14},{9,15},{10,... | collective-permute-start | bytes 589832 | tf_op jit(solution)/shard_map/ppermute | solution.py:263
  8.2 0.5 %collective-permute-start.1 = (bf16[2,384,128]{2,1,0:T(8,128)(2,1)}, bf16[2,384,128]{2,1,0:T(8,128)(2,1)S(1)}, u32[]{:S(2)}, u32[]{:S(2)}) collective-permute-start(bf16[2,384,128]{2,1,0:T(8,128)(2,1)} %shard_map.92.rest_0_), channel_id=1, source_target_pairs={{0,4},{1,5},{2,6},{3,7},{4,0},{5,1},{6,2},{7,3},{8,12},{9,13},{10,... | collective-permute-start | bytes 589832 | tf_op jit(solution)/shard_map/ppermute | solution.py:263
  8.7 0.1 collective-permute-start
  9.5 0.0 copy-done.4
  9.5 0.0 copy-done.3
  9.5 0.0 copy-done.2
  9.5 0.0 copy-start
  9.5 1.4 %copy-done = bf16[48,16,1024]{2,1,0:T(8,128)(2,1)S(1)} copy-done((bf16[48,16,1024]{2,1,0:T(8,128)(2,1)S(1)}, bf16[48,16,1024]{2,1,0:T(8,128)(2,1)}, u32[]{:S(2)}) %copy-start) | copy-done | bytes 1572888
  10.9 0.0 copy-start.1
  10.9 1.2 %copy-done.1 = bf16[16,4,64,64]{3,2,1,0:T(8,128)(2,1)S(1)} copy-done((bf16[16,4,64,64]{3,2,1,0:T(8,128)(2,1)S(1)}, bf16[16,4,64,64]{3,2,1,0:T(8,128)(2,1)}, u32[]{:S(2)}) %copy-start.1) | copy-done | bytes 524312
  12.2 0.0 copy-start.6
  12.2 0.7 %copy-done.6 = s32[16,4]{0,1:T(4,128)S(1)} copy-done((s32[16,4]{0,1:T(4,128)S(1)}, s32[16,4]{0,1:T(4,128)}, u32[]{:S(2)}) %copy-start.6) | copy-done | bytes 280
  12.9 0.0 copy-start.5
  12.9 0.0 copy-start.7
  12.9 4.9 %shard_map.91 = (f32[16,384,128]{2,1,0:T(8,128)S(1)}, bf16[8,768,128]{2,1,0:T(8,128)(2,1)S(1)}, f32[768,128]{1,0:T(8,128)S(1)}, bf16[16,128]{1,0:T(8,128)(2,1)S(...) custom-call(s32[4,16]{1,0:T(4,128)S(1)} %bitcast.2, s32[1]{0:T(128)S(6)} %copy.10.days_ref, ...), custom_call_target="tpu_custom_call" | custom-call | flops 10000000000 | bytes 10000000 | tf_op jit(solution)/shard_map/pallas_call | solution.py:251
  17.8 0.7 %collective-permute-done.piece_ref = bf16[2,384,128]{2,1,0:T(8,128)(2,1)S(1)} collective-permute-done((bf16[2,384,128]{2,1,0:T(8,128)(2,1)}, bf16[2,384,128]{2,1,0:T(8,128)(2,1)S(1)}, u32[]{:S(2)}, u32[]{:S(2)}) %collective-permute-start) | collective-permute-done | bytes 196640 | tf_op jit(solution)/shard_map/ppermute | solution.py:263
  18.5 0.1 collective-permute-start.4
  18.6 0.0 collective-permute-done.1.piece_ref
  18.6 0.5 %collective-permute-start.5 = (bf16[2,384,128]{2,1,0:T(8,128)(2,1)S(1)}, bf16[2,384,128]{2,1,0:T(8,128)(2,1)S(1)}, u32[]{:S(2)}, u32[]{:S(2)}) collective-permute-start(bf16[2,384,128]{2,1,0:T(8,128)(2,1)S(1)} %shard_map.94.rest_2_), channel_id=1, source_target_pairs={{0,1},{1,0},{2,3},{3,2},{4,5},{5,4},{6,7},{7,6},{8,9},{9,8},{10,11... | collective-permute-start | bytes 589832 | tf_op jit(solution)/shard_map/ppermute | solution.py:263
  19.2 0.0 collective-permute-done.2.piece_ref
  19.2 0.1 collective-permute-start.6
  19.3 0.0 collective-permute-done.3.rest_4_
  19.3 0.7 %collective-permute-done.4.rest_5_ = bf16[2,384,128]{2,1,0:T(8,128)(2,1)S(1)} collective-permute-done((bf16[2,384,128]{2,1,0:T(8,128)(2,1)S(1)}, bf16[2,384,128]{2,1,0:T(8,128)(2,1)S(1)}, u32[]{:S(2)}, u32[]{:S(2)}) %collective-permute-start.4) | collective-permute-done | bytes 196640 | tf_op jit(solution)/shard_map/ppermute | solution.py:263
  20.0 0.3 collective-permute-done.5.rest_6_
  20.3 0.4 collective-permute-done.6.rest_7_
  20.7 0.0 copy-done.5
  20.7 0.0 copy-done.7
  20.7 3.0 %shard_map.96 = (f32[8,768,128]{2,1,0:T(8,128)S(1)}, bf16[9,16,128]{2,1,0:T(8,128)(2,1)S(1)}) custom-call(s32[2,16]{1,0:T(2,128)S(1)} %bitcast.3, s32[1]{0:T(128)S(6)} %copy.10.days_ref, f32[16,384,128]{2,1,0:T(8,128)S(1)} %get-tuple-element.15.running_ref, bf16[16,128,256]{2,1,0:T(8,128)(2,1)S(1)} %get-tuple-element.16.weight_ref, ...), custom_call_target="tpu_custom_call" | custom-call | flops 10000000000 | bytes 10000000 | tf_op jit(solution)/shard_map/pallas_call | solution.py:251
  23.7 3.7 %collective-permute-start.9 = (bf16[9,16,128]{2,1,0:T(8,128)(2,1)S(1)}, bf16[9,16,128]{2,1,0:T(8,128)(2,1)S(1)}, u32[]{:S(2)}, u32[]{:S(2)}) collective-permute-start(bf16[9,16,128]{2,1,0:T(8,128)(2,1)S(1)} %get-tuple-element.21), channel_id=1, source_target_pairs={{0,24},{8,16},{16,8},{24,0},{1,25},{9,17},{17,9},{25,1},{2,26},{10... | collective-permute-start | bytes 110600 | tf_op jit(solution)/shard_map/ppermute | solution.py:263
  27.4 0.0 collective-permute-start.8
  27.4 0.8 %collective-permute-start.7 = (bf16[9,16,128]{2,1,0:T(8,128)(2,1)S(1)}, bf16[9,16,128]{2,1,0:T(8,128)(2,1)S(1)}, u32[]{:S(2)}, u32[]{:S(2)}) collective-permute-start(bf16[9,16,128]{2,1,0:T(8,128)(2,1)S(1)} %get-tuple-element.21), channel_id=1, source_target_pairs={{0,8},{8,0},{16,24},{24,16},{1,9},{9,1},{17,25},{25,17},{2,10},{10... | collective-permute-start | bytes 110600 | tf_op jit(solution)/shard_map/ppermute | solution.py:263
  28.2 1.4 %collective-permute-done.9.rest_2_.rest_5_ = bf16[9,16,128]{2,1,0:T(8,128)(2,1)S(1)} collective-permute-done((bf16[9,16,128]{2,1,0:T(8,128)(2,1)S(1)}, bf16[9,16,128]{2,1,0:T(8,128)(2,1)S(1)}, u32[]{:S(2)}, u32[]{:S(2)}) %collective-permute-start.9) | collective-permute-done | bytes 36896 | tf_op jit(solution)/shard_map/ppermute | solution.py:263
  29.6 2.7 %collective-permute-done.8.rest_1_.rest_4_ = bf16[9,16,128]{2,1,0:T(8,128)(2,1)S(1)} collective-permute-done((bf16[9,16,128]{2,1,0:T(8,128)(2,1)S(1)}, bf16[9,16,128]{2,1,0:T(8,128)(2,1)S(1)}, u32[]{:S(2)}, u32[]{:S(2)}) %collective-permute-start.8) | collective-permute-done | bytes 36896 | tf_op jit(solution)/shard_map/ppermute | solution.py:263
  32.3 0.0 collective-permute-done.7.rest_0_.rest_3_
  32.3 2.8 %shard_map.97 = (f32[8,768,128]{2,1,0:T(8,128)S(1)}, bf16[8,16,128]{2,1,0:T(8,128)(2,1)S(1)}) custom-call(s32[1]{0:T(128)S(6)} %copy.10.days_ref, f32[8,768,128]{2,1,0:T(8,128)S(1)} %get-tuple-element.20.forcing_ref, f32[768,128]{1,0:T(8,128)S(1)} %get-tuple-element.18.retain_ref, bf16[16,128,128]{2,1,0:T(8,128)(2,1)S(1)} %get-tuple-element.17.inverse_ref, ...), custom_call_target="tpu_custom_call" | custom-call | flops 10000000000 | bytes 10000000 | tf_op jit(solution)/shard_map/pallas_call | solution.py:251
  35.1 1.8 %collective-permute-start.12 = (bf16[8,16,128]{2,1,0:T(8,128)(2,1)S(1)}, bf16[8,16,128]{2,1,0:T(8,128)(2,1)S(1)}, u32[]{:S(2)}, u32[]{:S(2)}) collective-permute-start(bf16[8,16,128]{2,1,0:T(8,128)(2,1)S(1)} %get-tuple-element.24), channel_id=1, source_target_pairs={{0,24},{8,16},{16,8},{24,0},{1,25},{9,17},{17,9},{25,1},{2,26},{10... | collective-permute-start | bytes 98312 | tf_op jit(solution)/shard_map/ppermute | solution.py:263
  36.8 0.4 collective-permute-start.11
  37.2 2.3 %collective-permute-start.10 = (bf16[8,16,128]{2,1,0:T(8,128)(2,1)S(1)}, bf16[8,16,128]{2,1,0:T(8,128)(2,1)S(1)}, u32[]{:S(2)}, u32[]{:S(2)}) collective-permute-start(bf16[8,16,128]{2,1,0:T(8,128)(2,1)S(1)} %get-tuple-element.24), channel_id=1, source_target_pairs={{0,8},{8,0},{16,24},{24,16},{1,9},{9,1},{17,25},{25,17},{2,10},{10... | collective-permute-start | bytes 98312 | tf_op jit(solution)/shard_map/ppermute | solution.py:263
  39.5 0.5 %shard_map.98.partial_ref = f32[768,128]{1,0:T(8,128)S(1)} custom-call(f32[8,768,128]{2,1,0:T(8,128)S(1)} %get-tuple-element.22.adjoint_ref, f32[768,128]{1,0:T(8,128)S(1)} %get-tuple-element.18.retain_ref, bf16[8,768,128]{2,1,0:T(8,128)(2,1)S(1)} %get-tuple-element.23.moved_ref), custom_call_target="tpu_custom_call" | custom-call | flops 1000000000 | bytes 1000000 | tf_op jit(solution)/shard_map/pallas_call | solution.py:251
  40.0 1.0 %collective-permute-done.12.rest_2_ = bf16[8,16,128]{2,1,0:T(8,128)(2,1)S(1)} collective-permute-done((bf16[8,16,128]{2,1,0:T(8,128)(2,1)S(1)}, bf16[8,16,128]{2,1,0:T(8,128)(2,1)S(1)}, u32[]{:S(2)}, u32[]{:S(2)}) %collective-permute-start.12) | collective-permute-done | bytes 32800 | tf_op jit(solution)/shard_map/ppermute | solution.py:263
  41.0 0.7 %collective-permute-done.11.rest_1_ = bf16[8,16,128]{2,1,0:T(8,128)(2,1)S(1)} collective-permute-done((bf16[8,16,128]{2,1,0:T(8,128)(2,1)S(1)}, bf16[8,16,128]{2,1,0:T(8,128)(2,1)S(1)}, u32[]{:S(2)}, u32[]{:S(2)}) %collective-permute-start.11) | collective-permute-done | bytes 32800 | tf_op jit(solution)/shard_map/ppermute | solution.py:263
  41.7 0.1 collective-permute-done.10.rest_0_
  41.8 1.3 %shard_map.99 = f32[48,1024]{1,0:T(8,128)} custom-call(f32[768,128]{1,0:T(8,128)S(1)} %shard_map.98.partial_ref, f32[768,128]{1,0:T(8,128)S(1)} %get-tuple-element.18.retain_ref, bf16[8,768,128]{2,1,0:T(8,128)(2,1)S(1)} %get-tuple-element.23.moved_ref, bf16[8,16,128]{2,1,0:T(8,128)(2,1)S(1)} %collective-permute-done.10.rest_0_, ...), custom_call_target="tpu_custom_call" | custom-call | flops 10000000000 | bytes 10000000 | tf_op jit(solution)/shard_map/pallas_call | solution.py:251
  (3 shorter events, 0.0 us)
Async XLA Ops:
  0.0 9.5 %copy-start.4 = (f32[48,1024]{1,0:T(8,128)S(1)}, f32[48,1024]{1,0:T(8,128)}, u32[]{:S(2)}) copy-start(f32[48,1024]{1,0:T(8,128)} %retention_ref.1) | copy-start | bytes 589828
  0.0 9.5 %copy-start.3 = (bf16[16,64,64]{2,1,0:T(8,128)(2,1)S(1)}, bf16[16,64,64]{2,1,0:T(8,128)(2,1)}, u32[]{:S(2)}) copy-start(bf16[16,64,64]{2,1,0:T(8,128)(2,1)} %inverse_ref.1) | copy-start | bytes 393220
  0.0 9.5 %copy-start.2 = (bf16[16,2,64,64]{3,2,1,0:T(8,128)(2,1)S(1)}, bf16[16,2,64,64]{3,2,1,0:T(8,128)(2,1)}, u32[]{:S(2)}) copy-start(bf16[16,2,64,64]{3,2,1,0:T(8,128)(2,1)} %remote_weight_ref.1) | copy-start | bytes 786436
  4.3 15.0 %collective-permute-start.3 = (bf16[2,384,128]{2,1,0:T(8,128)(2,1)}, bf16[2,384,128]{2,1,0:T(8,128)(2,1)S(1)}, u32[]{:S(2)}, u32[]{:S(2)}) collective-permute-start(bf16[2,384,128]{2,1,0:T(8,128)(2,1)} %shard_map.92.rest_0_), channel_id=1, source_target_pairs={{0,1},{1,0},{2,3},{3,2},{4,5},{5,4},{6,7},{7,6},{8,9},{9,8},{10,11... | collective-permute-start | bytes 589832 | tf_op jit(solution)/shard_map/ppermute | solution.py:263
  4.8 14.4 %collective-permute-start.2 = (bf16[2,384,128]{2,1,0:T(8,128)(2,1)}, bf16[2,384,128]{2,1,0:T(8,128)(2,1)S(1)}, u32[]{:S(2)}, u32[]{:S(2)}) collective-permute-start(bf16[2,384,128]{2,1,0:T(8,128)(2,1)} %shard_map.92.rest_0_), channel_id=1, source_target_pairs={{0,6},{1,7},{2,4},{3,5},{4,2},{5,3},{6,0},{7,1},{8,14},{9,15},{10,... | collective-permute-start | bytes 589832 | tf_op jit(solution)/shard_map/ppermute | solution.py:263
  8.2 10.4 %collective-permute-start.1 = (bf16[2,384,128]{2,1,0:T(8,128)(2,1)}, bf16[2,384,128]{2,1,0:T(8,128)(2,1)S(1)}, u32[]{:S(2)}, u32[]{:S(2)}) collective-permute-start(bf16[2,384,128]{2,1,0:T(8,128)(2,1)} %shard_map.92.rest_0_), channel_id=1, source_target_pairs={{0,4},{1,5},{2,6},{3,7},{4,0},{5,1},{6,2},{7,3},{8,12},{9,13},{10,... | collective-permute-start | bytes 589832 | tf_op jit(solution)/shard_map/ppermute | solution.py:263
  8.7 9.8 %collective-permute-start = (bf16[2,384,128]{2,1,0:T(8,128)(2,1)}, bf16[2,384,128]{2,1,0:T(8,128)(2,1)S(1)}, u32[]{:S(2)}, u32[]{:S(2)}) collective-permute-start(bf16[2,384,128]{2,1,0:T(8,128)(2,1)} %shard_map.92.rest_0_), channel_id=1, source_target_pairs={{0,2},{1,3},{2,0},{3,1},{4,6},{5,7},{6,4},{7,5},{8,10},{9,11},{10,... | collective-permute-start | bytes 589832 | tf_op jit(solution)/shard_map/ppermute | solution.py:263
  9.5 1.4 %copy-start = (bf16[48,16,1024]{2,1,0:T(8,128)(2,1)S(1)}, bf16[48,16,1024]{2,1,0:T(8,128)(2,1)}, u32[]{:S(2)}) copy-start(bf16[48,16,1024]{2,1,0:T(8,128)(2,1)} %z_ref.3) | copy-start | bytes 4718596
  10.9 1.2 %copy-start.1 = (bf16[16,4,64,64]{3,2,1,0:T(8,128)(2,1)S(1)}, bf16[16,4,64,64]{3,2,1,0:T(8,128)(2,1)}, u32[]{:S(2)}) copy-start(bf16[16,4,64,64]{3,2,1,0:T(8,128)(2,1)} %weight_ref.1) | copy-start | bytes 1572868
  12.2 0.7 %copy-start.6 = (s32[16,4]{0,1:T(4,128)S(1)}, s32[16,4]{0,1:T(4,128)}, u32[]{:S(2)}) copy-start(s32[16,4]{0,1:T(4,128)} %param.10) | copy-start | bytes 772
  12.9 7.9 %copy-start.5 = (bf16[2,384,128]{2,1,0:T(8,128)(2,1)S(1)}, bf16[2,384,128]{2,1,0:T(8,128)(2,1)}, u32[]{:S(2)}) copy-start(bf16[2,384,128]{2,1,0:T(8,128)(2,1)} %shard_map.92.rest_0_) | copy-start | bytes 589828
  12.9 7.9 %copy-start.7 = (s32[16,2]{0,1:T(2,128)S(1)}, s32[16,2]{0,1:T(2,128)}, u32[]{:S(2)}) copy-start(s32[16,2]{0,1:T(2,128)} %param.11) | copy-start | bytes 388
  18.5 1.5 %collective-permute-start.4 = (bf16[2,384,128]{2,1,0:T(8,128)(2,1)S(1)}, bf16[2,384,128]{2,1,0:T(8,128)(2,1)S(1)}, u32[]{:S(2)}, u32[]{:S(2)}) collective-permute-start(bf16[2,384,128]{2,1,0:T(8,128)(2,1)S(1)} %shard_map.93.rest_1_), channel_id=1, source_target_pairs={{0,1},{1,0},{2,3},{3,2},{4,5},{5,4},{6,7},{7,6},{8,9},{9,8},{10,11... | collective-permute-start | bytes 589832 | tf_op jit(solution)/shard_map/ppermute | solution.py:263
  18.6 1.7 %collective-permute-start.5 = (bf16[2,384,128]{2,1,0:T(8,128)(2,1)S(1)}, bf16[2,384,128]{2,1,0:T(8,128)(2,1)S(1)}, u32[]{:S(2)}, u32[]{:S(2)}) collective-permute-start(bf16[2,384,128]{2,1,0:T(8,128)(2,1)S(1)} %shard_map.94.rest_2_), channel_id=1, source_target_pairs={{0,1},{1,0},{2,3},{3,2},{4,5},{5,4},{6,7},{7,6},{8,9},{9,8},{10,11... | collective-permute-start | bytes 589832 | tf_op jit(solution)/shard_map/ppermute | solution.py:263
  19.2 1.5 %collective-permute-start.6 = (bf16[2,384,128]{2,1,0:T(8,128)(2,1)S(1)}, bf16[2,384,128]{2,1,0:T(8,128)(2,1)S(1)}, u32[]{:S(2)}, u32[]{:S(2)}) collective-permute-start(bf16[2,384,128]{2,1,0:T(8,128)(2,1)S(1)} %shard_map.95.rest_3_), channel_id=1, source_target_pairs={{0,1},{1,0},{2,3},{3,2},{4,5},{5,4},{6,7},{7,6},{8,9},{9,8},{10,11... | collective-permute-start | bytes 589832 | tf_op jit(solution)/shard_map/ppermute | solution.py:263
  23.7 5.8 %collective-permute-start.9 = (bf16[9,16,128]{2,1,0:T(8,128)(2,1)S(1)}, bf16[9,16,128]{2,1,0:T(8,128)(2,1)S(1)}, u32[]{:S(2)}, u32[]{:S(2)}) collective-permute-start(bf16[9,16,128]{2,1,0:T(8,128)(2,1)S(1)} %get-tuple-element.21), channel_id=1, source_target_pairs={{0,24},{8,16},{16,8},{24,0},{1,25},{9,17},{17,9},{25,1},{2,26},{10... | collective-permute-start | bytes 110600 | tf_op jit(solution)/shard_map/ppermute | solution.py:263
  27.4 4.9 %collective-permute-start.8 = (bf16[9,16,128]{2,1,0:T(8,128)(2,1)S(1)}, bf16[9,16,128]{2,1,0:T(8,128)(2,1)S(1)}, u32[]{:S(2)}, u32[]{:S(2)}) collective-permute-start(bf16[9,16,128]{2,1,0:T(8,128)(2,1)S(1)} %get-tuple-element.21), channel_id=1, source_target_pairs={{0,16},{8,24},{16,0},{24,8},{1,17},{9,25},{17,1},{25,9},{2,18},{10... | collective-permute-start | bytes 110600 | tf_op jit(solution)/shard_map/ppermute | solution.py:263
  27.4 4.9 %collective-permute-start.7 = (bf16[9,16,128]{2,1,0:T(8,128)(2,1)S(1)}, bf16[9,16,128]{2,1,0:T(8,128)(2,1)S(1)}, u32[]{:S(2)}, u32[]{:S(2)}) collective-permute-start(bf16[9,16,128]{2,1,0:T(8,128)(2,1)S(1)} %get-tuple-element.21), channel_id=1, source_target_pairs={{0,8},{8,0},{16,24},{24,16},{1,9},{9,1},{17,25},{25,17},{2,10},{10... | collective-permute-start | bytes 110600 | tf_op jit(solution)/shard_map/ppermute | solution.py:263
  35.1 5.9 %collective-permute-start.12 = (bf16[8,16,128]{2,1,0:T(8,128)(2,1)S(1)}, bf16[8,16,128]{2,1,0:T(8,128)(2,1)S(1)}, u32[]{:S(2)}, u32[]{:S(2)}) collective-permute-start(bf16[8,16,128]{2,1,0:T(8,128)(2,1)S(1)} %get-tuple-element.24), channel_id=1, source_target_pairs={{0,24},{8,16},{16,8},{24,0},{1,25},{9,17},{17,9},{25,1},{2,26},{10... | collective-permute-start | bytes 98312 | tf_op jit(solution)/shard_map/ppermute | solution.py:263
  36.8 4.9 %collective-permute-start.11 = (bf16[8,16,128]{2,1,0:T(8,128)(2,1)S(1)}, bf16[8,16,128]{2,1,0:T(8,128)(2,1)S(1)}, u32[]{:S(2)}, u32[]{:S(2)}) collective-permute-start(bf16[8,16,128]{2,1,0:T(8,128)(2,1)S(1)} %get-tuple-element.24), channel_id=1, source_target_pairs={{0,16},{8,24},{16,0},{24,8},{1,17},{9,25},{17,1},{25,9},{2,18},{10... | collective-permute-start | bytes 98312 | tf_op jit(solution)/shard_map/ppermute | solution.py:263
  37.2 4.5 %collective-permute-start.10 = (bf16[8,16,128]{2,1,0:T(8,128)(2,1)S(1)}, bf16[8,16,128]{2,1,0:T(8,128)(2,1)S(1)}, u32[]{:S(2)}, u32[]{:S(2)}) collective-permute-start(bf16[8,16,128]{2,1,0:T(8,128)(2,1)S(1)} %get-tuple-element.24), channel_id=1, source_target_pairs={{0,8},{8,0},{16,24},{24,16},{1,9},{9,1},{17,25},{25,17},{2,10},{10... | collective-permute-start | bytes 98312 | tf_op jit(solution)/shard_map/ppermute | solution.py:263

commit v8 on v6

--- a/solution.py
+++ b/solution.py
@@ -90,9 +90,18 @@
     product = jnp.ones((blocks, LANES), jnp.float32)
     for day in range(days):
         product = product * retain_ref[pl.ds(day * blocks, blocks), :]
-    high = product.astype(jnp.bfloat16).astype(jnp.float32)
-    half = lax.broadcasted_iota(jnp.int32, product.shape, 1) < size
-    product_ref[...] = jnp.where(half, high, product - high).astype(jnp.bfloat16)
+    product_ref[...] = packed(product, size)
+
+
+def packed(value, size):
+    high = value.astype(jnp.bfloat16).astype(jnp.float32)
+    half = lax.broadcasted_iota(jnp.int32, value.shape, 1) < size
+    return jnp.where(half, high, value - high).astype(jnp.bfloat16)
+
+
+def unpacked(terms):
+    terms = terms.astype(jnp.float32)
+    return terms + pltpu.roll(terms, LANES // 2, 1)
 
 
 def pass_kernel(piece_ref, product_ref, out_ref):
@@ -104,7 +113,7 @@
 ):
     days, blocks, size, probes = dims
     piece_refs = rest[: 2 * pieces]
-    forcing_ref, message_ref, remote = rest[2 * pieces :]
+    forcing_ref, message_ref, remote, source = rest[2 * pieces :]
     pairs = forcing_ref.shape[0]
     count = links_ref.shape[0]
     bound = piece_refs[0].shape[0]
@@ -121,8 +130,9 @@
             places.append((distance % 2) * held + (distance // 2) * bound + link % bound)
         far = jnp.concatenate([remote[place] for place in places], axis=1)
         total = lax.dot_general(far, weight_ref[block], TURNED, preferred_element_type=jnp.float32)
-        source = (running_ref[block] - total).astype(jnp.bfloat16)
-        drive = lax.dot_general(source, inverse_ref[block], TURNED, preferred_element_type=jnp.float32)
+        source[block] = (running_ref[block] - total).astype(jnp.bfloat16)
+    for block in range(blocks):
+        drive = lax.dot_general(source[block], inverse_ref[block], TURNED, preferred_element_type=jnp.float32)
         for pair in range(pairs):
             forcing_ref[pair, pl.ds(block, days, stride=blocks), :] = jnp.where(
                 seen, drive[pair * days : (pair + 1) * days], 0.0
@@ -142,32 +152,40 @@
         message_ref[pair] = value.astype(jnp.bfloat16)
 
 
-def collect(piece_refs, inbox):
+def carried(pairs, value_refs, factor_refs, backward):
     me = lax.axis_index("tm")
-    for k, ref in enumerate(piece_refs):
-        inbox[me ^ (k + 1)] = ref[...]
-
-
-def carried(pairs, inbox, products, backward):
-    me, count = lax.axis_index("tm"), inbox.shape[0]
-    carries = [jnp.zeros(inbox.shape[2:], jnp.float32)] * pairs
-    for slab in range(count - 1, 0, -1) if backward else range(count - 1):
-        valid = slab > me if backward else slab < me
-        terms = products[slab, pairs].astype(jnp.float32)
-        factor = terms + pltpu.roll(terms, LANES // 2, 1)
-        for pair in range(pairs):
-            update = inbox[slab, pair].astype(jnp.float32) + factor * carries[pair]
+    shape = value_refs[0].shape[1:]
+    carries, through = [jnp.zeros(shape, jnp.float32)] * pairs, jnp.ones(shape, jnp.float32)
+    for level, (values, factors) in enumerate(zip(value_refs, factor_refs)):
+        valid = (me >> level) % 2 == (0 if backward else 1)
+        for pair in range(pairs):
+            update = carries[pair] + through * values[pair].astype(jnp.float32)
             carries[pair] = jnp.where(valid, update, carries[pair])
+        through = jnp.where(valid, through * unpacked(factors[pairs]), through)
     return carries
 
 
+def merge_kernel(dims, level, backward, mine_ref, other_ref, mine_factor_ref, other_factor_ref, merged_ref):
+    days, blocks, size, probes = dims
+    pairs = size * probes // LANES
+    upper = (lax.axis_index("tm") >> level) % 2 == 1
+    mine_factor, other_factor = unpacked(mine_factor_ref[pairs]), unpacked(other_factor_ref[pairs])
+    mine_last = jnp.logical_xor(upper, backward)
+    factor = jnp.where(mine_last, mine_factor, other_factor)
+    for pair in range(pairs):
+        mine, other = mine_ref[pair].astype(jnp.float32), other_ref[pair].astype(jnp.float32)
+        last, first = jnp.where(mine_last, mine, other), jnp.where(mine_last, other, mine)
+        merged_ref[pair] = (last + factor * first).astype(jnp.bfloat16)
+    if merged_ref.shape[0] > pairs:
+        merged_ref[pairs] = packed(mine_factor * other_factor, size)
+
+
 def adjoint_kernel(dims, hops, days_ref, forcing_ref, retain_ref, inverse_ref, *rest):
     days, blocks, size, probes = dims
     pairs = forcing_ref.shape[0]
-    adjoint_ref, message_ref, stage, inbox = rest[hops:]
-    collect(rest[:hops], inbox)
+    adjoint_ref, message_ref, stage, stored = rest[hops:]
     seen = lax.broadcasted_iota(jnp.int32, (days, LANES), 0) < days_ref[0]
-    states = carried(pairs, inbox, inbox, False)
+    states = carried(pairs, rest[:hops], rest[:hops], False)
     for day in range(days):
         rows = pl.ds(day * blocks, blocks)
         factor = retain_ref[rows, :]
@@ -175,10 +193,11 @@
             states[pair] = factor * states[pair] + forcing_ref[pair, rows, :]
             stage[pair, rows, :] = states[pair]
     for block in range(blocks):
-        stored = jnp.concatenate(
-            [stage[pair, pl.ds(block, days, stride=blocks), :].astype(jnp.bfloat16) for pair in range(pairs)], axis=0
-        )
-        adjoint = jnp.dot(stored, inverse_ref[block], preferred_element_type=jnp.float32)
+        for pair in range(pairs):
+            rows = stage[pair, pl.ds(block, days, stride=blocks), :]
+            stored[block, pl.ds(pair * days, days), :] = rows.astype(jnp.bfloat16)
+    for block in range(blocks):
+        adjoint = jnp.dot(stored[block], inverse_ref[block], preferred_element_type=jnp.float32)
         for pair in range(pairs):
             adjoint_ref[pair, pl.ds(block, days, stride=blocks), :] = jnp.where(
                 seen, adjoint[pair * days : (pair + 1) * days], 0.0
@@ -211,10 +230,8 @@
 def variance_kernel(dims, hops, partial_ref, retain_ref, moved_ref, *rest):
     days, blocks, size, probes = dims
     pairs = moved_ref.shape[0]
-    out_ref, stage, inbox, products = rest[2 * hops :]
-    collect(rest[:hops], inbox)
-    collect(rest[hops : 2 * hops], products)
-    carries = carried(pairs, inbox, products, True)
+    out_ref, stage = rest[2 * hops :]
+    carries = carried(pairs, rest[:hops], rest[hops : 2 * hops], True)
     reach = jnp.ones((blocks, LANES), jnp.float32)
     for day in reversed(range(days)):
         rows = pl.ds(day * blocks, blocks)
@@ -299,31 +316,42 @@
     for bits in range(2, groups, 2):
         same += call(pass_kernel, [(outgoing.shape, bf16)], [], 0, 10**5, 0, pieces[bits], product)
     other = [crossed(piece, "space", 1) for piece in same]
-    slabs = lax.axis_size("tm")
-    hops = slabs - 1
-    exchange = lambda message: [crossed(message, "tm", bits) for bits in range(hops, 0, -1)][::-1]
-    inbox = pltpu.VMEM((slabs, pairs + 1, blocks, LANES), bf16)
+    hops = (lax.axis_size("tm") - 1).bit_length()
+
+    def exchange(message, factors, others, backward):
+        sent, received = [message], []
+        for level in range(hops):
+            received.append(crossed(sent[level], "tm", 1 << level))
+            if level < hops - 1:
+                mine, other = (factors[level], others[level]) if backward else (sent[level], received[level])
+                sent += call(
+                    functools.partial(merge_kernel, dims, level, backward),
+                    [(message.shape, bf16)], [], 0, 10**5, 0, sent[level], received[level], mine, other,
+                )
+        return sent, received
+
     forcing, message = call(
         functools.partial(forward_kernel, dims, len(same)),
         [big, ((pairs + 1, blocks, LANES), bf16)],
-        [pltpu.VMEM((2 * held, pairs * days, LANES), bf16)], 10**10, 10**7, 2,
+        [pltpu.VMEM((2 * held, pairs * days, LANES), bf16), pltpu.VMEM((blocks, pairs * days, LANES), bf16)],
+        10**10, 10**7, 2,
         far_table, slab_days, running, remote_weight, inverse, retain, product, *same, *other,
     )
-    ends = exchange(message)
+    sent, ends = exchange(message, None, None, False)
     adjoint, message = call(
         functools.partial(adjoint_kernel, dims, hops),
         [big, ((pairs, blocks, LANES), bf16)],
-        [pltpu.VMEM(*big), inbox], 10**10, 10**7, 1,
+        [pltpu.VMEM(*big), pltpu.VMEM((blocks, pairs * days, LANES), bf16)], 10**10, 10**7, 1,
         slab_days, forcing, retain, inverse, *ends,
     )
-    starts = exchange(message)
+    _, starts = exchange(message, sent, ends, True)
     (partial,) = call(
         functools.partial(own_kernel, dims), [((rows, LANES), f32)], [], 10**9, 10**6, 0, adjoint, retain, moved
     )
     (variance,) = call(
         functools.partial(variance_kernel, dims, hops),
         [((days, blocks * size), f32)],
-        [pltpu.VMEM((rows, LANES), f32), pltpu.VMEM((slabs, pairs, blocks, LANES), bf16), inbox], 10**10, 10**7, 0,
+        [pltpu.VMEM((rows, LANES), f32)], 10**10, 10**7, 0,
         partial, retain, moved, *starts, *ends,
     )
     return variance

time: 43.6 us -> 44.9 us (1.030)
  waiting for transfers between devices: 8.02 us -> 10.6 us
  Pallas kernels: 17.2 us -> 15.9 us
    ppermute x13 -> x11, waiting for transfers between devices: 8.02 us -> 10.6 us  [crossed(): lax.ppermute(block, axis, [(i, i ^ bits) for i in range(lax.axis_size(axi...]
    pallas_call x9 -> x11, Pallas kernels: 17.2 us -> 15.9 us  [call(): pl.pallas_call(kernel, out_shape=[jax.ShapeDtypeStruct(shape, kind) for s...]
    ppermute x13 -> x11, starting transfers between devices: 14.1 us -> 14.1 us  [crossed(): lax.ppermute(block, axis, [(i, i ^ bits) for i in range(lax.axis_size(axi...]
  transfers between devices with their start and end apart: 13 -> 11, of which waited for: 9 -> 8; matrix products, arithmetic and copies ran while one was open for 0% -> 0% of each run, Pallas kernels for 13% -> 12%
where the time goes in v8:
time: 44.9 us; the launch traced here: 44.6 us
  Pallas kernels  15.9 us (35%)
  starting transfers between devices  14.1 us (31%)
  waiting for transfers between devices  10.6 us (24%)
  local copies, waits for them, and re-layouts  3.33 us (7%)
  between operations  0.75 us (2%)
    pallas_call x11, Pallas kernels, call(): pl.pallas_call(kernel, out_shape=[jax.ShapeDtypeStruct(shape, kind) for s...  15.9 us
    ppermute x11, starting transfers between devices, crossed(): lax.ppermute(block, axis, [(i, i ^ bits) for i in range(lax.axis_size(axi...  14.1 us
    ppermute x11, waiting for transfers between devices, crossed(): lax.ppermute(block, axis, [(i, i ^ bits) for i in range(lax.axis_size(axi...  10.6 us
    unnamed x16, local copies, waits for them, and re-layouts  3.33 us
  transfers between devices with their start and end apart: 11, of which 8 were waited for; matrix products, arithmetic and copies ran while one was open for 0% of the time, Pallas kernels for 12%

profile of v8, /device:TPU:0, one launch (start us, length us, event | category | flops | bytes accessed | tf_op | source)
XLA Modules:
  0.0 44.6 jit_solution(8765435696059521769)
XLA Ops:
  0.0 0.0 copy-start.4
  0.0 0.0 copy-start.3
  0.0 0.0 copy-start.2
  0.0 3.0 %shard_map.92.rest_0_ = bf16[2,384,128]{2,1,0:T(8,128)(2,1)} custom-call(s32[1,2]{1,0:T(1,128)} %shared_ref.1, bf16[48,16,1024]{2,1,0:T(8,128)(2,1)} %z_ref.3), custom_call_target="tpu_custom_call" | custom-call | flops 1000000000 | bytes 4000000 | tf_op jit(solution)/shard_map/pallas_call | solution.py:256
  3.0 0.5 %collective-permute-start.3 = (bf16[2,384,128]{2,1,0:T(8,128)(2,1)}, bf16[2,384,128]{2,1,0:T(8,128)(2,1)S(1)}, u32[]{:S(2)}, u32[]{:S(2)}) collective-permute-start(bf16[2,384,128]{2,1,0:T(8,128)(2,1)} %shard_map.92.rest_0_), channel_id=1, source_target_pairs={{0,1},{1,0},{2,3},{3,2},{4,5},{5,4},{6,7},{7,6},{8,9},{9,8},{10,11... | collective-permute-start | bytes 589832 | tf_op jit(solution)/shard_map/ppermute | solution.py:268
  3.4 3.4 %collective-permute-start.2 = (bf16[2,384,128]{2,1,0:T(8,128)(2,1)}, bf16[2,384,128]{2,1,0:T(8,128)(2,1)S(1)}, u32[]{:S(2)}, u32[]{:S(2)}) collective-permute-start(bf16[2,384,128]{2,1,0:T(8,128)(2,1)} %shard_map.92.rest_0_), channel_id=1, source_target_pairs={{0,6},{1,7},{2,4},{3,5},{4,2},{5,3},{6,0},{7,1},{8,14},{9,15},{10,... | collective-permute-start | bytes 589832 | tf_op jit(solution)/shard_map/ppermute | solution.py:268
  6.9 0.5 %collective-permute-start.1 = (bf16[2,384,128]{2,1,0:T(8,128)(2,1)}, bf16[2,384,128]{2,1,0:T(8,128)(2,1)S(1)}, u32[]{:S(2)}, u32[]{:S(2)}) collective-permute-start(bf16[2,384,128]{2,1,0:T(8,128)(2,1)} %shard_map.92.rest_0_), channel_id=1, source_target_pairs={{0,4},{1,5},{2,6},{3,7},{4,0},{5,1},{6,2},{7,3},{8,12},{9,13},{10,... | collective-permute-start | bytes 589832 | tf_op jit(solution)/shard_map/ppermute | solution.py:268
  7.4 0.1 collective-permute-start
  8.1 0.0 copy-done.4
  8.1 0.0 copy-done.3
  8.1 0.0 copy-done.2
  8.1 0.0 copy-start
  8.1 1.4 %copy-done = bf16[48,16,1024]{2,1,0:T(8,128)(2,1)S(1)} copy-done((bf16[48,16,1024]{2,1,0:T(8,128)(2,1)S(1)}, bf16[48,16,1024]{2,1,0:T(8,128)(2,1)}, u32[]{:S(2)}) %copy-start) | copy-done | bytes 1572888
  9.5 0.0 copy-start.1
  9.5 1.2 %copy-done.1 = bf16[16,4,64,64]{3,2,1,0:T(8,128)(2,1)S(1)} copy-done((bf16[16,4,64,64]{3,2,1,0:T(8,128)(2,1)S(1)}, bf16[16,4,64,64]{3,2,1,0:T(8,128)(2,1)}, u32[]{:S(2)}) %copy-start.1) | copy-done | bytes 524312
  10.8 0.0 copy-start.6
  10.8 0.7 %copy-done.6 = s32[16,4]{0,1:T(4,128)S(1)} copy-done((s32[16,4]{0,1:T(4,128)S(1)}, s32[16,4]{0,1:T(4,128)}, u32[]{:S(2)}) %copy-start.6) | copy-done | bytes 280
  11.4 0.0 copy-start.5
  11.4 0.0 copy-start.7
  11.4 4.9 %shard_map.91 = (f32[16,384,128]{2,1,0:T(8,128)S(1)}, bf16[8,768,128]{2,1,0:T(8,128)(2,1)S(1)}, f32[768,128]{1,0:T(8,128)S(1)}, bf16[16,128]{1,0:T(8,128)(2,1)S(...) custom-call(s32[4,16]{1,0:T(4,128)S(1)} %bitcast.2, s32[1]{0:T(128)S(6)} %copy.10.days_ref, ...), custom_call_target="tpu_custom_call" | custom-call | flops 10000000000 | bytes 10000000 | tf_op jit(solution)/shard_map/pallas_call | solution.py:256
  16.4 0.8 %collective-permute-done.piece_ref = bf16[2,384,128]{2,1,0:T(8,128)(2,1)S(1)} collective-permute-done((bf16[2,384,128]{2,1,0:T(8,128)(2,1)}, bf16[2,384,128]{2,1,0:T(8,128)(2,1)S(1)}, u32[]{:S(2)}, u32[]{:S(2)}) %collective-permute-start) | collective-permute-done | bytes 196640 | tf_op jit(solution)/shard_map/ppermute | solution.py:268
  17.2 0.1 collective-permute-start.4
  17.3 0.0 collective-permute-done.1.piece_ref
  17.3 0.5 %collective-permute-start.5 = (bf16[2,384,128]{2,1,0:T(8,128)(2,1)S(1)}, bf16[2,384,128]{2,1,0:T(8,128)(2,1)S(1)}, u32[]{:S(2)}, u32[]{:S(2)}) collective-permute-start(bf16[2,384,128]{2,1,0:T(8,128)(2,1)S(1)} %shard_map.94.rest_2_), channel_id=1, source_target_pairs={{0,1},{1,0},{2,3},{3,2},{4,5},{5,4},{6,7},{7,6},{8,9},{9,8},{10,11... | collective-permute-start | bytes 589832 | tf_op jit(solution)/shard_map/ppermute | solution.py:268
  17.8 0.0 collective-permute-done.2.piece_ref
  17.9 0.1 collective-permute-start.6
  18.0 0.0 collective-permute-done.3.rest_4_
  18.0 0.7 %collective-permute-done.4.rest_5_ = bf16[2,384,128]{2,1,0:T(8,128)(2,1)S(1)} collective-permute-done((bf16[2,384,128]{2,1,0:T(8,128)(2,1)S(1)}, bf16[2,384,128]{2,1,0:T(8,128)(2,1)S(1)}, u32[]{:S(2)}, u32[]{:S(2)}) %collective-permute-start.4) | collective-permute-done | bytes 196640 | tf_op jit(solution)/shard_map/ppermute | solution.py:268
  18.7 0.3 collective-permute-done.5.rest_6_
  19.0 0.4 collective-permute-done.6.rest_7_
  19.4 0.0 copy-done.5
  19.4 0.0 copy-done.7
  19.4 3.0 %shard_map.96 = (f32[8,768,128]{2,1,0:T(8,128)S(1)}, bf16[9,16,128]{2,1,0:T(8,128)(2,1)S(1)}) custom-call(s32[2,16]{1,0:T(2,128)S(1)} %bitcast.3, s32[1]{0:T(128)S(6)} %copy.10.days_ref, f32[16,384,128]{2,1,0:T(8,128)S(1)} %get-tuple-element.15.running_ref, bf16[16,128,256]{2,1,0:T(8,128)(2,1)S(1)} %get-tuple-element.16.weight_ref, ...), custom_call_target="tpu_custom_call" | custom-call | flops 10000000000 | bytes 10000000 | tf_op jit(solution)/shard_map/pallas_call | solution.py:256
  22.4 1.6 %collective-permute-start.7 = (bf16[9,16,128]{2,1,0:T(8,128)(2,1)S(1)}, bf16[9,16,128]{2,1,0:T(8,128)(2,1)S(1)}, u32[]{:S(2)}, u32[]{:S(2)}) collective-permute-start(bf16[9,16,128]{2,1,0:T(8,128)(2,1)S(1)} %get-tuple-element.21.mine_ref.mine_factor_ref), channel_id=1, source_target_pairs={{0,8},{8,0},{16,24},{24,16},{1,9},{9,1},{17,25},{25,17},{2,10},{10... | collective-permute-start | bytes 110600 | tf_op jit(solution)/shard_map/ppermute | solution.py:268
  24.1 2.4 %collective-permute-done.7.other_ref.other_factor_ref.rest_0_.rest_2_ = bf16[9,16,128]{2,1,0:T(8,128)(2,1)S(1)} collective-permute-done((bf16[9,16,128]{2,1,0:T(8,128)(2,1)S(1)}, bf16[9,16,128]{2,1,0:T(8,128)(2,1)S(1)}, u32[]{:S(2)}, u32[]{:S(2)}) %collective-permute-start.7) | collective-permute-done | bytes 36896 | tf_op jit(solution)/shard_map/ppermute | solution.py:268
  26.5 0.1 shard_map.97
  26.5 2.7 %collective-permute-start.8 = (bf16[9,16,128]{2,1,0:T(8,128)(2,1)S(1)}, bf16[9,16,128]{2,1,0:T(8,128)(2,1)S(1)}, u32[]{:S(2)}, u32[]{:S(2)}) collective-permute-start(bf16[9,16,128]{2,1,0:T(8,128)(2,1)S(1)} %shard_map.97), channel_id=1, source_target_pairs={{0,16},{8,24},{16,0},{24,8},{1,17},{9,25},{17,1},{25,9},{2,18},{10... | collective-permute-start | bytes 110600 | tf_op jit(solution)/shard_map/ppermute | solution.py:268
  29.2 2.3 %collective-permute-done.8.rest_1_.rest_3_ = bf16[9,16,128]{2,1,0:T(8,128)(2,1)S(1)} collective-permute-done((bf16[9,16,128]{2,1,0:T(8,128)(2,1)S(1)}, bf16[9,16,128]{2,1,0:T(8,128)(2,1)S(1)}, u32[]{:S(2)}, u32[]{:S(2)}) %collective-permute-start.8) | collective-permute-done | bytes 36896 | tf_op jit(solution)/shard_map/ppermute | solution.py:268
  31.5 2.9 %shard_map.98 = (f32[8,768,128]{2,1,0:T(8,128)S(1)}, bf16[8,16,128]{2,1,0:T(8,128)(2,1)S(1)}) custom-call(s32[1]{0:T(128)S(6)} %copy.10.days_ref, f32[8,768,128]{2,1,0:T(8,128)S(1)} %get-tuple-element.20.forcing_ref, f32[768,128]{1,0:T(8,128)S(1)} %get-tuple-element.18.retain_ref, bf16[16,128,128]{2,1,0:T(8,128)(2,1)S(1)} %get-tuple-element.17.inverse_ref, ...), custom_call_target="tpu_custom_call" | custom-call | flops 10000000000 | bytes 10000000 | tf_op jit(solution)/shard_map/pallas_call | solution.py:256
  34.4 1.6 %collective-permute-start.9 = (bf16[8,16,128]{2,1,0:T(8,128)(2,1)S(1)}, bf16[8,16,128]{2,1,0:T(8,128)(2,1)S(1)}, u32[]{:S(2)}, u32[]{:S(2)}) collective-permute-start(bf16[8,16,128]{2,1,0:T(8,128)(2,1)S(1)} %get-tuple-element.24.mine_ref), channel_id=1, source_target_pairs={{0,8},{8,0},{16,24},{24,16},{1,9},{9,1},{17,25},{25,17},{2,10},{10... | collective-permute-start | bytes 98312 | tf_op jit(solution)/shard_map/ppermute | solution.py:268
  36.0 2.3 %collective-permute-done.9.other_ref.rest_0_ = bf16[8,16,128]{2,1,0:T(8,128)(2,1)S(1)} collective-permute-done((bf16[8,16,128]{2,1,0:T(8,128)(2,1)S(1)}, bf16[8,16,128]{2,1,0:T(8,128)(2,1)S(1)}, u32[]{:S(2)}, u32[]{:S(2)}) %collective-permute-start.9) | collective-permute-done | bytes 32800 | tf_op jit(solution)/shard_map/ppermute | solution.py:268
  38.4 0.1 shard_map.100
  38.4 3.0 %collective-permute-start.10 = (bf16[8,16,128]{2,1,0:T(8,128)(2,1)S(1)}, bf16[8,16,128]{2,1,0:T(8,128)(2,1)S(1)}, u32[]{:S(2)}, u32[]{:S(2)}) collective-permute-start(bf16[8,16,128]{2,1,0:T(8,128)(2,1)S(1)} %shard_map.100), channel_id=1, source_target_pairs={{0,16},{8,24},{16,0},{24,8},{1,17},{9,25},{17,1},{25,9},{2,18},{10... | collective-permute-start | bytes 98312 | tf_op jit(solution)/shard_map/ppermute | solution.py:268
  41.4 0.5 %shard_map.99.partial_ref = f32[768,128]{1,0:T(8,128)S(1)} custom-call(f32[8,768,128]{2,1,0:T(8,128)S(1)} %get-tuple-element.22.adjoint_ref, f32[768,128]{1,0:T(8,128)S(1)} %get-tuple-element.18.retain_ref, bf16[8,768,128]{2,1,0:T(8,128)(2,1)S(1)} %get-tuple-element.23.moved_ref), custom_call_target="tpu_custom_call" | custom-call | flops 1000000000 | bytes 1000000 | tf_op jit(solution)/shard_map/pallas_call | solution.py:256
  41.9 1.4 %collective-permute-done.10.rest_1_ = bf16[8,16,128]{2,1,0:T(8,128)(2,1)S(1)} collective-permute-done((bf16[8,16,128]{2,1,0:T(8,128)(2,1)S(1)}, bf16[8,16,128]{2,1,0:T(8,128)(2,1)S(1)}, u32[]{:S(2)}, u32[]{:S(2)}) %collective-permute-start.10) | collective-permute-done | bytes 32800 | tf_op jit(solution)/shard_map/ppermute | solution.py:268
  43.3 1.3 %shard_map.101 = f32[48,1024]{1,0:T(8,128)} custom-call(f32[768,128]{1,0:T(8,128)S(1)} %shard_map.99.partial_ref, f32[768,128]{1,0:T(8,128)S(1)} %get-tuple-element.18.retain_ref, bf16[8,768,128]{2,1,0:T(8,128)(2,1)S(1)} %get-tuple-element.23.moved_ref, bf16[8,16,128]{2,1,0:T(8,128)(2,1)S(1)} %collective-permute-done.9.other_ref.rest_0_, ...), custom_call_target="tpu_custom_call" | custom-call | flops 10000000000 | bytes 10000000 | tf_op jit(solution)/shard_map/pallas_call | solution.py:256
  (3 shorter events, 0.0 us)
Async XLA Ops:
  0.0 8.1 %copy-start.4 = (f32[48,1024]{1,0:T(8,128)S(1)}, f32[48,1024]{1,0:T(8,128)}, u32[]{:S(2)}) copy-start(f32[48,1024]{1,0:T(8,128)} %retention_ref.1) | copy-start | bytes 589828
  0.0 8.1 %copy-start.3 = (bf16[16,64,64]{2,1,0:T(8,128)(2,1)S(1)}, bf16[16,64,64]{2,1,0:T(8,128)(2,1)}, u32[]{:S(2)}) copy-start(bf16[16,64,64]{2,1,0:T(8,128)(2,1)} %inverse_ref.1) | copy-start | bytes 393220
  0.0 8.1 %copy-start.2 = (bf16[16,2,64,64]{3,2,1,0:T(8,128)(2,1)S(1)}, bf16[16,2,64,64]{3,2,1,0:T(8,128)(2,1)}, u32[]{:S(2)}) copy-start(bf16[16,2,64,64]{3,2,1,0:T(8,128)(2,1)} %remote_weight_ref.1) | copy-start | bytes 786436
  3.0 15.0 %collective-permute-start.3 = (bf16[2,384,128]{2,1,0:T(8,128)(2,1)}, bf16[2,384,128]{2,1,0:T(8,128)(2,1)S(1)}, u32[]{:S(2)}, u32[]{:S(2)}) collective-permute-start(bf16[2,384,128]{2,1,0:T(8,128)(2,1)} %shard_map.92.rest_0_), channel_id=1, source_target_pairs={{0,1},{1,0},{2,3},{3,2},{4,5},{5,4},{6,7},{7,6},{8,9},{9,8},{10,11... | collective-permute-start | bytes 589832 | tf_op jit(solution)/shard_map/ppermute | solution.py:268
  3.4 14.4 %collective-permute-start.2 = (bf16[2,384,128]{2,1,0:T(8,128)(2,1)}, bf16[2,384,128]{2,1,0:T(8,128)(2,1)S(1)}, u32[]{:S(2)}, u32[]{:S(2)}) collective-permute-start(bf16[2,384,128]{2,1,0:T(8,128)(2,1)} %shard_map.92.rest_0_), channel_id=1, source_target_pairs={{0,6},{1,7},{2,4},{3,5},{4,2},{5,3},{6,0},{7,1},{8,14},{9,15},{10,... | collective-permute-start | bytes 589832 | tf_op jit(solution)/shard_map/ppermute | solution.py:268
  6.9 10.4 %collective-permute-start.1 = (bf16[2,384,128]{2,1,0:T(8,128)(2,1)}, bf16[2,384,128]{2,1,0:T(8,128)(2,1)S(1)}, u32[]{:S(2)}, u32[]{:S(2)}) collective-permute-start(bf16[2,384,128]{2,1,0:T(8,128)(2,1)} %shard_map.92.rest_0_), channel_id=1, source_target_pairs={{0,4},{1,5},{2,6},{3,7},{4,0},{5,1},{6,2},{7,3},{8,12},{9,13},{10,... | collective-permute-start | bytes 589832 | tf_op jit(solution)/shard_map/ppermute | solution.py:268
  7.4 9.8 %collective-permute-start = (bf16[2,384,128]{2,1,0:T(8,128)(2,1)}, bf16[2,384,128]{2,1,0:T(8,128)(2,1)S(1)}, u32[]{:S(2)}, u32[]{:S(2)}) collective-permute-start(bf16[2,384,128]{2,1,0:T(8,128)(2,1)} %shard_map.92.rest_0_), channel_id=1, source_target_pairs={{0,2},{1,3},{2,0},{3,1},{4,6},{5,7},{6,4},{7,5},{8,10},{9,11},{10,... | collective-permute-start | bytes 589832 | tf_op jit(solution)/shard_map/ppermute | solution.py:268
  8.1 1.4 %copy-start = (bf16[48,16,1024]{2,1,0:T(8,128)(2,1)S(1)}, bf16[48,16,1024]{2,1,0:T(8,128)(2,1)}, u32[]{:S(2)}) copy-start(bf16[48,16,1024]{2,1,0:T(8,128)(2,1)} %z_ref.3) | copy-start | bytes 4718596
  9.5 1.2 %copy-start.1 = (bf16[16,4,64,64]{3,2,1,0:T(8,128)(2,1)S(1)}, bf16[16,4,64,64]{3,2,1,0:T(8,128)(2,1)}, u32[]{:S(2)}) copy-start(bf16[16,4,64,64]{3,2,1,0:T(8,128)(2,1)} %weight_ref.1) | copy-start | bytes 1572868
  10.8 0.7 %copy-start.6 = (s32[16,4]{0,1:T(4,128)S(1)}, s32[16,4]{0,1:T(4,128)}, u32[]{:S(2)}) copy-start(s32[16,4]{0,1:T(4,128)} %param.10) | copy-start | bytes 772
  11.4 7.9 %copy-start.5 = (bf16[2,384,128]{2,1,0:T(8,128)(2,1)S(1)}, bf16[2,384,128]{2,1,0:T(8,128)(2,1)}, u32[]{:S(2)}) copy-start(bf16[2,384,128]{2,1,0:T(8,128)(2,1)} %shard_map.92.rest_0_) | copy-start | bytes 589828
  11.4 7.9 %copy-start.7 = (s32[16,2]{0,1:T(2,128)S(1)}, s32[16,2]{0,1:T(2,128)}, u32[]{:S(2)}) copy-start(s32[16,2]{0,1:T(2,128)} %param.11) | copy-start | bytes 388
  17.2 1.5 %collective-permute-start.4 = (bf16[2,384,128]{2,1,0:T(8,128)(2,1)S(1)}, bf16[2,384,128]{2,1,0:T(8,128)(2,1)S(1)}, u32[]{:S(2)}, u32[]{:S(2)}) collective-permute-start(bf16[2,384,128]{2,1,0:T(8,128)(2,1)S(1)} %shard_map.93.rest_1_), channel_id=1, source_target_pairs={{0,1},{1,0},{2,3},{3,2},{4,5},{5,4},{6,7},{7,6},{8,9},{9,8},{10,11... | collective-permute-start | bytes 589832 | tf_op jit(solution)/shard_map/ppermute | solution.py:268
  17.3 1.7 %collective-permute-start.5 = (bf16[2,384,128]{2,1,0:T(8,128)(2,1)S(1)}, bf16[2,384,128]{2,1,0:T(8,128)(2,1)S(1)}, u32[]{:S(2)}, u32[]{:S(2)}) collective-permute-start(bf16[2,384,128]{2,1,0:T(8,128)(2,1)S(1)} %shard_map.94.rest_2_), channel_id=1, source_target_pairs={{0,1},{1,0},{2,3},{3,2},{4,5},{5,4},{6,7},{7,6},{8,9},{9,8},{10,11... | collective-permute-start | bytes 589832 | tf_op jit(solution)/shard_map/ppermute | solution.py:268
  17.9 1.5 %collective-permute-start.6 = (bf16[2,384,128]{2,1,0:T(8,128)(2,1)S(1)}, bf16[2,384,128]{2,1,0:T(8,128)(2,1)S(1)}, u32[]{:S(2)}, u32[]{:S(2)}) collective-permute-start(bf16[2,384,128]{2,1,0:T(8,128)(2,1)S(1)} %shard_map.95.rest_3_), channel_id=1, source_target_pairs={{0,1},{1,0},{2,3},{3,2},{4,5},{5,4},{6,7},{7,6},{8,9},{9,8},{10,11... | collective-permute-start | bytes 589832 | tf_op jit(solution)/shard_map/ppermute | solution.py:268
  22.4 4.0 %collective-permute-start.7 = (bf16[9,16,128]{2,1,0:T(8,128)(2,1)S(1)}, bf16[9,16,128]{2,1,0:T(8,128)(2,1)S(1)}, u32[]{:S(2)}, u32[]{:S(2)}) collective-permute-start(bf16[9,16,128]{2,1,0:T(8,128)(2,1)S(1)} %get-tuple-element.21.mine_ref.mine_factor_ref), channel_id=1, source_target_pairs={{0,8},{8,0},{16,24},{24,16},{1,9},{9,1},{17,25},{25,17},{2,10},{10... | collective-permute-start | bytes 110600 | tf_op jit(solution)/shard_map/ppermute | solution.py:268
  26.5 4.9 %collective-permute-start.8 = (bf16[9,16,128]{2,1,0:T(8,128)(2,1)S(1)}, bf16[9,16,128]{2,1,0:T(8,128)(2,1)S(1)}, u32[]{:S(2)}, u32[]{:S(2)}) collective-permute-start(bf16[9,16,128]{2,1,0:T(8,128)(2,1)S(1)} %shard_map.97), channel_id=1, source_target_pairs={{0,16},{8,24},{16,0},{24,8},{1,17},{9,25},{17,1},{25,9},{2,18},{10... | collective-permute-start | bytes 110600 | tf_op jit(solution)/shard_map/ppermute | solution.py:268
  34.4 4.0 %collective-permute-start.9 = (bf16[8,16,128]{2,1,0:T(8,128)(2,1)S(1)}, bf16[8,16,128]{2,1,0:T(8,128)(2,1)S(1)}, u32[]{:S(2)}, u32[]{:S(2)}) collective-permute-start(bf16[8,16,128]{2,1,0:T(8,128)(2,1)S(1)} %get-tuple-element.24.mine_ref), channel_id=1, source_target_pairs={{0,8},{8,0},{16,24},{24,16},{1,9},{9,1},{17,25},{25,17},{2,10},{10... | collective-permute-start | bytes 98312 | tf_op jit(solution)/shard_map/ppermute | solution.py:268
  38.4 4.9 %collective-permute-start.10 = (bf16[8,16,128]{2,1,0:T(8,128)(2,1)S(1)}, bf16[8,16,128]{2,1,0:T(8,128)(2,1)S(1)}, u32[]{:S(2)}, u32[]{:S(2)}) collective-permute-start(bf16[8,16,128]{2,1,0:T(8,128)(2,1)S(1)} %shard_map.100), channel_id=1, source_target_pairs={{0,16},{8,24},{16,0},{24,8},{1,17},{9,25},{17,1},{25,9},{2,18},{10... | collective-permute-start | bytes 98312 | tf_op jit(solution)/shard_map/ppermute | solution.py:268

commit v9 on v6

--- a/solution.py
+++ b/solution.py
@@ -25,6 +25,16 @@
     return jnp.concatenate(
         [jnp.concatenate([weight, zero], axis=1), jnp.concatenate([zero, weight], axis=1)], axis=0
     )
+
+
+def paired(tiles):
+    return jnp.concatenate([jnp.concatenate(tiles[half::2], axis=0) for half in range(2)], axis=1)
+
+
+def unpaired(value, days):
+    return [
+        value[row : row + days, lane : lane + LANES] for row in range(0, value.shape[0], days) for lane in (0, LANES)
+    ]
 
 
 def outgoing_kernel(dims, shared_ref, z_ref, outgoing_ref):
@@ -51,7 +61,7 @@
 
 def local_kernel(
     dims, links_ref, days_ref, z_ref, weight_ref, remote_weight_ref, inverse_ref, retention_ref,
-    running_ref, moved_ref, retain_ref, product_ref, remote_doubled_ref, inverse_doubled_ref, stage, turned,
+    running_ref, moved_ref, retain_ref, product_ref, remote_doubled_ref, inverse_fourfold_ref, stage, turned,
 ):
     days, blocks, size, probes = dims
     pairs = size * probes // LANES
@@ -77,7 +87,7 @@
         remote_doubled_ref[block] = jnp.concatenate(
             [doubled(remote_weight_ref[block, k]) for k in range(remote_weight_ref.shape[1])], axis=1
         )
-        inverse_doubled_ref[block] = doubled(inverse_ref[block])
+        inverse_fourfold_ref[block] = doubled(doubled(inverse_ref[block]))
     observed = days_ref[0]
     shape = (days, LANES)
     first = lax.broadcasted_iota(jnp.int32, shape, 1) < size
@@ -104,7 +114,7 @@
 ):
     days, blocks, size, probes = dims
     piece_refs = rest[: 2 * pieces]
-    forcing_ref, message_ref, remote = rest[2 * pieces :]
+    forcing_ref, message_ref, remote, source = rest[2 * pieces :]
     pairs = forcing_ref.shape[0]
     count = links_ref.shape[0]
     bound = piece_refs[0].shape[0]
@@ -121,12 +131,14 @@
             places.append((distance % 2) * held + (distance // 2) * bound + link % bound)
         far = jnp.concatenate([remote[place] for place in places], axis=1)
         total = lax.dot_general(far, weight_ref[block], TURNED, preferred_element_type=jnp.float32)
-        source = (running_ref[block] - total).astype(jnp.bfloat16)
-        drive = lax.dot_general(source, inverse_ref[block], TURNED, preferred_element_type=jnp.float32)
-        for pair in range(pairs):
-            forcing_ref[pair, pl.ds(block, days, stride=blocks), :] = jnp.where(
-                seen, drive[pair * days : (pair + 1) * days], 0.0
-            )
+        source[block] = (running_ref[block] - total).astype(jnp.bfloat16)
+    for block in range(blocks):
+        drive = lax.dot_general(
+            paired([source[block, pl.ds(pair * days, days), :] for pair in range(pairs)]),
+            inverse_ref[block], TURNED, preferred_element_type=jnp.float32,
+        )
+        for pair, tile in enumerate(unpaired(drive, days)):
+            forcing_ref[pair, pl.ds(block, days, stride=blocks), :] = jnp.where(seen, tile, 0.0)
     states = [jnp.zeros((blocks, LANES), jnp.float32)] * pairs
     for day in range(days):
         rows = pl.ds(day * blocks, blocks)
@@ -161,28 +173,43 @@
     return carries
 
 
-def adjoint_kernel(dims, hops, days_ref, forcing_ref, retain_ref, inverse_ref, *rest):
+def states_kernel(dims, forcing_ref, retain_ref, states_ref, through_ref, stage, products):
     days, blocks, size, probes = dims
     pairs = forcing_ref.shape[0]
-    adjoint_ref, message_ref, stage, inbox = rest[hops:]
+    states = [jnp.zeros((blocks, LANES), jnp.float32)] * pairs
+    product = jnp.ones((blocks, LANES), jnp.float32)
+    for day in range(days):
+        rows = pl.ds(day * blocks, blocks)
+        factor = retain_ref[rows, :]
+        product = product * factor
+        products[rows, :] = product
+        for pair in range(pairs):
+            states[pair] = factor * states[pair] + forcing_ref[pair, rows, :]
+            stage[pair, rows, :] = states[pair]
+    for block in range(blocks):
+        through_ref[block] = products[pl.ds(block, days, stride=blocks), :]
+        for pair in range(pairs):
+            states_ref[block, pl.ds(pair * days, days), :] = stage[pair, pl.ds(block, days, stride=blocks), :]
+
+
+def adjoint_kernel(dims, hops, days_ref, states_ref, through_ref, retain_ref, inverse_ref, *rest):
+    days, blocks, size, probes = dims
+    adjoint_ref, message_ref, inbox, enter = rest[hops:]
+    pairs = adjoint_ref.shape[0]
     collect(rest[:hops], inbox)
     seen = lax.broadcasted_iota(jnp.int32, (days, LANES), 0) < days_ref[0]
-    states = carried(pairs, inbox, inbox, False)
-    for day in range(days):
-        rows = pl.ds(day * blocks, blocks)
-        factor = retain_ref[rows, :]
-        for pair in range(pairs):
-            states[pair] = factor * states[pair] + forcing_ref[pair, rows, :]
-            stage[pair, rows, :] = states[pair]
-    for block in range(blocks):
-        stored = jnp.concatenate(
-            [stage[pair, pl.ds(block, days, stride=blocks), :].astype(jnp.bfloat16) for pair in range(pairs)], axis=0
-        )
-        adjoint = jnp.dot(stored, inverse_ref[block], preferred_element_type=jnp.float32)
-        for pair in range(pairs):
-            adjoint_ref[pair, pl.ds(block, days, stride=blocks), :] = jnp.where(
-                seen, adjoint[pair * days : (pair + 1) * days], 0.0
-            )
+    for pair, carry in enumerate(carried(pairs, inbox, inbox, False)):
+        enter[pair] = carry
+    for block in range(blocks):
+        through = through_ref[block]
+        stored = [
+            (states_ref[block, pl.ds(pair * days, days), :] + through * enter[pair, pl.ds(block, 1), :])
+            .astype(jnp.bfloat16)
+            for pair in range(pairs)
+        ]
+        adjoint = jnp.dot(paired(stored), inverse_ref[block], preferred_element_type=jnp.float32)
+        for pair, tile in enumerate(unpaired(adjoint, days)):
+            adjoint_ref[pair, pl.ds(block, days, stride=blocks), :] = jnp.where(seen, tile, 0.0)
     carries = [jnp.zeros((blocks, LANES), jnp.float32)] * pairs
     for day in reversed(range(days)):
         rows = pl.ds(day * blocks, blocks)
@@ -289,7 +316,7 @@
             ((rows, LANES), f32),
             ((blocks, LANES), bf16),
             ((blocks, LANES, far * LANES), bf16),
-            ((blocks, LANES, LANES), bf16),
+            ((blocks, 2 * LANES, 2 * LANES), bf16),
         ],
         [pltpu.VMEM(*big), pltpu.VMEM((blocks, pairs * days, LANES), bf16)],
         10**10, 10**7, 2,
@@ -306,15 +333,22 @@
     forcing, message = call(
         functools.partial(forward_kernel, dims, len(same)),
         [big, ((pairs + 1, blocks, LANES), bf16)],
-        [pltpu.VMEM((2 * held, pairs * days, LANES), bf16)], 10**10, 10**7, 2,
+        [pltpu.VMEM((2 * held, pairs * days, LANES), bf16), pltpu.VMEM((blocks, pairs * days, LANES), bf16)],
+        10**10, 10**7, 2,
         far_table, slab_days, running, remote_weight, inverse, retain, product, *same, *other,
     )
     ends = exchange(message)
+    by_block = (blocks, pairs * days, LANES)
+    states, through = call(
+        functools.partial(states_kernel, dims),
+        [(by_block, f32), ((blocks, days, LANES), f32)],
+        [pltpu.VMEM(*big), pltpu.VMEM((rows, LANES), f32)], 10**9, 10**6, 0, forcing, retain,
+    )
     adjoint, message = call(
         functools.partial(adjoint_kernel, dims, hops),
         [big, ((pairs, blocks, LANES), bf16)],
-        [pltpu.VMEM(*big), inbox], 10**10, 10**7, 1,
-        slab_days, forcing, retain, inverse, *ends,
+        [inbox, pltpu.VMEM((pairs, blocks, LANES), f32)], 10**10, 10**7, 1,
+        slab_days, states, through, retain, inverse, *ends,
     )
     starts = exchange(message)
     (partial,) = call(

time: 43.6 us -> 41.2 us (0.945)
  waiting for transfers between devices: 8.02 us -> 6.09 us
  Pallas kernels: 17.2 us -> 16.7 us
    ppermute x13, waiting for transfers between devices: 8.02 us -> 6.09 us  [crossed(): lax.ppermute(block, axis, [(i, i ^ bits) for i in range(lax.axis_size(axi...]
    pallas_call x9 -> x10, Pallas kernels: 17.2 us -> 16.7 us  [call(): pl.pallas_call(kernel, out_shape=[jax.ShapeDtypeStruct(shape, kind) for s...]
  transfers between devices with their start and end apart: 13 -> 13, of which waited for: 9 -> 8; matrix products, arithmetic and copies ran while one was open for 0% -> 0% of each run, Pallas kernels for 13% -> 18%
where the time goes in v9:
time: 41.2 us; the launch traced here: 41 us
  Pallas kernels  16.7 us (41%)
  starting transfers between devices  14.1 us (34%)
  waiting for transfers between devices  6.09 us (15%)
  local copies, waits for them, and re-layouts  3.33 us (8%)
  between operations  0.77 us (2%)
    pallas_call x10, Pallas kernels, call(): pl.pallas_call(kernel, out_shape=[jax.ShapeDtypeStruct(shape, kind) for s...  16.7 us
    ppermute x13, starting transfers between devices, crossed(): lax.ppermute(block, axis, [(i, i ^ bits) for i in range(lax.axis_size(axi...  14.1 us
    ppermute x13, waiting for transfers between devices, crossed(): lax.ppermute(block, axis, [(i, i ^ bits) for i in range(lax.axis_size(axi...  6.09 us
    unnamed x16, local copies, waits for them, and re-layouts  3.33 us
  transfers between devices with their start and end apart: 13, of which 8 were waited for; matrix products, arithmetic and copies ran while one was open for 0% of the time, Pallas kernels for 18%

profile of v9, /device:TPU:0, one launch (start us, length us, event | category | flops | bytes accessed | tf_op | source)
XLA Modules:
  0.0 41.0 jit_solution(1687721301280650784)
XLA Ops:
  0.0 0.0 copy-start.4
  0.0 0.0 copy-start.3
  0.0 0.0 copy-start.2
  0.0 3.0 %shard_map.92.rest_0_ = bf16[2,384,128]{2,1,0:T(8,128)(2,1)} custom-call(s32[1,2]{1,0:T(1,128)} %shared_ref.1, bf16[48,16,1024]{2,1,0:T(8,128)(2,1)} %z_ref.3), custom_call_target="tpu_custom_call" | custom-call | flops 1000000000 | bytes 4000000 | tf_op jit(solution)/shard_map/pallas_call | solution.py:266
  3.0 0.5 %collective-permute-start.3 = (bf16[2,384,128]{2,1,0:T(8,128)(2,1)}, bf16[2,384,128]{2,1,0:T(8,128)(2,1)S(1)}, u32[]{:S(2)}, u32[]{:S(2)}) collective-permute-start(bf16[2,384,128]{2,1,0:T(8,128)(2,1)} %shard_map.92.rest_0_), channel_id=1, source_target_pairs={{0,1},{1,0},{2,3},{3,2},{4,5},{5,4},{6,7},{7,6},{8,9},{9,8},{10,11... | collective-permute-start | bytes 589832 | tf_op jit(solution)/shard_map/ppermute | solution.py:278
  3.4 3.4 %collective-permute-start.2 = (bf16[2,384,128]{2,1,0:T(8,128)(2,1)}, bf16[2,384,128]{2,1,0:T(8,128)(2,1)S(1)}, u32[]{:S(2)}, u32[]{:S(2)}) collective-permute-start(bf16[2,384,128]{2,1,0:T(8,128)(2,1)} %shard_map.92.rest_0_), channel_id=1, source_target_pairs={{0,6},{1,7},{2,4},{3,5},{4,2},{5,3},{6,0},{7,1},{8,14},{9,15},{10,... | collective-permute-start | bytes 589832 | tf_op jit(solution)/shard_map/ppermute | solution.py:278
  6.9 0.5 %collective-permute-start.1 = (bf16[2,384,128]{2,1,0:T(8,128)(2,1)}, bf16[2,384,128]{2,1,0:T(8,128)(2,1)S(1)}, u32[]{:S(2)}, u32[]{:S(2)}) collective-permute-start(bf16[2,384,128]{2,1,0:T(8,128)(2,1)} %shard_map.92.rest_0_), channel_id=1, source_target_pairs={{0,4},{1,5},{2,6},{3,7},{4,0},{5,1},{6,2},{7,3},{8,12},{9,13},{10,... | collective-permute-start | bytes 589832 | tf_op jit(solution)/shard_map/ppermute | solution.py:278
  7.4 0.1 collective-permute-start
  8.1 0.0 copy-done.4
  8.1 0.0 copy-done.3
  8.1 0.0 copy-done.2
  8.1 0.0 copy-start
  8.1 1.4 %copy-done = bf16[48,16,1024]{2,1,0:T(8,128)(2,1)S(1)} copy-done((bf16[48,16,1024]{2,1,0:T(8,128)(2,1)S(1)}, bf16[48,16,1024]{2,1,0:T(8,128)(2,1)}, u32[]{:S(2)}) %copy-start) | copy-done | bytes 1572888
  9.5 0.0 copy-start.1
  9.5 1.2 %copy-done.1 = bf16[16,4,64,64]{3,2,1,0:T(8,128)(2,1)S(1)} copy-done((bf16[16,4,64,64]{3,2,1,0:T(8,128)(2,1)S(1)}, bf16[16,4,64,64]{3,2,1,0:T(8,128)(2,1)}, u32[]{:S(2)}) %copy-start.1) | copy-done | bytes 524312
  10.8 0.0 copy-start.6
  10.8 0.7 %copy-done.6 = s32[16,4]{0,1:T(4,128)S(1)} copy-done((s32[16,4]{0,1:T(4,128)S(1)}, s32[16,4]{0,1:T(4,128)}, u32[]{:S(2)}) %copy-start.6) | copy-done | bytes 280
  11.4 0.0 copy-start.5
  11.4 0.0 copy-start.7
  11.4 4.9 %shard_map.91 = (f32[16,384,128]{2,1,0:T(8,128)S(1)}, bf16[8,768,128]{2,1,0:T(8,128)(2,1)S(1)}, f32[768,128]{1,0:T(8,128)S(1)}, bf16[16,128]{1,0:T(8,128)(2,1)S(...) custom-call(s32[4,16]{1,0:T(4,128)S(1)} %bitcast.2, s32[1]{0:T(128)S(6)} %copy.10.days_ref, ...), custom_call_target="tpu_custom_call" | custom-call | flops 10000000000 | bytes 10000000 | tf_op jit(solution)/shard_map/pallas_call | solution.py:266
  16.4 0.8 %collective-permute-done.piece_ref = bf16[2,384,128]{2,1,0:T(8,128)(2,1)S(1)} collective-permute-done((bf16[2,384,128]{2,1,0:T(8,128)(2,1)}, bf16[2,384,128]{2,1,0:T(8,128)(2,1)S(1)}, u32[]{:S(2)}, u32[]{:S(2)}) %collective-permute-start) | collective-permute-done | bytes 196640 | tf_op jit(solution)/shard_map/ppermute | solution.py:278
  17.2 0.1 collective-permute-start.4
  17.3 0.0 collective-permute-done.1.piece_ref
  17.3 0.5 %collective-permute-start.5 = (bf16[2,384,128]{2,1,0:T(8,128)(2,1)S(1)}, bf16[2,384,128]{2,1,0:T(8,128)(2,1)S(1)}, u32[]{:S(2)}, u32[]{:S(2)}) collective-permute-start(bf16[2,384,128]{2,1,0:T(8,128)(2,1)S(1)} %shard_map.94.rest_2_), channel_id=1, source_target_pairs={{0,1},{1,0},{2,3},{3,2},{4,5},{5,4},{6,7},{7,6},{8,9},{9,8},{10,11... | collective-permute-start | bytes 589832 | tf_op jit(solution)/shard_map/ppermute | solution.py:278
  17.8 0.0 collective-permute-done.2.piece_ref
  17.9 0.1 collective-permute-start.6
  18.0 0.0 collective-permute-done.3.rest_4_
  18.0 0.7 %collective-permute-done.4.rest_5_ = bf16[2,384,128]{2,1,0:T(8,128)(2,1)S(1)} collective-permute-done((bf16[2,384,128]{2,1,0:T(8,128)(2,1)S(1)}, bf16[2,384,128]{2,1,0:T(8,128)(2,1)S(1)}, u32[]{:S(2)}, u32[]{:S(2)}) %collective-permute-start.4) | collective-permute-done | bytes 196640 | tf_op jit(solution)/shard_map/ppermute | solution.py:278
  18.7 0.3 collective-permute-done.5.rest_6_
  19.0 0.4 collective-permute-done.6.rest_7_
  19.4 0.0 copy-done.5
  19.4 0.0 copy-done.7
  19.4 3.2 %shard_map.96 = (f32[8,768,128]{2,1,0:T(8,128)S(1)}, bf16[9,16,128]{2,1,0:T(8,128)(2,1)S(1)}) custom-call(s32[2,16]{1,0:T(2,128)S(1)} %bitcast.3, s32[1]{0:T(128)S(6)} %copy.10.days_ref, f32[16,384,128]{2,1,0:T(8,128)S(1)} %get-tuple-element.17.running_ref, bf16[16,128,256]{2,1,0:T(8,128)(2,1)S(1)} %get-tuple-element.18.weight_ref, ...), custom_call_target="tpu_custom_call" | custom-call | flops 10000000000 | bytes 10000000 | tf_op jit(solution)/shard_map/pallas_call | solution.py:266
  22.5 3.7 %collective-permute-start.9 = (bf16[9,16,128]{2,1,0:T(8,128)(2,1)S(1)}, bf16[9,16,128]{2,1,0:T(8,128)(2,1)S(1)}, u32[]{:S(2)}, u32[]{:S(2)}) collective-permute-start(bf16[9,16,128]{2,1,0:T(8,128)(2,1)S(1)} %get-tuple-element.25), channel_id=1, source_target_pairs={{0,24},{8,16},{16,8},{24,0},{1,25},{9,17},{17,9},{25,1},{2,26},{10... | collective-permute-start | bytes 110600 | tf_op jit(solution)/shard_map/ppermute | solution.py:278
  26.2 0.0 collective-permute-start.8
  26.2 0.8 %collective-permute-start.7 = (bf16[9,16,128]{2,1,0:T(8,128)(2,1)S(1)}, bf16[9,16,128]{2,1,0:T(8,128)(2,1)S(1)}, u32[]{:S(2)}, u32[]{:S(2)}) collective-permute-start(bf16[9,16,128]{2,1,0:T(8,128)(2,1)S(1)} %get-tuple-element.25), channel_id=1, source_target_pairs={{0,8},{8,0},{16,24},{24,16},{1,9},{9,1},{17,25},{25,17},{2,10},{10... | collective-permute-start | bytes 110600 | tf_op jit(solution)/shard_map/ppermute | solution.py:278
  27.0 1.9 %shard_map.97 = (f32[16,384,128]{2,1,0:T(8,128)S(1)}, f32[16,48,128]{2,1,0:T(8,128)S(1)}) custom-call(f32[8,768,128]{2,1,0:T(8,128)S(1)} %get-tuple-element.22.forcing_ref, f32[768,128]{1,0:T(8,128)S(1)} %get-tuple-element.20.retain_ref), custom_call_target="tpu_custom_call" | custom-call | flops 1000000000 | bytes 1000000 | tf_op jit(solution)/shard_map/pallas_call | solution.py:266
  28.9 0.0 collective-permute-done.9.rest_2_.rest_5_
  28.9 2.2 %collective-permute-done.8.rest_1_.rest_4_ = bf16[9,16,128]{2,1,0:T(8,128)(2,1)S(1)} collective-permute-done((bf16[9,16,128]{2,1,0:T(8,128)(2,1)S(1)}, bf16[9,16,128]{2,1,0:T(8,128)(2,1)S(1)}, u32[]{:S(2)}, u32[]{:S(2)}) %collective-permute-start.8) | collective-permute-done | bytes 36896 | tf_op jit(solution)/shard_map/ppermute | solution.py:278
  31.1 0.0 collective-permute-done.7.rest_0_.rest_3_
  31.1 1.9 %shard_map.98 = (f32[8,768,128]{2,1,0:T(8,128)S(1)}, bf16[8,16,128]{2,1,0:T(8,128)(2,1)S(1)}) custom-call(s32[1]{0:T(128)S(6)} %copy.10.days_ref, f32[16,384,128]{2,1,0:T(8,128)S(1)} %get-tuple-element.23.states_ref, f32[16,48,128]{2,1,0:T(8,128)S(1)} %get-tuple-element.24.through_ref, f32[768,128]{1,0:T(8,128)S(1)} %get-tuple-element.20.retain_ref, ...), custom_call_target="tpu_custom_call" | custom-call | flops 10000000000 | bytes 10000000 | tf_op jit(solution)/shard_map/pallas_call | solution.py:266
  32.9 1.8 %collective-permute-start.12 = (bf16[8,16,128]{2,1,0:T(8,128)(2,1)S(1)}, bf16[8,16,128]{2,1,0:T(8,128)(2,1)S(1)}, u32[]{:S(2)}, u32[]{:S(2)}) collective-permute-start(bf16[8,16,128]{2,1,0:T(8,128)(2,1)S(1)} %get-tuple-element.28), channel_id=1, source_target_pairs={{0,24},{8,16},{16,8},{24,0},{1,25},{9,17},{17,9},{25,1},{2,26},{10... | collective-permute-start | bytes 98312 | tf_op jit(solution)/shard_map/ppermute | solution.py:278
  34.7 0.4 collective-permute-start.11
  35.1 2.3 %collective-permute-start.10 = (bf16[8,16,128]{2,1,0:T(8,128)(2,1)S(1)}, bf16[8,16,128]{2,1,0:T(8,128)(2,1)S(1)}, u32[]{:S(2)}, u32[]{:S(2)}) collective-permute-start(bf16[8,16,128]{2,1,0:T(8,128)(2,1)S(1)} %get-tuple-element.28), channel_id=1, source_target_pairs={{0,8},{8,0},{16,24},{24,16},{1,9},{9,1},{17,25},{25,17},{2,10},{10... | collective-permute-start | bytes 98312 | tf_op jit(solution)/shard_map/ppermute | solution.py:278
  37.4 0.5 %shard_map.99.partial_ref = f32[768,128]{1,0:T(8,128)S(1)} custom-call(f32[8,768,128]{2,1,0:T(8,128)S(1)} %get-tuple-element.26.adjoint_ref, f32[768,128]{1,0:T(8,128)S(1)} %get-tuple-element.20.retain_ref, bf16[8,768,128]{2,1,0:T(8,128)(2,1)S(1)} %get-tuple-element.27.moved_ref), custom_call_target="tpu_custom_call" | custom-call | flops 1000000000 | bytes 1000000 | tf_op jit(solution)/shard_map/pallas_call | solution.py:266
  37.9 1.0 %collective-permute-done.12.rest_2_ = bf16[8,16,128]{2,1,0:T(8,128)(2,1)S(1)} collective-permute-done((bf16[8,16,128]{2,1,0:T(8,128)(2,1)S(1)}, bf16[8,16,128]{2,1,0:T(8,128)(2,1)S(1)}, u32[]{:S(2)}, u32[]{:S(2)}) %collective-permute-start.12) | collective-permute-done | bytes 32800 | tf_op jit(solution)/shard_map/ppermute | solution.py:278
  38.9 0.7 %collective-permute-done.11.rest_1_ = bf16[8,16,128]{2,1,0:T(8,128)(2,1)S(1)} collective-permute-done((bf16[8,16,128]{2,1,0:T(8,128)(2,1)S(1)}, bf16[8,16,128]{2,1,0:T(8,128)(2,1)S(1)}, u32[]{:S(2)}, u32[]{:S(2)}) %collective-permute-start.11) | collective-permute-done | bytes 32800 | tf_op jit(solution)/shard_map/ppermute | solution.py:278
  39.5 0.1 collective-permute-done.10.rest_0_
  39.6 1.3 %shard_map.100 = f32[48,1024]{1,0:T(8,128)} custom-call(f32[768,128]{1,0:T(8,128)S(1)} %shard_map.99.partial_ref, f32[768,128]{1,0:T(8,128)S(1)} %get-tuple-element.20.retain_ref, bf16[8,768,128]{2,1,0:T(8,128)(2,1)S(1)} %get-tuple-element.27.moved_ref, bf16[8,16,128]{2,1,0:T(8,128)(2,1)S(1)} %collective-permute-done.10.rest_0_, ...), custom_call_target="tpu_custom_call" | custom-call | flops 10000000000 | bytes 10000000 | tf_op jit(solution)/shard_map/pallas_call | solution.py:266
  (3 shorter events, 0.0 us)
Async XLA Ops:
  0.0 8.1 %copy-start.4 = (f32[48,1024]{1,0:T(8,128)S(1)}, f32[48,1024]{1,0:T(8,128)}, u32[]{:S(2)}) copy-start(f32[48,1024]{1,0:T(8,128)} %retention_ref.1) | copy-start | bytes 589828
  0.0 8.1 %copy-start.3 = (bf16[16,64,64]{2,1,0:T(8,128)(2,1)S(1)}, bf16[16,64,64]{2,1,0:T(8,128)(2,1)}, u32[]{:S(2)}) copy-start(bf16[16,64,64]{2,1,0:T(8,128)(2,1)} %inverse_ref.1) | copy-start | bytes 393220
  0.0 8.1 %copy-start.2 = (bf16[16,2,64,64]{3,2,1,0:T(8,128)(2,1)S(1)}, bf16[16,2,64,64]{3,2,1,0:T(8,128)(2,1)}, u32[]{:S(2)}) copy-start(bf16[16,2,64,64]{3,2,1,0:T(8,128)(2,1)} %remote_weight_ref.1) | copy-start | bytes 786436
  3.0 15.0 %collective-permute-start.3 = (bf16[2,384,128]{2,1,0:T(8,128)(2,1)}, bf16[2,384,128]{2,1,0:T(8,128)(2,1)S(1)}, u32[]{:S(2)}, u32[]{:S(2)}) collective-permute-start(bf16[2,384,128]{2,1,0:T(8,128)(2,1)} %shard_map.92.rest_0_), channel_id=1, source_target_pairs={{0,1},{1,0},{2,3},{3,2},{4,5},{5,4},{6,7},{7,6},{8,9},{9,8},{10,11... | collective-permute-start | bytes 589832 | tf_op jit(solution)/shard_map/ppermute | solution.py:278
  3.4 14.4 %collective-permute-start.2 = (bf16[2,384,128]{2,1,0:T(8,128)(2,1)}, bf16[2,384,128]{2,1,0:T(8,128)(2,1)S(1)}, u32[]{:S(2)}, u32[]{:S(2)}) collective-permute-start(bf16[2,384,128]{2,1,0:T(8,128)(2,1)} %shard_map.92.rest_0_), channel_id=1, source_target_pairs={{0,6},{1,7},{2,4},{3,5},{4,2},{5,3},{6,0},{7,1},{8,14},{9,15},{10,... | collective-permute-start | bytes 589832 | tf_op jit(solution)/shard_map/ppermute | solution.py:278
  6.9 10.4 %collective-permute-start.1 = (bf16[2,384,128]{2,1,0:T(8,128)(2,1)}, bf16[2,384,128]{2,1,0:T(8,128)(2,1)S(1)}, u32[]{:S(2)}, u32[]{:S(2)}) collective-permute-start(bf16[2,384,128]{2,1,0:T(8,128)(2,1)} %shard_map.92.rest_0_), channel_id=1, source_target_pairs={{0,4},{1,5},{2,6},{3,7},{4,0},{5,1},{6,2},{7,3},{8,12},{9,13},{10,... | collective-permute-start | bytes 589832 | tf_op jit(solution)/shard_map/ppermute | solution.py:278
  7.4 9.8 %collective-permute-start = (bf16[2,384,128]{2,1,0:T(8,128)(2,1)}, bf16[2,384,128]{2,1,0:T(8,128)(2,1)S(1)}, u32[]{:S(2)}, u32[]{:S(2)}) collective-permute-start(bf16[2,384,128]{2,1,0:T(8,128)(2,1)} %shard_map.92.rest_0_), channel_id=1, source_target_pairs={{0,2},{1,3},{2,0},{3,1},{4,6},{5,7},{6,4},{7,5},{8,10},{9,11},{10,... | collective-permute-start | bytes 589832 | tf_op jit(solution)/shard_map/ppermute | solution.py:278
  8.1 1.4 %copy-start = (bf16[48,16,1024]{2,1,0:T(8,128)(2,1)S(1)}, bf16[48,16,1024]{2,1,0:T(8,128)(2,1)}, u32[]{:S(2)}) copy-start(bf16[48,16,1024]{2,1,0:T(8,128)(2,1)} %z_ref.3) | copy-start | bytes 4718596
  9.5 1.2 %copy-start.1 = (bf16[16,4,64,64]{3,2,1,0:T(8,128)(2,1)S(1)}, bf16[16,4,64,64]{3,2,1,0:T(8,128)(2,1)}, u32[]{:S(2)}) copy-start(bf16[16,4,64,64]{3,2,1,0:T(8,128)(2,1)} %weight_ref.1) | copy-start | bytes 1572868
  10.8 0.7 %copy-start.6 = (s32[16,4]{0,1:T(4,128)S(1)}, s32[16,4]{0,1:T(4,128)}, u32[]{:S(2)}) copy-start(s32[16,4]{0,1:T(4,128)} %param.10) | copy-start | bytes 772
  11.4 7.9 %copy-start.5 = (bf16[2,384,128]{2,1,0:T(8,128)(2,1)S(1)}, bf16[2,384,128]{2,1,0:T(8,128)(2,1)}, u32[]{:S(2)}) copy-start(bf16[2,384,128]{2,1,0:T(8,128)(2,1)} %shard_map.92.rest_0_) | copy-start | bytes 589828
  11.4 7.9 %copy-start.7 = (s32[16,2]{0,1:T(2,128)S(1)}, s32[16,2]{0,1:T(2,128)}, u32[]{:S(2)}) copy-start(s32[16,2]{0,1:T(2,128)} %param.11) | copy-start | bytes 388
  17.2 1.5 %collective-permute-start.4 = (bf16[2,384,128]{2,1,0:T(8,128)(2,1)S(1)}, bf16[2,384,128]{2,1,0:T(8,128)(2,1)S(1)}, u32[]{:S(2)}, u32[]{:S(2)}) collective-permute-start(bf16[2,384,128]{2,1,0:T(8,128)(2,1)S(1)} %shard_map.93.rest_1_), channel_id=1, source_target_pairs={{0,1},{1,0},{2,3},{3,2},{4,5},{5,4},{6,7},{7,6},{8,9},{9,8},{10,11... | collective-permute-start | bytes 589832 | tf_op jit(solution)/shard_map/ppermute | solution.py:278
  17.3 1.7 %collective-permute-start.5 = (bf16[2,384,128]{2,1,0:T(8,128)(2,1)S(1)}, bf16[2,384,128]{2,1,0:T(8,128)(2,1)S(1)}, u32[]{:S(2)}, u32[]{:S(2)}) collective-permute-start(bf16[2,384,128]{2,1,0:T(8,128)(2,1)S(1)} %shard_map.94.rest_2_), channel_id=1, source_target_pairs={{0,1},{1,0},{2,3},{3,2},{4,5},{5,4},{6,7},{7,6},{8,9},{9,8},{10,11... | collective-permute-start | bytes 589832 | tf_op jit(solution)/shard_map/ppermute | solution.py:278
  17.9 1.5 %collective-permute-start.6 = (bf16[2,384,128]{2,1,0:T(8,128)(2,1)S(1)}, bf16[2,384,128]{2,1,0:T(8,128)(2,1)S(1)}, u32[]{:S(2)}, u32[]{:S(2)}) collective-permute-start(bf16[2,384,128]{2,1,0:T(8,128)(2,1)S(1)} %shard_map.95.rest_3_), channel_id=1, source_target_pairs={{0,1},{1,0},{2,3},{3,2},{4,5},{5,4},{6,7},{7,6},{8,9},{9,8},{10,11... | collective-permute-start | bytes 589832 | tf_op jit(solution)/shard_map/ppermute | solution.py:278
  22.5 6.3 %collective-permute-start.9 = (bf16[9,16,128]{2,1,0:T(8,128)(2,1)S(1)}, bf16[9,16,128]{2,1,0:T(8,128)(2,1)S(1)}, u32[]{:S(2)}, u32[]{:S(2)}) collective-permute-start(bf16[9,16,128]{2,1,0:T(8,128)(2,1)S(1)} %get-tuple-element.25), channel_id=1, source_target_pairs={{0,24},{8,16},{16,8},{24,0},{1,25},{9,17},{17,9},{25,1},{2,26},{10... | collective-permute-start | bytes 110600 | tf_op jit(solution)/shard_map/ppermute | solution.py:278
  26.2 4.9 %collective-permute-start.8 = (bf16[9,16,128]{2,1,0:T(8,128)(2,1)S(1)}, bf16[9,16,128]{2,1,0:T(8,128)(2,1)S(1)}, u32[]{:S(2)}, u32[]{:S(2)}) collective-permute-start(bf16[9,16,128]{2,1,0:T(8,128)(2,1)S(1)} %get-tuple-element.25), channel_id=1, source_target_pairs={{0,16},{8,24},{16,0},{24,8},{1,17},{9,25},{17,1},{25,9},{2,18},{10... | collective-permute-start | bytes 110600 | tf_op jit(solution)/shard_map/ppermute | solution.py:278
  26.2 4.9 %collective-permute-start.7 = (bf16[9,16,128]{2,1,0:T(8,128)(2,1)S(1)}, bf16[9,16,128]{2,1,0:T(8,128)(2,1)S(1)}, u32[]{:S(2)}, u32[]{:S(2)}) collective-permute-start(bf16[9,16,128]{2,1,0:T(8,128)(2,1)S(1)} %get-tuple-element.25), channel_id=1, source_target_pairs={{0,8},{8,0},{16,24},{24,16},{1,9},{9,1},{17,25},{25,17},{2,10},{10... | collective-permute-start | bytes 110600 | tf_op jit(solution)/shard_map/ppermute | solution.py:278
  32.9 6.0 %collective-permute-start.12 = (bf16[8,16,128]{2,1,0:T(8,128)(2,1)S(1)}, bf16[8,16,128]{2,1,0:T(8,128)(2,1)S(1)}, u32[]{:S(2)}, u32[]{:S(2)}) collective-permute-start(bf16[8,16,128]{2,1,0:T(8,128)(2,1)S(1)} %get-tuple-element.28), channel_id=1, source_target_pairs={{0,24},{8,16},{16,8},{24,0},{1,25},{9,17},{17,9},{25,1},{2,26},{10... | collective-permute-start | bytes 98312 | tf_op jit(solution)/shard_map/ppermute | solution.py:278
  34.7 4.9 %collective-permute-start.11 = (bf16[8,16,128]{2,1,0:T(8,128)(2,1)S(1)}, bf16[8,16,128]{2,1,0:T(8,128)(2,1)S(1)}, u32[]{:S(2)}, u32[]{:S(2)}) collective-permute-start(bf16[8,16,128]{2,1,0:T(8,128)(2,1)S(1)} %get-tuple-element.28), channel_id=1, source_target_pairs={{0,16},{8,24},{16,0},{24,8},{1,17},{9,25},{17,1},{25,9},{2,18},{10... | collective-permute-start | bytes 98312 | tf_op jit(solution)/shard_map/ppermute | solution.py:278
  35.1 4.5 %collective-permute-start.10 = (bf16[8,16,128]{2,1,0:T(8,128)(2,1)S(1)}, bf16[8,16,128]{2,1,0:T(8,128)(2,1)S(1)}, u32[]{:S(2)}, u32[]{:S(2)}) collective-permute-start(bf16[8,16,128]{2,1,0:T(8,128)(2,1)S(1)} %get-tuple-element.28), channel_id=1, source_target_pairs={{0,8},{8,0},{16,24},{24,16},{1,9},{9,1},{17,25},{25,17},{2,10},{10... | collective-permute-start | bytes 98312 | tf_op jit(solution)/shard_map/ppermute | solution.py:278

commit v10 on v9

--- a/solution.py
+++ b/solution.py
@@ -25,16 +25,6 @@
     return jnp.concatenate(
         [jnp.concatenate([weight, zero], axis=1), jnp.concatenate([zero, weight], axis=1)], axis=0
     )
-
-
-def paired(tiles):
-    return jnp.concatenate([jnp.concatenate(tiles[half::2], axis=0) for half in range(2)], axis=1)
-
-
-def unpaired(value, days):
-    return [
-        value[row : row + days, lane : lane + LANES] for row in range(0, value.shape[0], days) for lane in (0, LANES)
-    ]
 
 
 def outgoing_kernel(dims, shared_ref, z_ref, outgoing_ref):
@@ -46,26 +36,23 @@
     picks = [
         (column == row * blocks + shared_ref[0, m]).astype(jnp.float32).astype(jnp.bfloat16) for m in range(count)
     ]
-    picked = jnp.dot(jnp.concatenate(picks, axis=0), z, preferred_element_type=jnp.float32).astype(jnp.bfloat16)
+    picked = jnp.dot(jnp.concatenate(picks, axis=0), z, preferred_element_type=jnp.float32)
     step = 2 * LANES
-    for start in range(0, size * probes, step):
-        moved = jnp.dot(picked, permutation(size, probes, start, step), preferred_element_type=jnp.float32)
-        moved = moved.astype(jnp.bfloat16)
-        for half in range(2):
-            pair = start // LANES + half
-            for m in range(count):
-                outgoing_ref[m, pl.ds(pair * days, days), :] = moved[
-                    m * days : (m + 1) * days, half * LANES : (half + 1) * LANES
-                ]
-
-
-def local_kernel(
-    dims, links_ref, days_ref, z_ref, weight_ref, remote_weight_ref, inverse_ref, retention_ref,
-    running_ref, moved_ref, retain_ref, product_ref, remote_doubled_ref, inverse_fourfold_ref, stage, turned,
-):
+    shift = step // size
+    ranges = size * probes // step
+    shifted = [picked] + [pltpu.roll(picked, size * probes - i * shift, 1) for i in range(1, ranges)]
+    shifted = jnp.concatenate(shifted, axis=0).astype(jnp.bfloat16)
+    moved = jnp.dot(shifted, permutation(size, probes, 0, step), preferred_element_type=jnp.float32)
+    moved = moved.astype(jnp.bfloat16)
+    for pair in range(size * probes // LANES):
+        for m in range(count):
+            row, lane = (pair // 2 * count + m) * days, pair % 2 * LANES
+            outgoing_ref[m, pl.ds(pair * days, days), :] = moved[row : row + days, lane : lane + LANES]
+
+
+def turn_kernel(dims, z_ref, moved_ref, turned_ref, stage):
     days, blocks, size, probes = dims
     pairs = size * probes // LANES
-    count = links_ref.shape[0]
     z = z_ref[...].reshape(days * blocks, size * probes)
     step = 2 * LANES
     for start in range(0, size * probes, step):
@@ -78,16 +65,24 @@
     for block in range(blocks):
         for pair in range(pairs):
             rows = stage[pair, pl.ds(block, days, stride=blocks), :]
-            turned[block, pl.ds(pair * days, days), :] = rows.astype(jnp.bfloat16)
-    for block in range(blocks):
-        near = jnp.concatenate([turned[links_ref[k, block]] for k in range(count)], axis=1)
+            turned_ref[block, pl.ds(pair * days, days), :] = rows.astype(jnp.bfloat16)
+
+
+def local_kernel(
+    dims, links_ref, days_ref, turned_ref, weight_ref, remote_weight_ref, inverse_ref, retention_ref,
+    running_ref, retain_ref, product_ref, remote_doubled_ref, inverse_doubled_ref,
+):
+    days, blocks, size, probes = dims
+    count = links_ref.shape[0]
+    for block in range(blocks):
+        near = jnp.concatenate([turned_ref[links_ref[k, block]] for k in range(count)], axis=1)
         weight = jnp.concatenate([doubled(weight_ref[block, k]) for k in range(count)], axis=1)
         total = lax.dot_general(near, weight, TURNED, preferred_element_type=jnp.float32)
-        running_ref[block] = turned[block].astype(jnp.float32) - total
+        running_ref[block] = turned_ref[block].astype(jnp.float32) - total
         remote_doubled_ref[block] = jnp.concatenate(
             [doubled(remote_weight_ref[block, k]) for k in range(remote_weight_ref.shape[1])], axis=1
         )
-        inverse_fourfold_ref[block] = doubled(doubled(inverse_ref[block]))
+        inverse_doubled_ref[block] = doubled(inverse_ref[block])
     observed = days_ref[0]
     shape = (days, LANES)
     first = lax.broadcasted_iota(jnp.int32, shape, 1) < size
@@ -121,7 +116,8 @@
     held = pieces * bound
     me = lax.axis_index("space")
     for k, ref in enumerate(piece_refs):
-        remote[pl.ds(k * bound, bound)] = ref[...]
+        chip = (pieces - k) % pieces
+        remote[pl.ds(k // pieces * held + chip % pieces * bound, bound)] = ref[...]
     seen = lax.broadcasted_iota(jnp.int32, (days, LANES), 0) < days_ref[0]
     for block in range(blocks):
         places = []
@@ -133,12 +129,11 @@
         total = lax.dot_general(far, weight_ref[block], TURNED, preferred_element_type=jnp.float32)
         source[block] = (running_ref[block] - total).astype(jnp.bfloat16)
     for block in range(blocks):
-        drive = lax.dot_general(
-            paired([source[block, pl.ds(pair * days, days), :] for pair in range(pairs)]),
-            inverse_ref[block], TURNED, preferred_element_type=jnp.float32,
-        )
-        for pair, tile in enumerate(unpaired(drive, days)):
-            forcing_ref[pair, pl.ds(block, days, stride=blocks), :] = jnp.where(seen, tile, 0.0)
+        drive = lax.dot_general(source[block], inverse_ref[block], TURNED, preferred_element_type=jnp.float32)
+        for pair in range(pairs):
+            forcing_ref[pair, pl.ds(block, days, stride=blocks), :] = jnp.where(
+                seen, drive[pair * days : (pair + 1) * days], 0.0
+            )
     states = [jnp.zeros((blocks, LANES), jnp.float32)] * pairs
     for day in range(days):
         rows = pl.ds(day * blocks, blocks)
@@ -207,9 +202,11 @@
             .astype(jnp.bfloat16)
             for pair in range(pairs)
         ]
-        adjoint = jnp.dot(paired(stored), inverse_ref[block], preferred_element_type=jnp.float32)
-        for pair, tile in enumerate(unpaired(adjoint, days)):
-            adjoint_ref[pair, pl.ds(block, days, stride=blocks), :] = jnp.where(seen, tile, 0.0)
+        adjoint = jnp.dot(jnp.concatenate(stored, axis=0), inverse_ref[block], preferred_element_type=jnp.float32)
+        for pair in range(pairs):
+            adjoint_ref[pair, pl.ds(block, days, stride=blocks), :] = jnp.where(
+                seen, adjoint[pair * days : (pair + 1) * days], 0.0
+            )
     carries = [jnp.zeros((blocks, LANES), jnp.float32)] * pairs
     for day in reversed(range(days)):
         rows = pl.ds(day * blocks, blocks)
@@ -308,24 +305,29 @@
         [], 10**9, 4 * 10**6, 1, shared_blocks, probes, limit=63 * 1024 * 1024,
     )
     pieces = {bits: crossed(outgoing, "space", bits) for bits in range(groups - 2, 0, -2)}
-    running, moved, retain, product, remote_weight, inverse = call(
+    by_block = (blocks, pairs * days, LANES)
+    moved, turned = call(
+        functools.partial(turn_kernel, dims),
+        [((pairs, rows, LANES), bf16), (by_block, bf16)],
+        [pltpu.VMEM(*big)], 10**10, 10**7, 0, probes,
+    )
+    running, retain, product, remote_weight, inverse = call(
         functools.partial(local_kernel, dims),
         [
-            ((blocks, pairs * days, LANES), f32),
-            ((pairs, rows, LANES), bf16),
+            (by_block, f32),
             ((rows, LANES), f32),
             ((blocks, LANES), bf16),
             ((blocks, LANES, far * LANES), bf16),
-            ((blocks, 2 * LANES, 2 * LANES), bf16),
+            ((blocks, LANES, LANES), bf16),
         ],
-        [pltpu.VMEM(*big), pltpu.VMEM((blocks, pairs * days, LANES), bf16)],
-        10**10, 10**7, 2,
-        near_table, slab_days, probes, local_coupling, remote_coupling, block_inverse, retention,
-    )
-    same = [outgoing]
-    for bits in range(2, groups, 2):
-        same += call(pass_kernel, [(outgoing.shape, bf16)], [], 0, 10**5, 0, pieces[bits], product)
-    other = [crossed(piece, "space", 1) for piece in same]
+        [], 10**10, 10**7, 2,
+        near_table, slab_days, turned, local_coupling, remote_coupling, block_inverse, retention,
+    )
+    same, other = {0: outgoing}, {0: crossed(outgoing, "space", 1)}
+    for bits in range(groups - 2, 0, -2):
+        (same[bits],) = call(pass_kernel, [(outgoing.shape, bf16)], [], 0, 10**5, 0, pieces[bits], product)
+        other[bits] = crossed(same[bits], "space", 1)
+    same, other = list(same.values()), list(other.values())
     slabs = lax.axis_size("tm")
     hops = slabs - 1
     exchange = lambda message: [crossed(message, "tm", bits) for bits in range(hops, 0, -1)][::-1]
@@ -338,7 +340,6 @@
         far_table, slab_days, running, remote_weight, inverse, retain, product, *same, *other,
     )
     ends = exchange(message)
-    by_block = (blocks, pairs * days, LANES)
     states, through = call(
         functools.partial(states_kernel, dims),
         [(by_block, f32), ((blocks, days, LANES), f32)],

time: 41.2 us -> 40.9 us (level)
  local copies, waits for them, and re-layouts: 3.33 us -> 1.44 us
  waiting for transfers between devices: 6.09 us -> 7.58 us
    unnamed x16, local copies, waits for them, and re-layouts: 3.33 us -> 1.44 us
    ppermute x13, waiting for transfers between devices: 6.09 us -> 7.58 us  [crossed(): lax.ppermute(block, axis, [(i, i ^ bits) for i in range(lax.axis_size(axi...]
    pallas_call x10 -> x11, Pallas kernels: 16.7 us -> 16.8 us  [call(): pl.pallas_call(kernel, out_shape=[jax.ShapeDtypeStruct(shape, kind) for s...]
  transfers between devices with their start and end apart: 13 -> 13, of which waited for: 8 -> 9; matrix products, arithmetic and copies ran while one was open for 0% -> 0% of each run, Pallas kernels for 18% -> 19%
where the time goes in v10:
time: 40.9 us; the launch traced here: 40.7 us
  Pallas kernels  16.8 us (41%)
  starting transfers between devices  14.1 us (34%)
  waiting for transfers between devices  7.58 us (19%)
  local copies, waits for them, and re-layouts  1.44 us (4%)
  between operations  0.78 us (2%)
    pallas_call x11, Pallas kernels, call(): pl.pallas_call(kernel, out_shape=[jax.ShapeDtypeStruct(shape, kind) for s...  16.8 us
    ppermute x13, starting transfers between devices, crossed(): lax.ppermute(block, axis, [(i, i ^ bits) for i in range(lax.axis_size(axi...  14.1 us
    ppermute x13, waiting for transfers between devices, crossed(): lax.ppermute(block, axis, [(i, i ^ bits) for i in range(lax.axis_size(axi...  7.58 us
    unnamed x16, local copies, waits for them, and re-layouts  1.44 us
  transfers between devices with their start and end apart: 13, of which 9 were waited for; matrix products, arithmetic and copies ran while one was open for 0% of the time, Pallas kernels for 19%

profile of v10, /device:TPU:0, one launch (start us, length us, event | category | flops | bytes accessed | tf_op | source)
XLA Modules:
  0.0 40.7 jit_solution(4153803627916149612)
XLA Ops:
  0.0 0.0 copy-start.2
  0.0 0.0 copy-start.3
  0.0 0.0 copy-start.4
  0.0 2.9 %shard_map.93.rest_0_ = bf16[2,384,128]{2,1,0:T(8,128)(2,1)} custom-call(s32[1,2]{1,0:T(1,128)} %shared_ref.1, bf16[48,16,1024]{2,1,0:T(8,128)(2,1)} %z_ref.3), custom_call_target="tpu_custom_call" | custom-call | flops 1000000000 | bytes 4000000 | tf_op jit(solution)/shard_map/pallas_call | solution.py:263
  2.9 0.5 %collective-permute-start.3 = (bf16[2,384,128]{2,1,0:T(8,128)(2,1)}, bf16[2,384,128]{2,1,0:T(8,128)(2,1)S(1)}, u32[]{:S(2)}, u32[]{:S(2)}) collective-permute-start(bf16[2,384,128]{2,1,0:T(8,128)(2,1)} %shard_map.93.rest_0_), channel_id=1, source_target_pairs={{0,1},{1,0},{2,3},{3,2},{4,5},{5,4},{6,7},{7,6},{8,9},{9,8},{10,11... | collective-permute-start | bytes 589832 | tf_op jit(solution)/shard_map/ppermute | solution.py:275
  3.4 2.5 %collective-permute-start.2 = (bf16[2,384,128]{2,1,0:T(8,128)(2,1)}, bf16[2,384,128]{2,1,0:T(8,128)(2,1)S(1)}, u32[]{:S(2)}, u32[]{:S(2)}) collective-permute-start(bf16[2,384,128]{2,1,0:T(8,128)(2,1)} %shard_map.93.rest_0_), channel_id=1, source_target_pairs={{0,2},{1,3},{2,0},{3,1},{4,6},{5,7},{6,4},{7,5},{8,10},{9,11},{10,... | collective-permute-start | bytes 589832 | tf_op jit(solution)/shard_map/ppermute | solution.py:275
  5.9 1.5 %collective-permute-start.1 = (bf16[2,384,128]{2,1,0:T(8,128)(2,1)}, bf16[2,384,128]{2,1,0:T(8,128)(2,1)S(1)}, u32[]{:S(2)}, u32[]{:S(2)}) collective-permute-start(bf16[2,384,128]{2,1,0:T(8,128)(2,1)} %shard_map.93.rest_0_), channel_id=1, source_target_pairs={{0,4},{1,5},{2,6},{3,7},{4,0},{5,1},{6,2},{7,3},{8,12},{9,13},{10,... | collective-permute-start | bytes 589832 | tf_op jit(solution)/shard_map/ppermute | solution.py:275
  7.4 0.0 collective-permute-start
  7.4 0.0 copy-start
  7.4 1.4 %copy-done = bf16[48,16,1024]{2,1,0:T(8,128)(2,1)S(1)} copy-done((bf16[48,16,1024]{2,1,0:T(8,128)(2,1)S(1)}, bf16[48,16,1024]{2,1,0:T(8,128)(2,1)}, u32[]{:S(2)}) %copy-start) | copy-done | bytes 1572888
  8.8 0.0 copy-start.1
  8.8 0.0 copy-start.6
  8.8 2.9 %shard_map.91 = (bf16[8,768,128]{2,1,0:T(8,128)(2,1)S(1)}, bf16[16,384,128]{2,1,0:T(8,128)(2,1)S(1)}) custom-call(bf16[48,16,1024]{2,1,0:T(8,128)(2,1)S(1)} %copy-done), custom_call_target="tpu_custom_call" | custom-call | flops 10000000000 | bytes 10000000 | tf_op jit(solution)/shard_map/pallas_call | solution.py:263
  12.4 0.0 copy-done.2
  12.4 0.0 copy-done.3
  12.4 0.0 copy-done.4
  12.4 0.0 copy-done.1
  12.4 0.0 copy-done.6
  12.4 0.0 copy-start.5
  12.5 0.0 copy-start.7
  12.5 2.5 %shard_map.92 = (f32[16,384,128]{2,1,0:T(8,128)S(1)}, f32[768,128]{1,0:T(8,128)S(1)}, bf16[16,128]{1,0:T(8,128)(2,1)S(1)}, bf16[16,128,256]{2,1,0:T(8,128)(2,1)S(1)}, bf16[16,128,128]{2,1,0:T(8,128)(2,1)S(1)}) custom-call(s32[4,16]{1,0:T(4,128)S(1)} %bitcast.2, s32[1]{0:T(128)S(6)} %copy.10.days_ref, bf16[16,384,128]{2,1,0:T(8,128)(2,1)S(1)} %get-tuple-element.18.turned_ref, ...), custom_call_target="tpu_custom_call" | custom-call | flops 10000000000 | bytes 10000000 | tf_op jit(solution)/shard_map/pallas_call | solution.py:263
  15.0 2.2 %collective-permute-done.piece_ref = bf16[2,384,128]{2,1,0:T(8,128)(2,1)S(1)} collective-permute-done((bf16[2,384,128]{2,1,0:T(8,128)(2,1)}, bf16[2,384,128]{2,1,0:T(8,128)(2,1)S(1)}, u32[]{:S(2)}, u32[]{:S(2)}) %collective-permute-start) | collective-permute-done | bytes 196640 | tf_op jit(solution)/shard_map/ppermute | solution.py:275
  17.2 0.1 collective-permute-start.4
  17.3 0.1 collective-permute-done.1.piece_ref
  17.4 0.5 %collective-permute-start.5 = (bf16[2,384,128]{2,1,0:T(8,128)(2,1)S(1)}, bf16[2,384,128]{2,1,0:T(8,128)(2,1)S(1)}, u32[]{:S(2)}, u32[]{:S(2)}) collective-permute-start(bf16[2,384,128]{2,1,0:T(8,128)(2,1)S(1)} %shard_map.95.rest_2_), channel_id=1, source_target_pairs={{0,1},{1,0},{2,3},{3,2},{4,5},{5,4},{6,7},{7,6},{8,9},{9,8},{10,11... | collective-permute-start | bytes 589832 | tf_op jit(solution)/shard_map/ppermute | solution.py:275
  17.9 0.0 collective-permute-done.2.piece_ref
  17.9 0.1 collective-permute-start.6
  18.0 0.0 collective-permute-done.3.rest_4_
  18.0 0.7 %collective-permute-done.4.rest_5_ = bf16[2,384,128]{2,1,0:T(8,128)(2,1)S(1)} collective-permute-done((bf16[2,384,128]{2,1,0:T(8,128)(2,1)S(1)}, bf16[2,384,128]{2,1,0:T(8,128)(2,1)S(1)}, u32[]{:S(2)}, u32[]{:S(2)}) %collective-permute-start.4) | collective-permute-done | bytes 196640 | tf_op jit(solution)/shard_map/ppermute | solution.py:275
  18.7 0.3 collective-permute-done.5.rest_6_
  19.0 0.4 collective-permute-done.6.rest_7_
  19.4 0.0 copy-done.5
  19.4 0.0 copy-done.7
  19.4 3.0 %shard_map.97 = (f32[8,768,128]{2,1,0:T(8,128)S(1)}, bf16[9,16,128]{2,1,0:T(8,128)(2,1)S(1)}) custom-call(s32[2,16]{1,0:T(2,128)S(1)} %bitcast.3, s32[1]{0:T(128)S(6)} %copy.10.days_ref, f32[16,384,128]{2,1,0:T(8,128)S(1)} %get-tuple-element.19.running_ref, bf16[16,128,256]{2,1,0:T(8,128)(2,1)S(1)} %get-tuple-element.20.weight_ref, ...), custom_call_target="tpu_custom_call" | custom-call | flops 10000000000 | bytes 10000000 | tf_op jit(solution)/shard_map/pallas_call | solution.py:263
  22.4 3.7 %collective-permute-start.9 = (bf16[9,16,128]{2,1,0:T(8,128)(2,1)S(1)}, bf16[9,16,128]{2,1,0:T(8,128)(2,1)S(1)}, u32[]{:S(2)}, u32[]{:S(2)}) collective-permute-start(bf16[9,16,128]{2,1,0:T(8,128)(2,1)S(1)} %get-tuple-element.27), channel_id=1, source_target_pairs={{0,24},{8,16},{16,8},{24,0},{1,25},{9,17},{17,9},{25,1},{2,26},{10... | collective-permute-start | bytes 110600 | tf_op jit(solution)/shard_map/ppermute | solution.py:275
  26.1 0.0 collective-permute-start.8
  26.1 0.8 %collective-permute-start.7 = (bf16[9,16,128]{2,1,0:T(8,128)(2,1)S(1)}, bf16[9,16,128]{2,1,0:T(8,128)(2,1)S(1)}, u32[]{:S(2)}, u32[]{:S(2)}) collective-permute-start(bf16[9,16,128]{2,1,0:T(8,128)(2,1)S(1)} %get-tuple-element.27), channel_id=1, source_target_pairs={{0,8},{8,0},{16,24},{24,16},{1,9},{9,1},{17,25},{25,17},{2,10},{10... | collective-permute-start | bytes 110600 | tf_op jit(solution)/shard_map/ppermute | solution.py:275
  26.9 1.9 %shard_map.98 = (f32[16,384,128]{2,1,0:T(8,128)S(1)}, f32[16,48,128]{2,1,0:T(8,128)S(1)}) custom-call(f32[8,768,128]{2,1,0:T(8,128)S(1)} %get-tuple-element.24.forcing_ref, f32[768,128]{1,0:T(8,128)S(1)} %get-tuple-element.22.retain_ref), custom_call_target="tpu_custom_call" | custom-call | flops 1000000000 | bytes 1000000 | tf_op jit(solution)/shard_map/pallas_call | solution.py:263
  28.8 0.0 collective-permute-done.9.rest_2_.rest_5_
  28.8 2.2 %collective-permute-done.8.rest_1_.rest_4_ = bf16[9,16,128]{2,1,0:T(8,128)(2,1)S(1)} collective-permute-done((bf16[9,16,128]{2,1,0:T(8,128)(2,1)S(1)}, bf16[9,16,128]{2,1,0:T(8,128)(2,1)S(1)}, u32[]{:S(2)}, u32[]{:S(2)}) %collective-permute-start.8) | collective-permute-done | bytes 36896 | tf_op jit(solution)/shard_map/ppermute | solution.py:275
  30.9 0.0 collective-permute-done.7.rest_0_.rest_3_
  30.9 1.7 %shard_map.99 = (f32[8,768,128]{2,1,0:T(8,128)S(1)}, bf16[8,16,128]{2,1,0:T(8,128)(2,1)S(1)}) custom-call(s32[1]{0:T(128)S(6)} %copy.10.days_ref, f32[16,384,128]{2,1,0:T(8,128)S(1)} %get-tuple-element.25.states_ref, f32[16,48,128]{2,1,0:T(8,128)S(1)} %get-tuple-element.26.through_ref, f32[768,128]{1,0:T(8,128)S(1)} %get-tuple-element.22.retain_ref, ...), custom_call_target="tpu_custom_call" | custom-call | flops 10000000000 | bytes 10000000 | tf_op jit(solution)/shard_map/pallas_call | solution.py:263
  32.6 1.8 %collective-permute-start.12 = (bf16[8,16,128]{2,1,0:T(8,128)(2,1)S(1)}, bf16[8,16,128]{2,1,0:T(8,128)(2,1)S(1)}, u32[]{:S(2)}, u32[]{:S(2)}) collective-permute-start(bf16[8,16,128]{2,1,0:T(8,128)(2,1)S(1)} %get-tuple-element.30), channel_id=1, source_target_pairs={{0,24},{8,16},{16,8},{24,0},{1,25},{9,17},{17,9},{25,1},{2,26},{10... | collective-permute-start | bytes 98312 | tf_op jit(solution)/shard_map/ppermute | solution.py:275
  34.4 0.4 collective-permute-start.11
  34.8 2.3 %collective-permute-start.10 = (bf16[8,16,128]{2,1,0:T(8,128)(2,1)S(1)}, bf16[8,16,128]{2,1,0:T(8,128)(2,1)S(1)}, u32[]{:S(2)}, u32[]{:S(2)}) collective-permute-start(bf16[8,16,128]{2,1,0:T(8,128)(2,1)S(1)} %get-tuple-element.30), channel_id=1, source_target_pairs={{0,8},{8,0},{16,24},{24,16},{1,9},{9,1},{17,25},{25,17},{2,10},{10... | collective-permute-start | bytes 98312 | tf_op jit(solution)/shard_map/ppermute | solution.py:275
  37.1 0.5 %shard_map.100.partial_ref = f32[768,128]{1,0:T(8,128)S(1)} custom-call(f32[8,768,128]{2,1,0:T(8,128)S(1)} %get-tuple-element.28.adjoint_ref, f32[768,128]{1,0:T(8,128)S(1)} %get-tuple-element.22.retain_ref, bf16[8,768,128]{2,1,0:T(8,128)(2,1)S(1)} %get-tuple-element.29.moved_ref), custom_call_target="tpu_custom_call" | custom-call | flops 1000000000 | bytes 1000000 | tf_op jit(solution)/shard_map/pallas_call | solution.py:263
  37.6 1.0 %collective-permute-done.12.rest_2_ = bf16[8,16,128]{2,1,0:T(8,128)(2,1)S(1)} collective-permute-done((bf16[8,16,128]{2,1,0:T(8,128)(2,1)S(1)}, bf16[8,16,128]{2,1,0:T(8,128)(2,1)S(1)}, u32[]{:S(2)}, u32[]{:S(2)}) %collective-permute-start.12) | collective-permute-done | bytes 32800 | tf_op jit(solution)/shard_map/ppermute | solution.py:275
  38.6 0.7 %collective-permute-done.11.rest_1_ = bf16[8,16,128]{2,1,0:T(8,128)(2,1)S(1)} collective-permute-done((bf16[8,16,128]{2,1,0:T(8,128)(2,1)S(1)}, bf16[8,16,128]{2,1,0:T(8,128)(2,1)S(1)}, u32[]{:S(2)}, u32[]{:S(2)}) %collective-permute-start.11) | collective-permute-done | bytes 32800 | tf_op jit(solution)/shard_map/ppermute | solution.py:275
  39.3 0.1 collective-permute-done.10.rest_0_
  39.3 1.3 %shard_map.101 = f32[48,1024]{1,0:T(8,128)} custom-call(f32[768,128]{1,0:T(8,128)S(1)} %shard_map.100.partial_ref, f32[768,128]{1,0:T(8,128)S(1)} %get-tuple-element.22.retain_ref, bf16[8,768,128]{2,1,0:T(8,128)(2,1)S(1)} %get-tuple-element.29.moved_ref, bf16[8,16,128]{2,1,0:T(8,128)(2,1)S(1)} %collective-permute-done.10.rest_0_, ...), custom_call_target="tpu_custom_call" | custom-call | flops 10000000000 | bytes 10000000 | tf_op jit(solution)/shard_map/pallas_call | solution.py:263
  (3 shorter events, 0.0 us)
Async XLA Ops:
  0.0 12.4 %copy-start.2 = (bf16[16,2,64,64]{3,2,1,0:T(8,128)(2,1)S(1)}, bf16[16,2,64,64]{3,2,1,0:T(8,128)(2,1)}, u32[]{:S(2)}) copy-start(bf16[16,2,64,64]{3,2,1,0:T(8,128)(2,1)} %remote_weight_ref.1) | copy-start | bytes 786436
  0.0 12.4 %copy-start.3 = (bf16[16,64,64]{2,1,0:T(8,128)(2,1)S(1)}, bf16[16,64,64]{2,1,0:T(8,128)(2,1)}, u32[]{:S(2)}) copy-start(bf16[16,64,64]{2,1,0:T(8,128)(2,1)} %inverse_ref.1) | copy-start | bytes 393220
  0.0 12.4 %copy-start.4 = (f32[48,1024]{1,0:T(8,128)S(1)}, f32[48,1024]{1,0:T(8,128)}, u32[]{:S(2)}) copy-start(f32[48,1024]{1,0:T(8,128)} %retention_ref.1) | copy-start | bytes 589828
  2.9 15.1 %collective-permute-start.3 = (bf16[2,384,128]{2,1,0:T(8,128)(2,1)}, bf16[2,384,128]{2,1,0:T(8,128)(2,1)S(1)}, u32[]{:S(2)}, u32[]{:S(2)}) collective-permute-start(bf16[2,384,128]{2,1,0:T(8,128)(2,1)} %shard_map.93.rest_0_), channel_id=1, source_target_pairs={{0,1},{1,0},{2,3},{3,2},{4,5},{5,4},{6,7},{7,6},{8,9},{9,8},{10,11... | collective-permute-start | bytes 589832 | tf_op jit(solution)/shard_map/ppermute | solution.py:275
  3.4 14.5 %collective-permute-start.2 = (bf16[2,384,128]{2,1,0:T(8,128)(2,1)}, bf16[2,384,128]{2,1,0:T(8,128)(2,1)S(1)}, u32[]{:S(2)}, u32[]{:S(2)}) collective-permute-start(bf16[2,384,128]{2,1,0:T(8,128)(2,1)} %shard_map.93.rest_0_), channel_id=1, source_target_pairs={{0,2},{1,3},{2,0},{3,1},{4,6},{5,7},{6,4},{7,5},{8,10},{9,11},{10,... | collective-permute-start | bytes 589832 | tf_op jit(solution)/shard_map/ppermute | solution.py:275
  5.9 11.5 %collective-permute-start.1 = (bf16[2,384,128]{2,1,0:T(8,128)(2,1)}, bf16[2,384,128]{2,1,0:T(8,128)(2,1)S(1)}, u32[]{:S(2)}, u32[]{:S(2)}) collective-permute-start(bf16[2,384,128]{2,1,0:T(8,128)(2,1)} %shard_map.93.rest_0_), channel_id=1, source_target_pairs={{0,4},{1,5},{2,6},{3,7},{4,0},{5,1},{6,2},{7,3},{8,12},{9,13},{10,... | collective-permute-start | bytes 589832 | tf_op jit(solution)/shard_map/ppermute | solution.py:275
  7.4 9.8 %collective-permute-start = (bf16[2,384,128]{2,1,0:T(8,128)(2,1)}, bf16[2,384,128]{2,1,0:T(8,128)(2,1)S(1)}, u32[]{:S(2)}, u32[]{:S(2)}) collective-permute-start(bf16[2,384,128]{2,1,0:T(8,128)(2,1)} %shard_map.93.rest_0_), channel_id=1, source_target_pairs={{0,6},{1,7},{2,4},{3,5},{4,2},{5,3},{6,0},{7,1},{8,14},{9,15},{10,... | collective-permute-start | bytes 589832 | tf_op jit(solution)/shard_map/ppermute | solution.py:275
  7.4 1.4 %copy-start = (bf16[48,16,1024]{2,1,0:T(8,128)(2,1)S(1)}, bf16[48,16,1024]{2,1,0:T(8,128)(2,1)}, u32[]{:S(2)}) copy-start(bf16[48,16,1024]{2,1,0:T(8,128)(2,1)} %z_ref.3) | copy-start | bytes 4718596
  8.8 3.6 %copy-start.1 = (bf16[16,4,64,64]{3,2,1,0:T(8,128)(2,1)S(1)}, bf16[16,4,64,64]{3,2,1,0:T(8,128)(2,1)}, u32[]{:S(2)}) copy-start(bf16[16,4,64,64]{3,2,1,0:T(8,128)(2,1)} %weight_ref.1) | copy-start | bytes 1572868
  8.8 3.6 %copy-start.6 = (s32[16,4]{0,1:T(4,128)S(1)}, s32[16,4]{0,1:T(4,128)}, u32[]{:S(2)}) copy-start(s32[16,4]{0,1:T(4,128)} %param.10) | copy-start | bytes 772
  12.4 7.0 %copy-start.5 = (bf16[2,384,128]{2,1,0:T(8,128)(2,1)S(1)}, bf16[2,384,128]{2,1,0:T(8,128)(2,1)}, u32[]{:S(2)}) copy-start(bf16[2,384,128]{2,1,0:T(8,128)(2,1)} %shard_map.93.rest_0_) | copy-start | bytes 589828
  12.5 7.0 %copy-start.7 = (s32[16,2]{0,1:T(2,128)S(1)}, s32[16,2]{0,1:T(2,128)}, u32[]{:S(2)}) copy-start(s32[16,2]{0,1:T(2,128)} %param.11) | copy-start | bytes 388
  17.2 1.5 %collective-permute-start.4 = (bf16[2,384,128]{2,1,0:T(8,128)(2,1)S(1)}, bf16[2,384,128]{2,1,0:T(8,128)(2,1)S(1)}, u32[]{:S(2)}, u32[]{:S(2)}) collective-permute-start(bf16[2,384,128]{2,1,0:T(8,128)(2,1)S(1)} %shard_map.94.rest_1_), channel_id=1, source_target_pairs={{0,1},{1,0},{2,3},{3,2},{4,5},{5,4},{6,7},{7,6},{8,9},{9,8},{10,11... | collective-permute-start | bytes 589832 | tf_op jit(solution)/shard_map/ppermute | solution.py:275
  17.4 1.6 %collective-permute-start.5 = (bf16[2,384,128]{2,1,0:T(8,128)(2,1)S(1)}, bf16[2,384,128]{2,1,0:T(8,128)(2,1)S(1)}, u32[]{:S(2)}, u32[]{:S(2)}) collective-permute-start(bf16[2,384,128]{2,1,0:T(8,128)(2,1)S(1)} %shard_map.95.rest_2_), channel_id=1, source_target_pairs={{0,1},{1,0},{2,3},{3,2},{4,5},{5,4},{6,7},{7,6},{8,9},{9,8},{10,11... | collective-permute-start | bytes 589832 | tf_op jit(solution)/shard_map/ppermute | solution.py:275
  17.9 1.5 %collective-permute-start.6 = (bf16[2,384,128]{2,1,0:T(8,128)(2,1)S(1)}, bf16[2,384,128]{2,1,0:T(8,128)(2,1)S(1)}, u32[]{:S(2)}, u32[]{:S(2)}) collective-permute-start(bf16[2,384,128]{2,1,0:T(8,128)(2,1)S(1)} %shard_map.96.rest_3_), channel_id=1, source_target_pairs={{0,1},{1,0},{2,3},{3,2},{4,5},{5,4},{6,7},{7,6},{8,9},{9,8},{10,11... | collective-permute-start | bytes 589832 | tf_op jit(solution)/shard_map/ppermute | solution.py:275
  22.4 6.3 %collective-permute-start.9 = (bf16[9,16,128]{2,1,0:T(8,128)(2,1)S(1)}, bf16[9,16,128]{2,1,0:T(8,128)(2,1)S(1)}, u32[]{:S(2)}, u32[]{:S(2)}) collective-permute-start(bf16[9,16,128]{2,1,0:T(8,128)(2,1)S(1)} %get-tuple-element.27), channel_id=1, source_target_pairs={{0,24},{8,16},{16,8},{24,0},{1,25},{9,17},{17,9},{25,1},{2,26},{10... | collective-permute-start | bytes 110600 | tf_op jit(solution)/shard_map/ppermute | solution.py:275
  26.1 4.9 %collective-permute-start.8 = (bf16[9,16,128]{2,1,0:T(8,128)(2,1)S(1)}, bf16[9,16,128]{2,1,0:T(8,128)(2,1)S(1)}, u32[]{:S(2)}, u32[]{:S(2)}) collective-permute-start(bf16[9,16,128]{2,1,0:T(8,128)(2,1)S(1)} %get-tuple-element.27), channel_id=1, source_target_pairs={{0,16},{8,24},{16,0},{24,8},{1,17},{9,25},{17,1},{25,9},{2,18},{10... | collective-permute-start | bytes 110600 | tf_op jit(solution)/shard_map/ppermute | solution.py:275
  26.1 4.9 %collective-permute-start.7 = (bf16[9,16,128]{2,1,0:T(8,128)(2,1)S(1)}, bf16[9,16,128]{2,1,0:T(8,128)(2,1)S(1)}, u32[]{:S(2)}, u32[]{:S(2)}) collective-permute-start(bf16[9,16,128]{2,1,0:T(8,128)(2,1)S(1)} %get-tuple-element.27), channel_id=1, source_target_pairs={{0,8},{8,0},{16,24},{24,16},{1,9},{9,1},{17,25},{25,17},{2,10},{10... | collective-permute-start | bytes 110600 | tf_op jit(solution)/shard_map/ppermute | solution.py:275
  32.6 6.0 %collective-permute-start.12 = (bf16[8,16,128]{2,1,0:T(8,128)(2,1)S(1)}, bf16[8,16,128]{2,1,0:T(8,128)(2,1)S(1)}, u32[]{:S(2)}, u32[]{:S(2)}) collective-permute-start(bf16[8,16,128]{2,1,0:T(8,128)(2,1)S(1)} %get-tuple-element.30), channel_id=1, source_target_pairs={{0,24},{8,16},{16,8},{24,0},{1,25},{9,17},{17,9},{25,1},{2,26},{10... | collective-permute-start | bytes 98312 | tf_op jit(solution)/shard_map/ppermute | solution.py:275
  34.4 4.9 %collective-permute-start.11 = (bf16[8,16,128]{2,1,0:T(8,128)(2,1)S(1)}, bf16[8,16,128]{2,1,0:T(8,128)(2,1)S(1)}, u32[]{:S(2)}, u32[]{:S(2)}) collective-permute-start(bf16[8,16,128]{2,1,0:T(8,128)(2,1)S(1)} %get-tuple-element.30), channel_id=1, source_target_pairs={{0,16},{8,24},{16,0},{24,8},{1,17},{9,25},{17,1},{25,9},{2,18},{10... | collective-permute-start | bytes 98312 | tf_op jit(solution)/shard_map/ppermute | solution.py:275
  34.8 4.5 %collective-permute-start.10 = (bf16[8,16,128]{2,1,0:T(8,128)(2,1)S(1)}, bf16[8,16,128]{2,1,0:T(8,128)(2,1)S(1)}, u32[]{:S(2)}, u32[]{:S(2)}) collective-permute-start(bf16[8,16,128]{2,1,0:T(8,128)(2,1)S(1)} %get-tuple-element.30), channel_id=1, source_target_pairs={{0,8},{8,0},{16,24},{24,16},{1,9},{9,1},{17,25},{25,17},{2,10},{10... | collective-permute-start | bytes 98312 | tf_op jit(solution)/shard_map/ppermute | solution.py:275

commit v11 on v10

--- a/solution.py
+++ b/solution.py
@@ -108,8 +108,8 @@
     dims, pieces, links_ref, days_ref, running_ref, weight_ref, inverse_ref, retain_ref, product_ref, *rest
 ):
     days, blocks, size, probes = dims
-    piece_refs = rest[: 2 * pieces]
-    forcing_ref, message_ref, remote, source = rest[2 * pieces :]
+    piece_refs = rest[pieces - 1 : 3 * pieces - 1]
+    forcing_ref, message_ref, remote, source = rest[3 * pieces - 1 :]
     pairs = forcing_ref.shape[0]
     count = links_ref.shape[0]
     bound = piece_refs[0].shape[0]
@@ -328,6 +328,7 @@
         (same[bits],) = call(pass_kernel, [(outgoing.shape, bf16)], [], 0, 10**5, 0, pieces[bits], product)
         other[bits] = crossed(same[bits], "space", 1)
     same, other = list(same.values()), list(other.values())
+    raw = [pieces[bits] for bits in range(2, groups, 2)]
     slabs = lax.axis_size("tm")
     hops = slabs - 1
     exchange = lambda message: [crossed(message, "tm", bits) for bits in range(hops, 0, -1)][::-1]
@@ -337,7 +338,8 @@
         [big, ((pairs + 1, blocks, LANES), bf16)],
         [pltpu.VMEM((2 * held, pairs * days, LANES), bf16), pltpu.VMEM((blocks, pairs * days, LANES), bf16)],
         10**10, 10**7, 2,
-        far_table, slab_days, running, remote_weight, inverse, retain, product, *same, *other,
+        far_table, slab_days, running, remote_weight, inverse, retain, product, *raw, *same, *other,
+        apart=range(7, 7 + len(raw)),
     )
     ends = exchange(message)
     states, through = call(

time: 40.9 us -> 40.4 us (0.988)
  waiting for transfers between devices: 7.58 us -> 7.14 us
    ppermute x13, waiting for transfers between devices: 7.58 us -> 7.14 us  [crossed(): lax.ppermute(block, axis, [(i, i ^ bits) for i in range(lax.axis_size(axi...]
  transfers between devices with their start and end apart: 13 -> 13, of which waited for: 9 -> 8; matrix products, arithmetic and copies ran while one was open for 0% -> 0% of each run, Pallas kernels for 19% -> 20%
where the time goes in v11:
time: 40.4 us; the launch traced here: 40.2 us
  Pallas kernels  16.9 us (42%)
  starting transfers between devices  14 us (35%)
  waiting for transfers between devices  7.14 us (18%)
  local copies, waits for them, and re-layouts  1.44 us (4%)
  between operations  0.8 us (2%)
    pallas_call x11, Pallas kernels, call(): pl.pallas_call(kernel, out_shape=[jax.ShapeDtypeStruct(shape, kind) for s...  16.9 us
    ppermute x13, starting transfers between devices, crossed(): lax.ppermute(block, axis, [(i, i ^ bits) for i in range(lax.axis_size(axi...  14 us
    ppermute x13, waiting for transfers between devices, crossed(): lax.ppermute(block, axis, [(i, i ^ bits) for i in range(lax.axis_size(axi...  7.14 us
    unnamed x16, local copies, waits for them, and re-layouts  1.44 us
  transfers between devices with their start and end apart: 13, of which 8 were waited for; matrix products, arithmetic and copies ran while one was open for 0% of the time, Pallas kernels for 20%

profile of v11, /device:TPU:0, one launch (start us, length us, event | category | flops | bytes accessed | tf_op | source)
XLA Modules:
  0.0 40.2 jit_solution(6945104176799223047)
XLA Ops:
  0.0 0.0 copy-start.2
  0.0 0.0 copy-start.3
  0.0 0.0 copy-start.4
  0.0 2.9 %shard_map.93.rest_3_ = bf16[2,384,128]{2,1,0:T(8,128)(2,1)} custom-call(s32[1,2]{1,0:T(1,128)} %shared_ref.1, bf16[48,16,1024]{2,1,0:T(8,128)(2,1)} %z_ref.3), custom_call_target="tpu_custom_call" | custom-call | flops 1000000000 | bytes 4000000 | tf_op jit(solution)/shard_map/pallas_call | solution.py:263
  2.9 0.5 %collective-permute-start.3 = (bf16[2,384,128]{2,1,0:T(8,128)(2,1)}, bf16[2,384,128]{2,1,0:T(8,128)(2,1)S(1)}, u32[]{:S(2)}, u32[]{:S(2)}) collective-permute-start(bf16[2,384,128]{2,1,0:T(8,128)(2,1)} %shard_map.93.rest_3_), channel_id=1, source_target_pairs={{0,1},{1,0},{2,3},{3,2},{4,5},{5,4},{6,7},{7,6},{8,9},{9,8},{10,11... | collective-permute-start | bytes 589832 | tf_op jit(solution)/shard_map/ppermute | solution.py:275
  3.4 3.4 %collective-permute-start.2 = (bf16[2,384,128]{2,1,0:T(8,128)(2,1)}, bf16[2,384,128]{2,1,0:T(8,128)(2,1)S(1)}, u32[]{:S(2)}, u32[]{:S(2)}) collective-permute-start(bf16[2,384,128]{2,1,0:T(8,128)(2,1)} %shard_map.93.rest_3_), channel_id=1, source_target_pairs={{0,6},{1,7},{2,4},{3,5},{4,2},{5,3},{6,0},{7,1},{8,14},{9,15},{10,... | collective-permute-start | bytes 589832 | tf_op jit(solution)/shard_map/ppermute | solution.py:275
  6.9 0.5 %collective-permute-start.1 = (bf16[2,384,128]{2,1,0:T(8,128)(2,1)}, bf16[2,384,128]{2,1,0:T(8,128)(2,1)S(1)}, u32[]{:S(2)}, u32[]{:S(2)}) collective-permute-start(bf16[2,384,128]{2,1,0:T(8,128)(2,1)} %shard_map.93.rest_3_), channel_id=1, source_target_pairs={{0,4},{1,5},{2,6},{3,7},{4,0},{5,1},{6,2},{7,3},{8,12},{9,13},{10,... | collective-permute-start | bytes 589832 | tf_op jit(solution)/shard_map/ppermute | solution.py:275
  7.4 0.1 collective-permute-start
  7.4 0.0 copy-start
  7.4 1.4 %copy-done = bf16[48,16,1024]{2,1,0:T(8,128)(2,1)S(1)} copy-done((bf16[48,16,1024]{2,1,0:T(8,128)(2,1)S(1)}, bf16[48,16,1024]{2,1,0:T(8,128)(2,1)}, u32[]{:S(2)}) %copy-start) | copy-done | bytes 1572888
  8.8 0.0 copy-start.1
  8.8 0.0 copy-start.6
  8.8 2.9 %shard_map.91 = (bf16[8,768,128]{2,1,0:T(8,128)(2,1)S(1)}, bf16[16,384,128]{2,1,0:T(8,128)(2,1)S(1)}) custom-call(bf16[48,16,1024]{2,1,0:T(8,128)(2,1)S(1)} %copy-done), custom_call_target="tpu_custom_call" | custom-call | flops 10000000000 | bytes 10000000 | tf_op jit(solution)/shard_map/pallas_call | solution.py:263
  12.4 0.0 copy-done.2
  12.4 0.0 copy-done.3
  12.4 0.0 copy-done.4
  12.4 0.0 copy-done.1
  12.4 0.0 copy-done.6
  12.4 0.0 copy-start.5
  12.5 0.0 copy-start.7
  12.5 2.5 %shard_map.92 = (f32[16,384,128]{2,1,0:T(8,128)S(1)}, f32[768,128]{1,0:T(8,128)S(1)}, bf16[16,128]{1,0:T(8,128)(2,1)S(1)}, bf16[16,128,256]{2,1,0:T(8,128)(2,1)S(1)}, bf16[16,128,128]{2,1,0:T(8,128)(2,1)S(1)}) custom-call(s32[4,16]{1,0:T(4,128)S(1)} %bitcast.2, s32[1]{0:T(128)S(6)} %copy.10.days_ref, bf16[16,384,128]{2,1,0:T(8,128)(2,1)S(1)} %get-tuple-element.18.turned_ref, ...), custom_call_target="tpu_custom_call" | custom-call | flops 10000000000 | bytes 10000000 | tf_op jit(solution)/shard_map/pallas_call | solution.py:263
  15.0 0.0 collective-permute-done.2.piece_ref.rest_2_
  15.0 0.1 collective-permute-start.4
  15.1 1.8 %collective-permute-done.1.piece_ref.rest_1_ = bf16[2,384,128]{2,1,0:T(8,128)(2,1)S(1)} collective-permute-done((bf16[2,384,128]{2,1,0:T(8,128)(2,1)}, bf16[2,384,128]{2,1,0:T(8,128)(2,1)S(1)}, u32[]{:S(2)}, u32[]{:S(2)}) %collective-permute-start.1) | collective-permute-done | bytes 196640 | tf_op jit(solution)/shard_map/ppermute | solution.py:275
  16.9 0.1 collective-permute-start.5
  17.0 0.2 collective-permute-done.piece_ref.rest_0_
  17.2 0.4 collective-permute-start.6
  17.5 0.0 collective-permute-done.3.rest_7_
  17.5 0.0 collective-permute-done.4.rest_8_
  17.5 0.8 %collective-permute-done.5.rest_9_ = bf16[2,384,128]{2,1,0:T(8,128)(2,1)S(1)} collective-permute-done((bf16[2,384,128]{2,1,0:T(8,128)(2,1)S(1)}, bf16[2,384,128]{2,1,0:T(8,128)(2,1)S(1)}, u32[]{:S(2)}, u32[]{:S(2)}) %collective-permute-start.5) | collective-permute-done | bytes 196640 | tf_op jit(solution)/shard_map/ppermute | solution.py:275
  18.4 0.3 collective-permute-done.6.rest_10_
  18.7 0.0 copy-done.5
  18.7 0.0 copy-done.7
  18.7 3.0 %shard_map.97 = (f32[8,768,128]{2,1,0:T(8,128)S(1)}, bf16[9,16,128]{2,1,0:T(8,128)(2,1)S(1)}) custom-call(s32[2,16]{1,0:T(2,128)S(1)} %bitcast.3, s32[1]{0:T(128)S(6)} %copy.10.days_ref, f32[16,384,128]{2,1,0:T(8,128)S(1)} %get-tuple-element.19.running_ref, bf16[16,128,256]{2,1,0:T(8,128)(2,1)S(1)} %get-tuple-element.20.weight_ref, ...), custom_call_target="tpu_custom_call" | custom-call | flops 10000000000 | bytes 10000000 | tf_op jit(solution)/shard_map/pallas_call | solution.py:263
  21.7 3.8 %collective-permute-start.9 = (bf16[9,16,128]{2,1,0:T(8,128)(2,1)S(1)}, bf16[9,16,128]{2,1,0:T(8,128)(2,1)S(1)}, u32[]{:S(2)}, u32[]{:S(2)}) collective-permute-start(bf16[9,16,128]{2,1,0:T(8,128)(2,1)S(1)} %get-tuple-element.27), channel_id=1, source_target_pairs={{0,24},{8,16},{16,8},{24,0},{1,25},{9,17},{17,9},{25,1},{2,26},{10... | collective-permute-start | bytes 110600 | tf_op jit(solution)/shard_map/ppermute | solution.py:275
  25.6 0.0 collective-permute-start.8
  25.6 0.6 %collective-permute-start.7 = (bf16[9,16,128]{2,1,0:T(8,128)(2,1)S(1)}, bf16[9,16,128]{2,1,0:T(8,128)(2,1)S(1)}, u32[]{:S(2)}, u32[]{:S(2)}) collective-permute-start(bf16[9,16,128]{2,1,0:T(8,128)(2,1)S(1)} %get-tuple-element.27), channel_id=1, source_target_pairs={{0,8},{8,0},{16,24},{24,16},{1,9},{9,1},{17,25},{25,17},{2,10},{10... | collective-permute-start | bytes 110600 | tf_op jit(solution)/shard_map/ppermute | solution.py:275
  26.2 1.9 %shard_map.98 = (f32[16,384,128]{2,1,0:T(8,128)S(1)}, f32[16,48,128]{2,1,0:T(8,128)S(1)}) custom-call(f32[8,768,128]{2,1,0:T(8,128)S(1)} %get-tuple-element.24.forcing_ref, f32[768,128]{1,0:T(8,128)S(1)} %get-tuple-element.22.retain_ref), custom_call_target="tpu_custom_call" | custom-call | flops 1000000000 | bytes 1000000 | tf_op jit(solution)/shard_map/pallas_call | solution.py:263
  28.1 0.0 collective-permute-done.9.rest_2_.rest_5_
  28.1 2.3 %collective-permute-done.8.rest_1_.rest_4_ = bf16[9,16,128]{2,1,0:T(8,128)(2,1)S(1)} collective-permute-done((bf16[9,16,128]{2,1,0:T(8,128)(2,1)S(1)}, bf16[9,16,128]{2,1,0:T(8,128)(2,1)S(1)}, u32[]{:S(2)}, u32[]{:S(2)}) %collective-permute-start.8) | collective-permute-done | bytes 36896 | tf_op jit(solution)/shard_map/ppermute | solution.py:275
  30.4 0.0 collective-permute-done.7.rest_0_.rest_3_
  30.4 1.7 %shard_map.99 = (f32[8,768,128]{2,1,0:T(8,128)S(1)}, bf16[8,16,128]{2,1,0:T(8,128)(2,1)S(1)}) custom-call(s32[1]{0:T(128)S(6)} %copy.10.days_ref, f32[16,384,128]{2,1,0:T(8,128)S(1)} %get-tuple-element.25.states_ref, f32[16,48,128]{2,1,0:T(8,128)S(1)} %get-tuple-element.26.through_ref, f32[768,128]{1,0:T(8,128)S(1)} %get-tuple-element.22.retain_ref, ...), custom_call_target="tpu_custom_call" | custom-call | flops 10000000000 | bytes 10000000 | tf_op jit(solution)/shard_map/pallas_call | solution.py:263
  32.1 1.7 %collective-permute-start.12 = (bf16[8,16,128]{2,1,0:T(8,128)(2,1)S(1)}, bf16[8,16,128]{2,1,0:T(8,128)(2,1)S(1)}, u32[]{:S(2)}, u32[]{:S(2)}) collective-permute-start(bf16[8,16,128]{2,1,0:T(8,128)(2,1)S(1)} %get-tuple-element.30), channel_id=1, source_target_pairs={{0,24},{8,16},{16,8},{24,0},{1,25},{9,17},{17,9},{25,1},{2,26},{10... | collective-permute-start | bytes 98312 | tf_op jit(solution)/shard_map/ppermute | solution.py:275
  33.9 0.4 %collective-permute-start.11 = (bf16[8,16,128]{2,1,0:T(8,128)(2,1)S(1)}, bf16[8,16,128]{2,1,0:T(8,128)(2,1)S(1)}, u32[]{:S(2)}, u32[]{:S(2)}) collective-permute-start(bf16[8,16,128]{2,1,0:T(8,128)(2,1)S(1)} %get-tuple-element.30), channel_id=1, source_target_pairs={{0,16},{8,24},{16,0},{24,8},{1,17},{9,25},{17,1},{25,9},{2,18},{10... | collective-permute-start | bytes 98312 | tf_op jit(solution)/shard_map/ppermute | solution.py:275
  34.3 2.3 %collective-permute-start.10 = (bf16[8,16,128]{2,1,0:T(8,128)(2,1)S(1)}, bf16[8,16,128]{2,1,0:T(8,128)(2,1)S(1)}, u32[]{:S(2)}, u32[]{:S(2)}) collective-permute-start(bf16[8,16,128]{2,1,0:T(8,128)(2,1)S(1)} %get-tuple-element.30), channel_id=1, source_target_pairs={{0,8},{8,0},{16,24},{24,16},{1,9},{9,1},{17,25},{25,17},{2,10},{10... | collective-permute-start | bytes 98312 | tf_op jit(solution)/shard_map/ppermute | solution.py:275
  36.6 0.5 %shard_map.100.partial_ref = f32[768,128]{1,0:T(8,128)S(1)} custom-call(f32[8,768,128]{2,1,0:T(8,128)S(1)} %get-tuple-element.28.adjoint_ref, f32[768,128]{1,0:T(8,128)S(1)} %get-tuple-element.22.retain_ref, bf16[8,768,128]{2,1,0:T(8,128)(2,1)S(1)} %get-tuple-element.29.moved_ref), custom_call_target="tpu_custom_call" | custom-call | flops 1000000000 | bytes 1000000 | tf_op jit(solution)/shard_map/pallas_call | solution.py:263
  37.1 1.1 %collective-permute-done.12.rest_2_ = bf16[8,16,128]{2,1,0:T(8,128)(2,1)S(1)} collective-permute-done((bf16[8,16,128]{2,1,0:T(8,128)(2,1)S(1)}, bf16[8,16,128]{2,1,0:T(8,128)(2,1)S(1)}, u32[]{:S(2)}, u32[]{:S(2)}) %collective-permute-start.12) | collective-permute-done | bytes 32800 | tf_op jit(solution)/shard_map/ppermute | solution.py:275
  38.2 0.5 %collective-permute-done.11.rest_1_ = bf16[8,16,128]{2,1,0:T(8,128)(2,1)S(1)} collective-permute-done((bf16[8,16,128]{2,1,0:T(8,128)(2,1)S(1)}, bf16[8,16,128]{2,1,0:T(8,128)(2,1)S(1)}, u32[]{:S(2)}, u32[]{:S(2)}) %collective-permute-start.11) | collective-permute-done | bytes 32800 | tf_op jit(solution)/shard_map/ppermute | solution.py:275
  38.7 0.2 collective-permute-done.10.rest_0_
  38.9 1.3 %shard_map.101 = f32[48,1024]{1,0:T(8,128)} custom-call(f32[768,128]{1,0:T(8,128)S(1)} %shard_map.100.partial_ref, f32[768,128]{1,0:T(8,128)S(1)} %get-tuple-element.22.retain_ref, bf16[8,768,128]{2,1,0:T(8,128)(2,1)S(1)} %get-tuple-element.29.moved_ref, bf16[8,16,128]{2,1,0:T(8,128)(2,1)S(1)} %collective-permute-done.10.rest_0_, ...), custom_call_target="tpu_custom_call" | custom-call | flops 10000000000 | bytes 10000000 | tf_op jit(solution)/shard_map/pallas_call | solution.py:263
  (3 shorter events, 0.0 us)
Async XLA Ops:
  0.0 12.4 %copy-start.2 = (bf16[16,2,64,64]{3,2,1,0:T(8,128)(2,1)S(1)}, bf16[16,2,64,64]{3,2,1,0:T(8,128)(2,1)}, u32[]{:S(2)}) copy-start(bf16[16,2,64,64]{3,2,1,0:T(8,128)(2,1)} %remote_weight_ref.1) | copy-start | bytes 786436
  0.0 12.4 %copy-start.3 = (bf16[16,64,64]{2,1,0:T(8,128)(2,1)S(1)}, bf16[16,64,64]{2,1,0:T(8,128)(2,1)}, u32[]{:S(2)}) copy-start(bf16[16,64,64]{2,1,0:T(8,128)(2,1)} %inverse_ref.1) | copy-start | bytes 393220
  0.0 12.4 %copy-start.4 = (f32[48,1024]{1,0:T(8,128)S(1)}, f32[48,1024]{1,0:T(8,128)}, u32[]{:S(2)}) copy-start(f32[48,1024]{1,0:T(8,128)} %retention_ref.1) | copy-start | bytes 589828
  2.9 14.6 %collective-permute-start.3 = (bf16[2,384,128]{2,1,0:T(8,128)(2,1)}, bf16[2,384,128]{2,1,0:T(8,128)(2,1)S(1)}, u32[]{:S(2)}, u32[]{:S(2)}) collective-permute-start(bf16[2,384,128]{2,1,0:T(8,128)(2,1)} %shard_map.93.rest_3_), channel_id=1, source_target_pairs={{0,1},{1,0},{2,3},{3,2},{4,5},{5,4},{6,7},{7,6},{8,9},{9,8},{10,11... | collective-permute-start | bytes 589832 | tf_op jit(solution)/shard_map/ppermute | solution.py:275
  3.4 11.6 %collective-permute-start.2 = (bf16[2,384,128]{2,1,0:T(8,128)(2,1)}, bf16[2,384,128]{2,1,0:T(8,128)(2,1)S(1)}, u32[]{:S(2)}, u32[]{:S(2)}) collective-permute-start(bf16[2,384,128]{2,1,0:T(8,128)(2,1)} %shard_map.93.rest_3_), channel_id=1, source_target_pairs={{0,6},{1,7},{2,4},{3,5},{4,2},{5,3},{6,0},{7,1},{8,14},{9,15},{10,... | collective-permute-start | bytes 589832 | tf_op jit(solution)/shard_map/ppermute | solution.py:275
  6.9 10.0 %collective-permute-start.1 = (bf16[2,384,128]{2,1,0:T(8,128)(2,1)}, bf16[2,384,128]{2,1,0:T(8,128)(2,1)S(1)}, u32[]{:S(2)}, u32[]{:S(2)}) collective-permute-start(bf16[2,384,128]{2,1,0:T(8,128)(2,1)} %shard_map.93.rest_3_), channel_id=1, source_target_pairs={{0,4},{1,5},{2,6},{3,7},{4,0},{5,1},{6,2},{7,3},{8,12},{9,13},{10,... | collective-permute-start | bytes 589832 | tf_op jit(solution)/shard_map/ppermute | solution.py:275
  7.4 9.8 %collective-permute-start = (bf16[2,384,128]{2,1,0:T(8,128)(2,1)}, bf16[2,384,128]{2,1,0:T(8,128)(2,1)S(1)}, u32[]{:S(2)}, u32[]{:S(2)}) collective-permute-start(bf16[2,384,128]{2,1,0:T(8,128)(2,1)} %shard_map.93.rest_3_), channel_id=1, source_target_pairs={{0,2},{1,3},{2,0},{3,1},{4,6},{5,7},{6,4},{7,5},{8,10},{9,11},{10,... | collective-permute-start | bytes 589832 | tf_op jit(solution)/shard_map/ppermute | solution.py:275
  7.4 1.4 %copy-start = (bf16[48,16,1024]{2,1,0:T(8,128)(2,1)S(1)}, bf16[48,16,1024]{2,1,0:T(8,128)(2,1)}, u32[]{:S(2)}) copy-start(bf16[48,16,1024]{2,1,0:T(8,128)(2,1)} %z_ref.3) | copy-start | bytes 4718596
  8.8 3.6 %copy-start.1 = (bf16[16,4,64,64]{3,2,1,0:T(8,128)(2,1)S(1)}, bf16[16,4,64,64]{3,2,1,0:T(8,128)(2,1)}, u32[]{:S(2)}) copy-start(bf16[16,4,64,64]{3,2,1,0:T(8,128)(2,1)} %weight_ref.1) | copy-start | bytes 1572868
  8.8 3.6 %copy-start.6 = (s32[16,4]{0,1:T(4,128)S(1)}, s32[16,4]{0,1:T(4,128)}, u32[]{:S(2)}) copy-start(s32[16,4]{0,1:T(4,128)} %param.10) | copy-start | bytes 772
  12.4 6.2 %copy-start.5 = (bf16[2,384,128]{2,1,0:T(8,128)(2,1)S(1)}, bf16[2,384,128]{2,1,0:T(8,128)(2,1)}, u32[]{:S(2)}) copy-start(bf16[2,384,128]{2,1,0:T(8,128)(2,1)} %shard_map.93.rest_3_) | copy-start | bytes 589828
  12.5 6.2 %copy-start.7 = (s32[16,2]{0,1:T(2,128)S(1)}, s32[16,2]{0,1:T(2,128)}, u32[]{:S(2)}) copy-start(s32[16,2]{0,1:T(2,128)} %param.11) | copy-start | bytes 388
  15.0 2.5 %collective-permute-start.4 = (bf16[2,384,128]{2,1,0:T(8,128)(2,1)S(1)}, bf16[2,384,128]{2,1,0:T(8,128)(2,1)S(1)}, u32[]{:S(2)}, u32[]{:S(2)}) collective-permute-start(bf16[2,384,128]{2,1,0:T(8,128)(2,1)S(1)} %shard_map.94.rest_4_), channel_id=1, source_target_pairs={{0,1},{1,0},{2,3},{3,2},{4,5},{5,4},{6,7},{7,6},{8,9},{9,8},{10,11... | collective-permute-start | bytes 589832 | tf_op jit(solution)/shard_map/ppermute | solution.py:275
  16.9 1.5 %collective-permute-start.5 = (bf16[2,384,128]{2,1,0:T(8,128)(2,1)S(1)}, bf16[2,384,128]{2,1,0:T(8,128)(2,1)S(1)}, u32[]{:S(2)}, u32[]{:S(2)}) collective-permute-start(bf16[2,384,128]{2,1,0:T(8,128)(2,1)S(1)} %shard_map.95.rest_5_), channel_id=1, source_target_pairs={{0,1},{1,0},{2,3},{3,2},{4,5},{5,4},{6,7},{7,6},{8,9},{9,8},{10,11... | collective-permute-start | bytes 589832 | tf_op jit(solution)/shard_map/ppermute | solution.py:275
  17.2 1.5 %collective-permute-start.6 = (bf16[2,384,128]{2,1,0:T(8,128)(2,1)S(1)}, bf16[2,384,128]{2,1,0:T(8,128)(2,1)S(1)}, u32[]{:S(2)}, u32[]{:S(2)}) collective-permute-start(bf16[2,384,128]{2,1,0:T(8,128)(2,1)S(1)} %shard_map.96.rest_6_), channel_id=1, source_target_pairs={{0,1},{1,0},{2,3},{3,2},{4,5},{5,4},{6,7},{7,6},{8,9},{9,8},{10,11... | collective-permute-start | bytes 589832 | tf_op jit(solution)/shard_map/ppermute | solution.py:275
  21.7 6.4 %collective-permute-start.9 = (bf16[9,16,128]{2,1,0:T(8,128)(2,1)S(1)}, bf16[9,16,128]{2,1,0:T(8,128)(2,1)S(1)}, u32[]{:S(2)}, u32[]{:S(2)}) collective-permute-start(bf16[9,16,128]{2,1,0:T(8,128)(2,1)S(1)} %get-tuple-element.27), channel_id=1, source_target_pairs={{0,24},{8,16},{16,8},{24,0},{1,25},{9,17},{17,9},{25,1},{2,26},{10... | collective-permute-start | bytes 110600 | tf_op jit(solution)/shard_map/ppermute | solution.py:275
  25.6 4.9 %collective-permute-start.8 = (bf16[9,16,128]{2,1,0:T(8,128)(2,1)S(1)}, bf16[9,16,128]{2,1,0:T(8,128)(2,1)S(1)}, u32[]{:S(2)}, u32[]{:S(2)}) collective-permute-start(bf16[9,16,128]{2,1,0:T(8,128)(2,1)S(1)} %get-tuple-element.27), channel_id=1, source_target_pairs={{0,16},{8,24},{16,0},{24,8},{1,17},{9,25},{17,1},{25,9},{2,18},{10... | collective-permute-start | bytes 110600 | tf_op jit(solution)/shard_map/ppermute | solution.py:275
  25.6 4.9 %collective-permute-start.7 = (bf16[9,16,128]{2,1,0:T(8,128)(2,1)S(1)}, bf16[9,16,128]{2,1,0:T(8,128)(2,1)S(1)}, u32[]{:S(2)}, u32[]{:S(2)}) collective-permute-start(bf16[9,16,128]{2,1,0:T(8,128)(2,1)S(1)} %get-tuple-element.27), channel_id=1, source_target_pairs={{0,8},{8,0},{16,24},{24,16},{1,9},{9,1},{17,25},{25,17},{2,10},{10... | collective-permute-start | bytes 110600 | tf_op jit(solution)/shard_map/ppermute | solution.py:275
  32.1 6.1 %collective-permute-start.12 = (bf16[8,16,128]{2,1,0:T(8,128)(2,1)S(1)}, bf16[8,16,128]{2,1,0:T(8,128)(2,1)S(1)}, u32[]{:S(2)}, u32[]{:S(2)}) collective-permute-start(bf16[8,16,128]{2,1,0:T(8,128)(2,1)S(1)} %get-tuple-element.30), channel_id=1, source_target_pairs={{0,24},{8,16},{16,8},{24,0},{1,25},{9,17},{17,9},{25,1},{2,26},{10... | collective-permute-start | bytes 98312 | tf_op jit(solution)/shard_map/ppermute | solution.py:275
  33.9 4.9 %collective-permute-start.11 = (bf16[8,16,128]{2,1,0:T(8,128)(2,1)S(1)}, bf16[8,16,128]{2,1,0:T(8,128)(2,1)S(1)}, u32[]{:S(2)}, u32[]{:S(2)}) collective-permute-start(bf16[8,16,128]{2,1,0:T(8,128)(2,1)S(1)} %get-tuple-element.30), channel_id=1, source_target_pairs={{0,16},{8,24},{16,0},{24,8},{1,17},{9,25},{17,1},{25,9},{2,18},{10... | collective-permute-start | bytes 98312 | tf_op jit(solution)/shard_map/ppermute | solution.py:275
  34.3 4.6 %collective-permute-start.10 = (bf16[8,16,128]{2,1,0:T(8,128)(2,1)S(1)}, bf16[8,16,128]{2,1,0:T(8,128)(2,1)S(1)}, u32[]{:S(2)}, u32[]{:S(2)}) collective-permute-start(bf16[8,16,128]{2,1,0:T(8,128)(2,1)S(1)} %get-tuple-element.30), channel_id=1, source_target_pairs={{0,8},{8,0},{16,24},{24,16},{1,9},{9,1},{17,25},{25,17},{2,10},{10... | collective-permute-start | bytes 98312 | tf_op jit(solution)/shard_map/ppermute | solution.py:275

commit v12 on v11

--- a/solution.py
+++ b/solution.py
@@ -27,22 +27,37 @@
     )
 
 
-def outgoing_kernel(dims, shared_ref, z_ref, outgoing_ref):
+def outgoing_kernel(dims, shared_hbm, z_hbm, outgoing_ref, shared_ref, z_ref, listed, arrived):
     days, blocks, size, probes = dims
     count = outgoing_ref.shape[0]
-    z = z_ref[...].reshape(days * blocks, size * probes)
-    row = lax.broadcasted_iota(jnp.int32, (days, days * blocks), 0)
-    column = lax.broadcasted_iota(jnp.int32, (days, days * blocks), 1)
-    picks = [
-        (column == row * blocks + shared_ref[0, m]).astype(jnp.float32).astype(jnp.bfloat16) for m in range(count)
+    parts = arrived.shape[0]
+    part = days // parts
+    copies = [
+        pltpu.make_async_copy(z_hbm.at[pl.ds(i * part, part)], z_ref.at[pl.ds(i * part, part)], arrived.at[i])
+        for i in range(parts)
     ]
-    picked = jnp.dot(jnp.concatenate(picks, axis=0), z, preferred_element_type=jnp.float32)
+    listing = pltpu.make_async_copy(shared_hbm, shared_ref, listed)
+    listing.start()
+    for copy in copies:
+        copy.start()
+    row = lax.broadcasted_iota(jnp.int32, (part, part * blocks), 0)
+    column = lax.broadcasted_iota(jnp.int32, (part, part * blocks), 1)
+    move = permutation(size, probes, 0, 2 * LANES)
+    listing.wait()
+    picks = [(column == row * blocks + shared_ref[0, m]).astype(jnp.float32) for m in range(count)]
+    picks = jnp.concatenate(picks, axis=0).astype(jnp.bfloat16)
+    picked = []
+    for i, copy in enumerate(copies):
+        copy.wait()
+        z = z_ref[pl.ds(i * part, part)].reshape(part * blocks, size * probes)
+        picked.append(jnp.dot(picks, z, preferred_element_type=jnp.float32))
+    picked = jnp.concatenate([rows[m * part : (m + 1) * part] for m in range(count) for rows in picked], axis=0)
     step = 2 * LANES
     shift = step // size
     ranges = size * probes // step
     shifted = [picked] + [pltpu.roll(picked, size * probes - i * shift, 1) for i in range(1, ranges)]
     shifted = jnp.concatenate(shifted, axis=0).astype(jnp.bfloat16)
-    moved = jnp.dot(shifted, permutation(size, probes, 0, step), preferred_element_type=jnp.float32)
+    moved = jnp.dot(shifted, move, preferred_element_type=jnp.float32)
     moved = moved.astype(jnp.bfloat16)
     for pair in range(size * probes // LANES):
         for m in range(count):
@@ -235,27 +250,36 @@
 def variance_kernel(dims, hops, partial_ref, retain_ref, moved_ref, *rest):
     days, blocks, size, probes = dims
     pairs = moved_ref.shape[0]
-    out_ref, stage, inbox, products = rest[2 * hops :]
+    out_hbm, stage, inbox, products, out_ref, left = rest[2 * hops :]
     collect(rest[:hops], inbox)
     collect(rest[hops : 2 * hops], products)
     carries = carried(pairs, inbox, products, True)
     reach = jnp.ones((blocks, LANES), jnp.float32)
-    for day in reversed(range(days)):
-        rows = pl.ds(day * blocks, blocks)
-        total = None
-        for pair in range(pairs):
-            term = carries[pair] * moved_ref[pair, rows, :].astype(jnp.float32)
-            total = term if total is None else total + term
-        stage[rows, :] = partial_ref[rows, :] + reach * total
-        reach = reach * retain_ref[rows, :]
-    lane = lax.broadcasted_iota(jnp.int32, (days, LANES), 1)
-    for block in range(0, blocks, 2):
-        both = [stage[pl.ds(block + half, days, stride=blocks), :] for half in range(2)]
-        both = [value + pltpu.roll(value, size, 1) for value in both]
-        out_ref[:, pl.ds(block * size, LANES)] = jnp.where(lane < size, both[0], both[1]) * (1.0 / probes)
-
-
-def call(kernel, outs, scratch, flops, moved, scalars, *operands, apart=(), limit=VMEM_LIMIT):
+    parts = left.shape[0]
+    part = days // parts
+    lane = lax.broadcasted_iota(jnp.int32, (part, LANES), 1)
+    copies = []
+    for first in reversed(range(0, days, part)):
+        for day in reversed(range(first, first + part)):
+            rows = pl.ds(day * blocks, blocks)
+            total = None
+            for pair in range(pairs):
+                term = carries[pair] * moved_ref[pair, rows, :].astype(jnp.float32)
+                total = term if total is None else total + term
+            stage[rows, :] = partial_ref[rows, :] + reach * total
+            reach = reach * retain_ref[rows, :]
+        done = pl.ds(first, part)
+        for block in range(0, blocks, 2):
+            both = [stage[pl.ds(first * blocks + block + half, part, stride=blocks), :] for half in range(2)]
+            both = [value + pltpu.roll(value, size, 1) for value in both]
+            out_ref[done, pl.ds(block * size, LANES)] = jnp.where(lane < size, both[0], both[1]) * (1.0 / probes)
+        copies.append(pltpu.make_async_copy(out_ref.at[done], out_hbm.at[done], left.at[len(copies)]))
+        copies[-1].start()
+    for copy in copies:
+        copy.wait()
+
+
+def call(kernel, outs, scratch, flops, moved, scalars, *operands, apart=(), limit=VMEM_LIMIT, out_space=pltpu.VMEM):
     in_specs = [
         pl.BlockSpec(memory_space=pltpu.SMEM if i < scalars else pl.ANY if i in apart else pltpu.VMEM)
         for i in range(len(operands))
@@ -264,7 +288,7 @@
         kernel,
         out_shape=[jax.ShapeDtypeStruct(shape, kind) for shape, kind in outs],
         in_specs=in_specs,
-        out_specs=[pl.BlockSpec(memory_space=pltpu.VMEM) for _ in outs],
+        out_specs=[pl.BlockSpec(memory_space=out_space) for _ in outs],
         scratch_shapes=scratch,
         compiler_params=pltpu.CompilerParams(vmem_limit_bytes=limit),
         cost_estimate=pl.CostEstimate(flops=flops, bytes_accessed=moved, transcendentals=0),
@@ -302,7 +326,13 @@
     (outgoing,) = call(
         functools.partial(outgoing_kernel, dims),
         [((bound, pairs * days, LANES), bf16)],
-        [], 10**9, 4 * 10**6, 1, shared_blocks, probes, limit=63 * 1024 * 1024,
+        [
+            pltpu.SMEM(shared_blocks.shape, jnp.int32),
+            pltpu.VMEM(probes.shape, bf16),
+            pltpu.SemaphoreType.DMA,
+            pltpu.SemaphoreType.DMA((2,)),
+        ],
+        10**9, 4 * 10**6, 0, shared_blocks, probes, apart=(0, 1), limit=63 * 1024 * 1024,
     )
     pieces = {bits: crossed(outgoing, "space", bits) for bits in range(groups - 2, 0, -2)}
     by_block = (blocks, pairs * days, LANES)
@@ -360,8 +390,14 @@
     (variance,) = call(
         functools.partial(variance_kernel, dims, hops),
         [((days, blocks * size), f32)],
-        [pltpu.VMEM((rows, LANES), f32), pltpu.VMEM((slabs, pairs, blocks, LANES), bf16), inbox], 10**10, 10**7, 0,
-        partial, retain, moved, *starts, *ends,
+        [
+            pltpu.VMEM((rows, LANES), f32),
+            pltpu.VMEM((slabs, pairs, blocks, LANES), bf16),
+            inbox,
+            pltpu.VMEM((days, blocks * size), f32),
+            pltpu.SemaphoreType.DMA((2,)),
+        ],
+        10**10, 10**7, 0, partial, retain, moved, *starts, *ends, out_space=pl.ANY,
     )
     return variance
 

time: 40.4 us -> 40.3 us (level)
  no operation moved by 1% of the time
where the time goes in v12:
time: 40.3 us; the launch traced here: 40.1 us
  Pallas kernels  16.7 us (41%)
  starting transfers between devices  14.2 us (35%)
  waiting for transfers between devices  7 us (17%)
  local copies, waits for them, and re-layouts  1.44 us (4%)
  between operations  0.8 us (2%)
    pallas_call x11, Pallas kernels, call(): pl.pallas_call(kernel, out_shape=[jax.ShapeDtypeStruct(shape, kind) for s...  16.7 us
    ppermute x13, starting transfers between devices, crossed(): lax.ppermute(block, axis, [(i, i ^ bits) for i in range(lax.axis_size(axi...  14.2 us
    ppermute x13, waiting for transfers between devices, crossed(): lax.ppermute(block, axis, [(i, i ^ bits) for i in range(lax.axis_size(axi...  7 us
    unnamed x16, local copies, waits for them, and re-layouts  1.44 us
  transfers between devices with their start and end apart: 13, of which 8 were waited for; matrix products, arithmetic and copies ran while one was open for 0% of the time, Pallas kernels for 20%

profile of v12, /device:TPU:0, one launch (start us, length us, event | category | flops | bytes accessed | tf_op | source)
XLA Modules:
  0.0 40.1 jit_solution(9609219533606933355)
XLA Ops:
  0.0 0.0 copy-start.2
  0.0 0.0 copy-start.3
  0.0 0.0 copy-start.4
  0.0 2.8 %shard_map.93.rest_3_ = bf16[2,384,128]{2,1,0:T(8,128)(2,1)} custom-call(s32[1,2]{1,0:T(1,128)} %shared_hbm.1, bf16[48,16,1024]{2,1,0:T(8,128)(2,1)} %z_hbm.1), custom_call_target="tpu_custom_call" | custom-call | flops 1000000000 | bytes 4000000 | tf_op jit(solution)/shard_map/pallas_call | solution.py:287
  2.8 0.5 %collective-permute-start.3 = (bf16[2,384,128]{2,1,0:T(8,128)(2,1)}, bf16[2,384,128]{2,1,0:T(8,128)(2,1)S(1)}, u32[]{:S(2)}, u32[]{:S(2)}) collective-permute-start(bf16[2,384,128]{2,1,0:T(8,128)(2,1)} %shard_map.93.rest_3_), channel_id=1, source_target_pairs={{0,1},{1,0},{2,3},{3,2},{4,5},{5,4},{6,7},{7,6},{8,9},{9,8},{10,11... | collective-permute-start | bytes 589832 | tf_op jit(solution)/shard_map/ppermute | solution.py:299
  3.3 3.5 %collective-permute-start.2 = (bf16[2,384,128]{2,1,0:T(8,128)(2,1)}, bf16[2,384,128]{2,1,0:T(8,128)(2,1)S(1)}, u32[]{:S(2)}, u32[]{:S(2)}) collective-permute-start(bf16[2,384,128]{2,1,0:T(8,128)(2,1)} %shard_map.93.rest_3_), channel_id=1, source_target_pairs={{0,6},{1,7},{2,4},{3,5},{4,2},{5,3},{6,0},{7,1},{8,14},{9,15},{10,... | collective-permute-start | bytes 589832 | tf_op jit(solution)/shard_map/ppermute | solution.py:299
  6.9 0.5 %collective-permute-start.1 = (bf16[2,384,128]{2,1,0:T(8,128)(2,1)}, bf16[2,384,128]{2,1,0:T(8,128)(2,1)S(1)}, u32[]{:S(2)}, u32[]{:S(2)}) collective-permute-start(bf16[2,384,128]{2,1,0:T(8,128)(2,1)} %shard_map.93.rest_3_), channel_id=1, source_target_pairs={{0,4},{1,5},{2,6},{3,7},{4,0},{5,1},{6,2},{7,3},{8,12},{9,13},{10,... | collective-permute-start | bytes 589832 | tf_op jit(solution)/shard_map/ppermute | solution.py:299
  7.4 0.1 collective-permute-start
  7.5 0.0 copy-start
  7.5 1.4 %copy-done = bf16[48,16,1024]{2,1,0:T(8,128)(2,1)S(1)} copy-done((bf16[48,16,1024]{2,1,0:T(8,128)(2,1)S(1)}, bf16[48,16,1024]{2,1,0:T(8,128)(2,1)}, u32[]{:S(2)}) %copy-start) | copy-done | bytes 1572888
  8.9 0.0 copy-start.1
  8.9 0.0 copy-start.6
  8.9 2.9 %shard_map.91 = (bf16[8,768,128]{2,1,0:T(8,128)(2,1)S(1)}, bf16[16,384,128]{2,1,0:T(8,128)(2,1)S(1)}) custom-call(bf16[48,16,1024]{2,1,0:T(8,128)(2,1)S(1)} %copy-done), custom_call_target="tpu_custom_call" | custom-call | flops 10000000000 | bytes 10000000 | tf_op jit(solution)/shard_map/pallas_call | solution.py:287
  12.5 0.0 copy-done.2
  12.5 0.0 copy-done.3
  12.5 0.0 copy-done.4
  12.5 0.0 copy-done.1
  12.5 0.0 copy-done.6
  12.5 0.0 copy-start.5
  12.6 0.0 copy-start.7
  12.6 2.5 %shard_map.92 = (f32[16,384,128]{2,1,0:T(8,128)S(1)}, f32[768,128]{1,0:T(8,128)S(1)}, bf16[16,128]{1,0:T(8,128)(2,1)S(1)}, bf16[16,128,256]{2,1,0:T(8,128)(2,1)S(1)}, bf16[16,128,128]{2,1,0:T(8,128)(2,1)S(1)}) custom-call(s32[4,16]{1,0:T(4,128)S(1)} %bitcast.2, s32[1]{0:T(128)S(6)} %copy.10.days_ref, bf16[16,384,128]{2,1,0:T(8,128)(2,1)S(1)} %get-tuple-element.18.turned_ref, ...), custom_call_target="tpu_custom_call" | custom-call | flops 10000000000 | bytes 10000000 | tf_op jit(solution)/shard_map/pallas_call | solution.py:287
  15.1 0.0 collective-permute-done.2.piece_ref.rest_2_
  15.1 0.1 collective-permute-start.4
  15.2 1.6 %collective-permute-done.1.piece_ref.rest_1_ = bf16[2,384,128]{2,1,0:T(8,128)(2,1)S(1)} collective-permute-done((bf16[2,384,128]{2,1,0:T(8,128)(2,1)}, bf16[2,384,128]{2,1,0:T(8,128)(2,1)S(1)}, u32[]{:S(2)}, u32[]{:S(2)}) %collective-permute-start.1) | collective-permute-done | bytes 196640 | tf_op jit(solution)/shard_map/ppermute | solution.py:299
  16.8 0.1 collective-permute-start.5
  16.9 0.2 collective-permute-done.piece_ref.rest_0_
  17.1 0.4 collective-permute-start.6
  17.5 0.0 collective-permute-done.3.rest_7_
  17.5 0.0 collective-permute-done.4.rest_8_
  17.5 0.8 %collective-permute-done.5.rest_9_ = bf16[2,384,128]{2,1,0:T(8,128)(2,1)S(1)} collective-permute-done((bf16[2,384,128]{2,1,0:T(8,128)(2,1)S(1)}, bf16[2,384,128]{2,1,0:T(8,128)(2,1)S(1)}, u32[]{:S(2)}, u32[]{:S(2)}) %collective-permute-start.5) | collective-permute-done | bytes 196640 | tf_op jit(solution)/shard_map/ppermute | solution.py:299
  18.3 0.3 collective-permute-done.6.rest_10_
  18.6 0.0 copy-done.5
  18.6 0.0 copy-done.7
  18.6 3.0 %shard_map.97 = (f32[8,768,128]{2,1,0:T(8,128)S(1)}, bf16[9,16,128]{2,1,0:T(8,128)(2,1)S(1)}) custom-call(s32[2,16]{1,0:T(2,128)S(1)} %bitcast.3, s32[1]{0:T(128)S(6)} %copy.10.days_ref, f32[16,384,128]{2,1,0:T(8,128)S(1)} %get-tuple-element.19.running_ref, bf16[16,128,256]{2,1,0:T(8,128)(2,1)S(1)} %get-tuple-element.20.weight_ref, ...), custom_call_target="tpu_custom_call" | custom-call | flops 10000000000 | bytes 10000000 | tf_op jit(solution)/shard_map/pallas_call | solution.py:287
  21.7 3.8 %collective-permute-start.9 = (bf16[9,16,128]{2,1,0:T(8,128)(2,1)S(1)}, bf16[9,16,128]{2,1,0:T(8,128)(2,1)S(1)}, u32[]{:S(2)}, u32[]{:S(2)}) collective-permute-start(bf16[9,16,128]{2,1,0:T(8,128)(2,1)S(1)} %get-tuple-element.27), channel_id=1, source_target_pairs={{0,24},{8,16},{16,8},{24,0},{1,25},{9,17},{17,9},{25,1},{2,26},{10... | collective-permute-start | bytes 110600 | tf_op jit(solution)/shard_map/ppermute | solution.py:299
  25.5 0.0 collective-permute-start.8
  25.5 0.6 %collective-permute-start.7 = (bf16[9,16,128]{2,1,0:T(8,128)(2,1)S(1)}, bf16[9,16,128]{2,1,0:T(8,128)(2,1)S(1)}, u32[]{:S(2)}, u32[]{:S(2)}) collective-permute-start(bf16[9,16,128]{2,1,0:T(8,128)(2,1)S(1)} %get-tuple-element.27), channel_id=1, source_target_pairs={{0,8},{8,0},{16,24},{24,16},{1,9},{9,1},{17,25},{25,17},{2,10},{10... | collective-permute-start | bytes 110600 | tf_op jit(solution)/shard_map/ppermute | solution.py:299
  26.2 1.9 %shard_map.98 = (f32[16,384,128]{2,1,0:T(8,128)S(1)}, f32[16,48,128]{2,1,0:T(8,128)S(1)}) custom-call(f32[8,768,128]{2,1,0:T(8,128)S(1)} %get-tuple-element.24.forcing_ref, f32[768,128]{1,0:T(8,128)S(1)} %get-tuple-element.22.retain_ref), custom_call_target="tpu_custom_call" | custom-call | flops 1000000000 | bytes 1000000 | tf_op jit(solution)/shard_map/pallas_call | solution.py:287
  28.1 0.0 collective-permute-done.9.rest_2_.rest_5_
  28.1 2.3 %collective-permute-done.8.rest_1_.rest_4_ = bf16[9,16,128]{2,1,0:T(8,128)(2,1)S(1)} collective-permute-done((bf16[9,16,128]{2,1,0:T(8,128)(2,1)S(1)}, bf16[9,16,128]{2,1,0:T(8,128)(2,1)S(1)}, u32[]{:S(2)}, u32[]{:S(2)}) %collective-permute-start.8) | collective-permute-done | bytes 36896 | tf_op jit(solution)/shard_map/ppermute | solution.py:299
  30.4 0.0 collective-permute-done.7.rest_0_.rest_3_
  30.4 1.7 %shard_map.99 = (f32[8,768,128]{2,1,0:T(8,128)S(1)}, bf16[8,16,128]{2,1,0:T(8,128)(2,1)S(1)}) custom-call(s32[1]{0:T(128)S(6)} %copy.10.days_ref, f32[16,384,128]{2,1,0:T(8,128)S(1)} %get-tuple-element.25.states_ref, f32[16,48,128]{2,1,0:T(8,128)S(1)} %get-tuple-element.26.through_ref, f32[768,128]{1,0:T(8,128)S(1)} %get-tuple-element.22.retain_ref, ...), custom_call_target="tpu_custom_call" | custom-call | flops 10000000000 | bytes 10000000 | tf_op jit(solution)/shard_map/pallas_call | solution.py:287
  32.1 1.7 %collective-permute-start.12 = (bf16[8,16,128]{2,1,0:T(8,128)(2,1)S(1)}, bf16[8,16,128]{2,1,0:T(8,128)(2,1)S(1)}, u32[]{:S(2)}, u32[]{:S(2)}) collective-permute-start(bf16[8,16,128]{2,1,0:T(8,128)(2,1)S(1)} %get-tuple-element.30), channel_id=1, source_target_pairs={{0,24},{8,16},{16,8},{24,0},{1,25},{9,17},{17,9},{25,1},{2,26},{10... | collective-permute-start | bytes 98312 | tf_op jit(solution)/shard_map/ppermute | solution.py:299
  33.8 0.4 %collective-permute-start.11 = (bf16[8,16,128]{2,1,0:T(8,128)(2,1)S(1)}, bf16[8,16,128]{2,1,0:T(8,128)(2,1)S(1)}, u32[]{:S(2)}, u32[]{:S(2)}) collective-permute-start(bf16[8,16,128]{2,1,0:T(8,128)(2,1)S(1)} %get-tuple-element.30), channel_id=1, source_target_pairs={{0,16},{8,24},{16,0},{24,8},{1,17},{9,25},{17,1},{25,9},{2,18},{10... | collective-permute-start | bytes 98312 | tf_op jit(solution)/shard_map/ppermute | solution.py:299
  34.3 2.3 %collective-permute-start.10 = (bf16[8,16,128]{2,1,0:T(8,128)(2,1)S(1)}, bf16[8,16,128]{2,1,0:T(8,128)(2,1)S(1)}, u32[]{:S(2)}, u32[]{:S(2)}) collective-permute-start(bf16[8,16,128]{2,1,0:T(8,128)(2,1)S(1)} %get-tuple-element.30), channel_id=1, source_target_pairs={{0,8},{8,0},{16,24},{24,16},{1,9},{9,1},{17,25},{25,17},{2,10},{10... | collective-permute-start | bytes 98312 | tf_op jit(solution)/shard_map/ppermute | solution.py:299
  36.5 0.5 %shard_map.100.partial_ref = f32[768,128]{1,0:T(8,128)S(1)} custom-call(f32[8,768,128]{2,1,0:T(8,128)S(1)} %get-tuple-element.28.adjoint_ref, f32[768,128]{1,0:T(8,128)S(1)} %get-tuple-element.22.retain_ref, bf16[8,768,128]{2,1,0:T(8,128)(2,1)S(1)} %get-tuple-element.29.moved_ref), custom_call_target="tpu_custom_call" | custom-call | flops 1000000000 | bytes 1000000 | tf_op jit(solution)/shard_map/pallas_call | solution.py:287
  37.0 1.1 %collective-permute-done.12.rest_2_ = bf16[8,16,128]{2,1,0:T(8,128)(2,1)S(1)} collective-permute-done((bf16[8,16,128]{2,1,0:T(8,128)(2,1)S(1)}, bf16[8,16,128]{2,1,0:T(8,128)(2,1)S(1)}, u32[]{:S(2)}, u32[]{:S(2)}) %collective-permute-start.12) | collective-permute-done | bytes 32800 | tf_op jit(solution)/shard_map/ppermute | solution.py:299
  38.1 0.5 %collective-permute-done.11.rest_1_ = bf16[8,16,128]{2,1,0:T(8,128)(2,1)S(1)} collective-permute-done((bf16[8,16,128]{2,1,0:T(8,128)(2,1)S(1)}, bf16[8,16,128]{2,1,0:T(8,128)(2,1)S(1)}, u32[]{:S(2)}, u32[]{:S(2)}) %collective-permute-start.11) | collective-permute-done | bytes 32800 | tf_op jit(solution)/shard_map/ppermute | solution.py:299
  38.7 0.1 collective-permute-done.10.rest_0_
  38.8 1.3 %shard_map.101 = f32[48,1024]{1,0:T(8,128)} custom-call(f32[768,128]{1,0:T(8,128)S(1)} %shard_map.100.partial_ref, f32[768,128]{1,0:T(8,128)S(1)} %get-tuple-element.22.retain_ref, bf16[8,768,128]{2,1,0:T(8,128)(2,1)S(1)} %get-tuple-element.29.moved_ref, bf16[8,16,128]{2,1,0:T(8,128)(2,1)S(1)} %collective-permute-done.10.rest_0_, ...), custom_call_target="tpu_custom_call" | custom-call | flops 10000000000 | bytes 10000000 | tf_op jit(solution)/shard_map/pallas_call | solution.py:287
  (3 shorter events, 0.0 us)
Async XLA Ops:
  0.0 12.5 %copy-start.2 = (bf16[16,2,64,64]{3,2,1,0:T(8,128)(2,1)S(1)}, bf16[16,2,64,64]{3,2,1,0:T(8,128)(2,1)}, u32[]{:S(2)}) copy-start(bf16[16,2,64,64]{3,2,1,0:T(8,128)(2,1)} %remote_weight_ref.1) | copy-start | bytes 786436
  0.0 12.5 %copy-start.3 = (bf16[16,64,64]{2,1,0:T(8,128)(2,1)S(1)}, bf16[16,64,64]{2,1,0:T(8,128)(2,1)}, u32[]{:S(2)}) copy-start(bf16[16,64,64]{2,1,0:T(8,128)(2,1)} %inverse_ref.1) | copy-start | bytes 393220
  0.0 12.5 %copy-start.4 = (f32[48,1024]{1,0:T(8,128)S(1)}, f32[48,1024]{1,0:T(8,128)}, u32[]{:S(2)}) copy-start(f32[48,1024]{1,0:T(8,128)} %retention_ref.1) | copy-start | bytes 589828
  2.8 14.6 %collective-permute-start.3 = (bf16[2,384,128]{2,1,0:T(8,128)(2,1)}, bf16[2,384,128]{2,1,0:T(8,128)(2,1)S(1)}, u32[]{:S(2)}, u32[]{:S(2)}) collective-permute-start(bf16[2,384,128]{2,1,0:T(8,128)(2,1)} %shard_map.93.rest_3_), channel_id=1, source_target_pairs={{0,1},{1,0},{2,3},{3,2},{4,5},{5,4},{6,7},{7,6},{8,9},{9,8},{10,11... | collective-permute-start | bytes 589832 | tf_op jit(solution)/shard_map/ppermute | solution.py:299
  3.3 11.7 %collective-permute-start.2 = (bf16[2,384,128]{2,1,0:T(8,128)(2,1)}, bf16[2,384,128]{2,1,0:T(8,128)(2,1)S(1)}, u32[]{:S(2)}, u32[]{:S(2)}) collective-permute-start(bf16[2,384,128]{2,1,0:T(8,128)(2,1)} %shard_map.93.rest_3_), channel_id=1, source_target_pairs={{0,6},{1,7},{2,4},{3,5},{4,2},{5,3},{6,0},{7,1},{8,14},{9,15},{10,... | collective-permute-start | bytes 589832 | tf_op jit(solution)/shard_map/ppermute | solution.py:299
  6.9 9.9 %collective-permute-start.1 = (bf16[2,384,128]{2,1,0:T(8,128)(2,1)}, bf16[2,384,128]{2,1,0:T(8,128)(2,1)S(1)}, u32[]{:S(2)}, u32[]{:S(2)}) collective-permute-start(bf16[2,384,128]{2,1,0:T(8,128)(2,1)} %shard_map.93.rest_3_), channel_id=1, source_target_pairs={{0,4},{1,5},{2,6},{3,7},{4,0},{5,1},{6,2},{7,3},{8,12},{9,13},{10,... | collective-permute-start | bytes 589832 | tf_op jit(solution)/shard_map/ppermute | solution.py:299
  7.4 9.7 %collective-permute-start = (bf16[2,384,128]{2,1,0:T(8,128)(2,1)}, bf16[2,384,128]{2,1,0:T(8,128)(2,1)S(1)}, u32[]{:S(2)}, u32[]{:S(2)}) collective-permute-start(bf16[2,384,128]{2,1,0:T(8,128)(2,1)} %shard_map.93.rest_3_), channel_id=1, source_target_pairs={{0,2},{1,3},{2,0},{3,1},{4,6},{5,7},{6,4},{7,5},{8,10},{9,11},{10,... | collective-permute-start | bytes 589832 | tf_op jit(solution)/shard_map/ppermute | solution.py:299
  7.5 1.4 %copy-start = (bf16[48,16,1024]{2,1,0:T(8,128)(2,1)S(1)}, bf16[48,16,1024]{2,1,0:T(8,128)(2,1)}, u32[]{:S(2)}) copy-start(bf16[48,16,1024]{2,1,0:T(8,128)(2,1)} %z_hbm.1) | copy-start | bytes 4718596
  8.9 3.6 %copy-start.1 = (bf16[16,4,64,64]{3,2,1,0:T(8,128)(2,1)S(1)}, bf16[16,4,64,64]{3,2,1,0:T(8,128)(2,1)}, u32[]{:S(2)}) copy-start(bf16[16,4,64,64]{3,2,1,0:T(8,128)(2,1)} %weight_ref.1) | copy-start | bytes 1572868
  8.9 3.6 %copy-start.6 = (s32[16,4]{0,1:T(4,128)S(1)}, s32[16,4]{0,1:T(4,128)}, u32[]{:S(2)}) copy-start(s32[16,4]{0,1:T(4,128)} %param.10) | copy-start | bytes 772
  12.5 6.1 %copy-start.5 = (bf16[2,384,128]{2,1,0:T(8,128)(2,1)S(1)}, bf16[2,384,128]{2,1,0:T(8,128)(2,1)}, u32[]{:S(2)}) copy-start(bf16[2,384,128]{2,1,0:T(8,128)(2,1)} %shard_map.93.rest_3_) | copy-start | bytes 589828
  12.6 6.1 %copy-start.7 = (s32[16,2]{0,1:T(2,128)S(1)}, s32[16,2]{0,1:T(2,128)}, u32[]{:S(2)}) copy-start(s32[16,2]{0,1:T(2,128)} %param.11) | copy-start | bytes 388
  15.1 2.4 %collective-permute-start.4 = (bf16[2,384,128]{2,1,0:T(8,128)(2,1)S(1)}, bf16[2,384,128]{2,1,0:T(8,128)(2,1)S(1)}, u32[]{:S(2)}, u32[]{:S(2)}) collective-permute-start(bf16[2,384,128]{2,1,0:T(8,128)(2,1)S(1)} %shard_map.94.rest_4_), channel_id=1, source_target_pairs={{0,1},{1,0},{2,3},{3,2},{4,5},{5,4},{6,7},{7,6},{8,9},{9,8},{10,11... | collective-permute-start | bytes 589832 | tf_op jit(solution)/shard_map/ppermute | solution.py:299
  16.8 1.5 %collective-permute-start.5 = (bf16[2,384,128]{2,1,0:T(8,128)(2,1)S(1)}, bf16[2,384,128]{2,1,0:T(8,128)(2,1)S(1)}, u32[]{:S(2)}, u32[]{:S(2)}) collective-permute-start(bf16[2,384,128]{2,1,0:T(8,128)(2,1)S(1)} %shard_map.95.rest_5_), channel_id=1, source_target_pairs={{0,1},{1,0},{2,3},{3,2},{4,5},{5,4},{6,7},{7,6},{8,9},{9,8},{10,11... | collective-permute-start | bytes 589832 | tf_op jit(solution)/shard_map/ppermute | solution.py:299
  17.1 1.5 %collective-permute-start.6 = (bf16[2,384,128]{2,1,0:T(8,128)(2,1)S(1)}, bf16[2,384,128]{2,1,0:T(8,128)(2,1)S(1)}, u32[]{:S(2)}, u32[]{:S(2)}) collective-permute-start(bf16[2,384,128]{2,1,0:T(8,128)(2,1)S(1)} %shard_map.96.rest_6_), channel_id=1, source_target_pairs={{0,1},{1,0},{2,3},{3,2},{4,5},{5,4},{6,7},{7,6},{8,9},{9,8},{10,11... | collective-permute-start | bytes 589832 | tf_op jit(solution)/shard_map/ppermute | solution.py:299
  21.7 6.4 %collective-permute-start.9 = (bf16[9,16,128]{2,1,0:T(8,128)(2,1)S(1)}, bf16[9,16,128]{2,1,0:T(8,128)(2,1)S(1)}, u32[]{:S(2)}, u32[]{:S(2)}) collective-permute-start(bf16[9,16,128]{2,1,0:T(8,128)(2,1)S(1)} %get-tuple-element.27), channel_id=1, source_target_pairs={{0,24},{8,16},{16,8},{24,0},{1,25},{9,17},{17,9},{25,1},{2,26},{10... | collective-permute-start | bytes 110600 | tf_op jit(solution)/shard_map/ppermute | solution.py:299
  25.5 4.9 %collective-permute-start.8 = (bf16[9,16,128]{2,1,0:T(8,128)(2,1)S(1)}, bf16[9,16,128]{2,1,0:T(8,128)(2,1)S(1)}, u32[]{:S(2)}, u32[]{:S(2)}) collective-permute-start(bf16[9,16,128]{2,1,0:T(8,128)(2,1)S(1)} %get-tuple-element.27), channel_id=1, source_target_pairs={{0,16},{8,24},{16,0},{24,8},{1,17},{9,25},{17,1},{25,9},{2,18},{10... | collective-permute-start | bytes 110600 | tf_op jit(solution)/shard_map/ppermute | solution.py:299
  25.5 4.9 %collective-permute-start.7 = (bf16[9,16,128]{2,1,0:T(8,128)(2,1)S(1)}, bf16[9,16,128]{2,1,0:T(8,128)(2,1)S(1)}, u32[]{:S(2)}, u32[]{:S(2)}) collective-permute-start(bf16[9,16,128]{2,1,0:T(8,128)(2,1)S(1)} %get-tuple-element.27), channel_id=1, source_target_pairs={{0,8},{8,0},{16,24},{24,16},{1,9},{9,1},{17,25},{25,17},{2,10},{10... | collective-permute-start | bytes 110600 | tf_op jit(solution)/shard_map/ppermute | solution.py:299
  32.1 6.0 %collective-permute-start.12 = (bf16[8,16,128]{2,1,0:T(8,128)(2,1)S(1)}, bf16[8,16,128]{2,1,0:T(8,128)(2,1)S(1)}, u32[]{:S(2)}, u32[]{:S(2)}) collective-permute-start(bf16[8,16,128]{2,1,0:T(8,128)(2,1)S(1)} %get-tuple-element.30), channel_id=1, source_target_pairs={{0,24},{8,16},{16,8},{24,0},{1,25},{9,17},{17,9},{25,1},{2,26},{10... | collective-permute-start | bytes 98312 | tf_op jit(solution)/shard_map/ppermute | solution.py:299
  33.8 4.9 %collective-permute-start.11 = (bf16[8,16,128]{2,1,0:T(8,128)(2,1)S(1)}, bf16[8,16,128]{2,1,0:T(8,128)(2,1)S(1)}, u32[]{:S(2)}, u32[]{:S(2)}) collective-permute-start(bf16[8,16,128]{2,1,0:T(8,128)(2,1)S(1)} %get-tuple-element.30), channel_id=1, source_target_pairs={{0,16},{8,24},{16,0},{24,8},{1,17},{9,25},{17,1},{25,9},{2,18},{10... | collective-permute-start | bytes 98312 | tf_op jit(solution)/shard_map/ppermute | solution.py:299
  34.3 4.5 %collective-permute-start.10 = (bf16[8,16,128]{2,1,0:T(8,128)(2,1)S(1)}, bf16[8,16,128]{2,1,0:T(8,128)(2,1)S(1)}, u32[]{:S(2)}, u32[]{:S(2)}) collective-permute-start(bf16[8,16,128]{2,1,0:T(8,128)(2,1)S(1)} %get-tuple-element.30), channel_id=1, source_target_pairs={{0,8},{8,0},{16,24},{24,16},{1,9},{9,1},{17,25},{25,17},{2,10},{10... | collective-permute-start | bytes 98312 | tf_op jit(solution)/shard_map/ppermute | solution.py:299

commit v13 on v12

--- a/solution.py
+++ b/solution.py
@@ -18,6 +18,10 @@
     origin = (column % size) * probes + column // size
     row = lax.broadcasted_iota(jnp.int32, (total, width), 0)
     return (row == origin).astype(jnp.float32).astype(jnp.bfloat16)
+
+
+def turned_pair(weight):
+    return doubled(weight).astype(jnp.float32).T.astype(jnp.bfloat16)
 
 
 def doubled(weight):
@@ -42,27 +46,23 @@
         copy.start()
     row = lax.broadcasted_iota(jnp.int32, (part, part * blocks), 0)
     column = lax.broadcasted_iota(jnp.int32, (part, part * blocks), 1)
-    move = permutation(size, probes, 0, 2 * LANES)
+    step = 2 * LANES
+    shift, ranges = step // size, size * probes // step
+    move = permutation(size, probes, 0, step)
     listing.wait()
     picks = [(column == row * blocks + shared_ref[0, m]).astype(jnp.float32) for m in range(count)]
     picks = jnp.concatenate(picks, axis=0).astype(jnp.bfloat16)
-    picked = []
     for i, copy in enumerate(copies):
         copy.wait()
         z = z_ref[pl.ds(i * part, part)].reshape(part * blocks, size * probes)
-        picked.append(jnp.dot(picks, z, preferred_element_type=jnp.float32))
-    picked = jnp.concatenate([rows[m * part : (m + 1) * part] for m in range(count) for rows in picked], axis=0)
-    step = 2 * LANES
-    shift = step // size
-    ranges = size * probes // step
-    shifted = [picked] + [pltpu.roll(picked, size * probes - i * shift, 1) for i in range(1, ranges)]
-    shifted = jnp.concatenate(shifted, axis=0).astype(jnp.bfloat16)
-    moved = jnp.dot(shifted, move, preferred_element_type=jnp.float32)
-    moved = moved.astype(jnp.bfloat16)
-    for pair in range(size * probes // LANES):
-        for m in range(count):
-            row, lane = (pair // 2 * count + m) * days, pair % 2 * LANES
-            outgoing_ref[m, pl.ds(pair * days, days), :] = moved[row : row + days, lane : lane + LANES]
+        picked = jnp.dot(picks, z, preferred_element_type=jnp.float32)
+        shifted = [picked] + [pltpu.roll(picked, size * probes - k * shift, 1) for k in range(1, ranges)]
+        shifted = jnp.concatenate(shifted, axis=0).astype(jnp.bfloat16)
+        moved = jnp.dot(shifted, move, preferred_element_type=jnp.float32).astype(jnp.bfloat16)
+        for pair in range(size * probes // LANES):
+            for m in range(count):
+                row, lane = (pair // 2 * count + m) * part, pair % 2 * LANES
+                outgoing_ref[m, pl.ds(pair * days + i * part, part), :] = moved[row : row + part, lane : lane + LANES]
 
 
 def turn_kernel(dims, z_ref, moved_ref, turned_ref, stage):
@@ -85,7 +85,7 @@
 
 def local_kernel(
     dims, links_ref, days_ref, turned_ref, weight_ref, remote_weight_ref, inverse_ref, retention_ref,
-    running_ref, retain_ref, product_ref, remote_doubled_ref, inverse_doubled_ref,
+    running_ref, retain_ref, product_ref, remote_turned_ref, inverse_turned_ref, inverse_doubled_ref,
 ):
     days, blocks, size, probes = dims
     count = links_ref.shape[0]
@@ -94,9 +94,10 @@
         weight = jnp.concatenate([doubled(weight_ref[block, k]) for k in range(count)], axis=1)
         total = lax.dot_general(near, weight, TURNED, preferred_element_type=jnp.float32)
         running_ref[block] = turned_ref[block].astype(jnp.float32) - total
-        remote_doubled_ref[block] = jnp.concatenate(
-            [doubled(remote_weight_ref[block, k]) for k in range(remote_weight_ref.shape[1])], axis=1
+        remote_turned_ref[block] = jnp.concatenate(
+            [turned_pair(remote_weight_ref[block, k]) for k in range(remote_weight_ref.shape[1])], axis=0
         )
+        inverse_turned_ref[block] = turned_pair(inverse_ref[block])
         inverse_doubled_ref[block] = doubled(inverse_ref[block])
     observed = days_ref[0]
     shape = (days, LANES)
@@ -141,10 +142,10 @@
             distance = (link // bound) ^ me
             places.append((distance % 2) * held + (distance // 2) * bound + link % bound)
         far = jnp.concatenate([remote[place] for place in places], axis=1)
-        total = lax.dot_general(far, weight_ref[block], TURNED, preferred_element_type=jnp.float32)
+        total = jnp.dot(far, weight_ref[block], preferred_element_type=jnp.float32)
         source[block] = (running_ref[block] - total).astype(jnp.bfloat16)
     for block in range(blocks):
-        drive = lax.dot_general(source[block], inverse_ref[block], TURNED, preferred_element_type=jnp.float32)
+        drive = jnp.dot(source[block], inverse_ref[block], preferred_element_type=jnp.float32)
         for pair in range(pairs):
             forcing_ref[pair, pl.ds(block, days, stride=blocks), :] = jnp.where(
                 seen, drive[pair * days : (pair + 1) * days], 0.0
@@ -330,7 +331,7 @@
             pltpu.SMEM(shared_blocks.shape, jnp.int32),
             pltpu.VMEM(probes.shape, bf16),
             pltpu.SemaphoreType.DMA,
-            pltpu.SemaphoreType.DMA((2,)),
+            pltpu.SemaphoreType.DMA((days // 16,)),
         ],
         10**9, 4 * 10**6, 0, shared_blocks, probes, apart=(0, 1), limit=63 * 1024 * 1024,
     )
@@ -341,13 +342,14 @@
         [((pairs, rows, LANES), bf16), (by_block, bf16)],
         [pltpu.VMEM(*big)], 10**10, 10**7, 0, probes,
     )
-    running, retain, product, remote_weight, inverse = call(
+    running, retain, product, remote_weight, inverse_turned, inverse = call(
         functools.partial(local_kernel, dims),
         [
             (by_block, f32),
             ((rows, LANES), f32),
             ((blocks, LANES), bf16),
-            ((blocks, LANES, far * LANES), bf16),
+            ((blocks, far * LANES, LANES), bf16),
+            ((blocks, LANES, LANES), bf16),
             ((blocks, LANES, LANES), bf16),
         ],
         [], 10**10, 10**7, 2,
@@ -368,7 +370,7 @@
         [big, ((pairs + 1, blocks, LANES), bf16)],
         [pltpu.VMEM((2 * held, pairs * days, LANES), bf16), pltpu.VMEM((blocks, pairs * days, LANES), bf16)],
         10**10, 10**7, 2,
-        far_table, slab_days, running, remote_weight, inverse, retain, product, *raw, *same, *other,
+        far_table, slab_days, running, remote_weight, inverse_turned, retain, product, *raw, *same, *other,
         apart=range(7, 7 + len(raw)),
     )
     ends = exchange(message)

time: 40.3 us -> 40.9 us (1.015)
  Pallas kernels: 16.7 us -> 17.4 us
    pallas_call x11, Pallas kernels: 16.7 us -> 17.4 us  [call(): pl.pallas_call(kernel, out_shape=[jax.ShapeDtypeStruct(shape, kind) for s...]
  transfers between devices with their start and end apart: 13 -> 13, of which waited for: 8 -> 8; matrix products, arithmetic and copies ran while one was open for 0% -> 0% of each run, Pallas kernels for 20% -> 19%
where the time goes in v13:
time: 40.9 us; the launch traced here: 40.7 us
  Pallas kernels  17.4 us (43%)
  starting transfers between devices  14.2 us (35%)
  waiting for transfers between devices  6.94 us (17%)
  local copies, waits for them, and re-layouts  1.44 us (4%)
  between operations  0.8 us (2%)
    pallas_call x11, Pallas kernels, call(): pl.pallas_call(kernel, out_shape=[jax.ShapeDtypeStruct(shape, kind) for s...  17.4 us
    ppermute x13, starting transfers between devices, crossed(): lax.ppermute(block, axis, [(i, i ^ bits) for i in range(lax.axis_size(axi...  14.2 us
    ppermute x13, waiting for transfers between devices, crossed(): lax.ppermute(block, axis, [(i, i ^ bits) for i in range(lax.axis_size(axi...  6.94 us
    unnamed x16, local copies, waits for them, and re-layouts  1.44 us
  transfers between devices with their start and end apart: 13, of which 8 were waited for; matrix products, arithmetic and copies ran while one was open for 0% of the time, Pallas kernels for 19%

profile of v13, /device:TPU:0, one launch (start us, length us, event | category | flops | bytes accessed | tf_op | source)
XLA Modules:
  0.0 40.7 jit_solution(6070345051699210147)
XLA Ops:
  0.0 0.0 copy-start.2
  0.0 0.0 copy-start.3
  0.0 0.0 copy-start.4
  0.0 3.3 %shard_map.93.rest_3_ = bf16[2,384,128]{2,1,0:T(8,128)(2,1)} custom-call(s32[1,2]{1,0:T(1,128)} %shared_hbm.1, bf16[48,16,1024]{2,1,0:T(8,128)(2,1)} %z_hbm.1), custom_call_target="tpu_custom_call" | custom-call | flops 1000000000 | bytes 4000000 | tf_op jit(solution)/shard_map/pallas_call | solution.py:288
  3.4 0.5 %collective-permute-start.3 = (bf16[2,384,128]{2,1,0:T(8,128)(2,1)}, bf16[2,384,128]{2,1,0:T(8,128)(2,1)S(1)}, u32[]{:S(2)}, u32[]{:S(2)}) collective-permute-start(bf16[2,384,128]{2,1,0:T(8,128)(2,1)} %shard_map.93.rest_3_), channel_id=1, source_target_pairs={{0,1},{1,0},{2,3},{3,2},{4,5},{5,4},{6,7},{7,6},{8,9},{9,8},{10,11... | collective-permute-start | bytes 589832 | tf_op jit(solution)/shard_map/ppermute | solution.py:300
  3.9 3.5 %collective-permute-start.2 = (bf16[2,384,128]{2,1,0:T(8,128)(2,1)}, bf16[2,384,128]{2,1,0:T(8,128)(2,1)S(1)}, u32[]{:S(2)}, u32[]{:S(2)}) collective-permute-start(bf16[2,384,128]{2,1,0:T(8,128)(2,1)} %shard_map.93.rest_3_), channel_id=1, source_target_pairs={{0,6},{1,7},{2,4},{3,5},{4,2},{5,3},{6,0},{7,1},{8,14},{9,15},{10,... | collective-permute-start | bytes 589832 | tf_op jit(solution)/shard_map/ppermute | solution.py:300
  7.4 0.5 %collective-permute-start.1 = (bf16[2,384,128]{2,1,0:T(8,128)(2,1)}, bf16[2,384,128]{2,1,0:T(8,128)(2,1)S(1)}, u32[]{:S(2)}, u32[]{:S(2)}) collective-permute-start(bf16[2,384,128]{2,1,0:T(8,128)(2,1)} %shard_map.93.rest_3_), channel_id=1, source_target_pairs={{0,4},{1,5},{2,6},{3,7},{4,0},{5,1},{6,2},{7,3},{8,12},{9,13},{10,... | collective-permute-start | bytes 589832 | tf_op jit(solution)/shard_map/ppermute | solution.py:300
  7.9 0.1 collective-permute-start
  8.1 0.0 copy-start
  8.1 1.4 %copy-done = bf16[48,16,1024]{2,1,0:T(8,128)(2,1)S(1)} copy-done((bf16[48,16,1024]{2,1,0:T(8,128)(2,1)S(1)}, bf16[48,16,1024]{2,1,0:T(8,128)(2,1)}, u32[]{:S(2)}) %copy-start) | copy-done | bytes 1572888
  9.5 0.0 copy-start.1
  9.5 0.0 copy-start.6
  9.5 2.9 %shard_map.91 = (bf16[8,768,128]{2,1,0:T(8,128)(2,1)S(1)}, bf16[16,384,128]{2,1,0:T(8,128)(2,1)S(1)}) custom-call(bf16[48,16,1024]{2,1,0:T(8,128)(2,1)S(1)} %copy-done), custom_call_target="tpu_custom_call" | custom-call | flops 10000000000 | bytes 10000000 | tf_op jit(solution)/shard_map/pallas_call | solution.py:288
  13.0 0.0 copy-done.2
  13.0 0.0 copy-done.3
  13.0 0.0 copy-done.4
  13.1 0.0 copy-done.1
  13.1 0.0 copy-done.6
  13.1 0.0 copy-start.5
  13.1 0.0 copy-start.7
  13.1 2.6 %shard_map.92 = (f32[16,384,128]{2,1,0:T(8,128)S(1)}, f32[768,128]{1,0:T(8,128)S(1)}, bf16[16,128]{1,0:T(8,128)(2,1)S(1)}, bf16[16,256,128]{2,1,0:T(8,128)(2,1)S...) custom-call(s32[4,16]{1,0:T(4,128)S(1)} %bitcast.2, s32[1]{0:T(128)S(6)} %copy.10.days_ref, ...), custom_call_target="tpu_custom_call" | custom-call | flops 10000000000 | bytes 10000000 | tf_op jit(solution)/shard_map/pallas_call | solution.py:288
  15.7 0.0 collective-permute-done.2.piece_ref.rest_2_
  15.7 0.1 collective-permute-start.4
  15.8 1.5 %collective-permute-done.1.piece_ref.rest_1_ = bf16[2,384,128]{2,1,0:T(8,128)(2,1)S(1)} collective-permute-done((bf16[2,384,128]{2,1,0:T(8,128)(2,1)}, bf16[2,384,128]{2,1,0:T(8,128)(2,1)S(1)}, u32[]{:S(2)}, u32[]{:S(2)}) %collective-permute-start.1) | collective-permute-done | bytes 196640 | tf_op jit(solution)/shard_map/ppermute | solution.py:300
  17.3 0.1 collective-permute-start.5
  17.4 0.2 collective-permute-done.piece_ref.rest_0_
  17.6 0.4 collective-permute-start.6
  18.0 0.0 collective-permute-done.3.rest_7_
  18.0 0.0 collective-permute-done.4.rest_8_
  18.0 0.8 %collective-permute-done.5.rest_9_ = bf16[2,384,128]{2,1,0:T(8,128)(2,1)S(1)} collective-permute-done((bf16[2,384,128]{2,1,0:T(8,128)(2,1)S(1)}, bf16[2,384,128]{2,1,0:T(8,128)(2,1)S(1)}, u32[]{:S(2)}, u32[]{:S(2)}) %collective-permute-start.5) | collective-permute-done | bytes 196640 | tf_op jit(solution)/shard_map/ppermute | solution.py:300
  18.8 0.3 collective-permute-done.6.rest_10_
  19.2 0.0 copy-done.5
  19.2 0.0 copy-done.7
  19.2 3.1 %shard_map.97 = (f32[8,768,128]{2,1,0:T(8,128)S(1)}, bf16[9,16,128]{2,1,0:T(8,128)(2,1)S(1)}) custom-call(s32[2,16]{1,0:T(2,128)S(1)} %bitcast.3, s32[1]{0:T(128)S(6)} %copy.10.days_ref, f32[16,384,128]{2,1,0:T(8,128)S(1)} %get-tuple-element.20.running_ref, bf16[16,256,128]{2,1,0:T(8,128)(2,1)S(1)} %get-tuple-element.21.weight_ref, ...), custom_call_target="tpu_custom_call" | custom-call | flops 10000000000 | bytes 10000000 | tf_op jit(solution)/shard_map/pallas_call | solution.py:288
  22.3 3.8 %collective-permute-start.9 = (bf16[9,16,128]{2,1,0:T(8,128)(2,1)S(1)}, bf16[9,16,128]{2,1,0:T(8,128)(2,1)S(1)}, u32[]{:S(2)}, u32[]{:S(2)}) collective-permute-start(bf16[9,16,128]{2,1,0:T(8,128)(2,1)S(1)} %get-tuple-element.29), channel_id=1, source_target_pairs={{0,24},{8,16},{16,8},{24,0},{1,25},{9,17},{17,9},{25,1},{2,26},{10... | collective-permute-start | bytes 110600 | tf_op jit(solution)/shard_map/ppermute | solution.py:300
  26.1 0.0 collective-permute-start.8
  26.1 0.6 %collective-permute-start.7 = (bf16[9,16,128]{2,1,0:T(8,128)(2,1)S(1)}, bf16[9,16,128]{2,1,0:T(8,128)(2,1)S(1)}, u32[]{:S(2)}, u32[]{:S(2)}) collective-permute-start(bf16[9,16,128]{2,1,0:T(8,128)(2,1)S(1)} %get-tuple-element.29), channel_id=1, source_target_pairs={{0,8},{8,0},{16,24},{24,16},{1,9},{9,1},{17,25},{25,17},{2,10},{10... | collective-permute-start | bytes 110600 | tf_op jit(solution)/shard_map/ppermute | solution.py:300
  26.8 1.9 %shard_map.98 = (f32[16,384,128]{2,1,0:T(8,128)S(1)}, f32[16,48,128]{2,1,0:T(8,128)S(1)}) custom-call(f32[8,768,128]{2,1,0:T(8,128)S(1)} %get-tuple-element.25.forcing_ref, f32[768,128]{1,0:T(8,128)S(1)} %get-tuple-element.23.retain_ref), custom_call_target="tpu_custom_call" | custom-call | flops 1000000000 | bytes 1000000 | tf_op jit(solution)/shard_map/pallas_call | solution.py:288
  28.7 0.0 collective-permute-done.9.rest_2_.rest_5_
  28.7 2.3 %collective-permute-done.8.rest_1_.rest_4_ = bf16[9,16,128]{2,1,0:T(8,128)(2,1)S(1)} collective-permute-done((bf16[9,16,128]{2,1,0:T(8,128)(2,1)S(1)}, bf16[9,16,128]{2,1,0:T(8,128)(2,1)S(1)}, u32[]{:S(2)}, u32[]{:S(2)}) %collective-permute-start.8) | collective-permute-done | bytes 36896 | tf_op jit(solution)/shard_map/ppermute | solution.py:300
  31.0 0.0 collective-permute-done.7.rest_0_.rest_3_
  31.0 1.7 %shard_map.99 = (f32[8,768,128]{2,1,0:T(8,128)S(1)}, bf16[8,16,128]{2,1,0:T(8,128)(2,1)S(1)}) custom-call(s32[1]{0:T(128)S(6)} %copy.10.days_ref, f32[16,384,128]{2,1,0:T(8,128)S(1)} %get-tuple-element.26.states_ref, f32[16,48,128]{2,1,0:T(8,128)S(1)} %get-tuple-element.27.through_ref, f32[768,128]{1,0:T(8,128)S(1)} %get-tuple-element.23.retain_ref, ...), custom_call_target="tpu_custom_call" | custom-call | flops 10000000000 | bytes 10000000 | tf_op jit(solution)/shard_map/pallas_call | solution.py:288
  32.7 1.7 %collective-permute-start.12 = (bf16[8,16,128]{2,1,0:T(8,128)(2,1)S(1)}, bf16[8,16,128]{2,1,0:T(8,128)(2,1)S(1)}, u32[]{:S(2)}, u32[]{:S(2)}) collective-permute-start(bf16[8,16,128]{2,1,0:T(8,128)(2,1)S(1)} %get-tuple-element.32), channel_id=1, source_target_pairs={{0,24},{8,16},{16,8},{24,0},{1,25},{9,17},{17,9},{25,1},{2,26},{10... | collective-permute-start | bytes 98312 | tf_op jit(solution)/shard_map/ppermute | solution.py:300
  34.4 0.4 %collective-permute-start.11 = (bf16[8,16,128]{2,1,0:T(8,128)(2,1)S(1)}, bf16[8,16,128]{2,1,0:T(8,128)(2,1)S(1)}, u32[]{:S(2)}, u32[]{:S(2)}) collective-permute-start(bf16[8,16,128]{2,1,0:T(8,128)(2,1)S(1)} %get-tuple-element.32), channel_id=1, source_target_pairs={{0,16},{8,24},{16,0},{24,8},{1,17},{9,25},{17,1},{25,9},{2,18},{10... | collective-permute-start | bytes 98312 | tf_op jit(solution)/shard_map/ppermute | solution.py:300
  34.9 2.3 %collective-permute-start.10 = (bf16[8,16,128]{2,1,0:T(8,128)(2,1)S(1)}, bf16[8,16,128]{2,1,0:T(8,128)(2,1)S(1)}, u32[]{:S(2)}, u32[]{:S(2)}) collective-permute-start(bf16[8,16,128]{2,1,0:T(8,128)(2,1)S(1)} %get-tuple-element.32), channel_id=1, source_target_pairs={{0,8},{8,0},{16,24},{24,16},{1,9},{9,1},{17,25},{25,17},{2,10},{10... | collective-permute-start | bytes 98312 | tf_op jit(solution)/shard_map/ppermute | solution.py:300
  37.1 0.5 %shard_map.100.partial_ref = f32[768,128]{1,0:T(8,128)S(1)} custom-call(f32[8,768,128]{2,1,0:T(8,128)S(1)} %get-tuple-element.30.adjoint_ref, f32[768,128]{1,0:T(8,128)S(1)} %get-tuple-element.23.retain_ref, bf16[8,768,128]{2,1,0:T(8,128)(2,1)S(1)} %get-tuple-element.31.moved_ref), custom_call_target="tpu_custom_call" | custom-call | flops 1000000000 | bytes 1000000 | tf_op jit(solution)/shard_map/pallas_call | solution.py:288
  37.6 1.1 %collective-permute-done.12.rest_2_ = bf16[8,16,128]{2,1,0:T(8,128)(2,1)S(1)} collective-permute-done((bf16[8,16,128]{2,1,0:T(8,128)(2,1)S(1)}, bf16[8,16,128]{2,1,0:T(8,128)(2,1)S(1)}, u32[]{:S(2)}, u32[]{:S(2)}) %collective-permute-start.12) | collective-permute-done | bytes 32800 | tf_op jit(solution)/shard_map/ppermute | solution.py:300
  38.7 0.5 %collective-permute-done.11.rest_1_ = bf16[8,16,128]{2,1,0:T(8,128)(2,1)S(1)} collective-permute-done((bf16[8,16,128]{2,1,0:T(8,128)(2,1)S(1)}, bf16[8,16,128]{2,1,0:T(8,128)(2,1)S(1)}, u32[]{:S(2)}, u32[]{:S(2)}) %collective-permute-start.11) | collective-permute-done | bytes 32800 | tf_op jit(solution)/shard_map/ppermute | solution.py:300
  39.3 0.1 collective-permute-done.10.rest_0_
  39.4 1.3 %shard_map.101 = f32[48,1024]{1,0:T(8,128)} custom-call(f32[768,128]{1,0:T(8,128)S(1)} %shard_map.100.partial_ref, f32[768,128]{1,0:T(8,128)S(1)} %get-tuple-element.23.retain_ref, bf16[8,768,128]{2,1,0:T(8,128)(2,1)S(1)} %get-tuple-element.31.moved_ref, bf16[8,16,128]{2,1,0:T(8,128)(2,1)S(1)} %collective-permute-done.10.rest_0_, ...), custom_call_target="tpu_custom_call" | custom-call | flops 10000000000 | bytes 10000000 | tf_op jit(solution)/shard_map/pallas_call | solution.py:288
  (3 shorter events, 0.0 us)
Async XLA Ops:
  0.0 13.0 %copy-start.2 = (bf16[16,2,64,64]{3,2,1,0:T(8,128)(2,1)S(1)}, bf16[16,2,64,64]{3,2,1,0:T(8,128)(2,1)}, u32[]{:S(2)}) copy-start(bf16[16,2,64,64]{3,2,1,0:T(8,128)(2,1)} %remote_weight_ref.1) | copy-start | bytes 786436
  0.0 13.0 %copy-start.3 = (bf16[16,64,64]{2,1,0:T(8,128)(2,1)S(1)}, bf16[16,64,64]{2,1,0:T(8,128)(2,1)}, u32[]{:S(2)}) copy-start(bf16[16,64,64]{2,1,0:T(8,128)(2,1)} %inverse_ref.1) | copy-start | bytes 393220
  0.0 13.0 %copy-start.4 = (f32[48,1024]{1,0:T(8,128)S(1)}, f32[48,1024]{1,0:T(8,128)}, u32[]{:S(2)}) copy-start(f32[48,1024]{1,0:T(8,128)} %retention_ref.1) | copy-start | bytes 589828
  3.4 14.6 %collective-permute-start.3 = (bf16[2,384,128]{2,1,0:T(8,128)(2,1)}, bf16[2,384,128]{2,1,0:T(8,128)(2,1)S(1)}, u32[]{:S(2)}, u32[]{:S(2)}) collective-permute-start(bf16[2,384,128]{2,1,0:T(8,128)(2,1)} %shard_map.93.rest_3_), channel_id=1, source_target_pairs={{0,1},{1,0},{2,3},{3,2},{4,5},{5,4},{6,7},{7,6},{8,9},{9,8},{10,11... | collective-permute-start | bytes 589832 | tf_op jit(solution)/shard_map/ppermute | solution.py:300
  3.9 11.8 %collective-permute-start.2 = (bf16[2,384,128]{2,1,0:T(8,128)(2,1)}, bf16[2,384,128]{2,1,0:T(8,128)(2,1)S(1)}, u32[]{:S(2)}, u32[]{:S(2)}) collective-permute-start(bf16[2,384,128]{2,1,0:T(8,128)(2,1)} %shard_map.93.rest_3_), channel_id=1, source_target_pairs={{0,6},{1,7},{2,4},{3,5},{4,2},{5,3},{6,0},{7,1},{8,14},{9,15},{10,... | collective-permute-start | bytes 589832 | tf_op jit(solution)/shard_map/ppermute | solution.py:300
  7.4 9.9 %collective-permute-start.1 = (bf16[2,384,128]{2,1,0:T(8,128)(2,1)}, bf16[2,384,128]{2,1,0:T(8,128)(2,1)S(1)}, u32[]{:S(2)}, u32[]{:S(2)}) collective-permute-start(bf16[2,384,128]{2,1,0:T(8,128)(2,1)} %shard_map.93.rest_3_), channel_id=1, source_target_pairs={{0,4},{1,5},{2,6},{3,7},{4,0},{5,1},{6,2},{7,3},{8,12},{9,13},{10,... | collective-permute-start | bytes 589832 | tf_op jit(solution)/shard_map/ppermute | solution.py:300
  7.9 9.7 %collective-permute-start = (bf16[2,384,128]{2,1,0:T(8,128)(2,1)}, bf16[2,384,128]{2,1,0:T(8,128)(2,1)S(1)}, u32[]{:S(2)}, u32[]{:S(2)}) collective-permute-start(bf16[2,384,128]{2,1,0:T(8,128)(2,1)} %shard_map.93.rest_3_), channel_id=1, source_target_pairs={{0,2},{1,3},{2,0},{3,1},{4,6},{5,7},{6,4},{7,5},{8,10},{9,11},{10,... | collective-permute-start | bytes 589832 | tf_op jit(solution)/shard_map/ppermute | solution.py:300
  8.1 1.4 %copy-start = (bf16[48,16,1024]{2,1,0:T(8,128)(2,1)S(1)}, bf16[48,16,1024]{2,1,0:T(8,128)(2,1)}, u32[]{:S(2)}) copy-start(bf16[48,16,1024]{2,1,0:T(8,128)(2,1)} %z_hbm.1) | copy-start | bytes 4718596
  9.5 3.6 %copy-start.1 = (bf16[16,4,64,64]{3,2,1,0:T(8,128)(2,1)S(1)}, bf16[16,4,64,64]{3,2,1,0:T(8,128)(2,1)}, u32[]{:S(2)}) copy-start(bf16[16,4,64,64]{3,2,1,0:T(8,128)(2,1)} %weight_ref.1) | copy-start | bytes 1572868
  9.5 3.6 %copy-start.6 = (s32[16,4]{0,1:T(4,128)S(1)}, s32[16,4]{0,1:T(4,128)}, u32[]{:S(2)}) copy-start(s32[16,4]{0,1:T(4,128)} %param.10) | copy-start | bytes 772
  13.1 6.1 %copy-start.5 = (bf16[2,384,128]{2,1,0:T(8,128)(2,1)S(1)}, bf16[2,384,128]{2,1,0:T(8,128)(2,1)}, u32[]{:S(2)}) copy-start(bf16[2,384,128]{2,1,0:T(8,128)(2,1)} %shard_map.93.rest_3_) | copy-start | bytes 589828
  13.1 6.1 %copy-start.7 = (s32[16,2]{0,1:T(2,128)S(1)}, s32[16,2]{0,1:T(2,128)}, u32[]{:S(2)}) copy-start(s32[16,2]{0,1:T(2,128)} %param.11) | copy-start | bytes 388
  15.7 2.3 %collective-permute-start.4 = (bf16[2,384,128]{2,1,0:T(8,128)(2,1)S(1)}, bf16[2,384,128]{2,1,0:T(8,128)(2,1)S(1)}, u32[]{:S(2)}, u32[]{:S(2)}) collective-permute-start(bf16[2,384,128]{2,1,0:T(8,128)(2,1)S(1)} %shard_map.94.rest_4_), channel_id=1, source_target_pairs={{0,1},{1,0},{2,3},{3,2},{4,5},{5,4},{6,7},{7,6},{8,9},{9,8},{10,11... | collective-permute-start | bytes 589832 | tf_op jit(solution)/shard_map/ppermute | solution.py:300
  17.3 1.5 %collective-permute-start.5 = (bf16[2,384,128]{2,1,0:T(8,128)(2,1)S(1)}, bf16[2,384,128]{2,1,0:T(8,128)(2,1)S(1)}, u32[]{:S(2)}, u32[]{:S(2)}) collective-permute-start(bf16[2,384,128]{2,1,0:T(8,128)(2,1)S(1)} %shard_map.95.rest_5_), channel_id=1, source_target_pairs={{0,1},{1,0},{2,3},{3,2},{4,5},{5,4},{6,7},{7,6},{8,9},{9,8},{10,11... | collective-permute-start | bytes 589832 | tf_op jit(solution)/shard_map/ppermute | solution.py:300
  17.6 1.5 %collective-permute-start.6 = (bf16[2,384,128]{2,1,0:T(8,128)(2,1)S(1)}, bf16[2,384,128]{2,1,0:T(8,128)(2,1)S(1)}, u32[]{:S(2)}, u32[]{:S(2)}) collective-permute-start(bf16[2,384,128]{2,1,0:T(8,128)(2,1)S(1)} %shard_map.96.rest_6_), channel_id=1, source_target_pairs={{0,1},{1,0},{2,3},{3,2},{4,5},{5,4},{6,7},{7,6},{8,9},{9,8},{10,11... | collective-permute-start | bytes 589832 | tf_op jit(solution)/shard_map/ppermute | solution.py:300
  22.3 6.4 %collective-permute-start.9 = (bf16[9,16,128]{2,1,0:T(8,128)(2,1)S(1)}, bf16[9,16,128]{2,1,0:T(8,128)(2,1)S(1)}, u32[]{:S(2)}, u32[]{:S(2)}) collective-permute-start(bf16[9,16,128]{2,1,0:T(8,128)(2,1)S(1)} %get-tuple-element.29), channel_id=1, source_target_pairs={{0,24},{8,16},{16,8},{24,0},{1,25},{9,17},{17,9},{25,1},{2,26},{10... | collective-permute-start | bytes 110600 | tf_op jit(solution)/shard_map/ppermute | solution.py:300
  26.1 4.9 %collective-permute-start.8 = (bf16[9,16,128]{2,1,0:T(8,128)(2,1)S(1)}, bf16[9,16,128]{2,1,0:T(8,128)(2,1)S(1)}, u32[]{:S(2)}, u32[]{:S(2)}) collective-permute-start(bf16[9,16,128]{2,1,0:T(8,128)(2,1)S(1)} %get-tuple-element.29), channel_id=1, source_target_pairs={{0,16},{8,24},{16,0},{24,8},{1,17},{9,25},{17,1},{25,9},{2,18},{10... | collective-permute-start | bytes 110600 | tf_op jit(solution)/shard_map/ppermute | solution.py:300
  26.1 4.9 %collective-permute-start.7 = (bf16[9,16,128]{2,1,0:T(8,128)(2,1)S(1)}, bf16[9,16,128]{2,1,0:T(8,128)(2,1)S(1)}, u32[]{:S(2)}, u32[]{:S(2)}) collective-permute-start(bf16[9,16,128]{2,1,0:T(8,128)(2,1)S(1)} %get-tuple-element.29), channel_id=1, source_target_pairs={{0,8},{8,0},{16,24},{24,16},{1,9},{9,1},{17,25},{25,17},{2,10},{10... | collective-permute-start | bytes 110600 | tf_op jit(solution)/shard_map/ppermute | solution.py:300
  32.7 6.0 %collective-permute-start.12 = (bf16[8,16,128]{2,1,0:T(8,128)(2,1)S(1)}, bf16[8,16,128]{2,1,0:T(8,128)(2,1)S(1)}, u32[]{:S(2)}, u32[]{:S(2)}) collective-permute-start(bf16[8,16,128]{2,1,0:T(8,128)(2,1)S(1)} %get-tuple-element.32), channel_id=1, source_target_pairs={{0,24},{8,16},{16,8},{24,0},{1,25},{9,17},{17,9},{25,1},{2,26},{10... | collective-permute-start | bytes 98312 | tf_op jit(solution)/shard_map/ppermute | solution.py:300
  34.4 4.9 %collective-permute-start.11 = (bf16[8,16,128]{2,1,0:T(8,128)(2,1)S(1)}, bf16[8,16,128]{2,1,0:T(8,128)(2,1)S(1)}, u32[]{:S(2)}, u32[]{:S(2)}) collective-permute-start(bf16[8,16,128]{2,1,0:T(8,128)(2,1)S(1)} %get-tuple-element.32), channel_id=1, source_target_pairs={{0,16},{8,24},{16,0},{24,8},{1,17},{9,25},{17,1},{25,9},{2,18},{10... | collective-permute-start | bytes 98312 | tf_op jit(solution)/shard_map/ppermute | solution.py:300
  34.9 4.5 %collective-permute-start.10 = (bf16[8,16,128]{2,1,0:T(8,128)(2,1)S(1)}, bf16[8,16,128]{2,1,0:T(8,128)(2,1)S(1)}, u32[]{:S(2)}, u32[]{:S(2)}) collective-permute-start(bf16[8,16,128]{2,1,0:T(8,128)(2,1)S(1)} %get-tuple-element.32), channel_id=1, source_target_pairs={{0,8},{8,0},{16,24},{24,16},{1,9},{9,1},{17,25},{25,17},{2,10},{10... | collective-permute-start | bytes 98312 | tf_op jit(solution)/shard_map/ppermute | solution.py:300

commit v14 on v12

--- a/solution.py
+++ b/solution.py
@@ -85,7 +85,7 @@
 
 def local_kernel(
     dims, links_ref, days_ref, turned_ref, weight_ref, remote_weight_ref, inverse_ref, retention_ref,
-    running_ref, retain_ref, product_ref, remote_doubled_ref, inverse_doubled_ref,
+    running_ref, retain_ref, product_ref, remote_doubled_ref, inverse_doubled_ref, through_ref, beyond_ref, stage,
 ):
     days, blocks, size, probes = dims
     count = links_ref.shape[0]
@@ -109,30 +109,44 @@
         retain_ref[pl.ds(block + 1, days, stride=blocks), :] = jnp.where(first, other, factor)
     product = jnp.ones((blocks, LANES), jnp.float32)
     for day in range(days):
-        product = product * retain_ref[pl.ds(day * blocks, blocks), :]
+        rows = pl.ds(day * blocks, blocks)
+        product = product * retain_ref[rows, :]
+        stage[0, rows, :] = product
+    after = jnp.ones((blocks, LANES), jnp.float32)
+    for day in reversed(range(days)):
+        rows = pl.ds(day * blocks, blocks)
+        stage[1, rows, :] = after
+        after = after * retain_ref[rows, :]
+    for block in range(blocks):
+        through_ref[block] = stage[0, pl.ds(block, days, stride=blocks), :]
+        beyond_ref[block] = stage[1, pl.ds(block, days, stride=blocks), :]
     high = product.astype(jnp.bfloat16).astype(jnp.float32)
     half = lax.broadcasted_iota(jnp.int32, product.shape, 1) < size
     product_ref[...] = jnp.where(half, high, product - high).astype(jnp.bfloat16)
 
 
-def pass_kernel(piece_ref, product_ref, out_ref):
-    out_ref[...] = piece_ref[...]
+def pass_kernel(*refs):
+    *piece_refs, product_ref, out_ref = refs
+    count = piece_refs[0].shape[0]
+    for k, ref in enumerate(piece_refs):
+        out_ref[pl.ds(k * count, count)] = ref[...]
 
 
 def forward_kernel(
-    dims, pieces, links_ref, days_ref, running_ref, weight_ref, inverse_ref, retain_ref, product_ref, *rest
+    dims, pieces, links_ref, days_ref, running_ref, weight_ref, inverse_ref, beyond_ref, product_ref, *rest
 ):
     days, blocks, size, probes = dims
-    piece_refs = rest[pieces - 1 : 3 * pieces - 1]
-    forcing_ref, message_ref, remote, source = rest[3 * pieces - 1 :]
+    piece_refs = rest[pieces - 1 : -5]
+    forcing_ref, message_ref, remote, source, ends = rest[-5:]
     pairs = forcing_ref.shape[0]
     count = links_ref.shape[0]
     bound = piece_refs[0].shape[0]
     held = pieces * bound
     me = lax.axis_index("space")
-    for k, ref in enumerate(piece_refs):
+    arrived = [ref.at[pl.ds(start, bound)] for ref in piece_refs for start in range(0, ref.shape[0], bound)]
+    for k, ref in enumerate(arrived):
         chip = (pieces - k) % pieces
-        remote[pl.ds(k // pieces * held + chip % pieces * bound, bound)] = ref[...]
+        remote[pl.ds(k // pieces * held + chip * bound, bound)] = ref[...]
     seen = lax.broadcasted_iota(jnp.int32, (days, LANES), 0) < days_ref[0]
     for block in range(blocks):
         places = []
@@ -145,17 +159,12 @@
         source[block] = (running_ref[block] - total).astype(jnp.bfloat16)
     for block in range(blocks):
         drive = lax.dot_general(source[block], inverse_ref[block], TURNED, preferred_element_type=jnp.float32)
-        for pair in range(pairs):
-            forcing_ref[pair, pl.ds(block, days, stride=blocks), :] = jnp.where(
-                seen, drive[pair * days : (pair + 1) * days], 0.0
-            )
-    states = [jnp.zeros((blocks, LANES), jnp.float32)] * pairs
-    for day in range(days):
-        rows = pl.ds(day * blocks, blocks)
-        factor = retain_ref[rows, :]
-        for pair in range(pairs):
-            states[pair] = factor * states[pair] + forcing_ref[pair, rows, :]
-    leave(message_ref, states)
+        beyond = beyond_ref[block]
+        for pair in range(pairs):
+            tile = jnp.where(seen, drive[pair * days : (pair + 1) * days], 0.0)
+            forcing_ref[pair, pl.ds(block, days, stride=blocks), :] = tile
+            ends[pair, pl.ds(block, 1), :] = jnp.sum(beyond * tile, axis=0, keepdims=True)
+    leave(message_ref, [ends[pair] for pair in range(pairs)])
     message_ref[pairs] = product_ref[...]
 
 
@@ -183,28 +192,24 @@
     return carries
 
 
-def states_kernel(dims, forcing_ref, retain_ref, states_ref, through_ref, stage, products):
+def states_kernel(dims, forcing_ref, retain_ref, states_ref, stage):
     days, blocks, size, probes = dims
     pairs = forcing_ref.shape[0]
     states = [jnp.zeros((blocks, LANES), jnp.float32)] * pairs
-    product = jnp.ones((blocks, LANES), jnp.float32)
     for day in range(days):
         rows = pl.ds(day * blocks, blocks)
         factor = retain_ref[rows, :]
-        product = product * factor
-        products[rows, :] = product
         for pair in range(pairs):
             states[pair] = factor * states[pair] + forcing_ref[pair, rows, :]
             stage[pair, rows, :] = states[pair]
     for block in range(blocks):
-        through_ref[block] = products[pl.ds(block, days, stride=blocks), :]
         for pair in range(pairs):
             states_ref[block, pl.ds(pair * days, days), :] = stage[pair, pl.ds(block, days, stride=blocks), :]
 
 
-def adjoint_kernel(dims, hops, days_ref, states_ref, through_ref, retain_ref, inverse_ref, *rest):
-    days, blocks, size, probes = dims
-    adjoint_ref, message_ref, inbox, enter = rest[hops:]
+def adjoint_kernel(dims, hops, days_ref, states_ref, through_ref, inverse_ref, *rest):
+    days, blocks, size, probes = dims
+    adjoint_ref, message_ref, inbox, enter, starts = rest[hops:]
     pairs = adjoint_ref.shape[0]
     collect(rest[:hops], inbox)
     seen = lax.broadcasted_iota(jnp.int32, (days, LANES), 0) < days_ref[0]
@@ -219,16 +224,10 @@
         ]
         adjoint = jnp.dot(jnp.concatenate(stored, axis=0), inverse_ref[block], preferred_element_type=jnp.float32)
         for pair in range(pairs):
-            adjoint_ref[pair, pl.ds(block, days, stride=blocks), :] = jnp.where(
-                seen, adjoint[pair * days : (pair + 1) * days], 0.0
-            )
-    carries = [jnp.zeros((blocks, LANES), jnp.float32)] * pairs
-    for day in reversed(range(days)):
-        rows = pl.ds(day * blocks, blocks)
-        factor = retain_ref[rows, :]
-        for pair in range(pairs):
-            carries[pair] = factor * (adjoint_ref[pair, rows, :] + carries[pair])
-    leave(message_ref, carries)
+            tile = jnp.where(seen, adjoint[pair * days : (pair + 1) * days], 0.0)
+            adjoint_ref[pair, pl.ds(block, days, stride=blocks), :] = tile
+            starts[pair, pl.ds(block, 1), :] = jnp.sum(through * tile, axis=0, keepdims=True)
+    leave(message_ref, [starts[pair] for pair in range(pairs)])
 
 
 def own_kernel(dims, adjoint_ref, retain_ref, moved_ref, partial_ref):
@@ -341,7 +340,7 @@
         [((pairs, rows, LANES), bf16), (by_block, bf16)],
         [pltpu.VMEM(*big)], 10**10, 10**7, 0, probes,
     )
-    running, retain, product, remote_weight, inverse = call(
+    running, retain, product, remote_weight, inverse, through, beyond = call(
         functools.partial(local_kernel, dims),
         [
             (by_block, f32),
@@ -349,39 +348,38 @@
             ((blocks, LANES), bf16),
             ((blocks, LANES, far * LANES), bf16),
             ((blocks, LANES, LANES), bf16),
+            ((blocks, days, LANES), f32),
+            ((blocks, days, LANES), f32),
         ],
-        [], 10**10, 10**7, 2,
+        [pltpu.VMEM((2, rows, LANES), f32)], 10**10, 10**7, 2,
         near_table, slab_days, turned, local_coupling, remote_coupling, block_inverse, retention,
     )
-    same, other = {0: outgoing}, {0: crossed(outgoing, "space", 1)}
-    for bits in range(groups - 2, 0, -2):
-        (same[bits],) = call(pass_kernel, [(outgoing.shape, bf16)], [], 0, 10**5, 0, pieces[bits], product)
-        other[bits] = crossed(same[bits], "space", 1)
-    same, other = list(same.values()), list(other.values())
+    same = [outgoing]
+    for batch in ([groups - 2], list(range(groups - 4, 0, -2))):
+        shape = (len(batch) * bound, pairs * days, LANES)
+        same += call(pass_kernel, [(shape, bf16)], [], 0, 10**5, 0, *[pieces[bits] for bits in batch], product)
+    other = [crossed(piece, "space", 1) for piece in same]
     raw = [pieces[bits] for bits in range(2, groups, 2)]
     slabs = lax.axis_size("tm")
     hops = slabs - 1
     exchange = lambda message: [crossed(message, "tm", bits) for bits in range(hops, 0, -1)][::-1]
     inbox = pltpu.VMEM((slabs, pairs + 1, blocks, LANES), bf16)
+    values = pltpu.VMEM((pairs, blocks, LANES), f32)
     forcing, message = call(
-        functools.partial(forward_kernel, dims, len(same)),
+        functools.partial(forward_kernel, dims, groups // 2),
         [big, ((pairs + 1, blocks, LANES), bf16)],
-        [pltpu.VMEM((2 * held, pairs * days, LANES), bf16), pltpu.VMEM((blocks, pairs * days, LANES), bf16)],
-        10**10, 10**7, 2,
-        far_table, slab_days, running, remote_weight, inverse, retain, product, *raw, *same, *other,
+        [pltpu.VMEM((2 * held, pairs * days, LANES), bf16), pltpu.VMEM(by_block, bf16), values], 10**10, 10**7, 2,
+        far_table, slab_days, running, remote_weight, inverse, beyond, product, *raw, *same, *other,
         apart=range(7, 7 + len(raw)),
     )
     ends = exchange(message)
-    states, through = call(
-        functools.partial(states_kernel, dims),
-        [(by_block, f32), ((blocks, days, LANES), f32)],
-        [pltpu.VMEM(*big), pltpu.VMEM((rows, LANES), f32)], 10**9, 10**6, 0, forcing, retain,
+    (states,) = call(
+        functools.partial(states_kernel, dims), [(by_block, f32)], [pltpu.VMEM(*big)], 10**9, 10**6, 0, forcing, retain
     )
     adjoint, message = call(
         functools.partial(adjoint_kernel, dims, hops),
         [big, ((pairs, blocks, LANES), bf16)],
-        [inbox, pltpu.VMEM((pairs, blocks, LANES), f32)], 10**10, 10**7, 1,
-        slab_days, states, through, retain, inverse, *ends,
+        [inbox, values, values], 10**10, 10**7, 1, slab_days, states, through, inverse, *ends,
     )
     starts = exchange(message)
     (partial,) = call(

time: 40.3 us -> 40 us (level)
    pallas_call x11 -> x10, Pallas kernels: 16.7 us -> 16.5 us  [call(): pl.pallas_call(kernel, out_shape=[jax.ShapeDtypeStruct(shape, kind) for s...]
    ppermute x13 -> x12, waiting for transfers between devices: 7 us -> 6.88 us  [crossed(): lax.ppermute(block, axis, [(i, i ^ bits) for i in range(lax.axis_size(axi...]
    ppermute x13 -> x12, starting transfers between devices: 14.2 us -> 14.2 us  [crossed(): lax.ppermute(block, axis, [(i, i ^ bits) for i in range(lax.axis_size(axi...]
  transfers between devices with their start and end apart: 13 -> 12, of which waited for: 8 -> 8; matrix products, arithmetic and copies ran while one was open for 0% -> 0% of each run, Pallas kernels for 20% -> 20%
where the time goes in v14:
time: 40 us; the launch traced here: 39.9 us
  Pallas kernels  16.5 us (41%)
  starting transfers between devices  14.2 us (36%)
  waiting for transfers between devices  6.88 us (17%)
  local copies, waits for them, and re-layouts  1.44 us (4%)
  between operations  0.79 us (2%)
    pallas_call x10, Pallas kernels, call(): pl.pallas_call(kernel, out_shape=[jax.ShapeDtypeStruct(shape, kind) for s...  16.5 us
    ppermute x12, starting transfers between devices, crossed(): lax.ppermute(block, axis, [(i, i ^ bits) for i in range(lax.axis_size(axi...  14.2 us
    ppermute x12, waiting for transfers between devices, crossed(): lax.ppermute(block, axis, [(i, i ^ bits) for i in range(lax.axis_size(axi...  6.88 us
    unnamed x16, local copies, waits for them, and re-layouts  1.44 us
  transfers between devices with their start and end apart: 12, of which 8 were waited for; matrix products, arithmetic and copies ran while one was open for 0% of the time, Pallas kernels for 20%

profile of v14, /device:TPU:0, one launch (start us, length us, event | category | flops | bytes accessed | tf_op | source)
XLA Modules:
  0.0 39.9 jit_solution(15893779447511337755)
XLA Ops:
  0.0 0.0 copy-start.2
  0.0 0.0 copy-start.3
  0.0 0.0 copy-start.4
  0.0 2.8 %shard_map.93.rest_3_ = bf16[2,384,128]{2,1,0:T(8,128)(2,1)} custom-call(s32[1,2]{1,0:T(1,128)} %shared_hbm.1, bf16[48,16,1024]{2,1,0:T(8,128)(2,1)} %z_hbm.1), custom_call_target="tpu_custom_call" | custom-call | flops 1000000000 | bytes 4000000 | tf_op jit(solution)/shard_map/pallas_call | solution.py:286
  2.8 4.0 %collective-permute-start.2 = (bf16[2,384,128]{2,1,0:T(8,128)(2,1)}, bf16[2,384,128]{2,1,0:T(8,128)(2,1)S(1)}, u32[]{:S(2)}, u32[]{:S(2)}) collective-permute-start(bf16[2,384,128]{2,1,0:T(8,128)(2,1)} %shard_map.93.rest_3_), channel_id=1, source_target_pairs={{0,6},{1,7},{2,4},{3,5},{4,2},{5,3},{6,0},{7,1},{8,14},{9,15},{10,... | collective-permute-start | bytes 589832 | tf_op jit(solution)/shard_map/ppermute | solution.py:298
  6.8 0.5 %collective-permute-start.1 = (bf16[2,384,128]{2,1,0:T(8,128)(2,1)}, bf16[2,384,128]{2,1,0:T(8,128)(2,1)S(1)}, u32[]{:S(2)}, u32[]{:S(2)}) collective-permute-start(bf16[2,384,128]{2,1,0:T(8,128)(2,1)} %shard_map.93.rest_3_), channel_id=1, source_target_pairs={{0,4},{1,5},{2,6},{3,7},{4,0},{5,1},{6,2},{7,3},{8,12},{9,13},{10,... | collective-permute-start | bytes 589832 | tf_op jit(solution)/shard_map/ppermute | solution.py:298
  7.3 0.1 collective-permute-start
  7.4 0.0 copy-start
  7.4 1.4 %copy-done = bf16[48,16,1024]{2,1,0:T(8,128)(2,1)S(1)} copy-done((bf16[48,16,1024]{2,1,0:T(8,128)(2,1)S(1)}, bf16[48,16,1024]{2,1,0:T(8,128)(2,1)}, u32[]{:S(2)}) %copy-start) | copy-done | bytes 1572888
  8.8 0.0 copy-start.1
  8.8 0.0 copy-start.6
  8.8 2.9 %shard_map.91 = (bf16[8,768,128]{2,1,0:T(8,128)(2,1)S(1)}, bf16[16,384,128]{2,1,0:T(8,128)(2,1)S(1)}) custom-call(bf16[48,16,1024]{2,1,0:T(8,128)(2,1)S(1)} %copy-done), custom_call_target="tpu_custom_call" | custom-call | flops 10000000000 | bytes 10000000 | tf_op jit(solution)/shard_map/pallas_call | solution.py:286
  12.4 0.0 copy-done.2
  12.4 0.0 copy-done.3
  12.4 0.0 copy-done.4
  12.4 0.0 copy-done.1
  12.4 0.0 copy-done.6
  12.5 0.0 copy-start.5
  12.5 0.0 copy-start.7
  12.5 2.8 %shard_map.92 = (f32[16,384,128]{2,1,0:T(8,128)S(1)}, f32[768,128]{1,0:T(8,128)S(1)}, bf16[16,128]{1,0:T(8,128)(2,1)S(1)}, bf16[16,128,256]{2,1,0:T(8,128)(2,1)S...) custom-call(s32[4,16]{1,0:T(4,128)S(1)} %bitcast.2, ...), custom_call_target="tpu_custom_call" | custom-call | flops 10000000000 | bytes 10000000 | tf_op jit(solution)/shard_map/pallas_call | solution.py:286
  15.3 0.8 %collective-permute-done.1.refs_0_.rest_1_ = bf16[2,384,128]{2,1,0:T(8,128)(2,1)S(1)} collective-permute-done((bf16[2,384,128]{2,1,0:T(8,128)(2,1)}, bf16[2,384,128]{2,1,0:T(8,128)(2,1)S(1)}, u32[]{:S(2)}, u32[]{:S(2)}) %collective-permute-start.1) | collective-permute-done | bytes 196640 | tf_op jit(solution)/shard_map/ppermute | solution.py:298
  16.1 0.3 collective-permute-done.refs_1_.rest_0_
  16.4 0.1 collective-permute-start.5
  16.5 0.0 copy-done.5
  16.5 0.5 %collective-permute-start.3 = (bf16[2,384,128]{2,1,0:T(8,128)(2,1)S(1)}, bf16[2,384,128]{2,1,0:T(8,128)(2,1)S(1)}, u32[]{:S(2)}, u32[]{:S(2)}) collective-permute-start(bf16[2,384,128]{2,1,0:T(8,128)(2,1)S(1)} %copy-done.5), channel_id=1, source_target_pairs={{0,1},{1,0},{2,3},{3,2},{4,5},{5,4},{6,7},{7,6},{8,9},{9,8},{10,11... | collective-permute-start | bytes 589832 | tf_op jit(solution)/shard_map/ppermute | solution.py:298
  17.0 0.0 collective-permute-done.2.refs_0_.rest_2_
  17.0 0.2 collective-permute-start.4
  17.2 1.3 %collective-permute-done.3.rest_6_ = bf16[2,384,128]{2,1,0:T(8,128)(2,1)S(1)} collective-permute-done((bf16[2,384,128]{2,1,0:T(8,128)(2,1)S(1)}, bf16[2,384,128]{2,1,0:T(8,128)(2,1)S(1)}, u32[]{:S(2)}, u32[]{:S(2)}) %collective-permute-start.3) | collective-permute-done | bytes 196640 | tf_op jit(solution)/shard_map/ppermute | solution.py:298
  18.5 0.3 collective-permute-done.4.rest_7_
  18.8 0.0 collective-permute-done.5.rest_8_
  18.8 0.0 copy-done.7
  18.8 2.8 %shard_map.96 = (f32[8,768,128]{2,1,0:T(8,128)S(1)}, bf16[9,16,128]{2,1,0:T(8,128)(2,1)S(1)}) custom-call(s32[2,16]{1,0:T(2,128)S(1)} %bitcast.3, s32[1]{0:T(128)S(6)} %copy.10.days_ref, f32[16,384,128]{2,1,0:T(8,128)S(1)} %get-tuple-element.19.running_ref, bf16[16,128,256]{2,1,0:T(8,128)(2,1)S(1)} %get-tuple-element.20.weight_ref, ...), custom_call_target="tpu_custom_call" | custom-call | flops 10000000000 | bytes 10000000 | tf_op jit(solution)/shard_map/pallas_call | solution.py:286
  21.6 3.7 %collective-permute-start.8 = (bf16[9,16,128]{2,1,0:T(8,128)(2,1)S(1)}, bf16[9,16,128]{2,1,0:T(8,128)(2,1)S(1)}, u32[]{:S(2)}, u32[]{:S(2)}) collective-permute-start(bf16[9,16,128]{2,1,0:T(8,128)(2,1)S(1)} %get-tuple-element.27), channel_id=1, source_target_pairs={{0,24},{8,16},{16,8},{24,0},{1,25},{9,17},{17,9},{25,1},{2,26},{10... | collective-permute-start | bytes 110600 | tf_op jit(solution)/shard_map/ppermute | solution.py:298
  25.3 0.0 collective-permute-start.7
  25.3 0.8 %collective-permute-start.6 = (bf16[9,16,128]{2,1,0:T(8,128)(2,1)S(1)}, bf16[9,16,128]{2,1,0:T(8,128)(2,1)S(1)}, u32[]{:S(2)}, u32[]{:S(2)}) collective-permute-start(bf16[9,16,128]{2,1,0:T(8,128)(2,1)S(1)} %get-tuple-element.27), channel_id=1, source_target_pairs={{0,8},{8,0},{16,24},{24,16},{1,9},{9,1},{17,25},{25,17},{2,10},{10... | collective-permute-start | bytes 110600 | tf_op jit(solution)/shard_map/ppermute | solution.py:298
  26.1 1.7 %shard_map.97.states_ref = f32[16,384,128]{2,1,0:T(8,128)S(1)} custom-call(f32[8,768,128]{2,1,0:T(8,128)S(1)} %get-tuple-element.24.forcing_ref, f32[768,128]{1,0:T(8,128)S(1)} %get-tuple-element.25.retain_ref), custom_call_target="tpu_custom_call" | custom-call | flops 1000000000 | bytes 1000000 | tf_op jit(solution)/shard_map/pallas_call | solution.py:286
  27.7 0.0 collective-permute-done.8.rest_2_.rest_5_
  27.8 2.4 %collective-permute-done.7.rest_1_.rest_4_ = bf16[9,16,128]{2,1,0:T(8,128)(2,1)S(1)} collective-permute-done((bf16[9,16,128]{2,1,0:T(8,128)(2,1)S(1)}, bf16[9,16,128]{2,1,0:T(8,128)(2,1)S(1)}, u32[]{:S(2)}, u32[]{:S(2)}) %collective-permute-start.7) | collective-permute-done | bytes 36896 | tf_op jit(solution)/shard_map/ppermute | solution.py:298
  30.1 0.0 collective-permute-done.6.rest_0_.rest_3_
  30.2 1.7 %shard_map.98 = (f32[8,768,128]{2,1,0:T(8,128)S(1)}, bf16[8,16,128]{2,1,0:T(8,128)(2,1)S(1)}) custom-call(s32[1]{0:T(128)S(6)} %copy.10.days_ref, f32[16,384,128]{2,1,0:T(8,128)S(1)} %shard_map.97.states_ref, f32[16,48,128]{2,1,0:T(8,128)S(1)} %get-tuple-element.26.through_ref, bf16[16,128,128]{2,1,0:T(8,128)(2,1)S(1)} %get-tuple-element.21.inverse_ref, ...), custom_call_target="tpu_custom_call" | custom-call | flops 10000000000 | bytes 10000000 | tf_op jit(solution)/shard_map/pallas_call | solution.py:286
  31.8 1.7 %collective-permute-start.11 = (bf16[8,16,128]{2,1,0:T(8,128)(2,1)S(1)}, bf16[8,16,128]{2,1,0:T(8,128)(2,1)S(1)}, u32[]{:S(2)}, u32[]{:S(2)}) collective-permute-start(bf16[8,16,128]{2,1,0:T(8,128)(2,1)S(1)} %get-tuple-element.30), channel_id=1, source_target_pairs={{0,24},{8,16},{16,8},{24,0},{1,25},{9,17},{17,9},{25,1},{2,26},{10... | collective-permute-start | bytes 98312 | tf_op jit(solution)/shard_map/ppermute | solution.py:298
  33.5 0.5 %collective-permute-start.10 = (bf16[8,16,128]{2,1,0:T(8,128)(2,1)S(1)}, bf16[8,16,128]{2,1,0:T(8,128)(2,1)S(1)}, u32[]{:S(2)}, u32[]{:S(2)}) collective-permute-start(bf16[8,16,128]{2,1,0:T(8,128)(2,1)S(1)} %get-tuple-element.30), channel_id=1, source_target_pairs={{0,16},{8,24},{16,0},{24,8},{1,17},{9,25},{17,1},{25,9},{2,18},{10... | collective-permute-start | bytes 98312 | tf_op jit(solution)/shard_map/ppermute | solution.py:298
  34.0 2.3 %collective-permute-start.9 = (bf16[8,16,128]{2,1,0:T(8,128)(2,1)S(1)}, bf16[8,16,128]{2,1,0:T(8,128)(2,1)S(1)}, u32[]{:S(2)}, u32[]{:S(2)}) collective-permute-start(bf16[8,16,128]{2,1,0:T(8,128)(2,1)S(1)} %get-tuple-element.30), channel_id=1, source_target_pairs={{0,8},{8,0},{16,24},{24,16},{1,9},{9,1},{17,25},{25,17},{2,10},{10... | collective-permute-start | bytes 98312 | tf_op jit(solution)/shard_map/ppermute | solution.py:298
  36.3 0.5 %shard_map.99.partial_ref = f32[768,128]{1,0:T(8,128)S(1)} custom-call(f32[8,768,128]{2,1,0:T(8,128)S(1)} %get-tuple-element.28.adjoint_ref, f32[768,128]{1,0:T(8,128)S(1)} %get-tuple-element.25.retain_ref, bf16[8,768,128]{2,1,0:T(8,128)(2,1)S(1)} %get-tuple-element.29.moved_ref), custom_call_target="tpu_custom_call" | custom-call | flops 1000000000 | bytes 1000000 | tf_op jit(solution)/shard_map/pallas_call | solution.py:286
  36.8 0.9 %collective-permute-done.11.rest_2_ = bf16[8,16,128]{2,1,0:T(8,128)(2,1)S(1)} collective-permute-done((bf16[8,16,128]{2,1,0:T(8,128)(2,1)S(1)}, bf16[8,16,128]{2,1,0:T(8,128)(2,1)S(1)}, u32[]{:S(2)}, u32[]{:S(2)}) %collective-permute-start.11) | collective-permute-done | bytes 32800 | tf_op jit(solution)/shard_map/ppermute | solution.py:298
  37.6 0.8 %collective-permute-done.10.rest_1_ = bf16[8,16,128]{2,1,0:T(8,128)(2,1)S(1)} collective-permute-done((bf16[8,16,128]{2,1,0:T(8,128)(2,1)S(1)}, bf16[8,16,128]{2,1,0:T(8,128)(2,1)S(1)}, u32[]{:S(2)}, u32[]{:S(2)}) %collective-permute-start.10) | collective-permute-done | bytes 32800 | tf_op jit(solution)/shard_map/ppermute | solution.py:298
  38.5 0.1 collective-permute-done.9.rest_0_
  38.5 1.3 %shard_map.100 = f32[48,1024]{1,0:T(8,128)} custom-call(f32[768,128]{1,0:T(8,128)S(1)} %shard_map.99.partial_ref, f32[768,128]{1,0:T(8,128)S(1)} %get-tuple-element.25.retain_ref, bf16[8,768,128]{2,1,0:T(8,128)(2,1)S(1)} %get-tuple-element.29.moved_ref, bf16[8,16,128]{2,1,0:T(8,128)(2,1)S(1)} %collective-permute-done.9.rest_0_, ...), custom_call_target="tpu_custom_call" | custom-call | flops 10000000000 | bytes 10000000 | tf_op jit(solution)/shard_map/pallas_call | solution.py:286
  (2 shorter events, 0.0 us)
Async XLA Ops:
  0.0 12.4 %copy-start.2 = (bf16[16,2,64,64]{3,2,1,0:T(8,128)(2,1)S(1)}, bf16[16,2,64,64]{3,2,1,0:T(8,128)(2,1)}, u32[]{:S(2)}) copy-start(bf16[16,2,64,64]{3,2,1,0:T(8,128)(2,1)} %remote_weight_ref.1) | copy-start | bytes 786436
  0.0 12.4 %copy-start.3 = (bf16[16,64,64]{2,1,0:T(8,128)(2,1)S(1)}, bf16[16,64,64]{2,1,0:T(8,128)(2,1)}, u32[]{:S(2)}) copy-start(bf16[16,64,64]{2,1,0:T(8,128)(2,1)} %inverse_ref.1) | copy-start | bytes 393220
  0.0 12.4 %copy-start.4 = (f32[48,1024]{1,0:T(8,128)S(1)}, f32[48,1024]{1,0:T(8,128)}, u32[]{:S(2)}) copy-start(f32[48,1024]{1,0:T(8,128)} %retention_ref.1) | copy-start | bytes 589828
  2.8 14.2 %collective-permute-start.2 = (bf16[2,384,128]{2,1,0:T(8,128)(2,1)}, bf16[2,384,128]{2,1,0:T(8,128)(2,1)S(1)}, u32[]{:S(2)}, u32[]{:S(2)}) collective-permute-start(bf16[2,384,128]{2,1,0:T(8,128)(2,1)} %shard_map.93.rest_3_), channel_id=1, source_target_pairs={{0,6},{1,7},{2,4},{3,5},{4,2},{5,3},{6,0},{7,1},{8,14},{9,15},{10,... | collective-permute-start | bytes 589832 | tf_op jit(solution)/shard_map/ppermute | solution.py:298
  6.8 9.3 %collective-permute-start.1 = (bf16[2,384,128]{2,1,0:T(8,128)(2,1)}, bf16[2,384,128]{2,1,0:T(8,128)(2,1)S(1)}, u32[]{:S(2)}, u32[]{:S(2)}) collective-permute-start(bf16[2,384,128]{2,1,0:T(8,128)(2,1)} %shard_map.93.rest_3_), channel_id=1, source_target_pairs={{0,4},{1,5},{2,6},{3,7},{4,0},{5,1},{6,2},{7,3},{8,12},{9,13},{10,... | collective-permute-start | bytes 589832 | tf_op jit(solution)/shard_map/ppermute | solution.py:298
  7.3 9.1 %collective-permute-start = (bf16[2,384,128]{2,1,0:T(8,128)(2,1)}, bf16[2,384,128]{2,1,0:T(8,128)(2,1)S(1)}, u32[]{:S(2)}, u32[]{:S(2)}) collective-permute-start(bf16[2,384,128]{2,1,0:T(8,128)(2,1)} %shard_map.93.rest_3_), channel_id=1, source_target_pairs={{0,2},{1,3},{2,0},{3,1},{4,6},{5,7},{6,4},{7,5},{8,10},{9,11},{10,... | collective-permute-start | bytes 589832 | tf_op jit(solution)/shard_map/ppermute | solution.py:298
  7.4 1.4 %copy-start = (bf16[48,16,1024]{2,1,0:T(8,128)(2,1)S(1)}, bf16[48,16,1024]{2,1,0:T(8,128)(2,1)}, u32[]{:S(2)}) copy-start(bf16[48,16,1024]{2,1,0:T(8,128)(2,1)} %z_hbm.1) | copy-start | bytes 4718596
  8.8 3.6 %copy-start.1 = (bf16[16,4,64,64]{3,2,1,0:T(8,128)(2,1)S(1)}, bf16[16,4,64,64]{3,2,1,0:T(8,128)(2,1)}, u32[]{:S(2)}) copy-start(bf16[16,4,64,64]{3,2,1,0:T(8,128)(2,1)} %weight_ref.1) | copy-start | bytes 1572868
  8.8 3.6 %copy-start.6 = (s32[16,4]{0,1:T(4,128)S(1)}, s32[16,4]{0,1:T(4,128)}, u32[]{:S(2)}) copy-start(s32[16,4]{0,1:T(4,128)} %param.10) | copy-start | bytes 772
  12.5 4.1 %copy-start.5 = (bf16[2,384,128]{2,1,0:T(8,128)(2,1)S(1)}, bf16[2,384,128]{2,1,0:T(8,128)(2,1)}, u32[]{:S(2)}) copy-start(bf16[2,384,128]{2,1,0:T(8,128)(2,1)} %shard_map.93.rest_3_) | copy-start | bytes 589828
  12.5 6.3 %copy-start.7 = (s32[16,2]{0,1:T(2,128)S(1)}, s32[16,2]{0,1:T(2,128)}, u32[]{:S(2)}) copy-start(s32[16,2]{0,1:T(2,128)} %param.11) | copy-start | bytes 388
  16.4 2.4 %collective-permute-start.5 = (bf16[4,384,128]{2,1,0:T(8,128)(2,1)S(1)}, bf16[4,384,128]{2,1,0:T(8,128)(2,1)S(1)}, u32[]{:S(2)}, u32[]{:S(2)}) collective-permute-start(bf16[4,384,128]{2,1,0:T(8,128)(2,1)S(1)} %shard_map.95.rest_5_), channel_id=1, source_target_pairs={{0,1},{1,0},{2,3},{3,2},{4,5},{5,4},{6,7},{7,6},{8,9},{9,8},{10,11... | collective-permute-start | bytes 1179656 | tf_op jit(solution)/shard_map/ppermute | solution.py:298
  16.5 2.0 %collective-permute-start.3 = (bf16[2,384,128]{2,1,0:T(8,128)(2,1)S(1)}, bf16[2,384,128]{2,1,0:T(8,128)(2,1)S(1)}, u32[]{:S(2)}, u32[]{:S(2)}) collective-permute-start(bf16[2,384,128]{2,1,0:T(8,128)(2,1)S(1)} %copy-done.5), channel_id=1, source_target_pairs={{0,1},{1,0},{2,3},{3,2},{4,5},{5,4},{6,7},{7,6},{8,9},{9,8},{10,11... | collective-permute-start | bytes 589832 | tf_op jit(solution)/shard_map/ppermute | solution.py:298
  17.0 1.8 %collective-permute-start.4 = (bf16[2,384,128]{2,1,0:T(8,128)(2,1)S(1)}, bf16[2,384,128]{2,1,0:T(8,128)(2,1)S(1)}, u32[]{:S(2)}, u32[]{:S(2)}) collective-permute-start(bf16[2,384,128]{2,1,0:T(8,128)(2,1)S(1)} %shard_map.94.rest_4_), channel_id=1, source_target_pairs={{0,1},{1,0},{2,3},{3,2},{4,5},{5,4},{6,7},{7,6},{8,9},{9,8},{10,11... | collective-permute-start | bytes 589832 | tf_op jit(solution)/shard_map/ppermute | solution.py:298
  21.6 6.1 %collective-permute-start.8 = (bf16[9,16,128]{2,1,0:T(8,128)(2,1)S(1)}, bf16[9,16,128]{2,1,0:T(8,128)(2,1)S(1)}, u32[]{:S(2)}, u32[]{:S(2)}) collective-permute-start(bf16[9,16,128]{2,1,0:T(8,128)(2,1)S(1)} %get-tuple-element.27), channel_id=1, source_target_pairs={{0,24},{8,16},{16,8},{24,0},{1,25},{9,17},{17,9},{25,1},{2,26},{10... | collective-permute-start | bytes 110600 | tf_op jit(solution)/shard_map/ppermute | solution.py:298
  25.3 4.9 %collective-permute-start.7 = (bf16[9,16,128]{2,1,0:T(8,128)(2,1)S(1)}, bf16[9,16,128]{2,1,0:T(8,128)(2,1)S(1)}, u32[]{:S(2)}, u32[]{:S(2)}) collective-permute-start(bf16[9,16,128]{2,1,0:T(8,128)(2,1)S(1)} %get-tuple-element.27), channel_id=1, source_target_pairs={{0,16},{8,24},{16,0},{24,8},{1,17},{9,25},{17,1},{25,9},{2,18},{10... | collective-permute-start | bytes 110600 | tf_op jit(solution)/shard_map/ppermute | solution.py:298
  25.3 4.9 %collective-permute-start.6 = (bf16[9,16,128]{2,1,0:T(8,128)(2,1)S(1)}, bf16[9,16,128]{2,1,0:T(8,128)(2,1)S(1)}, u32[]{:S(2)}, u32[]{:S(2)}) collective-permute-start(bf16[9,16,128]{2,1,0:T(8,128)(2,1)S(1)} %get-tuple-element.27), channel_id=1, source_target_pairs={{0,8},{8,0},{16,24},{24,16},{1,9},{9,1},{17,25},{25,17},{2,10},{10... | collective-permute-start | bytes 110600 | tf_op jit(solution)/shard_map/ppermute | solution.py:298
  31.8 5.8 %collective-permute-start.11 = (bf16[8,16,128]{2,1,0:T(8,128)(2,1)S(1)}, bf16[8,16,128]{2,1,0:T(8,128)(2,1)S(1)}, u32[]{:S(2)}, u32[]{:S(2)}) collective-permute-start(bf16[8,16,128]{2,1,0:T(8,128)(2,1)S(1)} %get-tuple-element.30), channel_id=1, source_target_pairs={{0,24},{8,16},{16,8},{24,0},{1,25},{9,17},{17,9},{25,1},{2,26},{10... | collective-permute-start | bytes 98312 | tf_op jit(solution)/shard_map/ppermute | solution.py:298
  33.5 4.9 %collective-permute-start.10 = (bf16[8,16,128]{2,1,0:T(8,128)(2,1)S(1)}, bf16[8,16,128]{2,1,0:T(8,128)(2,1)S(1)}, u32[]{:S(2)}, u32[]{:S(2)}) collective-permute-start(bf16[8,16,128]{2,1,0:T(8,128)(2,1)S(1)} %get-tuple-element.30), channel_id=1, source_target_pairs={{0,16},{8,24},{16,0},{24,8},{1,17},{9,25},{17,1},{25,9},{2,18},{10... | collective-permute-start | bytes 98312 | tf_op jit(solution)/shard_map/ppermute | solution.py:298
  34.0 4.5 %collective-permute-start.9 = (bf16[8,16,128]{2,1,0:T(8,128)(2,1)S(1)}, bf16[8,16,128]{2,1,0:T(8,128)(2,1)S(1)}, u32[]{:S(2)}, u32[]{:S(2)}) collective-permute-start(bf16[8,16,128]{2,1,0:T(8,128)(2,1)S(1)} %get-tuple-element.30), channel_id=1, source_target_pairs={{0,8},{8,0},{16,24},{24,16},{1,9},{9,1},{17,25},{25,17},{2,10},{10... | collective-permute-start | bytes 98312 | tf_op jit(solution)/shard_map/ppermute | solution.py:298

commit v15 on v14

--- a/solution.py
+++ b/solution.py
@@ -133,20 +133,21 @@
 
 
 def forward_kernel(
-    dims, pieces, links_ref, days_ref, running_ref, weight_ref, inverse_ref, beyond_ref, product_ref, *rest
+    dims, batches, links_ref, days_ref, running_ref, weight_ref, inverse_ref, beyond_ref, product_ref, *rest
 ):
     days, blocks, size, probes = dims
-    piece_refs = rest[pieces - 1 : -5]
+    piece_refs = rest[-5 - 2 * len(batches) : -5]
     forcing_ref, message_ref, remote, source, ends = rest[-5:]
     pairs = forcing_ref.shape[0]
     count = links_ref.shape[0]
-    bound = piece_refs[0].shape[0]
-    held = pieces * bound
+    held = remote.shape[0] // 2
+    bound = piece_refs[0].shape[0] // len(batches[0])
     me = lax.axis_index("space")
-    arrived = [ref.at[pl.ds(start, bound)] for ref in piece_refs for start in range(0, ref.shape[0], bound)]
-    for k, ref in enumerate(arrived):
-        chip = (pieces - k) % pieces
-        remote[pl.ds(k // pieces * held + chip * bound, bound)] = ref[...]
+    for core in range(2):
+        for ref, batch in zip(piece_refs[core * len(batches) :], batches):
+            for place, bits in enumerate(batch):
+                if bits not in batch[:place]:
+                    remote[pl.ds(core * held + bits // 2 * bound, bound)] = ref[pl.ds(place * bound, bound)]
     seen = lax.broadcasted_iota(jnp.int32, (days, LANES), 0) < days_ref[0]
     for block in range(blocks):
         places = []
@@ -354,8 +355,10 @@
         [pltpu.VMEM((2, rows, LANES), f32)], 10**10, 10**7, 2,
         near_table, slab_days, turned, local_coupling, remote_coupling, block_inverse, retention,
     )
-    same = [outgoing]
-    for batch in ([groups - 2], list(range(groups - 4, 0, -2))):
+    pieces[0] = outgoing
+    batches = [0, groups - 2, groups - 2], list(range(groups - 4, 0, -2))
+    same = []
+    for batch in batches:
         shape = (len(batch) * bound, pairs * days, LANES)
         same += call(pass_kernel, [(shape, bf16)], [], 0, 10**5, 0, *[pieces[bits] for bits in batch], product)
     other = [crossed(piece, "space", 1) for piece in same]
@@ -366,7 +369,7 @@
     inbox = pltpu.VMEM((slabs, pairs + 1, blocks, LANES), bf16)
     values = pltpu.VMEM((pairs, blocks, LANES), f32)
     forcing, message = call(
-        functools.partial(forward_kernel, dims, groups // 2),
+        functools.partial(forward_kernel, dims, batches),
         [big, ((pairs + 1, blocks, LANES), bf16)],
         [pltpu.VMEM((2 * held, pairs * days, LANES), bf16), pltpu.VMEM(by_block, bf16), values], 10**10, 10**7, 2,
         far_table, slab_days, running, remote_weight, inverse, beyond, product, *raw, *same, *other,

time: 40 us -> 39.6 us (0.990)
  starting transfers between devices: 14.2 us -> 13.7 us
    ppermute x12 -> x11, starting transfers between devices: 14.2 us -> 13.7 us  [crossed(): lax.ppermute(block, axis, [(i, i ^ bits) for i in range(lax.axis_size(axi...]
    ppermute x12 -> x11, waiting for transfers between devices: 6.88 us -> 6.98 us  [crossed(): lax.ppermute(block, axis, [(i, i ^ bits) for i in range(lax.axis_size(axi...]
  transfers between devices with their start and end apart: 12 -> 11, of which waited for: 8 -> 7; matrix products, arithmetic and copies ran while one was open for 0% -> 0% of each run, Pallas kernels for 20% -> 20%
where the time goes in v15:
time: 39.6 us; the launch traced here: 39.4 us
  Pallas kernels  16.5 us (42%)
  starting transfers between devices  13.7 us (35%)
  waiting for transfers between devices  6.98 us (18%)
  local copies, waits for them, and re-layouts  1.44 us (4%)
  between operations  0.8 us (2%)
    pallas_call x10, Pallas kernels, call(): pl.pallas_call(kernel, out_shape=[jax.ShapeDtypeStruct(shape, kind) for s...  16.5 us
    ppermute x11, starting transfers between devices, crossed(): lax.ppermute(block, axis, [(i, i ^ bits) for i in range(lax.axis_size(axi...  13.7 us
    ppermute x11, waiting for transfers between devices, crossed(): lax.ppermute(block, axis, [(i, i ^ bits) for i in range(lax.axis_size(axi...  6.98 us
    unnamed x16, local copies, waits for them, and re-layouts  1.44 us
  transfers between devices with their start and end apart: 11, of which 7 were waited for; matrix products, arithmetic and copies ran while one was open for 0% of the time, Pallas kernels for 20%

profile of v15, /device:TPU:0, one launch (start us, length us, event | category | flops | bytes accessed | tf_op | source)
XLA Modules:
  0.0 39.4 jit_solution(17554511893308639025)
XLA Ops:
  0.0 0.0 copy-start.3
  0.0 0.0 copy-start.4
  0.0 0.0 copy-start.5
  0.0 2.8 %shard_map.93.refs_0_ = bf16[2,384,128]{2,1,0:T(8,128)(2,1)} custom-call(s32[1,2]{1,0:T(1,128)} %shared_hbm.1, bf16[48,16,1024]{2,1,0:T(8,128)(2,1)} %z_hbm.1), custom_call_target="tpu_custom_call" | custom-call | flops 1000000000 | bytes 4000000 | tf_op jit(solution)/shard_map/pallas_call | solution.py:287
  2.8 4.0 %collective-permute-start.2 = (bf16[2,384,128]{2,1,0:T(8,128)(2,1)}, bf16[2,384,128]{2,1,0:T(8,128)(2,1)S(1)}, u32[]{:S(2)}, u32[]{:S(2)}) collective-permute-start(bf16[2,384,128]{2,1,0:T(8,128)(2,1)} %shard_map.93.refs_0_), channel_id=1, source_target_pairs={{0,6},{1,7},{2,4},{3,5},{4,2},{5,3},{6,0},{7,1},{8,14},{9,15},{10,... | collective-permute-start | bytes 589832 | tf_op jit(solution)/shard_map/ppermute | solution.py:299
  6.8 0.5 %collective-permute-start.1 = (bf16[2,384,128]{2,1,0:T(8,128)(2,1)}, bf16[2,384,128]{2,1,0:T(8,128)(2,1)S(1)}, u32[]{:S(2)}, u32[]{:S(2)}) collective-permute-start(bf16[2,384,128]{2,1,0:T(8,128)(2,1)} %shard_map.93.refs_0_), channel_id=1, source_target_pairs={{0,4},{1,5},{2,6},{3,7},{4,0},{5,1},{6,2},{7,3},{8,12},{9,13},{10,... | collective-permute-start | bytes 589832 | tf_op jit(solution)/shard_map/ppermute | solution.py:299
  7.3 0.1 collective-permute-start
  7.4 0.0 copy-start.1
  7.4 1.4 %copy-done.1 = bf16[48,16,1024]{2,1,0:T(8,128)(2,1)S(1)} copy-done((bf16[48,16,1024]{2,1,0:T(8,128)(2,1)S(1)}, bf16[48,16,1024]{2,1,0:T(8,128)(2,1)}, u32[]{:S(2)}) %copy-start.1) | copy-done | bytes 1572888
  8.8 0.0 copy-start.2
  8.8 0.0 copy-start.6
  8.8 2.9 %shard_map.91 = (bf16[8,768,128]{2,1,0:T(8,128)(2,1)S(1)}, bf16[16,384,128]{2,1,0:T(8,128)(2,1)S(1)}) custom-call(bf16[48,16,1024]{2,1,0:T(8,128)(2,1)S(1)} %copy-done.1), custom_call_target="tpu_custom_call" | custom-call | flops 10000000000 | bytes 10000000 | tf_op jit(solution)/shard_map/pallas_call | solution.py:287
  12.4 0.0 copy-done.3
  12.4 0.0 copy-done.4
  12.4 0.0 copy-done.5
  12.4 0.0 copy-done.2
  12.4 0.0 copy-done.6
  12.5 0.0 copy-start
  12.5 0.0 copy-start.7
  12.5 2.8 %shard_map.92 = (f32[16,384,128]{2,1,0:T(8,128)S(1)}, f32[768,128]{1,0:T(8,128)S(1)}, bf16[16,128]{1,0:T(8,128)(2,1)S(1)}, bf16[16,128,256]{2,1,0:T(8,128)(2,1)S...) custom-call(s32[4,16]{1,0:T(4,128)S(1)} %bitcast.2, ...), custom_call_target="tpu_custom_call" | custom-call | flops 10000000000 | bytes 10000000 | tf_op jit(solution)/shard_map/pallas_call | solution.py:287
  15.3 0.0 collective-permute-done.2.refs_1_.refs_2_.rest_2_
  15.3 0.0 copy-done
  15.3 0.1 collective-permute-start.3
  15.4 0.7 %collective-permute-done.1.refs_0_.rest_1_ = bf16[2,384,128]{2,1,0:T(8,128)(2,1)S(1)} collective-permute-done((bf16[2,384,128]{2,1,0:T(8,128)(2,1)}, bf16[2,384,128]{2,1,0:T(8,128)(2,1)S(1)}, u32[]{:S(2)}, u32[]{:S(2)}) %collective-permute-start.1) | collective-permute-done | bytes 196640 | tf_op jit(solution)/shard_map/ppermute | solution.py:299
  16.1 0.3 collective-permute-done.refs_1_.rest_0_
  16.4 0.1 collective-permute-start.4
  16.5 1.7 %collective-permute-done.4.rest_6_ = bf16[4,384,128]{2,1,0:T(8,128)(2,1)S(1)} collective-permute-done((bf16[4,384,128]{2,1,0:T(8,128)(2,1)S(1)}, bf16[4,384,128]{2,1,0:T(8,128)(2,1)S(1)}, u32[]{:S(2)}, u32[]{:S(2)}) %collective-permute-start.4) | collective-permute-done | bytes 393248 | tf_op jit(solution)/shard_map/ppermute | solution.py:299
  18.2 0.0 collective-permute-done.3.rest_5_
  18.2 0.0 copy-done.7
  18.2 2.8 %shard_map.96 = (f32[8,768,128]{2,1,0:T(8,128)S(1)}, bf16[9,16,128]{2,1,0:T(8,128)(2,1)S(1)}) custom-call(s32[2,16]{1,0:T(2,128)S(1)} %bitcast.3, s32[1]{0:T(128)S(6)} %copy.10.days_ref, f32[16,384,128]{2,1,0:T(8,128)S(1)} %get-tuple-element.19.running_ref, bf16[16,128,256]{2,1,0:T(8,128)(2,1)S(1)} %get-tuple-element.20.weight_ref, ...), custom_call_target="tpu_custom_call" | custom-call | flops 10000000000 | bytes 10000000 | tf_op jit(solution)/shard_map/pallas_call | solution.py:287
  21.0 3.8 %collective-permute-start.7 = (bf16[9,16,128]{2,1,0:T(8,128)(2,1)S(1)}, bf16[9,16,128]{2,1,0:T(8,128)(2,1)S(1)}, u32[]{:S(2)}, u32[]{:S(2)}) collective-permute-start(bf16[9,16,128]{2,1,0:T(8,128)(2,1)S(1)} %get-tuple-element.27), channel_id=1, source_target_pairs={{0,24},{8,16},{16,8},{24,0},{1,25},{9,17},{17,9},{25,1},{2,26},{10... | collective-permute-start | bytes 110600 | tf_op jit(solution)/shard_map/ppermute | solution.py:299
  24.8 0.0 collective-permute-start.6
  24.8 0.6 %collective-permute-start.5 = (bf16[9,16,128]{2,1,0:T(8,128)(2,1)S(1)}, bf16[9,16,128]{2,1,0:T(8,128)(2,1)S(1)}, u32[]{:S(2)}, u32[]{:S(2)}) collective-permute-start(bf16[9,16,128]{2,1,0:T(8,128)(2,1)S(1)} %get-tuple-element.27), channel_id=1, source_target_pairs={{0,8},{8,0},{16,24},{24,16},{1,9},{9,1},{17,25},{25,17},{2,10},{10... | collective-permute-start | bytes 110600 | tf_op jit(solution)/shard_map/ppermute | solution.py:299
  25.5 1.7 %shard_map.97.states_ref = f32[16,384,128]{2,1,0:T(8,128)S(1)} custom-call(f32[8,768,128]{2,1,0:T(8,128)S(1)} %get-tuple-element.24.forcing_ref, f32[768,128]{1,0:T(8,128)S(1)} %get-tuple-element.25.retain_ref), custom_call_target="tpu_custom_call" | custom-call | flops 1000000000 | bytes 1000000 | tf_op jit(solution)/shard_map/pallas_call | solution.py:287
  27.2 0.0 collective-permute-done.7.rest_2_.rest_5_
  27.2 2.5 %collective-permute-done.6.rest_1_.rest_4_ = bf16[9,16,128]{2,1,0:T(8,128)(2,1)S(1)} collective-permute-done((bf16[9,16,128]{2,1,0:T(8,128)(2,1)S(1)}, bf16[9,16,128]{2,1,0:T(8,128)(2,1)S(1)}, u32[]{:S(2)}, u32[]{:S(2)}) %collective-permute-start.6) | collective-permute-done | bytes 36896 | tf_op jit(solution)/shard_map/ppermute | solution.py:299
  29.7 0.0 collective-permute-done.5.rest_0_.rest_3_
  29.7 1.7 %shard_map.98 = (f32[8,768,128]{2,1,0:T(8,128)S(1)}, bf16[8,16,128]{2,1,0:T(8,128)(2,1)S(1)}) custom-call(s32[1]{0:T(128)S(6)} %copy.10.days_ref, f32[16,384,128]{2,1,0:T(8,128)S(1)} %shard_map.97.states_ref, f32[16,48,128]{2,1,0:T(8,128)S(1)} %get-tuple-element.26.through_ref, bf16[16,128,128]{2,1,0:T(8,128)(2,1)S(1)} %get-tuple-element.21.inverse_ref, ...), custom_call_target="tpu_custom_call" | custom-call | flops 10000000000 | bytes 10000000 | tf_op jit(solution)/shard_map/pallas_call | solution.py:287
  31.4 1.7 %collective-permute-start.10 = (bf16[8,16,128]{2,1,0:T(8,128)(2,1)S(1)}, bf16[8,16,128]{2,1,0:T(8,128)(2,1)S(1)}, u32[]{:S(2)}, u32[]{:S(2)}) collective-permute-start(bf16[8,16,128]{2,1,0:T(8,128)(2,1)S(1)} %get-tuple-element.30), channel_id=1, source_target_pairs={{0,24},{8,16},{16,8},{24,0},{1,25},{9,17},{17,9},{25,1},{2,26},{10... | collective-permute-start | bytes 98312 | tf_op jit(solution)/shard_map/ppermute | solution.py:299
  33.1 0.5 %collective-permute-start.9 = (bf16[8,16,128]{2,1,0:T(8,128)(2,1)S(1)}, bf16[8,16,128]{2,1,0:T(8,128)(2,1)S(1)}, u32[]{:S(2)}, u32[]{:S(2)}) collective-permute-start(bf16[8,16,128]{2,1,0:T(8,128)(2,1)S(1)} %get-tuple-element.30), channel_id=1, source_target_pairs={{0,16},{8,24},{16,0},{24,8},{1,17},{9,25},{17,1},{25,9},{2,18},{10... | collective-permute-start | bytes 98312 | tf_op jit(solution)/shard_map/ppermute | solution.py:299
  33.5 2.3 %collective-permute-start.8 = (bf16[8,16,128]{2,1,0:T(8,128)(2,1)S(1)}, bf16[8,16,128]{2,1,0:T(8,128)(2,1)S(1)}, u32[]{:S(2)}, u32[]{:S(2)}) collective-permute-start(bf16[8,16,128]{2,1,0:T(8,128)(2,1)S(1)} %get-tuple-element.30), channel_id=1, source_target_pairs={{0,8},{8,0},{16,24},{24,16},{1,9},{9,1},{17,25},{25,17},{2,10},{10... | collective-permute-start | bytes 98312 | tf_op jit(solution)/shard_map/ppermute | solution.py:299
  35.8 0.5 %shard_map.99.partial_ref = f32[768,128]{1,0:T(8,128)S(1)} custom-call(f32[8,768,128]{2,1,0:T(8,128)S(1)} %get-tuple-element.28.adjoint_ref, f32[768,128]{1,0:T(8,128)S(1)} %get-tuple-element.25.retain_ref, bf16[8,768,128]{2,1,0:T(8,128)(2,1)S(1)} %get-tuple-element.29.moved_ref), custom_call_target="tpu_custom_call" | custom-call | flops 1000000000 | bytes 1000000 | tf_op jit(solution)/shard_map/pallas_call | solution.py:287
  36.3 0.9 %collective-permute-done.10.rest_2_ = bf16[8,16,128]{2,1,0:T(8,128)(2,1)S(1)} collective-permute-done((bf16[8,16,128]{2,1,0:T(8,128)(2,1)S(1)}, bf16[8,16,128]{2,1,0:T(8,128)(2,1)S(1)}, u32[]{:S(2)}, u32[]{:S(2)}) %collective-permute-start.10) | collective-permute-done | bytes 32800 | tf_op jit(solution)/shard_map/ppermute | solution.py:299
  37.2 0.8 %collective-permute-done.9.rest_1_ = bf16[8,16,128]{2,1,0:T(8,128)(2,1)S(1)} collective-permute-done((bf16[8,16,128]{2,1,0:T(8,128)(2,1)S(1)}, bf16[8,16,128]{2,1,0:T(8,128)(2,1)S(1)}, u32[]{:S(2)}, u32[]{:S(2)}) %collective-permute-start.9) | collective-permute-done | bytes 32800 | tf_op jit(solution)/shard_map/ppermute | solution.py:299
  38.0 0.1 collective-permute-done.8.rest_0_
  38.1 1.3 %shard_map.100 = f32[48,1024]{1,0:T(8,128)} custom-call(f32[768,128]{1,0:T(8,128)S(1)} %shard_map.99.partial_ref, f32[768,128]{1,0:T(8,128)S(1)} %get-tuple-element.25.retain_ref, bf16[8,768,128]{2,1,0:T(8,128)(2,1)S(1)} %get-tuple-element.29.moved_ref, bf16[8,16,128]{2,1,0:T(8,128)(2,1)S(1)} %collective-permute-done.8.rest_0_, ...), custom_call_target="tpu_custom_call" | custom-call | flops 10000000000 | bytes 10000000 | tf_op jit(solution)/shard_map/pallas_call | solution.py:287
  (2 shorter events, 0.1 us)
Async XLA Ops:
  0.0 12.4 %copy-start.3 = (bf16[16,2,64,64]{3,2,1,0:T(8,128)(2,1)S(1)}, bf16[16,2,64,64]{3,2,1,0:T(8,128)(2,1)}, u32[]{:S(2)}) copy-start(bf16[16,2,64,64]{3,2,1,0:T(8,128)(2,1)} %remote_weight_ref.1) | copy-start | bytes 786436
  0.0 12.4 %copy-start.4 = (bf16[16,64,64]{2,1,0:T(8,128)(2,1)S(1)}, bf16[16,64,64]{2,1,0:T(8,128)(2,1)}, u32[]{:S(2)}) copy-start(bf16[16,64,64]{2,1,0:T(8,128)(2,1)} %inverse_ref.1) | copy-start | bytes 393220
  0.0 12.4 %copy-start.5 = (f32[48,1024]{1,0:T(8,128)S(1)}, f32[48,1024]{1,0:T(8,128)}, u32[]{:S(2)}) copy-start(f32[48,1024]{1,0:T(8,128)} %retention_ref.1) | copy-start | bytes 589828
  2.8 12.5 %collective-permute-start.2 = (bf16[2,384,128]{2,1,0:T(8,128)(2,1)}, bf16[2,384,128]{2,1,0:T(8,128)(2,1)S(1)}, u32[]{:S(2)}, u32[]{:S(2)}) collective-permute-start(bf16[2,384,128]{2,1,0:T(8,128)(2,1)} %shard_map.93.refs_0_), channel_id=1, source_target_pairs={{0,6},{1,7},{2,4},{3,5},{4,2},{5,3},{6,0},{7,1},{8,14},{9,15},{10,... | collective-permute-start | bytes 589832 | tf_op jit(solution)/shard_map/ppermute | solution.py:299
  6.8 9.3 %collective-permute-start.1 = (bf16[2,384,128]{2,1,0:T(8,128)(2,1)}, bf16[2,384,128]{2,1,0:T(8,128)(2,1)S(1)}, u32[]{:S(2)}, u32[]{:S(2)}) collective-permute-start(bf16[2,384,128]{2,1,0:T(8,128)(2,1)} %shard_map.93.refs_0_), channel_id=1, source_target_pairs={{0,4},{1,5},{2,6},{3,7},{4,0},{5,1},{6,2},{7,3},{8,12},{9,13},{10,... | collective-permute-start | bytes 589832 | tf_op jit(solution)/shard_map/ppermute | solution.py:299
  7.3 9.1 %collective-permute-start = (bf16[2,384,128]{2,1,0:T(8,128)(2,1)}, bf16[2,384,128]{2,1,0:T(8,128)(2,1)S(1)}, u32[]{:S(2)}, u32[]{:S(2)}) collective-permute-start(bf16[2,384,128]{2,1,0:T(8,128)(2,1)} %shard_map.93.refs_0_), channel_id=1, source_target_pairs={{0,2},{1,3},{2,0},{3,1},{4,6},{5,7},{6,4},{7,5},{8,10},{9,11},{10,... | collective-permute-start | bytes 589832 | tf_op jit(solution)/shard_map/ppermute | solution.py:299
  7.4 1.4 %copy-start.1 = (bf16[48,16,1024]{2,1,0:T(8,128)(2,1)S(1)}, bf16[48,16,1024]{2,1,0:T(8,128)(2,1)}, u32[]{:S(2)}) copy-start(bf16[48,16,1024]{2,1,0:T(8,128)(2,1)} %z_hbm.1) | copy-start | bytes 4718596
  8.8 3.6 %copy-start.2 = (bf16[16,4,64,64]{3,2,1,0:T(8,128)(2,1)S(1)}, bf16[16,4,64,64]{3,2,1,0:T(8,128)(2,1)}, u32[]{:S(2)}) copy-start(bf16[16,4,64,64]{3,2,1,0:T(8,128)(2,1)} %weight_ref.1) | copy-start | bytes 1572868
  8.8 3.6 %copy-start.6 = (s32[16,4]{0,1:T(4,128)S(1)}, s32[16,4]{0,1:T(4,128)}, u32[]{:S(2)}) copy-start(s32[16,4]{0,1:T(4,128)} %param.10) | copy-start | bytes 772
  12.5 2.8 %copy-start = (bf16[2,384,128]{2,1,0:T(8,128)(2,1)S(1)}, bf16[2,384,128]{2,1,0:T(8,128)(2,1)}, u32[]{:S(2)}) copy-start(bf16[2,384,128]{2,1,0:T(8,128)(2,1)} %shard_map.93.refs_0_) | copy-start | bytes 589828
  12.5 5.8 %copy-start.7 = (s32[16,2]{0,1:T(2,128)S(1)}, s32[16,2]{0,1:T(2,128)}, u32[]{:S(2)}) copy-start(s32[16,2]{0,1:T(2,128)} %param.11) | copy-start | bytes 388
  15.3 2.9 %collective-permute-start.3 = (bf16[6,384,128]{2,1,0:T(8,128)(2,1)S(1)}, bf16[6,384,128]{2,1,0:T(8,128)(2,1)S(1)}, u32[]{:S(2)}, u32[]{:S(2)}) collective-permute-start(bf16[6,384,128]{2,1,0:T(8,128)(2,1)S(1)} %shard_map.94.rest_3_), channel_id=1, source_target_pairs={{0,1},{1,0},{2,3},{3,2},{4,5},{5,4},{6,7},{7,6},{8,9},{9,8},{10,11... | collective-permute-start | bytes 1769480 | tf_op jit(solution)/shard_map/ppermute | solution.py:299
  16.4 1.8 %collective-permute-start.4 = (bf16[4,384,128]{2,1,0:T(8,128)(2,1)S(1)}, bf16[4,384,128]{2,1,0:T(8,128)(2,1)S(1)}, u32[]{:S(2)}, u32[]{:S(2)}) collective-permute-start(bf16[4,384,128]{2,1,0:T(8,128)(2,1)S(1)} %shard_map.95.rest_4_), channel_id=1, source_target_pairs={{0,1},{1,0},{2,3},{3,2},{4,5},{5,4},{6,7},{7,6},{8,9},{9,8},{10,11... | collective-permute-start | bytes 1179656 | tf_op jit(solution)/shard_map/ppermute | solution.py:299
  21.0 6.1 %collective-permute-start.7 = (bf16[9,16,128]{2,1,0:T(8,128)(2,1)S(1)}, bf16[9,16,128]{2,1,0:T(8,128)(2,1)S(1)}, u32[]{:S(2)}, u32[]{:S(2)}) collective-permute-start(bf16[9,16,128]{2,1,0:T(8,128)(2,1)S(1)} %get-tuple-element.27), channel_id=1, source_target_pairs={{0,24},{8,16},{16,8},{24,0},{1,25},{9,17},{17,9},{25,1},{2,26},{10... | collective-permute-start | bytes 110600 | tf_op jit(solution)/shard_map/ppermute | solution.py:299
  24.8 4.9 %collective-permute-start.6 = (bf16[9,16,128]{2,1,0:T(8,128)(2,1)S(1)}, bf16[9,16,128]{2,1,0:T(8,128)(2,1)S(1)}, u32[]{:S(2)}, u32[]{:S(2)}) collective-permute-start(bf16[9,16,128]{2,1,0:T(8,128)(2,1)S(1)} %get-tuple-element.27), channel_id=1, source_target_pairs={{0,16},{8,24},{16,0},{24,8},{1,17},{9,25},{17,1},{25,9},{2,18},{10... | collective-permute-start | bytes 110600 | tf_op jit(solution)/shard_map/ppermute | solution.py:299
  24.8 4.9 %collective-permute-start.5 = (bf16[9,16,128]{2,1,0:T(8,128)(2,1)S(1)}, bf16[9,16,128]{2,1,0:T(8,128)(2,1)S(1)}, u32[]{:S(2)}, u32[]{:S(2)}) collective-permute-start(bf16[9,16,128]{2,1,0:T(8,128)(2,1)S(1)} %get-tuple-element.27), channel_id=1, source_target_pairs={{0,8},{8,0},{16,24},{24,16},{1,9},{9,1},{17,25},{25,17},{2,10},{10... | collective-permute-start | bytes 110600 | tf_op jit(solution)/shard_map/ppermute | solution.py:299
  31.4 5.8 %collective-permute-start.10 = (bf16[8,16,128]{2,1,0:T(8,128)(2,1)S(1)}, bf16[8,16,128]{2,1,0:T(8,128)(2,1)S(1)}, u32[]{:S(2)}, u32[]{:S(2)}) collective-permute-start(bf16[8,16,128]{2,1,0:T(8,128)(2,1)S(1)} %get-tuple-element.30), channel_id=1, source_target_pairs={{0,24},{8,16},{16,8},{24,0},{1,25},{9,17},{17,9},{25,1},{2,26},{10... | collective-permute-start | bytes 98312 | tf_op jit(solution)/shard_map/ppermute | solution.py:299
  33.1 4.9 %collective-permute-start.9 = (bf16[8,16,128]{2,1,0:T(8,128)(2,1)S(1)}, bf16[8,16,128]{2,1,0:T(8,128)(2,1)S(1)}, u32[]{:S(2)}, u32[]{:S(2)}) collective-permute-start(bf16[8,16,128]{2,1,0:T(8,128)(2,1)S(1)} %get-tuple-element.30), channel_id=1, source_target_pairs={{0,16},{8,24},{16,0},{24,8},{1,17},{9,25},{17,1},{25,9},{2,18},{10... | collective-permute-start | bytes 98312 | tf_op jit(solution)/shard_map/ppermute | solution.py:299
  33.5 4.5 %collective-permute-start.8 = (bf16[8,16,128]{2,1,0:T(8,128)(2,1)S(1)}, bf16[8,16,128]{2,1,0:T(8,128)(2,1)S(1)}, u32[]{:S(2)}, u32[]{:S(2)}) collective-permute-start(bf16[8,16,128]{2,1,0:T(8,128)(2,1)S(1)} %get-tuple-element.30), channel_id=1, source_target_pairs={{0,8},{8,0},{16,24},{24,16},{1,9},{9,1},{17,25},{25,17},{2,10},{10... | collective-permute-start | bytes 98312 | tf_op jit(solution)/shard_map/ppermute | solution.py:299

commit v16 on v15

--- a/solution.py
+++ b/solution.py
@@ -84,8 +84,8 @@
 
 
 def local_kernel(
-    dims, links_ref, days_ref, turned_ref, weight_ref, remote_weight_ref, inverse_ref, retention_ref,
-    running_ref, retain_ref, product_ref, remote_doubled_ref, inverse_doubled_ref, through_ref, beyond_ref, stage,
+    dims, links_ref, turned_ref, weight_ref, remote_weight_ref, inverse_ref,
+    running_ref, remote_doubled_ref, inverse_doubled_ref,
 ):
     days, blocks, size, probes = dims
     count = links_ref.shape[0]
@@ -98,10 +98,17 @@
             [doubled(remote_weight_ref[block, k]) for k in range(remote_weight_ref.shape[1])], axis=1
         )
         inverse_doubled_ref[block] = doubled(inverse_ref[block])
+
+
+def retain_kernel(
+    dims, days_ref, retention_ref, retain_ref, product_ref, through_ref, beyond_ref, active_ref, stage
+):
+    days, blocks, size, probes = dims
     observed = days_ref[0]
     shape = (days, LANES)
     first = lax.broadcasted_iota(jnp.int32, shape, 1) < size
     seen = lax.broadcasted_iota(jnp.int32, shape, 0) < observed
+    active_ref[...] = jnp.where(seen, 1.0, 0.0)
     for block in range(0, blocks, 2):
         factor = jnp.where(seen, retention_ref[:, pl.ds(block * size, LANES)], 1.0)
         other = pltpu.roll(factor, size, 1)
@@ -126,14 +133,14 @@
 
 
 def pass_kernel(*refs):
-    *piece_refs, product_ref, out_ref = refs
+    *piece_refs, before_ref, out_ref = refs
     count = piece_refs[0].shape[0]
     for k, ref in enumerate(piece_refs):
         out_ref[pl.ds(k * count, count)] = ref[...]
 
 
 def forward_kernel(
-    dims, batches, links_ref, days_ref, running_ref, weight_ref, inverse_ref, beyond_ref, product_ref, *rest
+    dims, batches, links_ref, active_ref, running_ref, weight_ref, inverse_ref, beyond_ref, product_ref, *rest
 ):
     days, blocks, size, probes = dims
     piece_refs = rest[-5 - 2 * len(batches) : -5]
@@ -148,7 +155,7 @@
             for place, bits in enumerate(batch):
                 if bits not in batch[:place]:
                     remote[pl.ds(core * held + bits // 2 * bound, bound)] = ref[pl.ds(place * bound, bound)]
-    seen = lax.broadcasted_iota(jnp.int32, (days, LANES), 0) < days_ref[0]
+    active = active_ref[...]
     for block in range(blocks):
         places = []
         for k in range(count):
@@ -162,7 +169,7 @@
         drive = lax.dot_general(source[block], inverse_ref[block], TURNED, preferred_element_type=jnp.float32)
         beyond = beyond_ref[block]
         for pair in range(pairs):
-            tile = jnp.where(seen, drive[pair * days : (pair + 1) * days], 0.0)
+            tile = active * drive[pair * days : (pair + 1) * days]
             forcing_ref[pair, pl.ds(block, days, stride=blocks), :] = tile
             ends[pair, pl.ds(block, 1), :] = jnp.sum(beyond * tile, axis=0, keepdims=True)
     leave(message_ref, [ends[pair] for pair in range(pairs)])
@@ -208,12 +215,12 @@
             states_ref[block, pl.ds(pair * days, days), :] = stage[pair, pl.ds(block, days, stride=blocks), :]
 
 
-def adjoint_kernel(dims, hops, days_ref, states_ref, through_ref, inverse_ref, *rest):
+def adjoint_kernel(dims, hops, active_ref, states_ref, through_ref, inverse_ref, *rest):
     days, blocks, size, probes = dims
     adjoint_ref, message_ref, inbox, enter, starts = rest[hops:]
     pairs = adjoint_ref.shape[0]
     collect(rest[:hops], inbox)
-    seen = lax.broadcasted_iota(jnp.int32, (days, LANES), 0) < days_ref[0]
+    active = active_ref[...]
     for pair, carry in enumerate(carried(pairs, inbox, inbox, False)):
         enter[pair] = carry
     for block in range(blocks):
@@ -225,7 +232,7 @@
         ]
         adjoint = jnp.dot(jnp.concatenate(stored, axis=0), inverse_ref[block], preferred_element_type=jnp.float32)
         for pair in range(pairs):
-            tile = jnp.where(seen, adjoint[pair * days : (pair + 1) * days], 0.0)
+            tile = active * adjoint[pair * days : (pair + 1) * days]
             adjoint_ref[pair, pl.ds(block, days, stride=blocks), :] = tile
             starts[pair, pl.ds(block, 1), :] = jnp.sum(through * tile, axis=0, keepdims=True)
     leave(message_ref, [starts[pair] for pair in range(pairs)])
@@ -341,26 +348,28 @@
         [((pairs, rows, LANES), bf16), (by_block, bf16)],
         [pltpu.VMEM(*big)], 10**10, 10**7, 0, probes,
     )
-    running, retain, product, remote_weight, inverse, through, beyond = call(
+    running, remote_weight, inverse = call(
         functools.partial(local_kernel, dims),
+        [(by_block, f32), ((blocks, LANES, far * LANES), bf16), ((blocks, LANES, LANES), bf16)],
+        [], 10**10, 10**7, 1, near_table, turned, local_coupling, remote_coupling, block_inverse,
+    )
+    retain, product, through, beyond, active = call(
+        functools.partial(retain_kernel, dims),
         [
-            (by_block, f32),
             ((rows, LANES), f32),
             ((blocks, LANES), bf16),
-            ((blocks, LANES, far * LANES), bf16),
-            ((blocks, LANES, LANES), bf16),
             ((blocks, days, LANES), f32),
             ((blocks, days, LANES), f32),
+            ((days, LANES), f32),
         ],
-        [pltpu.VMEM((2, rows, LANES), f32)], 10**10, 10**7, 2,
-        near_table, slab_days, turned, local_coupling, remote_coupling, block_inverse, retention,
+        [pltpu.VMEM((2, rows, LANES), f32)], 10**6, 10**5, 1, slab_days, retention,
     )
     pieces[0] = outgoing
     batches = [0, groups - 2, groups - 2], list(range(groups - 4, 0, -2))
     same = []
     for batch in batches:
         shape = (len(batch) * bound, pairs * days, LANES)
-        same += call(pass_kernel, [(shape, bf16)], [], 0, 10**5, 0, *[pieces[bits] for bits in batch], product)
+        same += call(pass_kernel, [(shape, bf16)], [], 0, 10**5, 0, *[pieces[bits] for bits in batch], inverse)
     other = [crossed(piece, "space", 1) for piece in same]
     raw = [pieces[bits] for bits in range(2, groups, 2)]
     slabs = lax.axis_size("tm")
@@ -371,8 +380,8 @@
     forcing, message = call(
         functools.partial(forward_kernel, dims, batches),
         [big, ((pairs + 1, blocks, LANES), bf16)],
-        [pltpu.VMEM((2 * held, pairs * days, LANES), bf16), pltpu.VMEM(by_block, bf16), values], 10**10, 10**7, 2,
-        far_table, slab_days, running, remote_weight, inverse, beyond, product, *raw, *same, *other,
+        [pltpu.VMEM((2 * held, pairs * days, LANES), bf16), pltpu.VMEM(by_block, bf16), values], 10**10, 10**7, 1,
+        far_table, active, running, remote_weight, inverse, beyond, product, *raw, *same, *other,
         apart=range(7, 7 + len(raw)),
     )
     ends = exchange(message)
@@ -382,7 +391,7 @@
     adjoint, message = call(
         functools.partial(adjoint_kernel, dims, hops),
         [big, ((pairs, blocks, LANES), bf16)],
-        [inbox, values, values], 10**10, 10**7, 1, slab_days, states, through, inverse, *ends,
+        [inbox, values, values], 10**10, 10**7, 0, active, states, through, inverse, *ends,
     )
     starts = exchange(message)
     (partial,) = call(

time: 39.6 us -> 39.5 us (level)
    pallas_call x10 -> x11, Pallas kernels: 16.5 us -> 16.7 us  [call(): pl.pallas_call(kernel, out_shape=[jax.ShapeDtypeStruct(shape, kind) for s...]
where the time goes in v16:
time: 39.5 us; the launch traced here: 39.3 us
  Pallas kernels  16.7 us (42%)
  starting transfers between devices  13.7 us (35%)
  waiting for transfers between devices  6.7 us (17%)
  local copies, waits for them, and re-layouts  1.44 us (4%)
  between operations  0.82 us (2%)
    pallas_call x11, Pallas kernels, call(): pl.pallas_call(kernel, out_shape=[jax.ShapeDtypeStruct(shape, kind) for s...  16.7 us
    ppermute x11, starting transfers between devices, crossed(): lax.ppermute(block, axis, [(i, i ^ bits) for i in range(lax.axis_size(axi...  13.7 us
    ppermute x11, waiting for transfers between devices, crossed(): lax.ppermute(block, axis, [(i, i ^ bits) for i in range(lax.axis_size(axi...  6.7 us
    unnamed x16, local copies, waits for them, and re-layouts  1.44 us
  transfers between devices with their start and end apart: 11, of which 7 were waited for; matrix products, arithmetic and copies ran while one was open for 0% of the time, Pallas kernels for 20%

profile of v16, /device:TPU:0, one launch (start us, length us, event | category | flops | bytes accessed | tf_op | source)
XLA Modules:
  0.0 39.3 jit_solution(16011785072752689417)
XLA Ops:
  0.0 0.0 copy-start.4
  0.0 0.0 copy-start.5
  0.0 0.0 copy-start.6
  0.0 2.8 %shard_map.94.refs_0_ = bf16[2,384,128]{2,1,0:T(8,128)(2,1)} custom-call(s32[1,2]{1,0:T(1,128)} %shared_hbm.1, bf16[48,16,1024]{2,1,0:T(8,128)(2,1)} %z_hbm.1), custom_call_target="tpu_custom_call" | custom-call | flops 1000000000 | bytes 4000000 | tf_op jit(solution)/shard_map/pallas_call | solution.py:294
  2.8 4.0 %collective-permute-start.2 = (bf16[2,384,128]{2,1,0:T(8,128)(2,1)}, bf16[2,384,128]{2,1,0:T(8,128)(2,1)S(1)}, u32[]{:S(2)}, u32[]{:S(2)}) collective-permute-start(bf16[2,384,128]{2,1,0:T(8,128)(2,1)} %shard_map.94.refs_0_), channel_id=1, source_target_pairs={{0,6},{1,7},{2,4},{3,5},{4,2},{5,3},{6,0},{7,1},{8,14},{9,15},{10,... | collective-permute-start | bytes 589832 | tf_op jit(solution)/shard_map/ppermute | solution.py:306
  6.8 0.5 %collective-permute-start.1 = (bf16[2,384,128]{2,1,0:T(8,128)(2,1)}, bf16[2,384,128]{2,1,0:T(8,128)(2,1)S(1)}, u32[]{:S(2)}, u32[]{:S(2)}) collective-permute-start(bf16[2,384,128]{2,1,0:T(8,128)(2,1)} %shard_map.94.refs_0_), channel_id=1, source_target_pairs={{0,4},{1,5},{2,6},{3,7},{4,0},{5,1},{6,2},{7,3},{8,12},{9,13},{10,... | collective-permute-start | bytes 589832 | tf_op jit(solution)/shard_map/ppermute | solution.py:306
  7.3 0.1 collective-permute-start
  7.4 0.0 copy-start.2
  7.4 1.4 %copy-done.2 = bf16[48,16,1024]{2,1,0:T(8,128)(2,1)S(1)} copy-done((bf16[48,16,1024]{2,1,0:T(8,128)(2,1)S(1)}, bf16[48,16,1024]{2,1,0:T(8,128)(2,1)}, u32[]{:S(2)}) %copy-start.2) | copy-done | bytes 1572888
  8.8 0.0 copy-start.3
  8.8 2.9 %shard_map.92 = (bf16[8,768,128]{2,1,0:T(8,128)(2,1)S(1)}, bf16[16,384,128]{2,1,0:T(8,128)(2,1)S(1)}) custom-call(bf16[48,16,1024]{2,1,0:T(8,128)(2,1)S(1)} %copy-done.2), custom_call_target="tpu_custom_call" | custom-call | flops 10000000000 | bytes 10000000 | tf_op jit(solution)/shard_map/pallas_call | solution.py:294
  11.7 0.0 copy-done.4
  11.7 0.0 copy-done.5
  11.8 0.0 copy-done.6
  11.8 0.0 copy-done.3
  11.8 0.0 copy-start.1
  11.8 2.4 %shard_map.93 = (f32[16,384,128]{2,1,0:T(8,128)S(1)}, bf16[16,128,256]{2,1,0:T(8,128)(2,1)S(1)}, bf16[16,128,128]{2,1,0:T(8,128)(2,1)S(1)}) custom-call(s32[4,16]{1,0:T(4,128)S(1)} %bitcast.2, bf16[16,384,128]{2,1,0:T(8,128)(2,1)S(1)} %get-tuple-element.20.turned_ref, bf16[16,4,64,64]{3,2,1,0:T(8,128)(2,1)S(1)} %copy-done.3, ...), custom_call_target="tpu_custom_call" | custom-call | flops 10000000000 | bytes 10000000 | tf_op jit(solution)/shard_map/pallas_call | solution.py:294
  14.2 0.0 copy-start
  14.2 0.0 copy-start.7
  14.2 0.0 collective-permute-done.2.refs_1_.refs_2_.rest_2_
  14.2 0.0 copy-done.1
  14.3 0.1 collective-permute-start.3
  14.4 1.7 %collective-permute-done.1.refs_0_.rest_1_ = bf16[2,384,128]{2,1,0:T(8,128)(2,1)S(1)} collective-permute-done((bf16[2,384,128]{2,1,0:T(8,128)(2,1)}, bf16[2,384,128]{2,1,0:T(8,128)(2,1)S(1)}, u32[]{:S(2)}, u32[]{:S(2)}) %collective-permute-start.1) | collective-permute-done | bytes 196640 | tf_op jit(solution)/shard_map/ppermute | solution.py:306
  16.1 0.3 collective-permute-done.refs_1_.rest_0_
  16.4 0.1 collective-permute-start.4
  17.1 0.0 copy-done
  17.2 0.5 %shard_map.91 = (f32[768,128]{1,0:T(8,128)S(1)}, bf16[16,128]{1,0:T(8,128)(2,1)S(1)}, f32[16,48,128]{2,1,0:T(8,128)S(1)}, f32[16,48,128]{2,1,0:T(8,128)S(1)}, f32[48,128]{1,0:T(8,128)S(1)}) custom-call(s32[1]{0:T(128)S(6)} %copy.10.days_ref, f32[48,1024]{1,0:T(8,128)S(1)} %copy-done), custom_call_target="tpu_custom_call" | custom-call | flops 1000000 | bytes 100000 | tf_op jit(solution)/shard_map/pallas_call | solution.py:294
  17.7 0.6 %collective-permute-done.4.rest_6_ = bf16[4,384,128]{2,1,0:T(8,128)(2,1)S(1)} collective-permute-done((bf16[4,384,128]{2,1,0:T(8,128)(2,1)S(1)}, bf16[4,384,128]{2,1,0:T(8,128)(2,1)S(1)}, u32[]{:S(2)}, u32[]{:S(2)}) %collective-permute-start.4) | collective-permute-done | bytes 393248 | tf_op jit(solution)/shard_map/ppermute | solution.py:306
  18.2 0.0 collective-permute-done.3.rest_5_
  18.2 0.0 copy-done.7
  18.2 2.8 %shard_map.97 = (f32[8,768,128]{2,1,0:T(8,128)S(1)}, bf16[9,16,128]{2,1,0:T(8,128)(2,1)S(1)}) custom-call(s32[2,16]{1,0:T(2,128)S(1)} %bitcast.3, f32[48,128]{1,0:T(8,128)S(1)} %get-tuple-element.19.active_ref, f32[16,384,128]{2,1,0:T(8,128)S(1)} %get-tuple-element.21.running_ref, bf16[16,128,256]{2,1,0:T(8,128)(2,1)S(1)} %get-tuple-element.22.weight_ref, ...), custom_call_target="tpu_custom_call" | custom-call | flops 10000000000 | bytes 10000000 | tf_op jit(solution)/shard_map/pallas_call | solution.py:294
  21.0 3.7 %collective-permute-start.7 = (bf16[9,16,128]{2,1,0:T(8,128)(2,1)S(1)}, bf16[9,16,128]{2,1,0:T(8,128)(2,1)S(1)}, u32[]{:S(2)}, u32[]{:S(2)}) collective-permute-start(bf16[9,16,128]{2,1,0:T(8,128)(2,1)S(1)} %get-tuple-element.29), channel_id=1, source_target_pairs={{0,24},{8,16},{16,8},{24,0},{1,25},{9,17},{17,9},{25,1},{2,26},{10... | collective-permute-start | bytes 110600 | tf_op jit(solution)/shard_map/ppermute | solution.py:306
  24.7 0.0 collective-permute-start.6
  24.7 0.8 %collective-permute-start.5 = (bf16[9,16,128]{2,1,0:T(8,128)(2,1)S(1)}, bf16[9,16,128]{2,1,0:T(8,128)(2,1)S(1)}, u32[]{:S(2)}, u32[]{:S(2)}) collective-permute-start(bf16[9,16,128]{2,1,0:T(8,128)(2,1)S(1)} %get-tuple-element.29), channel_id=1, source_target_pairs={{0,8},{8,0},{16,24},{24,16},{1,9},{9,1},{17,25},{25,17},{2,10},{10... | collective-permute-start | bytes 110600 | tf_op jit(solution)/shard_map/ppermute | solution.py:306
  25.5 1.7 %shard_map.98.states_ref = f32[16,384,128]{2,1,0:T(8,128)S(1)} custom-call(f32[8,768,128]{2,1,0:T(8,128)S(1)} %get-tuple-element.26.forcing_ref, f32[768,128]{1,0:T(8,128)S(1)} %get-tuple-element.27.retain_ref), custom_call_target="tpu_custom_call" | custom-call | flops 1000000000 | bytes 1000000 | tf_op jit(solution)/shard_map/pallas_call | solution.py:294
  27.2 0.0 collective-permute-done.7.rest_2_.rest_5_
  27.2 2.4 %collective-permute-done.6.rest_1_.rest_4_ = bf16[9,16,128]{2,1,0:T(8,128)(2,1)S(1)} collective-permute-done((bf16[9,16,128]{2,1,0:T(8,128)(2,1)S(1)}, bf16[9,16,128]{2,1,0:T(8,128)(2,1)S(1)}, u32[]{:S(2)}, u32[]{:S(2)}) %collective-permute-start.6) | collective-permute-done | bytes 36896 | tf_op jit(solution)/shard_map/ppermute | solution.py:306
  29.6 0.0 collective-permute-done.5.rest_0_.rest_3_
  29.6 1.7 %shard_map.99 = (f32[8,768,128]{2,1,0:T(8,128)S(1)}, bf16[8,16,128]{2,1,0:T(8,128)(2,1)S(1)}) custom-call(f32[48,128]{1,0:T(8,128)S(1)} %get-tuple-element.19.active_ref, f32[16,384,128]{2,1,0:T(8,128)S(1)} %shard_map.98.states_ref, f32[16,48,128]{2,1,0:T(8,128)S(1)} %get-tuple-element.28.through_ref, ...), custom_call_target="tpu_custom_call" | custom-call | flops 10000000000 | bytes 10000000 | tf_op jit(solution)/shard_map/pallas_call | solution.py:294
  31.2 1.7 %collective-permute-start.10 = (bf16[8,16,128]{2,1,0:T(8,128)(2,1)S(1)}, bf16[8,16,128]{2,1,0:T(8,128)(2,1)S(1)}, u32[]{:S(2)}, u32[]{:S(2)}) collective-permute-start(bf16[8,16,128]{2,1,0:T(8,128)(2,1)S(1)} %get-tuple-element.32), channel_id=1, source_target_pairs={{0,24},{8,16},{16,8},{24,0},{1,25},{9,17},{17,9},{25,1},{2,26},{10... | collective-permute-start | bytes 98312 | tf_op jit(solution)/shard_map/ppermute | solution.py:306
  32.9 0.5 %collective-permute-start.9 = (bf16[8,16,128]{2,1,0:T(8,128)(2,1)S(1)}, bf16[8,16,128]{2,1,0:T(8,128)(2,1)S(1)}, u32[]{:S(2)}, u32[]{:S(2)}) collective-permute-start(bf16[8,16,128]{2,1,0:T(8,128)(2,1)S(1)} %get-tuple-element.32), channel_id=1, source_target_pairs={{0,16},{8,24},{16,0},{24,8},{1,17},{9,25},{17,1},{25,9},{2,18},{10... | collective-permute-start | bytes 98312 | tf_op jit(solution)/shard_map/ppermute | solution.py:306
  33.4 2.3 %collective-permute-start.8 = (bf16[8,16,128]{2,1,0:T(8,128)(2,1)S(1)}, bf16[8,16,128]{2,1,0:T(8,128)(2,1)S(1)}, u32[]{:S(2)}, u32[]{:S(2)}) collective-permute-start(bf16[8,16,128]{2,1,0:T(8,128)(2,1)S(1)} %get-tuple-element.32), channel_id=1, source_target_pairs={{0,8},{8,0},{16,24},{24,16},{1,9},{9,1},{17,25},{25,17},{2,10},{10... | collective-permute-start | bytes 98312 | tf_op jit(solution)/shard_map/ppermute | solution.py:306
  35.7 0.5 %shard_map.100.partial_ref = f32[768,128]{1,0:T(8,128)S(1)} custom-call(f32[8,768,128]{2,1,0:T(8,128)S(1)} %get-tuple-element.30.adjoint_ref, f32[768,128]{1,0:T(8,128)S(1)} %get-tuple-element.27.retain_ref, bf16[8,768,128]{2,1,0:T(8,128)(2,1)S(1)} %get-tuple-element.31.moved_ref), custom_call_target="tpu_custom_call" | custom-call | flops 1000000000 | bytes 1000000 | tf_op jit(solution)/shard_map/pallas_call | solution.py:294
  36.2 0.8 %collective-permute-done.10.rest_2_ = bf16[8,16,128]{2,1,0:T(8,128)(2,1)S(1)} collective-permute-done((bf16[8,16,128]{2,1,0:T(8,128)(2,1)S(1)}, bf16[8,16,128]{2,1,0:T(8,128)(2,1)S(1)}, u32[]{:S(2)}, u32[]{:S(2)}) %collective-permute-start.10) | collective-permute-done | bytes 32800 | tf_op jit(solution)/shard_map/ppermute | solution.py:306
  37.0 0.8 %collective-permute-done.9.rest_1_ = bf16[8,16,128]{2,1,0:T(8,128)(2,1)S(1)} collective-permute-done((bf16[8,16,128]{2,1,0:T(8,128)(2,1)S(1)}, bf16[8,16,128]{2,1,0:T(8,128)(2,1)S(1)}, u32[]{:S(2)}, u32[]{:S(2)}) %collective-permute-start.9) | collective-permute-done | bytes 32800 | tf_op jit(solution)/shard_map/ppermute | solution.py:306
  37.9 0.1 collective-permute-done.8.rest_0_
  37.9 1.4 %shard_map.101 = f32[48,1024]{1,0:T(8,128)} custom-call(f32[768,128]{1,0:T(8,128)S(1)} %shard_map.100.partial_ref, f32[768,128]{1,0:T(8,128)S(1)} %get-tuple-element.27.retain_ref, bf16[8,768,128]{2,1,0:T(8,128)(2,1)S(1)} %get-tuple-element.31.moved_ref, bf16[8,16,128]{2,1,0:T(8,128)(2,1)S(1)} %collective-permute-done.8.rest_0_, ...), custom_call_target="tpu_custom_call" | custom-call | flops 10000000000 | bytes 10000000 | tf_op jit(solution)/shard_map/pallas_call | solution.py:294
  (2 shorter events, 0.1 us)
Async XLA Ops:
  0.0 11.7 %copy-start.4 = (bf16[16,2,64,64]{3,2,1,0:T(8,128)(2,1)S(1)}, bf16[16,2,64,64]{3,2,1,0:T(8,128)(2,1)}, u32[]{:S(2)}) copy-start(bf16[16,2,64,64]{3,2,1,0:T(8,128)(2,1)} %remote_weight_ref.1) | copy-start | bytes 786436
  0.0 11.7 %copy-start.5 = (bf16[16,64,64]{2,1,0:T(8,128)(2,1)S(1)}, bf16[16,64,64]{2,1,0:T(8,128)(2,1)}, u32[]{:S(2)}) copy-start(bf16[16,64,64]{2,1,0:T(8,128)(2,1)} %inverse_ref.1) | copy-start | bytes 393220
  0.0 11.8 %copy-start.6 = (s32[16,4]{0,1:T(4,128)S(1)}, s32[16,4]{0,1:T(4,128)}, u32[]{:S(2)}) copy-start(s32[16,4]{0,1:T(4,128)} %param.10) | copy-start | bytes 772
  2.8 11.4 %collective-permute-start.2 = (bf16[2,384,128]{2,1,0:T(8,128)(2,1)}, bf16[2,384,128]{2,1,0:T(8,128)(2,1)S(1)}, u32[]{:S(2)}, u32[]{:S(2)}) collective-permute-start(bf16[2,384,128]{2,1,0:T(8,128)(2,1)} %shard_map.94.refs_0_), channel_id=1, source_target_pairs={{0,6},{1,7},{2,4},{3,5},{4,2},{5,3},{6,0},{7,1},{8,14},{9,15},{10,... | collective-permute-start | bytes 589832 | tf_op jit(solution)/shard_map/ppermute | solution.py:306
  6.8 9.3 %collective-permute-start.1 = (bf16[2,384,128]{2,1,0:T(8,128)(2,1)}, bf16[2,384,128]{2,1,0:T(8,128)(2,1)S(1)}, u32[]{:S(2)}, u32[]{:S(2)}) collective-permute-start(bf16[2,384,128]{2,1,0:T(8,128)(2,1)} %shard_map.94.refs_0_), channel_id=1, source_target_pairs={{0,4},{1,5},{2,6},{3,7},{4,0},{5,1},{6,2},{7,3},{8,12},{9,13},{10,... | collective-permute-start | bytes 589832 | tf_op jit(solution)/shard_map/ppermute | solution.py:306
  7.3 9.1 %collective-permute-start = (bf16[2,384,128]{2,1,0:T(8,128)(2,1)}, bf16[2,384,128]{2,1,0:T(8,128)(2,1)S(1)}, u32[]{:S(2)}, u32[]{:S(2)}) collective-permute-start(bf16[2,384,128]{2,1,0:T(8,128)(2,1)} %shard_map.94.refs_0_), channel_id=1, source_target_pairs={{0,2},{1,3},{2,0},{3,1},{4,6},{5,7},{6,4},{7,5},{8,10},{9,11},{10,... | collective-permute-start | bytes 589832 | tf_op jit(solution)/shard_map/ppermute | solution.py:306
  7.4 1.4 %copy-start.2 = (bf16[48,16,1024]{2,1,0:T(8,128)(2,1)S(1)}, bf16[48,16,1024]{2,1,0:T(8,128)(2,1)}, u32[]{:S(2)}) copy-start(bf16[48,16,1024]{2,1,0:T(8,128)(2,1)} %z_hbm.1) | copy-start | bytes 4718596
  8.8 2.9 %copy-start.3 = (bf16[16,4,64,64]{3,2,1,0:T(8,128)(2,1)S(1)}, bf16[16,4,64,64]{3,2,1,0:T(8,128)(2,1)}, u32[]{:S(2)}) copy-start(bf16[16,4,64,64]{3,2,1,0:T(8,128)(2,1)} %weight_ref.1) | copy-start | bytes 1572868
  11.8 2.5 %copy-start.1 = (bf16[2,384,128]{2,1,0:T(8,128)(2,1)S(1)}, bf16[2,384,128]{2,1,0:T(8,128)(2,1)}, u32[]{:S(2)}) copy-start(bf16[2,384,128]{2,1,0:T(8,128)(2,1)} %shard_map.94.refs_0_) | copy-start | bytes 589828
  14.2 2.9 %copy-start = (f32[48,1024]{1,0:T(8,128)S(1)}, f32[48,1024]{1,0:T(8,128)}, u32[]{:S(2)}) copy-start(f32[48,1024]{1,0:T(8,128)} %retention_ref.1) | copy-start | bytes 589828
  14.2 4.0 %copy-start.7 = (s32[16,2]{0,1:T(2,128)S(1)}, s32[16,2]{0,1:T(2,128)}, u32[]{:S(2)}) copy-start(s32[16,2]{0,1:T(2,128)} %param.11) | copy-start | bytes 388
  14.3 3.9 %collective-permute-start.3 = (bf16[6,384,128]{2,1,0:T(8,128)(2,1)S(1)}, bf16[6,384,128]{2,1,0:T(8,128)(2,1)S(1)}, u32[]{:S(2)}, u32[]{:S(2)}) collective-permute-start(bf16[6,384,128]{2,1,0:T(8,128)(2,1)S(1)} %shard_map.95.rest_3_), channel_id=1, source_target_pairs={{0,1},{1,0},{2,3},{3,2},{4,5},{5,4},{6,7},{7,6},{8,9},{9,8},{10,11... | collective-permute-start | bytes 1769480 | tf_op jit(solution)/shard_map/ppermute | solution.py:306
  16.4 1.8 %collective-permute-start.4 = (bf16[4,384,128]{2,1,0:T(8,128)(2,1)S(1)}, bf16[4,384,128]{2,1,0:T(8,128)(2,1)S(1)}, u32[]{:S(2)}, u32[]{:S(2)}) collective-permute-start(bf16[4,384,128]{2,1,0:T(8,128)(2,1)S(1)} %shard_map.96.rest_4_), channel_id=1, source_target_pairs={{0,1},{1,0},{2,3},{3,2},{4,5},{5,4},{6,7},{7,6},{8,9},{9,8},{10,11... | collective-permute-start | bytes 1179656 | tf_op jit(solution)/shard_map/ppermute | solution.py:306
  21.0 6.1 %collective-permute-start.7 = (bf16[9,16,128]{2,1,0:T(8,128)(2,1)S(1)}, bf16[9,16,128]{2,1,0:T(8,128)(2,1)S(1)}, u32[]{:S(2)}, u32[]{:S(2)}) collective-permute-start(bf16[9,16,128]{2,1,0:T(8,128)(2,1)S(1)} %get-tuple-element.29), channel_id=1, source_target_pairs={{0,24},{8,16},{16,8},{24,0},{1,25},{9,17},{17,9},{25,1},{2,26},{10... | collective-permute-start | bytes 110600 | tf_op jit(solution)/shard_map/ppermute | solution.py:306
  24.7 4.9 %collective-permute-start.6 = (bf16[9,16,128]{2,1,0:T(8,128)(2,1)S(1)}, bf16[9,16,128]{2,1,0:T(8,128)(2,1)S(1)}, u32[]{:S(2)}, u32[]{:S(2)}) collective-permute-start(bf16[9,16,128]{2,1,0:T(8,128)(2,1)S(1)} %get-tuple-element.29), channel_id=1, source_target_pairs={{0,16},{8,24},{16,0},{24,8},{1,17},{9,25},{17,1},{25,9},{2,18},{10... | collective-permute-start | bytes 110600 | tf_op jit(solution)/shard_map/ppermute | solution.py:306
  24.7 4.9 %collective-permute-start.5 = (bf16[9,16,128]{2,1,0:T(8,128)(2,1)S(1)}, bf16[9,16,128]{2,1,0:T(8,128)(2,1)S(1)}, u32[]{:S(2)}, u32[]{:S(2)}) collective-permute-start(bf16[9,16,128]{2,1,0:T(8,128)(2,1)S(1)} %get-tuple-element.29), channel_id=1, source_target_pairs={{0,8},{8,0},{16,24},{24,16},{1,9},{9,1},{17,25},{25,17},{2,10},{10... | collective-permute-start | bytes 110600 | tf_op jit(solution)/shard_map/ppermute | solution.py:306
  31.2 5.8 %collective-permute-start.10 = (bf16[8,16,128]{2,1,0:T(8,128)(2,1)S(1)}, bf16[8,16,128]{2,1,0:T(8,128)(2,1)S(1)}, u32[]{:S(2)}, u32[]{:S(2)}) collective-permute-start(bf16[8,16,128]{2,1,0:T(8,128)(2,1)S(1)} %get-tuple-element.32), channel_id=1, source_target_pairs={{0,24},{8,16},{16,8},{24,0},{1,25},{9,17},{17,9},{25,1},{2,26},{10... | collective-permute-start | bytes 98312 | tf_op jit(solution)/shard_map/ppermute | solution.py:306
  32.9 4.9 %collective-permute-start.9 = (bf16[8,16,128]{2,1,0:T(8,128)(2,1)S(1)}, bf16[8,16,128]{2,1,0:T(8,128)(2,1)S(1)}, u32[]{:S(2)}, u32[]{:S(2)}) collective-permute-start(bf16[8,16,128]{2,1,0:T(8,128)(2,1)S(1)} %get-tuple-element.32), channel_id=1, source_target_pairs={{0,16},{8,24},{16,0},{24,8},{1,17},{9,25},{17,1},{25,9},{2,18},{10... | collective-permute-start | bytes 98312 | tf_op jit(solution)/shard_map/ppermute | solution.py:306
  33.4 4.5 %collective-permute-start.8 = (bf16[8,16,128]{2,1,0:T(8,128)(2,1)S(1)}, bf16[8,16,128]{2,1,0:T(8,128)(2,1)S(1)}, u32[]{:S(2)}, u32[]{:S(2)}) collective-permute-start(bf16[8,16,128]{2,1,0:T(8,128)(2,1)S(1)} %get-tuple-element.32), channel_id=1, source_target_pairs={{0,8},{8,0},{16,24},{24,16},{1,9},{9,1},{17,25},{25,17},{2,10},{10... | collective-permute-start | bytes 98312 | tf_op jit(solution)/shard_map/ppermute | solution.py:306

commit v17 on v16

--- a/solution.py
+++ b/solution.py
@@ -156,7 +156,7 @@
                 if bits not in batch[:place]:
                     remote[pl.ds(core * held + bits // 2 * bound, bound)] = ref[pl.ds(place * bound, bound)]
     active = active_ref[...]
-    for block in range(blocks):
+    def make_source(block, _):
         places = []
         for k in range(count):
             link = links_ref[k, block]
@@ -165,13 +165,19 @@
         far = jnp.concatenate([remote[place] for place in places], axis=1)
         total = lax.dot_general(far, weight_ref[block], TURNED, preferred_element_type=jnp.float32)
         source[block] = (running_ref[block] - total).astype(jnp.bfloat16)
-    for block in range(blocks):
+        return _
+
+    def make_forcing(block, _):
         drive = lax.dot_general(source[block], inverse_ref[block], TURNED, preferred_element_type=jnp.float32)
         beyond = beyond_ref[block]
         for pair in range(pairs):
             tile = active * drive[pair * days : (pair + 1) * days]
             forcing_ref[pair, pl.ds(block, days, stride=blocks), :] = tile
             ends[pair, pl.ds(block, 1), :] = jnp.sum(beyond * tile, axis=0, keepdims=True)
+        return _
+
+    lax.fori_loop(0, blocks, make_source, 0, unroll=4)
+    lax.fori_loop(0, blocks, make_forcing, 0, unroll=4)
     leave(message_ref, [ends[pair] for pair in range(pairs)])
     message_ref[pairs] = product_ref[...]
 
@@ -223,7 +229,7 @@
     active = active_ref[...]
     for pair, carry in enumerate(carried(pairs, inbox, inbox, False)):
         enter[pair] = carry
-    for block in range(blocks):
+    def make_adjoint(block, _):
         through = through_ref[block]
         stored = [
             (states_ref[block, pl.ds(pair * days, days), :] + through * enter[pair, pl.ds(block, 1), :])
@@ -235,6 +241,9 @@
             tile = active * adjoint[pair * days : (pair + 1) * days]
             adjoint_ref[pair, pl.ds(block, days, stride=blocks), :] = tile
             starts[pair, pl.ds(block, 1), :] = jnp.sum(through * tile, axis=0, keepdims=True)
+        return _
+
+    lax.fori_loop(0, blocks, make_adjoint, 0, unroll=4)
     leave(message_ref, [starts[pair] for pair in range(pairs)])
 
 
@@ -267,14 +276,16 @@
     lane = lax.broadcasted_iota(jnp.int32, (part, LANES), 1)
     copies = []
     for first in reversed(range(0, days, part)):
-        for day in reversed(range(first, first + part)):
-            rows = pl.ds(day * blocks, blocks)
+        def finish(step, reach, first=first):
+            rows = pl.ds(pl.multiple_of((first + part - 1 - step) * blocks, blocks), blocks)
             total = None
             for pair in range(pairs):
                 term = carries[pair] * moved_ref[pair, rows, :].astype(jnp.float32)
                 total = term if total is None else total + term
             stage[rows, :] = partial_ref[rows, :] + reach * total
-            reach = reach * retain_ref[rows, :]
+            return reach * retain_ref[rows, :]
+
+        reach = lax.fori_loop(0, part, finish, reach, unroll=8)
         done = pl.ds(first, part)
         for block in range(0, blocks, 2):
             both = [stage[pl.ds(first * blocks + block + half, part, stride=blocks), :] for half in range(2)]

time: 39.5 us -> 40.9 us (1.035)
  Pallas kernels: 16.7 us -> 18.1 us
    pallas_call x11, Pallas kernels: 16.7 us -> 18.1 us  [call(): pl.pallas_call(kernel, out_shape=[jax.ShapeDtypeStruct(shape, kind) for s...]
where the time goes in v17:
time: 40.9 us; the launch traced here: 40.7 us
  Pallas kernels  18.1 us (44%)
  starting transfers between devices  13.7 us (33%)
  waiting for transfers between devices  6.71 us (16%)
  local copies, waits for them, and re-layouts  1.44 us (4%)
  between operations  0.83 us (2%)
    pallas_call x11, Pallas kernels, call(): pl.pallas_call(kernel, out_shape=[jax.ShapeDtypeStruct(shape, kind) for s...  18.1 us
    ppermute x11, starting transfers between devices, crossed(): lax.ppermute(block, axis, [(i, i ^ bits) for i in range(lax.axis_size(axi...  13.7 us
    ppermute x11, waiting for transfers between devices, crossed(): lax.ppermute(block, axis, [(i, i ^ bits) for i in range(lax.axis_size(axi...  6.71 us
    unnamed x16, local copies, waits for them, and re-layouts  1.44 us
  transfers between devices with their start and end apart: 11, of which 7 were waited for; matrix products, arithmetic and copies ran while one was open for 0% of the time, Pallas kernels for 20%

profile of v17, /device:TPU:0, one launch (start us, length us, event | category | flops | bytes accessed | tf_op | source)
XLA Modules:
  0.0 40.7 jit_solution(6414521877896467522)
XLA Ops:
  0.0 0.0 copy-start.4
  0.0 0.0 copy-start.5
  0.0 0.0 copy-start.6
  0.0 2.8 %shard_map.94.refs_0_ = bf16[2,384,128]{2,1,0:T(8,128)(2,1)} custom-call(s32[1,2]{1,0:T(1,128)} %shared_hbm.1, bf16[48,16,1024]{2,1,0:T(8,128)(2,1)} %z_hbm.1), custom_call_target="tpu_custom_call" | custom-call | flops 1000000000 | bytes 4000000 | tf_op jit(solution)/shard_map/pallas_call | solution.py:305
  2.8 4.0 %collective-permute-start.2 = (bf16[2,384,128]{2,1,0:T(8,128)(2,1)}, bf16[2,384,128]{2,1,0:T(8,128)(2,1)S(1)}, u32[]{:S(2)}, u32[]{:S(2)}) collective-permute-start(bf16[2,384,128]{2,1,0:T(8,128)(2,1)} %shard_map.94.refs_0_), channel_id=1, source_target_pairs={{0,6},{1,7},{2,4},{3,5},{4,2},{5,3},{6,0},{7,1},{8,14},{9,15},{10,... | collective-permute-start | bytes 589832 | tf_op jit(solution)/shard_map/ppermute | solution.py:317
  6.8 0.5 %collective-permute-start.1 = (bf16[2,384,128]{2,1,0:T(8,128)(2,1)}, bf16[2,384,128]{2,1,0:T(8,128)(2,1)S(1)}, u32[]{:S(2)}, u32[]{:S(2)}) collective-permute-start(bf16[2,384,128]{2,1,0:T(8,128)(2,1)} %shard_map.94.refs_0_), channel_id=1, source_target_pairs={{0,4},{1,5},{2,6},{3,7},{4,0},{5,1},{6,2},{7,3},{8,12},{9,13},{10,... | collective-permute-start | bytes 589832 | tf_op jit(solution)/shard_map/ppermute | solution.py:317
  7.3 0.1 collective-permute-start
  7.4 0.0 copy-start.2
  7.4 1.4 %copy-done.2 = bf16[48,16,1024]{2,1,0:T(8,128)(2,1)S(1)} copy-done((bf16[48,16,1024]{2,1,0:T(8,128)(2,1)S(1)}, bf16[48,16,1024]{2,1,0:T(8,128)(2,1)}, u32[]{:S(2)}) %copy-start.2) | copy-done | bytes 1572888
  8.8 0.0 copy-start.3
  8.8 2.9 %shard_map.92 = (bf16[8,768,128]{2,1,0:T(8,128)(2,1)S(1)}, bf16[16,384,128]{2,1,0:T(8,128)(2,1)S(1)}) custom-call(bf16[48,16,1024]{2,1,0:T(8,128)(2,1)S(1)} %copy-done.2), custom_call_target="tpu_custom_call" | custom-call | flops 10000000000 | bytes 10000000 | tf_op jit(solution)/shard_map/pallas_call | solution.py:305
  11.7 0.0 copy-done.4
  11.7 0.0 copy-done.5
  11.8 0.0 copy-done.6
  11.8 0.0 copy-done.3
  11.8 0.0 copy-start.1
  11.8 2.4 %shard_map.93 = (f32[16,384,128]{2,1,0:T(8,128)S(1)}, bf16[16,128,256]{2,1,0:T(8,128)(2,1)S(1)}, bf16[16,128,128]{2,1,0:T(8,128)(2,1)S(1)}) custom-call(s32[4,16]{1,0:T(4,128)S(1)} %bitcast.2, bf16[16,384,128]{2,1,0:T(8,128)(2,1)S(1)} %get-tuple-element.20.turned_ref, bf16[16,4,64,64]{3,2,1,0:T(8,128)(2,1)S(1)} %copy-done.3, ...), custom_call_target="tpu_custom_call" | custom-call | flops 10000000000 | bytes 10000000 | tf_op jit(solution)/shard_map/pallas_call | solution.py:305
  14.2 0.0 copy-start
  14.2 0.0 copy-start.7
  14.2 0.0 collective-permute-done.2.refs_1_.refs_2_.rest_2_
  14.2 0.0 copy-done.1
  14.3 0.1 collective-permute-start.3
  14.4 1.7 %collective-permute-done.1.refs_0_.rest_1_ = bf16[2,384,128]{2,1,0:T(8,128)(2,1)S(1)} collective-permute-done((bf16[2,384,128]{2,1,0:T(8,128)(2,1)}, bf16[2,384,128]{2,1,0:T(8,128)(2,1)S(1)}, u32[]{:S(2)}, u32[]{:S(2)}) %collective-permute-start.1) | collective-permute-done | bytes 196640 | tf_op jit(solution)/shard_map/ppermute | solution.py:317
  16.1 0.3 collective-permute-done.refs_1_.rest_0_
  16.4 0.1 collective-permute-start.4
  17.1 0.0 copy-done
  17.2 0.5 %shard_map.91 = (f32[768,128]{1,0:T(8,128)S(1)}, bf16[16,128]{1,0:T(8,128)(2,1)S(1)}, f32[16,48,128]{2,1,0:T(8,128)S(1)}, f32[16,48,128]{2,1,0:T(8,128)S(1)}, f32[48,128]{1,0:T(8,128)S(1)}) custom-call(s32[1]{0:T(128)S(6)} %copy.10.days_ref, f32[48,1024]{1,0:T(8,128)S(1)} %copy-done), custom_call_target="tpu_custom_call" | custom-call | flops 1000000 | bytes 100000 | tf_op jit(solution)/shard_map/pallas_call | solution.py:305
  17.7 0.6 %collective-permute-done.4.rest_6_ = bf16[4,384,128]{2,1,0:T(8,128)(2,1)S(1)} collective-permute-done((bf16[4,384,128]{2,1,0:T(8,128)(2,1)S(1)}, bf16[4,384,128]{2,1,0:T(8,128)(2,1)S(1)}, u32[]{:S(2)}, u32[]{:S(2)}) %collective-permute-start.4) | collective-permute-done | bytes 393248 | tf_op jit(solution)/shard_map/ppermute | solution.py:317
  18.2 0.0 collective-permute-done.3.rest_5_
  18.2 0.0 copy-done.7
  18.2 3.9 %shard_map.97 = (f32[8,768,128]{2,1,0:T(8,128)S(1)}, bf16[9,16,128]{2,1,0:T(8,128)(2,1)S(1)}) custom-call(s32[2,16]{1,0:T(2,128)S(1)} %bitcast.3, f32[48,128]{1,0:T(8,128)S(1)} %get-tuple-element.19.active_ref, f32[16,384,128]{2,1,0:T(8,128)S(1)} %get-tuple-element.21.running_ref, bf16[16,128,256]{2,1,0:T(8,128)(2,1)S(1)} %get-tuple-element.22.weight_ref, ...), custom_call_target="tpu_custom_call" | custom-call | flops 10000000000 | bytes 10000000 | tf_op jit(solution)/shard_map/pallas_call | solution.py:305
  22.2 3.7 %collective-permute-start.7 = (bf16[9,16,128]{2,1,0:T(8,128)(2,1)S(1)}, bf16[9,16,128]{2,1,0:T(8,128)(2,1)S(1)}, u32[]{:S(2)}, u32[]{:S(2)}) collective-permute-start(bf16[9,16,128]{2,1,0:T(8,128)(2,1)S(1)} %get-tuple-element.29), channel_id=1, source_target_pairs={{0,24},{8,16},{16,8},{24,0},{1,25},{9,17},{17,9},{25,1},{2,26},{10... | collective-permute-start | bytes 110600 | tf_op jit(solution)/shard_map/ppermute | solution.py:317
  25.8 0.0 collective-permute-start.6
  25.8 0.8 %collective-permute-start.5 = (bf16[9,16,128]{2,1,0:T(8,128)(2,1)S(1)}, bf16[9,16,128]{2,1,0:T(8,128)(2,1)S(1)}, u32[]{:S(2)}, u32[]{:S(2)}) collective-permute-start(bf16[9,16,128]{2,1,0:T(8,128)(2,1)S(1)} %get-tuple-element.29), channel_id=1, source_target_pairs={{0,8},{8,0},{16,24},{24,16},{1,9},{9,1},{17,25},{25,17},{2,10},{10... | collective-permute-start | bytes 110600 | tf_op jit(solution)/shard_map/ppermute | solution.py:317
  26.6 1.7 %shard_map.98.states_ref = f32[16,384,128]{2,1,0:T(8,128)S(1)} custom-call(f32[8,768,128]{2,1,0:T(8,128)S(1)} %get-tuple-element.26.forcing_ref, f32[768,128]{1,0:T(8,128)S(1)} %get-tuple-element.27.retain_ref), custom_call_target="tpu_custom_call" | custom-call | flops 1000000000 | bytes 1000000 | tf_op jit(solution)/shard_map/pallas_call | solution.py:305
  28.3 0.0 collective-permute-done.7.rest_2_.rest_5_
  28.3 2.4 %collective-permute-done.6.rest_1_.rest_4_ = bf16[9,16,128]{2,1,0:T(8,128)(2,1)S(1)} collective-permute-done((bf16[9,16,128]{2,1,0:T(8,128)(2,1)S(1)}, bf16[9,16,128]{2,1,0:T(8,128)(2,1)S(1)}, u32[]{:S(2)}, u32[]{:S(2)}) %collective-permute-start.6) | collective-permute-done | bytes 36896 | tf_op jit(solution)/shard_map/ppermute | solution.py:317
  30.7 0.0 collective-permute-done.5.rest_0_.rest_3_
  30.7 1.8 %shard_map.99 = (f32[8,768,128]{2,1,0:T(8,128)S(1)}, bf16[8,16,128]{2,1,0:T(8,128)(2,1)S(1)}) custom-call(f32[48,128]{1,0:T(8,128)S(1)} %get-tuple-element.19.active_ref, f32[16,384,128]{2,1,0:T(8,128)S(1)} %shard_map.98.states_ref, f32[16,48,128]{2,1,0:T(8,128)S(1)} %get-tuple-element.28.through_ref, ...), custom_call_target="tpu_custom_call" | custom-call | flops 10000000000 | bytes 10000000 | tf_op jit(solution)/shard_map/pallas_call | solution.py:305
  32.5 1.7 %collective-permute-start.10 = (bf16[8,16,128]{2,1,0:T(8,128)(2,1)S(1)}, bf16[8,16,128]{2,1,0:T(8,128)(2,1)S(1)}, u32[]{:S(2)}, u32[]{:S(2)}) collective-permute-start(bf16[8,16,128]{2,1,0:T(8,128)(2,1)S(1)} %get-tuple-element.32), channel_id=1, source_target_pairs={{0,24},{8,16},{16,8},{24,0},{1,25},{9,17},{17,9},{25,1},{2,26},{10... | collective-permute-start | bytes 98312 | tf_op jit(solution)/shard_map/ppermute | solution.py:317
  34.2 0.5 %collective-permute-start.9 = (bf16[8,16,128]{2,1,0:T(8,128)(2,1)S(1)}, bf16[8,16,128]{2,1,0:T(8,128)(2,1)S(1)}, u32[]{:S(2)}, u32[]{:S(2)}) collective-permute-start(bf16[8,16,128]{2,1,0:T(8,128)(2,1)S(1)} %get-tuple-element.32), channel_id=1, source_target_pairs={{0,16},{8,24},{16,0},{24,8},{1,17},{9,25},{17,1},{25,9},{2,18},{10... | collective-permute-start | bytes 98312 | tf_op jit(solution)/shard_map/ppermute | solution.py:317
  34.7 2.3 %collective-permute-start.8 = (bf16[8,16,128]{2,1,0:T(8,128)(2,1)S(1)}, bf16[8,16,128]{2,1,0:T(8,128)(2,1)S(1)}, u32[]{:S(2)}, u32[]{:S(2)}) collective-permute-start(bf16[8,16,128]{2,1,0:T(8,128)(2,1)S(1)} %get-tuple-element.32), channel_id=1, source_target_pairs={{0,8},{8,0},{16,24},{24,16},{1,9},{9,1},{17,25},{25,17},{2,10},{10... | collective-permute-start | bytes 98312 | tf_op jit(solution)/shard_map/ppermute | solution.py:317
  37.0 0.5 %shard_map.100.partial_ref = f32[768,128]{1,0:T(8,128)S(1)} custom-call(f32[8,768,128]{2,1,0:T(8,128)S(1)} %get-tuple-element.30.adjoint_ref, f32[768,128]{1,0:T(8,128)S(1)} %get-tuple-element.27.retain_ref, bf16[8,768,128]{2,1,0:T(8,128)(2,1)S(1)} %get-tuple-element.31.moved_ref), custom_call_target="tpu_custom_call" | custom-call | flops 1000000000 | bytes 1000000 | tf_op jit(solution)/shard_map/pallas_call | solution.py:305
  37.5 0.9 %collective-permute-done.10.rest_2_ = bf16[8,16,128]{2,1,0:T(8,128)(2,1)S(1)} collective-permute-done((bf16[8,16,128]{2,1,0:T(8,128)(2,1)S(1)}, bf16[8,16,128]{2,1,0:T(8,128)(2,1)S(1)}, u32[]{:S(2)}, u32[]{:S(2)}) %collective-permute-start.10) | collective-permute-done | bytes 32800 | tf_op jit(solution)/shard_map/ppermute | solution.py:317
  38.3 0.8 %collective-permute-done.9.rest_1_ = bf16[8,16,128]{2,1,0:T(8,128)(2,1)S(1)} collective-permute-done((bf16[8,16,128]{2,1,0:T(8,128)(2,1)S(1)}, bf16[8,16,128]{2,1,0:T(8,128)(2,1)S(1)}, u32[]{:S(2)}, u32[]{:S(2)}) %collective-permute-start.9) | collective-permute-done | bytes 32800 | tf_op jit(solution)/shard_map/ppermute | solution.py:317
  39.1 0.1 collective-permute-done.8.rest_0_
  39.2 1.5 %shard_map.101 = f32[48,1024]{1,0:T(8,128)} custom-call(f32[768,128]{1,0:T(8,128)S(1)} %shard_map.100.partial_ref, f32[768,128]{1,0:T(8,128)S(1)} %get-tuple-element.27.retain_ref, bf16[8,768,128]{2,1,0:T(8,128)(2,1)S(1)} %get-tuple-element.31.moved_ref, bf16[8,16,128]{2,1,0:T(8,128)(2,1)S(1)} %collective-permute-done.8.rest_0_, ...), custom_call_target="tpu_custom_call" | custom-call | flops 10000000000 | bytes 10000000 | tf_op jit(solution)/shard_map/pallas_call | solution.py:305
  (2 shorter events, 0.1 us)
Async XLA Ops:
  0.0 11.7 %copy-start.4 = (bf16[16,2,64,64]{3,2,1,0:T(8,128)(2,1)S(1)}, bf16[16,2,64,64]{3,2,1,0:T(8,128)(2,1)}, u32[]{:S(2)}) copy-start(bf16[16,2,64,64]{3,2,1,0:T(8,128)(2,1)} %remote_weight_ref.1) | copy-start | bytes 786436
  0.0 11.7 %copy-start.5 = (bf16[16,64,64]{2,1,0:T(8,128)(2,1)S(1)}, bf16[16,64,64]{2,1,0:T(8,128)(2,1)}, u32[]{:S(2)}) copy-start(bf16[16,64,64]{2,1,0:T(8,128)(2,1)} %inverse_ref.1) | copy-start | bytes 393220
  0.0 11.8 %copy-start.6 = (s32[16,4]{0,1:T(4,128)S(1)}, s32[16,4]{0,1:T(4,128)}, u32[]{:S(2)}) copy-start(s32[16,4]{0,1:T(4,128)} %param.10) | copy-start | bytes 772
  2.8 11.4 %collective-permute-start.2 = (bf16[2,384,128]{2,1,0:T(8,128)(2,1)}, bf16[2,384,128]{2,1,0:T(8,128)(2,1)S(1)}, u32[]{:S(2)}, u32[]{:S(2)}) collective-permute-start(bf16[2,384,128]{2,1,0:T(8,128)(2,1)} %shard_map.94.refs_0_), channel_id=1, source_target_pairs={{0,6},{1,7},{2,4},{3,5},{4,2},{5,3},{6,0},{7,1},{8,14},{9,15},{10,... | collective-permute-start | bytes 589832 | tf_op jit(solution)/shard_map/ppermute | solution.py:317
  6.8 9.3 %collective-permute-start.1 = (bf16[2,384,128]{2,1,0:T(8,128)(2,1)}, bf16[2,384,128]{2,1,0:T(8,128)(2,1)S(1)}, u32[]{:S(2)}, u32[]{:S(2)}) collective-permute-start(bf16[2,384,128]{2,1,0:T(8,128)(2,1)} %shard_map.94.refs_0_), channel_id=1, source_target_pairs={{0,4},{1,5},{2,6},{3,7},{4,0},{5,1},{6,2},{7,3},{8,12},{9,13},{10,... | collective-permute-start | bytes 589832 | tf_op jit(solution)/shard_map/ppermute | solution.py:317
  7.3 9.1 %collective-permute-start = (bf16[2,384,128]{2,1,0:T(8,128)(2,1)}, bf16[2,384,128]{2,1,0:T(8,128)(2,1)S(1)}, u32[]{:S(2)}, u32[]{:S(2)}) collective-permute-start(bf16[2,384,128]{2,1,0:T(8,128)(2,1)} %shard_map.94.refs_0_), channel_id=1, source_target_pairs={{0,2},{1,3},{2,0},{3,1},{4,6},{5,7},{6,4},{7,5},{8,10},{9,11},{10,... | collective-permute-start | bytes 589832 | tf_op jit(solution)/shard_map/ppermute | solution.py:317
  7.4 1.4 %copy-start.2 = (bf16[48,16,1024]{2,1,0:T(8,128)(2,1)S(1)}, bf16[48,16,1024]{2,1,0:T(8,128)(2,1)}, u32[]{:S(2)}) copy-start(bf16[48,16,1024]{2,1,0:T(8,128)(2,1)} %z_hbm.1) | copy-start | bytes 4718596
  8.8 2.9 %copy-start.3 = (bf16[16,4,64,64]{3,2,1,0:T(8,128)(2,1)S(1)}, bf16[16,4,64,64]{3,2,1,0:T(8,128)(2,1)}, u32[]{:S(2)}) copy-start(bf16[16,4,64,64]{3,2,1,0:T(8,128)(2,1)} %weight_ref.1) | copy-start | bytes 1572868
  11.8 2.5 %copy-start.1 = (bf16[2,384,128]{2,1,0:T(8,128)(2,1)S(1)}, bf16[2,384,128]{2,1,0:T(8,128)(2,1)}, u32[]{:S(2)}) copy-start(bf16[2,384,128]{2,1,0:T(8,128)(2,1)} %shard_map.94.refs_0_) | copy-start | bytes 589828
  14.2 2.9 %copy-start = (f32[48,1024]{1,0:T(8,128)S(1)}, f32[48,1024]{1,0:T(8,128)}, u32[]{:S(2)}) copy-start(f32[48,1024]{1,0:T(8,128)} %retention_ref.1) | copy-start | bytes 589828
  14.2 4.0 %copy-start.7 = (s32[16,2]{0,1:T(2,128)S(1)}, s32[16,2]{0,1:T(2,128)}, u32[]{:S(2)}) copy-start(s32[16,2]{0,1:T(2,128)} %param.11) | copy-start | bytes 388
  14.3 3.9 %collective-permute-start.3 = (bf16[6,384,128]{2,1,0:T(8,128)(2,1)S(1)}, bf16[6,384,128]{2,1,0:T(8,128)(2,1)S(1)}, u32[]{:S(2)}, u32[]{:S(2)}) collective-permute-start(bf16[6,384,128]{2,1,0:T(8,128)(2,1)S(1)} %shard_map.95.rest_3_), channel_id=1, source_target_pairs={{0,1},{1,0},{2,3},{3,2},{4,5},{5,4},{6,7},{7,6},{8,9},{9,8},{10,11... | collective-permute-start | bytes 1769480 | tf_op jit(solution)/shard_map/ppermute | solution.py:317
  16.4 1.8 %collective-permute-start.4 = (bf16[4,384,128]{2,1,0:T(8,128)(2,1)S(1)}, bf16[4,384,128]{2,1,0:T(8,128)(2,1)S(1)}, u32[]{:S(2)}, u32[]{:S(2)}) collective-permute-start(bf16[4,384,128]{2,1,0:T(8,128)(2,1)S(1)} %shard_map.96.rest_4_), channel_id=1, source_target_pairs={{0,1},{1,0},{2,3},{3,2},{4,5},{5,4},{6,7},{7,6},{8,9},{9,8},{10,11... | collective-permute-start | bytes 1179656 | tf_op jit(solution)/shard_map/ppermute | solution.py:317
  22.2 6.1 %collective-permute-start.7 = (bf16[9,16,128]{2,1,0:T(8,128)(2,1)S(1)}, bf16[9,16,128]{2,1,0:T(8,128)(2,1)S(1)}, u32[]{:S(2)}, u32[]{:S(2)}) collective-permute-start(bf16[9,16,128]{2,1,0:T(8,128)(2,1)S(1)} %get-tuple-element.29), channel_id=1, source_target_pairs={{0,24},{8,16},{16,8},{24,0},{1,25},{9,17},{17,9},{25,1},{2,26},{10... | collective-permute-start | bytes 110600 | tf_op jit(solution)/shard_map/ppermute | solution.py:317
  25.8 4.9 %collective-permute-start.6 = (bf16[9,16,128]{2,1,0:T(8,128)(2,1)S(1)}, bf16[9,16,128]{2,1,0:T(8,128)(2,1)S(1)}, u32[]{:S(2)}, u32[]{:S(2)}) collective-permute-start(bf16[9,16,128]{2,1,0:T(8,128)(2,1)S(1)} %get-tuple-element.29), channel_id=1, source_target_pairs={{0,16},{8,24},{16,0},{24,8},{1,17},{9,25},{17,1},{25,9},{2,18},{10... | collective-permute-start | bytes 110600 | tf_op jit(solution)/shard_map/ppermute | solution.py:317
  25.8 4.9 %collective-permute-start.5 = (bf16[9,16,128]{2,1,0:T(8,128)(2,1)S(1)}, bf16[9,16,128]{2,1,0:T(8,128)(2,1)S(1)}, u32[]{:S(2)}, u32[]{:S(2)}) collective-permute-start(bf16[9,16,128]{2,1,0:T(8,128)(2,1)S(1)} %get-tuple-element.29), channel_id=1, source_target_pairs={{0,8},{8,0},{16,24},{24,16},{1,9},{9,1},{17,25},{25,17},{2,10},{10... | collective-permute-start | bytes 110600 | tf_op jit(solution)/shard_map/ppermute | solution.py:317
  32.5 5.8 %collective-permute-start.10 = (bf16[8,16,128]{2,1,0:T(8,128)(2,1)S(1)}, bf16[8,16,128]{2,1,0:T(8,128)(2,1)S(1)}, u32[]{:S(2)}, u32[]{:S(2)}) collective-permute-start(bf16[8,16,128]{2,1,0:T(8,128)(2,1)S(1)} %get-tuple-element.32), channel_id=1, source_target_pairs={{0,24},{8,16},{16,8},{24,0},{1,25},{9,17},{17,9},{25,1},{2,26},{10... | collective-permute-start | bytes 98312 | tf_op jit(solution)/shard_map/ppermute | solution.py:317
  34.2 4.9 %collective-permute-start.9 = (bf16[8,16,128]{2,1,0:T(8,128)(2,1)S(1)}, bf16[8,16,128]{2,1,0:T(8,128)(2,1)S(1)}, u32[]{:S(2)}, u32[]{:S(2)}) collective-permute-start(bf16[8,16,128]{2,1,0:T(8,128)(2,1)S(1)} %get-tuple-element.32), channel_id=1, source_target_pairs={{0,16},{8,24},{16,0},{24,8},{1,17},{9,25},{17,1},{25,9},{2,18},{10... | collective-permute-start | bytes 98312 | tf_op jit(solution)/shard_map/ppermute | solution.py:317
  34.7 4.5 %collective-permute-start.8 = (bf16[8,16,128]{2,1,0:T(8,128)(2,1)S(1)}, bf16[8,16,128]{2,1,0:T(8,128)(2,1)S(1)}, u32[]{:S(2)}, u32[]{:S(2)}) collective-permute-start(bf16[8,16,128]{2,1,0:T(8,128)(2,1)S(1)} %get-tuple-element.32), channel_id=1, source_target_pairs={{0,8},{8,0},{16,24},{24,16},{1,9},{9,1},{17,25},{25,17},{2,10},{10... | collective-permute-start | bytes 98312 | tf_op jit(solution)/shard_map/ppermute | solution.py:317

commit v18 on v16

--- a/solution.py
+++ b/solution.py
@@ -137,6 +137,10 @@
     count = piece_refs[0].shape[0]
     for k, ref in enumerate(piece_refs):
         out_ref[pl.ds(k * count, count)] = ref[...]
+    filled = len(piece_refs) * count
+    if filled < out_ref.shape[0]:
+        room = out_ref.shape[0] - filled
+        out_ref[pl.ds(filled, room)] = piece_refs[0][pl.ds(0, room)]
 
 
 def forward_kernel(
@@ -148,13 +152,12 @@
     pairs = forcing_ref.shape[0]
     count = links_ref.shape[0]
     held = remote.shape[0] // 2
-    bound = piece_refs[0].shape[0] // len(batches[0])
+    bound = held // (lax.axis_size("space") // 2)
     me = lax.axis_index("space")
     for core in range(2):
         for ref, batch in zip(piece_refs[core * len(batches) :], batches):
             for place, bits in enumerate(batch):
-                if bits not in batch[:place]:
-                    remote[pl.ds(core * held + bits // 2 * bound, bound)] = ref[pl.ds(place * bound, bound)]
+                remote[pl.ds(core * held + bits // 2 * bound, bound)] = ref[pl.ds(place * bound, bound)]
     active = active_ref[...]
     for block in range(blocks):
         places = []
@@ -365,10 +368,10 @@
         [pltpu.VMEM((2, rows, LANES), f32)], 10**6, 10**5, 1, slab_days, retention,
     )
     pieces[0] = outgoing
-    batches = [0, groups - 2, groups - 2], list(range(groups - 4, 0, -2))
+    batches = [0, groups - 2], list(range(groups - 4, 0, -2))
     same = []
-    for batch in batches:
-        shape = (len(batch) * bound, pairs * days, LANES)
+    for extra, batch in zip((1, 0), batches):
+        shape = (len(batch) * bound + extra, pairs * days, LANES)
         same += call(pass_kernel, [(shape, bf16)], [], 0, 10**5, 0, *[pieces[bits] for bits in batch], inverse)
     other = [crossed(piece, "space", 1) for piece in same]
     raw = [pieces[bits] for bits in range(2, groups, 2)]

time: 39.5 us -> 39.5 us (level)
  no operation moved by 1% of the time
where the time goes in v18:
time: 39.5 us; the launch traced here: 39.3 us
  Pallas kernels  16.7 us (42%)
  starting transfers between devices  13.7 us (35%)
  waiting for transfers between devices  6.7 us (17%)
  local copies, waits for them, and re-layouts  1.44 us (4%)
  between operations  0.82 us (2%)
    pallas_call x11, Pallas kernels, call(): pl.pallas_call(kernel, out_shape=[jax.ShapeDtypeStruct(shape, kind) for s...  16.7 us
    ppermute x11, starting transfers between devices, crossed(): lax.ppermute(block, axis, [(i, i ^ bits) for i in range(lax.axis_size(axi...  13.7 us
    ppermute x11, waiting for transfers between devices, crossed(): lax.ppermute(block, axis, [(i, i ^ bits) for i in range(lax.axis_size(axi...  6.7 us
    unnamed x16, local copies, waits for them, and re-layouts  1.44 us
  transfers between devices with their start and end apart: 11, of which 7 were waited for; matrix products, arithmetic and copies ran while one was open for 0% of the time, Pallas kernels for 20%

profile of v18, /device:TPU:0, one launch (start us, length us, event | category | flops | bytes accessed | tf_op | source)
XLA Modules:
  0.0 39.3 jit_solution(197839003275758332)
XLA Ops:
  0.0 0.0 copy-start.4
  0.0 0.0 copy-start.5
  0.0 0.0 copy-start.6
  0.0 2.8 %shard_map.94.refs_0_ = bf16[2,384,128]{2,1,0:T(8,128)(2,1)} custom-call(s32[1,2]{1,0:T(1,128)} %shared_hbm.1, bf16[48,16,1024]{2,1,0:T(8,128)(2,1)} %z_hbm.1), custom_call_target="tpu_custom_call" | custom-call | flops 1000000000 | bytes 4000000 | tf_op jit(solution)/shard_map/pallas_call | solution.py:297
  2.8 4.0 %collective-permute-start.2 = (bf16[2,384,128]{2,1,0:T(8,128)(2,1)}, bf16[2,384,128]{2,1,0:T(8,128)(2,1)S(1)}, u32[]{:S(2)}, u32[]{:S(2)}) collective-permute-start(bf16[2,384,128]{2,1,0:T(8,128)(2,1)} %shard_map.94.refs_0_), channel_id=1, source_target_pairs={{0,6},{1,7},{2,4},{3,5},{4,2},{5,3},{6,0},{7,1},{8,14},{9,15},{10,... | collective-permute-start | bytes 589832 | tf_op jit(solution)/shard_map/ppermute | solution.py:309
  6.8 0.5 %collective-permute-start.1 = (bf16[2,384,128]{2,1,0:T(8,128)(2,1)}, bf16[2,384,128]{2,1,0:T(8,128)(2,1)S(1)}, u32[]{:S(2)}, u32[]{:S(2)}) collective-permute-start(bf16[2,384,128]{2,1,0:T(8,128)(2,1)} %shard_map.94.refs_0_), channel_id=1, source_target_pairs={{0,4},{1,5},{2,6},{3,7},{4,0},{5,1},{6,2},{7,3},{8,12},{9,13},{10,... | collective-permute-start | bytes 589832 | tf_op jit(solution)/shard_map/ppermute | solution.py:309
  7.3 0.1 collective-permute-start
  7.4 0.0 copy-start.2
  7.4 1.4 %copy-done.2 = bf16[48,16,1024]{2,1,0:T(8,128)(2,1)S(1)} copy-done((bf16[48,16,1024]{2,1,0:T(8,128)(2,1)S(1)}, bf16[48,16,1024]{2,1,0:T(8,128)(2,1)}, u32[]{:S(2)}) %copy-start.2) | copy-done | bytes 1572888
  8.8 0.0 copy-start.3
  8.8 2.9 %shard_map.92 = (bf16[8,768,128]{2,1,0:T(8,128)(2,1)S(1)}, bf16[16,384,128]{2,1,0:T(8,128)(2,1)S(1)}) custom-call(bf16[48,16,1024]{2,1,0:T(8,128)(2,1)S(1)} %copy-done.2), custom_call_target="tpu_custom_call" | custom-call | flops 10000000000 | bytes 10000000 | tf_op jit(solution)/shard_map/pallas_call | solution.py:297
  11.7 0.0 copy-done.4
  11.7 0.0 copy-done.5
  11.8 0.0 copy-done.6
  11.8 0.0 copy-done.3
  11.8 0.0 copy-start.1
  11.8 0.0 copy-start
  11.8 0.0 copy-start.7
  11.8 2.4 %shard_map.93 = (f32[16,384,128]{2,1,0:T(8,128)S(1)}, bf16[16,128,256]{2,1,0:T(8,128)(2,1)S(1)}, bf16[16,128,128]{2,1,0:T(8,128)(2,1)S(1)}) custom-call(s32[4,16]{1,0:T(4,128)S(1)} %bitcast.2, bf16[16,384,128]{2,1,0:T(8,128)(2,1)S(1)} %get-tuple-element.20.turned_ref, bf16[16,4,64,64]{3,2,1,0:T(8,128)(2,1)S(1)} %copy-done.3, ...), custom_call_target="tpu_custom_call" | custom-call | flops 10000000000 | bytes 10000000 | tf_op jit(solution)/shard_map/pallas_call | solution.py:297
  14.2 0.0 collective-permute-done.2.refs_1_.rest_2_
  14.2 0.0 copy-done.1
  14.3 0.1 collective-permute-start.3
  14.4 1.7 %collective-permute-done.1.refs_0_.rest_1_ = bf16[2,384,128]{2,1,0:T(8,128)(2,1)S(1)} collective-permute-done((bf16[2,384,128]{2,1,0:T(8,128)(2,1)}, bf16[2,384,128]{2,1,0:T(8,128)(2,1)S(1)}, u32[]{:S(2)}, u32[]{:S(2)}) %collective-permute-start.1) | collective-permute-done | bytes 196640 | tf_op jit(solution)/shard_map/ppermute | solution.py:309
  16.1 0.3 collective-permute-done.refs_1_.rest_0_
  16.4 0.1 collective-permute-start.4
  17.1 0.0 copy-done
  17.2 0.5 %shard_map.91 = (f32[768,128]{1,0:T(8,128)S(1)}, bf16[16,128]{1,0:T(8,128)(2,1)S(1)}, f32[16,48,128]{2,1,0:T(8,128)S(1)}, f32[16,48,128]{2,1,0:T(8,128)S(1)}, f32[48,128]{1,0:T(8,128)S(1)}) custom-call(s32[1]{0:T(128)S(6)} %copy.10.days_ref, f32[48,1024]{1,0:T(8,128)S(1)} %copy-done), custom_call_target="tpu_custom_call" | custom-call | flops 1000000 | bytes 100000 | tf_op jit(solution)/shard_map/pallas_call | solution.py:297
  17.7 0.6 %collective-permute-done.4.rest_6_ = bf16[4,384,128]{2,1,0:T(8,128)(2,1)S(1)} collective-permute-done((bf16[4,384,128]{2,1,0:T(8,128)(2,1)S(1)}, bf16[4,384,128]{2,1,0:T(8,128)(2,1)S(1)}, u32[]{:S(2)}, u32[]{:S(2)}) %collective-permute-start.4) | collective-permute-done | bytes 393248 | tf_op jit(solution)/shard_map/ppermute | solution.py:309
  18.2 0.0 collective-permute-done.3.rest_5_
  18.2 0.0 copy-done.7
  18.2 2.8 %shard_map.97 = (f32[8,768,128]{2,1,0:T(8,128)S(1)}, bf16[9,16,128]{2,1,0:T(8,128)(2,1)S(1)}) custom-call(s32[2,16]{1,0:T(2,128)S(1)} %bitcast.3, f32[48,128]{1,0:T(8,128)S(1)} %get-tuple-element.19.active_ref, f32[16,384,128]{2,1,0:T(8,128)S(1)} %get-tuple-element.21.running_ref, bf16[16,128,256]{2,1,0:T(8,128)(2,1)S(1)} %get-tuple-element.22.weight_ref, ...), custom_call_target="tpu_custom_call" | custom-call | flops 10000000000 | bytes 10000000 | tf_op jit(solution)/shard_map/pallas_call | solution.py:297
  21.0 3.7 %collective-permute-start.7 = (bf16[9,16,128]{2,1,0:T(8,128)(2,1)S(1)}, bf16[9,16,128]{2,1,0:T(8,128)(2,1)S(1)}, u32[]{:S(2)}, u32[]{:S(2)}) collective-permute-start(bf16[9,16,128]{2,1,0:T(8,128)(2,1)S(1)} %get-tuple-element.29), channel_id=1, source_target_pairs={{0,24},{8,16},{16,8},{24,0},{1,25},{9,17},{17,9},{25,1},{2,26},{10... | collective-permute-start | bytes 110600 | tf_op jit(solution)/shard_map/ppermute | solution.py:309
  24.7 0.0 collective-permute-start.6
  24.7 0.8 %collective-permute-start.5 = (bf16[9,16,128]{2,1,0:T(8,128)(2,1)S(1)}, bf16[9,16,128]{2,1,0:T(8,128)(2,1)S(1)}, u32[]{:S(2)}, u32[]{:S(2)}) collective-permute-start(bf16[9,16,128]{2,1,0:T(8,128)(2,1)S(1)} %get-tuple-element.29), channel_id=1, source_target_pairs={{0,8},{8,0},{16,24},{24,16},{1,9},{9,1},{17,25},{25,17},{2,10},{10... | collective-permute-start | bytes 110600 | tf_op jit(solution)/shard_map/ppermute | solution.py:309
  25.5 1.7 %shard_map.98.states_ref = f32[16,384,128]{2,1,0:T(8,128)S(1)} custom-call(f32[8,768,128]{2,1,0:T(8,128)S(1)} %get-tuple-element.26.forcing_ref, f32[768,128]{1,0:T(8,128)S(1)} %get-tuple-element.27.retain_ref), custom_call_target="tpu_custom_call" | custom-call | flops 1000000000 | bytes 1000000 | tf_op jit(solution)/shard_map/pallas_call | solution.py:297
  27.1 0.0 collective-permute-done.7.rest_2_.rest_5_
  27.1 2.4 %collective-permute-done.6.rest_1_.rest_4_ = bf16[9,16,128]{2,1,0:T(8,128)(2,1)S(1)} collective-permute-done((bf16[9,16,128]{2,1,0:T(8,128)(2,1)S(1)}, bf16[9,16,128]{2,1,0:T(8,128)(2,1)S(1)}, u32[]{:S(2)}, u32[]{:S(2)}) %collective-permute-start.6) | collective-permute-done | bytes 36896 | tf_op jit(solution)/shard_map/ppermute | solution.py:309
  29.5 0.0 collective-permute-done.5.rest_0_.rest_3_
  29.5 1.7 %shard_map.99 = (f32[8,768,128]{2,1,0:T(8,128)S(1)}, bf16[8,16,128]{2,1,0:T(8,128)(2,1)S(1)}) custom-call(f32[48,128]{1,0:T(8,128)S(1)} %get-tuple-element.19.active_ref, f32[16,384,128]{2,1,0:T(8,128)S(1)} %shard_map.98.states_ref, f32[16,48,128]{2,1,0:T(8,128)S(1)} %get-tuple-element.28.through_ref, ...), custom_call_target="tpu_custom_call" | custom-call | flops 10000000000 | bytes 10000000 | tf_op jit(solution)/shard_map/pallas_call | solution.py:297
  31.2 1.7 %collective-permute-start.10 = (bf16[8,16,128]{2,1,0:T(8,128)(2,1)S(1)}, bf16[8,16,128]{2,1,0:T(8,128)(2,1)S(1)}, u32[]{:S(2)}, u32[]{:S(2)}) collective-permute-start(bf16[8,16,128]{2,1,0:T(8,128)(2,1)S(1)} %get-tuple-element.32), channel_id=1, source_target_pairs={{0,24},{8,16},{16,8},{24,0},{1,25},{9,17},{17,9},{25,1},{2,26},{10... | collective-permute-start | bytes 98312 | tf_op jit(solution)/shard_map/ppermute | solution.py:309
  32.9 0.5 %collective-permute-start.9 = (bf16[8,16,128]{2,1,0:T(8,128)(2,1)S(1)}, bf16[8,16,128]{2,1,0:T(8,128)(2,1)S(1)}, u32[]{:S(2)}, u32[]{:S(2)}) collective-permute-start(bf16[8,16,128]{2,1,0:T(8,128)(2,1)S(1)} %get-tuple-element.32), channel_id=1, source_target_pairs={{0,16},{8,24},{16,0},{24,8},{1,17},{9,25},{17,1},{25,9},{2,18},{10... | collective-permute-start | bytes 98312 | tf_op jit(solution)/shard_map/ppermute | solution.py:309
  33.4 2.3 %collective-permute-start.8 = (bf16[8,16,128]{2,1,0:T(8,128)(2,1)S(1)}, bf16[8,16,128]{2,1,0:T(8,128)(2,1)S(1)}, u32[]{:S(2)}, u32[]{:S(2)}) collective-permute-start(bf16[8,16,128]{2,1,0:T(8,128)(2,1)S(1)} %get-tuple-element.32), channel_id=1, source_target_pairs={{0,8},{8,0},{16,24},{24,16},{1,9},{9,1},{17,25},{25,17},{2,10},{10... | collective-permute-start | bytes 98312 | tf_op jit(solution)/shard_map/ppermute | solution.py:309
  35.7 0.5 %shard_map.100.partial_ref = f32[768,128]{1,0:T(8,128)S(1)} custom-call(f32[8,768,128]{2,1,0:T(8,128)S(1)} %get-tuple-element.30.adjoint_ref, f32[768,128]{1,0:T(8,128)S(1)} %get-tuple-element.27.retain_ref, bf16[8,768,128]{2,1,0:T(8,128)(2,1)S(1)} %get-tuple-element.31.moved_ref), custom_call_target="tpu_custom_call" | custom-call | flops 1000000000 | bytes 1000000 | tf_op jit(solution)/shard_map/pallas_call | solution.py:297
  36.2 0.8 %collective-permute-done.10.rest_2_ = bf16[8,16,128]{2,1,0:T(8,128)(2,1)S(1)} collective-permute-done((bf16[8,16,128]{2,1,0:T(8,128)(2,1)S(1)}, bf16[8,16,128]{2,1,0:T(8,128)(2,1)S(1)}, u32[]{:S(2)}, u32[]{:S(2)}) %collective-permute-start.10) | collective-permute-done | bytes 32800 | tf_op jit(solution)/shard_map/ppermute | solution.py:309
  37.0 0.8 %collective-permute-done.9.rest_1_ = bf16[8,16,128]{2,1,0:T(8,128)(2,1)S(1)} collective-permute-done((bf16[8,16,128]{2,1,0:T(8,128)(2,1)S(1)}, bf16[8,16,128]{2,1,0:T(8,128)(2,1)S(1)}, u32[]{:S(2)}, u32[]{:S(2)}) %collective-permute-start.9) | collective-permute-done | bytes 32800 | tf_op jit(solution)/shard_map/ppermute | solution.py:309
  37.9 0.1 collective-permute-done.8.rest_0_
  37.9 1.4 %shard_map.101 = f32[48,1024]{1,0:T(8,128)} custom-call(f32[768,128]{1,0:T(8,128)S(1)} %shard_map.100.partial_ref, f32[768,128]{1,0:T(8,128)S(1)} %get-tuple-element.27.retain_ref, bf16[8,768,128]{2,1,0:T(8,128)(2,1)S(1)} %get-tuple-element.31.moved_ref, bf16[8,16,128]{2,1,0:T(8,128)(2,1)S(1)} %collective-permute-done.8.rest_0_, ...), custom_call_target="tpu_custom_call" | custom-call | flops 10000000000 | bytes 10000000 | tf_op jit(solution)/shard_map/pallas_call | solution.py:297
  (2 shorter events, 0.1 us)
Async XLA Ops:
  0.0 11.7 %copy-start.4 = (bf16[16,2,64,64]{3,2,1,0:T(8,128)(2,1)S(1)}, bf16[16,2,64,64]{3,2,1,0:T(8,128)(2,1)}, u32[]{:S(2)}) copy-start(bf16[16,2,64,64]{3,2,1,0:T(8,128)(2,1)} %remote_weight_ref.1) | copy-start | bytes 786436
  0.0 11.7 %copy-start.5 = (bf16[16,64,64]{2,1,0:T(8,128)(2,1)S(1)}, bf16[16,64,64]{2,1,0:T(8,128)(2,1)}, u32[]{:S(2)}) copy-start(bf16[16,64,64]{2,1,0:T(8,128)(2,1)} %inverse_ref.1) | copy-start | bytes 393220
  0.0 11.8 %copy-start.6 = (s32[16,4]{0,1:T(4,128)S(1)}, s32[16,4]{0,1:T(4,128)}, u32[]{:S(2)}) copy-start(s32[16,4]{0,1:T(4,128)} %param.10) | copy-start | bytes 772
  2.8 11.4 %collective-permute-start.2 = (bf16[2,384,128]{2,1,0:T(8,128)(2,1)}, bf16[2,384,128]{2,1,0:T(8,128)(2,1)S(1)}, u32[]{:S(2)}, u32[]{:S(2)}) collective-permute-start(bf16[2,384,128]{2,1,0:T(8,128)(2,1)} %shard_map.94.refs_0_), channel_id=1, source_target_pairs={{0,6},{1,7},{2,4},{3,5},{4,2},{5,3},{6,0},{7,1},{8,14},{9,15},{10,... | collective-permute-start | bytes 589832 | tf_op jit(solution)/shard_map/ppermute | solution.py:309
  6.8 9.3 %collective-permute-start.1 = (bf16[2,384,128]{2,1,0:T(8,128)(2,1)}, bf16[2,384,128]{2,1,0:T(8,128)(2,1)S(1)}, u32[]{:S(2)}, u32[]{:S(2)}) collective-permute-start(bf16[2,384,128]{2,1,0:T(8,128)(2,1)} %shard_map.94.refs_0_), channel_id=1, source_target_pairs={{0,4},{1,5},{2,6},{3,7},{4,0},{5,1},{6,2},{7,3},{8,12},{9,13},{10,... | collective-permute-start | bytes 589832 | tf_op jit(solution)/shard_map/ppermute | solution.py:309
  7.3 9.1 %collective-permute-start = (bf16[2,384,128]{2,1,0:T(8,128)(2,1)}, bf16[2,384,128]{2,1,0:T(8,128)(2,1)S(1)}, u32[]{:S(2)}, u32[]{:S(2)}) collective-permute-start(bf16[2,384,128]{2,1,0:T(8,128)(2,1)} %shard_map.94.refs_0_), channel_id=1, source_target_pairs={{0,2},{1,3},{2,0},{3,1},{4,6},{5,7},{6,4},{7,5},{8,10},{9,11},{10,... | collective-permute-start | bytes 589832 | tf_op jit(solution)/shard_map/ppermute | solution.py:309
  7.4 1.4 %copy-start.2 = (bf16[48,16,1024]{2,1,0:T(8,128)(2,1)S(1)}, bf16[48,16,1024]{2,1,0:T(8,128)(2,1)}, u32[]{:S(2)}) copy-start(bf16[48,16,1024]{2,1,0:T(8,128)(2,1)} %z_hbm.1) | copy-start | bytes 4718596
  8.8 2.9 %copy-start.3 = (bf16[16,4,64,64]{3,2,1,0:T(8,128)(2,1)S(1)}, bf16[16,4,64,64]{3,2,1,0:T(8,128)(2,1)}, u32[]{:S(2)}) copy-start(bf16[16,4,64,64]{3,2,1,0:T(8,128)(2,1)} %weight_ref.1) | copy-start | bytes 1572868
  11.8 2.5 %copy-start.1 = (bf16[2,384,128]{2,1,0:T(8,128)(2,1)S(1)}, bf16[2,384,128]{2,1,0:T(8,128)(2,1)}, u32[]{:S(2)}) copy-start(bf16[2,384,128]{2,1,0:T(8,128)(2,1)} %shard_map.94.refs_0_) | copy-start | bytes 589828
  11.8 5.4 %copy-start = (f32[48,1024]{1,0:T(8,128)S(1)}, f32[48,1024]{1,0:T(8,128)}, u32[]{:S(2)}) copy-start(f32[48,1024]{1,0:T(8,128)} %retention_ref.1) | copy-start | bytes 589828
  11.8 6.4 %copy-start.7 = (s32[16,2]{0,1:T(2,128)S(1)}, s32[16,2]{0,1:T(2,128)}, u32[]{:S(2)}) copy-start(s32[16,2]{0,1:T(2,128)} %param.11) | copy-start | bytes 388
  14.3 3.9 %collective-permute-start.3 = (bf16[5,384,128]{2,1,0:T(8,128)(2,1)S(1)}, bf16[5,384,128]{2,1,0:T(8,128)(2,1)S(1)}, u32[]{:S(2)}, u32[]{:S(2)}) collective-permute-start(bf16[5,384,128]{2,1,0:T(8,128)(2,1)S(1)} %shard_map.95.rest_3_), channel_id=1, source_target_pairs={{0,1},{1,0},{2,3},{3,2},{4,5},{5,4},{6,7},{7,6},{8,9},{9,8},{10,11... | collective-permute-start | bytes 1474568 | tf_op jit(solution)/shard_map/ppermute | solution.py:309
  16.4 1.8 %collective-permute-start.4 = (bf16[4,384,128]{2,1,0:T(8,128)(2,1)S(1)}, bf16[4,384,128]{2,1,0:T(8,128)(2,1)S(1)}, u32[]{:S(2)}, u32[]{:S(2)}) collective-permute-start(bf16[4,384,128]{2,1,0:T(8,128)(2,1)S(1)} %shard_map.96.rest_4_), channel_id=1, source_target_pairs={{0,1},{1,0},{2,3},{3,2},{4,5},{5,4},{6,7},{7,6},{8,9},{9,8},{10,11... | collective-permute-start | bytes 1179656 | tf_op jit(solution)/shard_map/ppermute | solution.py:309
  21.0 6.1 %collective-permute-start.7 = (bf16[9,16,128]{2,1,0:T(8,128)(2,1)S(1)}, bf16[9,16,128]{2,1,0:T(8,128)(2,1)S(1)}, u32[]{:S(2)}, u32[]{:S(2)}) collective-permute-start(bf16[9,16,128]{2,1,0:T(8,128)(2,1)S(1)} %get-tuple-element.29), channel_id=1, source_target_pairs={{0,24},{8,16},{16,8},{24,0},{1,25},{9,17},{17,9},{25,1},{2,26},{10... | collective-permute-start | bytes 110600 | tf_op jit(solution)/shard_map/ppermute | solution.py:309
  24.7 4.9 %collective-permute-start.6 = (bf16[9,16,128]{2,1,0:T(8,128)(2,1)S(1)}, bf16[9,16,128]{2,1,0:T(8,128)(2,1)S(1)}, u32[]{:S(2)}, u32[]{:S(2)}) collective-permute-start(bf16[9,16,128]{2,1,0:T(8,128)(2,1)S(1)} %get-tuple-element.29), channel_id=1, source_target_pairs={{0,16},{8,24},{16,0},{24,8},{1,17},{9,25},{17,1},{25,9},{2,18},{10... | collective-permute-start | bytes 110600 | tf_op jit(solution)/shard_map/ppermute | solution.py:309
  24.7 4.9 %collective-permute-start.5 = (bf16[9,16,128]{2,1,0:T(8,128)(2,1)S(1)}, bf16[9,16,128]{2,1,0:T(8,128)(2,1)S(1)}, u32[]{:S(2)}, u32[]{:S(2)}) collective-permute-start(bf16[9,16,128]{2,1,0:T(8,128)(2,1)S(1)} %get-tuple-element.29), channel_id=1, source_target_pairs={{0,8},{8,0},{16,24},{24,16},{1,9},{9,1},{17,25},{25,17},{2,10},{10... | collective-permute-start | bytes 110600 | tf_op jit(solution)/shard_map/ppermute | solution.py:309
  31.2 5.8 %collective-permute-start.10 = (bf16[8,16,128]{2,1,0:T(8,128)(2,1)S(1)}, bf16[8,16,128]{2,1,0:T(8,128)(2,1)S(1)}, u32[]{:S(2)}, u32[]{:S(2)}) collective-permute-start(bf16[8,16,128]{2,1,0:T(8,128)(2,1)S(1)} %get-tuple-element.32), channel_id=1, source_target_pairs={{0,24},{8,16},{16,8},{24,0},{1,25},{9,17},{17,9},{25,1},{2,26},{10... | collective-permute-start | bytes 98312 | tf_op jit(solution)/shard_map/ppermute | solution.py:309
  32.9 4.9 %collective-permute-start.9 = (bf16[8,16,128]{2,1,0:T(8,128)(2,1)S(1)}, bf16[8,16,128]{2,1,0:T(8,128)(2,1)S(1)}, u32[]{:S(2)}, u32[]{:S(2)}) collective-permute-start(bf16[8,16,128]{2,1,0:T(8,128)(2,1)S(1)} %get-tuple-element.32), channel_id=1, source_target_pairs={{0,16},{8,24},{16,0},{24,8},{1,17},{9,25},{17,1},{25,9},{2,18},{10... | collective-permute-start | bytes 98312 | tf_op jit(solution)/shard_map/ppermute | solution.py:309
  33.4 4.5 %collective-permute-start.8 = (bf16[8,16,128]{2,1,0:T(8,128)(2,1)S(1)}, bf16[8,16,128]{2,1,0:T(8,128)(2,1)S(1)}, u32[]{:S(2)}, u32[]{:S(2)}) collective-permute-start(bf16[8,16,128]{2,1,0:T(8,128)(2,1)S(1)} %get-tuple-element.32), channel_id=1, source_target_pairs={{0,8},{8,0},{16,24},{24,16},{1,9},{9,1},{17,25},{25,17},{2,10},{10... | collective-permute-start | bytes 98312 | tf_op jit(solution)/shard_map/ppermute | solution.py:309

commit v19 on v18

--- a/solution.py
+++ b/solution.py
@@ -65,7 +65,7 @@
             outgoing_ref[m, pl.ds(pair * days, days), :] = moved[row : row + days, lane : lane + LANES]
 
 
-def turn_kernel(dims, z_ref, moved_ref, turned_ref, stage):
+def turn_kernel(dims, z_ref, before_ref, moved_ref, turned_ref, stage):
     days, blocks, size, probes = dims
     pairs = size * probes // LANES
     z = z_ref[...].reshape(days * blocks, size * probes)
@@ -344,12 +344,13 @@
         ],
         10**9, 4 * 10**6, 0, shared_blocks, probes, apart=(0, 1), limit=63 * 1024 * 1024,
     )
+    own_swapped = crossed(outgoing, "space", 1)
     pieces = {bits: crossed(outgoing, "space", bits) for bits in range(groups - 2, 0, -2)}
     by_block = (blocks, pairs * days, LANES)
     moved, turned = call(
         functools.partial(turn_kernel, dims),
         [((pairs, rows, LANES), bf16), (by_block, bf16)],
-        [pltpu.VMEM(*big)], 10**10, 10**7, 0, probes,
+        [pltpu.VMEM(*big)], 10**10, 10**7, 0, probes, own_swapped, apart=(1,),
     )
     running, remote_weight, inverse = call(
         functools.partial(local_kernel, dims),
@@ -368,13 +369,13 @@
         [pltpu.VMEM((2, rows, LANES), f32)], 10**6, 10**5, 1, slab_days, retention,
     )
     pieces[0] = outgoing
-    batches = [0, groups - 2], list(range(groups - 4, 0, -2))
-    same = []
-    for extra, batch in zip((1, 0), batches):
-        shape = (len(batch) * bound + extra, pairs * days, LANES)
+    batches = [0], list(range(2, groups - 2, 2)), [groups - 2]
+    same, other = [outgoing], [own_swapped]
+    for batch in batches[1:]:
+        shape = (len(batch) * bound, pairs * days, LANES)
         same += call(pass_kernel, [(shape, bf16)], [], 0, 10**5, 0, *[pieces[bits] for bits in batch], inverse)
-    other = [crossed(piece, "space", 1) for piece in same]
-    raw = [pieces[bits] for bits in range(2, groups, 2)]
+        other.append(crossed(same[-1], "space", 1))
+    raw = [pieces[bits] for bits in range(groups - 2, 0, -2)]
     slabs = lax.axis_size("tm")
     hops = slabs - 1
     exchange = lambda message: [crossed(message, "tm", bits) for bits in range(hops, 0, -1)][::-1]

time: 39.5 us -> 40.7 us (1.030)
  waiting for transfers between devices: 6.7 us -> 7.41 us
  starting transfers between devices: 13.7 us -> 14.2 us
    ppermute x11 -> x12, waiting for transfers between devices: 6.7 us -> 7.41 us  [crossed(): lax.ppermute(block, axis, [(i, i ^ bits) for i in range(lax.axis_size(axi...]
    ppermute x11 -> x12, starting transfers between devices: 13.7 us -> 14.2 us  [crossed(): lax.ppermute(block, axis, [(i, i ^ bits) for i in range(lax.axis_size(axi...]
  transfers between devices with their start and end apart: 11 -> 12, of which waited for: 7 -> 6; matrix products, arithmetic and copies ran while one was open for 0% -> 0% of each run, Pallas kernels for 20% -> 20%
where the time goes in v19:
time: 40.7 us; the launch traced here: 40.5 us
  Pallas kernels  16.7 us (41%)
  starting transfers between devices  14.2 us (35%)
  waiting for transfers between devices  7.41 us (18%)
  local copies, waits for them, and re-layouts  1.44 us (4%)
  between operations  0.82 us (2%)
    pallas_call x11, Pallas kernels, call(): pl.pallas_call(kernel, out_shape=[jax.ShapeDtypeStruct(shape, kind) for s...  16.7 us
    ppermute x12, starting transfers between devices, crossed(): lax.ppermute(block, axis, [(i, i ^ bits) for i in range(lax.axis_size(axi...  14.2 us
    ppermute x12, waiting for transfers between devices, crossed(): lax.ppermute(block, axis, [(i, i ^ bits) for i in range(lax.axis_size(axi...  7.41 us
    unnamed x16, local copies, waits for them, and re-layouts  1.44 us
  transfers between devices with their start and end apart: 12, of which 6 were waited for; matrix products, arithmetic and copies ran while one was open for 0% of the time, Pallas kernels for 20%

profile of v19, /device:TPU:0, one launch (start us, length us, event | category | flops | bytes accessed | tf_op | source)
XLA Modules:
  0.0 40.5 jit_solution(14363735405604353491)
XLA Ops:
  0.0 0.0 copy-start.3
  0.0 0.0 copy-start.4
  0.0 0.0 copy-start.6
  0.0 2.8 %shard_map.92.rest_3_ = bf16[2,384,128]{2,1,0:T(8,128)(2,1)} custom-call(s32[1,2]{1,0:T(1,128)} %shared_hbm.1, bf16[48,16,1024]{2,1,0:T(8,128)(2,1)} %z_ref.1), custom_call_target="tpu_custom_call" | custom-call | flops 1000000000 | bytes 4000000 | tf_op jit(solution)/shard_map/pallas_call | solution.py:297
  2.8 0.5 %collective-permute-start = (bf16[2,384,128]{2,1,0:T(8,128)(2,1)}, bf16[2,384,128]{2,1,0:T(8,128)(2,1)S(1)}, u32[]{:S(2)}, u32[]{:S(2)}) collective-permute-start(bf16[2,384,128]{2,1,0:T(8,128)(2,1)} %shard_map.92.rest_3_), channel_id=1, source_target_pairs={{0,1},{1,0},{2,3},{3,2},{4,5},{5,4},{6,7},{7,6},{8,9},{9,8},{10,11... | collective-permute-start | bytes 589832 | tf_op jit(solution)/shard_map/ppermute | solution.py:309
  3.3 2.6 %collective-permute-start.3 = (bf16[2,384,128]{2,1,0:T(8,128)(2,1)}, bf16[2,384,128]{2,1,0:T(8,128)(2,1)S(1)}, u32[]{:S(2)}, u32[]{:S(2)}) collective-permute-start(bf16[2,384,128]{2,1,0:T(8,128)(2,1)} %shard_map.92.rest_3_), channel_id=1, source_target_pairs={{0,2},{1,3},{2,0},{3,1},{4,6},{5,7},{6,4},{7,5},{8,10},{9,11},{10,... | collective-permute-start | bytes 589832 | tf_op jit(solution)/shard_map/ppermute | solution.py:309
  5.9 1.5 %collective-permute-start.2 = (bf16[2,384,128]{2,1,0:T(8,128)(2,1)}, bf16[2,384,128]{2,1,0:T(8,128)(2,1)S(1)}, u32[]{:S(2)}, u32[]{:S(2)}) collective-permute-start(bf16[2,384,128]{2,1,0:T(8,128)(2,1)} %shard_map.92.rest_3_), channel_id=1, source_target_pairs={{0,4},{1,5},{2,6},{3,7},{4,0},{5,1},{6,2},{7,3},{8,12},{9,13},{10,... | collective-permute-start | bytes 589832 | tf_op jit(solution)/shard_map/ppermute | solution.py:309
  7.4 0.0 collective-permute-start.1
  7.5 0.0 collective-permute-done.before_ref.rest_6_
  7.5 0.0 copy-start.1
  7.5 1.4 %copy-done.1 = bf16[48,16,1024]{2,1,0:T(8,128)(2,1)S(1)} copy-done((bf16[48,16,1024]{2,1,0:T(8,128)(2,1)S(1)}, bf16[48,16,1024]{2,1,0:T(8,128)(2,1)}, u32[]{:S(2)}) %copy-start.1) | copy-done | bytes 1572888
  8.9 0.0 copy-start.2
  8.9 2.9 %shard_map.93 = (bf16[8,768,128]{2,1,0:T(8,128)(2,1)S(1)}, bf16[16,384,128]{2,1,0:T(8,128)(2,1)S(1)}) custom-call(bf16[48,16,1024]{2,1,0:T(8,128)(2,1)S(1)} %copy-done.1, bf16[2,384,128]{2,1,0:T(8,128)(2,1)S(1)} %collective-permute-done.before_ref.rest_6_), custom_call_target="tpu_custom_call" | custom-call | flops 10000000000 | bytes 10000000 | tf_op jit(solution)/shard_map/pallas_call | solution.py:297
  11.8 0.0 copy-done.3
  11.8 0.0 copy-done.4
  11.8 0.0 copy-done.6
  11.8 0.0 copy-done.2
  11.8 0.0 copy-start
  11.8 0.0 copy-start.5
  11.8 0.0 copy-start.7
  11.9 2.4 %shard_map.94 = (f32[16,384,128]{2,1,0:T(8,128)S(1)}, bf16[16,128,256]{2,1,0:T(8,128)(2,1)S(1)}, bf16[16,128,128]{2,1,0:T(8,128)(2,1)S(1)}) custom-call(s32[4,16]{1,0:T(4,128)S(1)} %bitcast.2, bf16[16,384,128]{2,1,0:T(8,128)(2,1)S(1)} %get-tuple-element.20.turned_ref, bf16[16,4,64,64]{3,2,1,0:T(8,128)(2,1)S(1)} %copy-done.2, ...), custom_call_target="tpu_custom_call" | custom-call | flops 10000000000 | bytes 10000000 | tf_op jit(solution)/shard_map/pallas_call | solution.py:297
  14.3 0.0 collective-permute-done.3.refs_0_.rest_2_
  14.3 3.0 %collective-permute-done.2.refs_1_.rest_1_ = bf16[2,384,128]{2,1,0:T(8,128)(2,1)S(1)} collective-permute-done((bf16[2,384,128]{2,1,0:T(8,128)(2,1)}, bf16[2,384,128]{2,1,0:T(8,128)(2,1)S(1)}, u32[]{:S(2)}, u32[]{:S(2)}) %collective-permute-start.2) | collective-permute-done | bytes 196640 | tf_op jit(solution)/shard_map/ppermute | solution.py:309
  17.3 0.1 collective-permute-start.4
  17.4 0.0 collective-permute-done.1.refs_0_.rest_0_
  17.4 0.5 %collective-permute-start.5 = (bf16[2,384,128]{2,1,0:T(8,128)(2,1)S(1)}, bf16[2,384,128]{2,1,0:T(8,128)(2,1)S(1)}, u32[]{:S(2)}, u32[]{:S(2)}) collective-permute-start(bf16[2,384,128]{2,1,0:T(8,128)(2,1)S(1)} %shard_map.96.rest_5_), channel_id=1, source_target_pairs={{0,1},{1,0},{2,3},{3,2},{4,5},{5,4},{6,7},{7,6},{8,9},{9,8},{10,11... | collective-permute-start | bytes 589832 | tf_op jit(solution)/shard_map/ppermute | solution.py:309
  18.6 0.0 copy-done
  18.6 0.5 %shard_map.91 = (f32[768,128]{1,0:T(8,128)S(1)}, bf16[16,128]{1,0:T(8,128)(2,1)S(1)}, f32[16,48,128]{2,1,0:T(8,128)S(1)}, f32[16,48,128]{2,1,0:T(8,128)S(1)}, f32[48,128]{1,0:T(8,128)S(1)}) custom-call(s32[1]{0:T(128)S(6)} %copy.10.days_ref, f32[48,1024]{1,0:T(8,128)S(1)} %copy-done), custom_call_target="tpu_custom_call" | custom-call | flops 1000000 | bytes 100000 | tf_op jit(solution)/shard_map/pallas_call | solution.py:297
  19.1 0.3 collective-permute-done.5.rest_8_
  19.4 0.0 collective-permute-done.4.rest_7_
  19.4 0.0 copy-done.5
  19.4 0.0 copy-done.7
  19.4 2.8 %shard_map.97 = (f32[8,768,128]{2,1,0:T(8,128)S(1)}, bf16[9,16,128]{2,1,0:T(8,128)(2,1)S(1)}) custom-call(s32[2,16]{1,0:T(2,128)S(1)} %bitcast.3, f32[48,128]{1,0:T(8,128)S(1)} %get-tuple-element.19.active_ref, f32[16,384,128]{2,1,0:T(8,128)S(1)} %get-tuple-element.21.running_ref, bf16[16,128,256]{2,1,0:T(8,128)(2,1)S(1)} %get-tuple-element.22.weight_ref, ...), custom_call_target="tpu_custom_call" | custom-call | flops 10000000000 | bytes 10000000 | tf_op jit(solution)/shard_map/pallas_call | solution.py:297
  22.2 3.7 %collective-permute-start.8 = (bf16[9,16,128]{2,1,0:T(8,128)(2,1)S(1)}, bf16[9,16,128]{2,1,0:T(8,128)(2,1)S(1)}, u32[]{:S(2)}, u32[]{:S(2)}) collective-permute-start(bf16[9,16,128]{2,1,0:T(8,128)(2,1)S(1)} %get-tuple-element.29), channel_id=1, source_target_pairs={{0,24},{8,16},{16,8},{24,0},{1,25},{9,17},{17,9},{25,1},{2,26},{10... | collective-permute-start | bytes 110600 | tf_op jit(solution)/shard_map/ppermute | solution.py:309
  25.9 0.0 collective-permute-start.7
  25.9 0.8 %collective-permute-start.6 = (bf16[9,16,128]{2,1,0:T(8,128)(2,1)S(1)}, bf16[9,16,128]{2,1,0:T(8,128)(2,1)S(1)}, u32[]{:S(2)}, u32[]{:S(2)}) collective-permute-start(bf16[9,16,128]{2,1,0:T(8,128)(2,1)S(1)} %get-tuple-element.29), channel_id=1, source_target_pairs={{0,8},{8,0},{16,24},{24,16},{1,9},{9,1},{17,25},{25,17},{2,10},{10... | collective-permute-start | bytes 110600 | tf_op jit(solution)/shard_map/ppermute | solution.py:309
  26.7 1.7 %shard_map.98.states_ref = f32[16,384,128]{2,1,0:T(8,128)S(1)} custom-call(f32[8,768,128]{2,1,0:T(8,128)S(1)} %get-tuple-element.26.forcing_ref, f32[768,128]{1,0:T(8,128)S(1)} %get-tuple-element.27.retain_ref), custom_call_target="tpu_custom_call" | custom-call | flops 1000000000 | bytes 1000000 | tf_op jit(solution)/shard_map/pallas_call | solution.py:297
  28.4 0.0 collective-permute-done.8.rest_2_.rest_5_
  28.4 2.4 %collective-permute-done.7.rest_1_.rest_4_ = bf16[9,16,128]{2,1,0:T(8,128)(2,1)S(1)} collective-permute-done((bf16[9,16,128]{2,1,0:T(8,128)(2,1)S(1)}, bf16[9,16,128]{2,1,0:T(8,128)(2,1)S(1)}, u32[]{:S(2)}, u32[]{:S(2)}) %collective-permute-start.7) | collective-permute-done | bytes 36896 | tf_op jit(solution)/shard_map/ppermute | solution.py:309
  30.8 0.0 collective-permute-done.6.rest_0_.rest_3_
  30.8 1.7 %shard_map.99 = (f32[8,768,128]{2,1,0:T(8,128)S(1)}, bf16[8,16,128]{2,1,0:T(8,128)(2,1)S(1)}) custom-call(f32[48,128]{1,0:T(8,128)S(1)} %get-tuple-element.19.active_ref, f32[16,384,128]{2,1,0:T(8,128)S(1)} %shard_map.98.states_ref, f32[16,48,128]{2,1,0:T(8,128)S(1)} %get-tuple-element.28.through_ref, ...), custom_call_target="tpu_custom_call" | custom-call | flops 10000000000 | bytes 10000000 | tf_op jit(solution)/shard_map/pallas_call | solution.py:297
  32.5 1.7 %collective-permute-start.11 = (bf16[8,16,128]{2,1,0:T(8,128)(2,1)S(1)}, bf16[8,16,128]{2,1,0:T(8,128)(2,1)S(1)}, u32[]{:S(2)}, u32[]{:S(2)}) collective-permute-start(bf16[8,16,128]{2,1,0:T(8,128)(2,1)S(1)} %get-tuple-element.32), channel_id=1, source_target_pairs={{0,24},{8,16},{16,8},{24,0},{1,25},{9,17},{17,9},{25,1},{2,26},{10... | collective-permute-start | bytes 98312 | tf_op jit(solution)/shard_map/ppermute | solution.py:309
  34.2 0.5 %collective-permute-start.10 = (bf16[8,16,128]{2,1,0:T(8,128)(2,1)S(1)}, bf16[8,16,128]{2,1,0:T(8,128)(2,1)S(1)}, u32[]{:S(2)}, u32[]{:S(2)}) collective-permute-start(bf16[8,16,128]{2,1,0:T(8,128)(2,1)S(1)} %get-tuple-element.32), channel_id=1, source_target_pairs={{0,16},{8,24},{16,0},{24,8},{1,17},{9,25},{17,1},{25,9},{2,18},{10... | collective-permute-start | bytes 98312 | tf_op jit(solution)/shard_map/ppermute | solution.py:309
  34.6 2.3 %collective-permute-start.9 = (bf16[8,16,128]{2,1,0:T(8,128)(2,1)S(1)}, bf16[8,16,128]{2,1,0:T(8,128)(2,1)S(1)}, u32[]{:S(2)}, u32[]{:S(2)}) collective-permute-start(bf16[8,16,128]{2,1,0:T(8,128)(2,1)S(1)} %get-tuple-element.32), channel_id=1, source_target_pairs={{0,8},{8,0},{16,24},{24,16},{1,9},{9,1},{17,25},{25,17},{2,10},{10... | collective-permute-start | bytes 98312 | tf_op jit(solution)/shard_map/ppermute | solution.py:309
  36.9 0.5 %shard_map.100.partial_ref = f32[768,128]{1,0:T(8,128)S(1)} custom-call(f32[8,768,128]{2,1,0:T(8,128)S(1)} %get-tuple-element.30.adjoint_ref, f32[768,128]{1,0:T(8,128)S(1)} %get-tuple-element.27.retain_ref, bf16[8,768,128]{2,1,0:T(8,128)(2,1)S(1)} %get-tuple-element.31.moved_ref), custom_call_target="tpu_custom_call" | custom-call | flops 1000000000 | bytes 1000000 | tf_op jit(solution)/shard_map/pallas_call | solution.py:297
  37.4 0.8 %collective-permute-done.11.rest_2_ = bf16[8,16,128]{2,1,0:T(8,128)(2,1)S(1)} collective-permute-done((bf16[8,16,128]{2,1,0:T(8,128)(2,1)S(1)}, bf16[8,16,128]{2,1,0:T(8,128)(2,1)S(1)}, u32[]{:S(2)}, u32[]{:S(2)}) %collective-permute-start.11) | collective-permute-done | bytes 32800 | tf_op jit(solution)/shard_map/ppermute | solution.py:309
  38.3 0.8 %collective-permute-done.10.rest_1_ = bf16[8,16,128]{2,1,0:T(8,128)(2,1)S(1)} collective-permute-done((bf16[8,16,128]{2,1,0:T(8,128)(2,1)S(1)}, bf16[8,16,128]{2,1,0:T(8,128)(2,1)S(1)}, u32[]{:S(2)}, u32[]{:S(2)}) %collective-permute-start.10) | collective-permute-done | bytes 32800 | tf_op jit(solution)/shard_map/ppermute | solution.py:309
  39.1 0.1 collective-permute-done.9.rest_0_
  39.2 1.3 %shard_map.101 = f32[48,1024]{1,0:T(8,128)} custom-call(f32[768,128]{1,0:T(8,128)S(1)} %shard_map.100.partial_ref, f32[768,128]{1,0:T(8,128)S(1)} %get-tuple-element.27.retain_ref, bf16[8,768,128]{2,1,0:T(8,128)(2,1)S(1)} %get-tuple-element.31.moved_ref, bf16[8,16,128]{2,1,0:T(8,128)(2,1)S(1)} %collective-permute-done.9.rest_0_, ...), custom_call_target="tpu_custom_call" | custom-call | flops 10000000000 | bytes 10000000 | tf_op jit(solution)/shard_map/pallas_call | solution.py:297
  (2 shorter events, 0.0 us)
Async XLA Ops:
  0.0 11.8 %copy-start.3 = (bf16[16,2,64,64]{3,2,1,0:T(8,128)(2,1)S(1)}, bf16[16,2,64,64]{3,2,1,0:T(8,128)(2,1)}, u32[]{:S(2)}) copy-start(bf16[16,2,64,64]{3,2,1,0:T(8,128)(2,1)} %remote_weight_ref.1) | copy-start | bytes 786436
  0.0 11.8 %copy-start.4 = (bf16[16,64,64]{2,1,0:T(8,128)(2,1)S(1)}, bf16[16,64,64]{2,1,0:T(8,128)(2,1)}, u32[]{:S(2)}) copy-start(bf16[16,64,64]{2,1,0:T(8,128)(2,1)} %inverse_ref.1) | copy-start | bytes 393220
  0.0 11.8 %copy-start.6 = (s32[16,4]{0,1:T(4,128)S(1)}, s32[16,4]{0,1:T(4,128)}, u32[]{:S(2)}) copy-start(s32[16,4]{0,1:T(4,128)} %param.10) | copy-start | bytes 772
  2.8 4.6 %collective-permute-start = (bf16[2,384,128]{2,1,0:T(8,128)(2,1)}, bf16[2,384,128]{2,1,0:T(8,128)(2,1)S(1)}, u32[]{:S(2)}, u32[]{:S(2)}) collective-permute-start(bf16[2,384,128]{2,1,0:T(8,128)(2,1)} %shard_map.92.rest_3_), channel_id=1, source_target_pairs={{0,1},{1,0},{2,3},{3,2},{4,5},{5,4},{6,7},{7,6},{8,9},{9,8},{10,11... | collective-permute-start | bytes 589832 | tf_op jit(solution)/shard_map/ppermute | solution.py:309
  3.3 10.9 %collective-permute-start.3 = (bf16[2,384,128]{2,1,0:T(8,128)(2,1)}, bf16[2,384,128]{2,1,0:T(8,128)(2,1)S(1)}, u32[]{:S(2)}, u32[]{:S(2)}) collective-permute-start(bf16[2,384,128]{2,1,0:T(8,128)(2,1)} %shard_map.92.rest_3_), channel_id=1, source_target_pairs={{0,2},{1,3},{2,0},{3,1},{4,6},{5,7},{6,4},{7,5},{8,10},{9,11},{10,... | collective-permute-start | bytes 589832 | tf_op jit(solution)/shard_map/ppermute | solution.py:309
  5.9 11.4 %collective-permute-start.2 = (bf16[2,384,128]{2,1,0:T(8,128)(2,1)}, bf16[2,384,128]{2,1,0:T(8,128)(2,1)S(1)}, u32[]{:S(2)}, u32[]{:S(2)}) collective-permute-start(bf16[2,384,128]{2,1,0:T(8,128)(2,1)} %shard_map.92.rest_3_), channel_id=1, source_target_pairs={{0,4},{1,5},{2,6},{3,7},{4,0},{5,1},{6,2},{7,3},{8,12},{9,13},{10,... | collective-permute-start | bytes 589832 | tf_op jit(solution)/shard_map/ppermute | solution.py:309
  7.4 10.0 %collective-permute-start.1 = (bf16[2,384,128]{2,1,0:T(8,128)(2,1)}, bf16[2,384,128]{2,1,0:T(8,128)(2,1)S(1)}, u32[]{:S(2)}, u32[]{:S(2)}) collective-permute-start(bf16[2,384,128]{2,1,0:T(8,128)(2,1)} %shard_map.92.rest_3_), channel_id=1, source_target_pairs={{0,6},{1,7},{2,4},{3,5},{4,2},{5,3},{6,0},{7,1},{8,14},{9,15},{10,... | collective-permute-start | bytes 589832 | tf_op jit(solution)/shard_map/ppermute | solution.py:309
  7.5 1.4 %copy-start.1 = (bf16[48,16,1024]{2,1,0:T(8,128)(2,1)S(1)}, bf16[48,16,1024]{2,1,0:T(8,128)(2,1)}, u32[]{:S(2)}) copy-start(bf16[48,16,1024]{2,1,0:T(8,128)(2,1)} %z_ref.1) | copy-start | bytes 4718596
  8.9 2.9 %copy-start.2 = (bf16[16,4,64,64]{3,2,1,0:T(8,128)(2,1)S(1)}, bf16[16,4,64,64]{3,2,1,0:T(8,128)(2,1)}, u32[]{:S(2)}) copy-start(bf16[16,4,64,64]{3,2,1,0:T(8,128)(2,1)} %weight_ref.1) | copy-start | bytes 1572868
  11.8 6.8 %copy-start = (f32[48,1024]{1,0:T(8,128)S(1)}, f32[48,1024]{1,0:T(8,128)}, u32[]{:S(2)}) copy-start(f32[48,1024]{1,0:T(8,128)} %retention_ref.1) | copy-start | bytes 589828
  11.8 7.6 %copy-start.5 = (bf16[2,384,128]{2,1,0:T(8,128)(2,1)S(1)}, bf16[2,384,128]{2,1,0:T(8,128)(2,1)}, u32[]{:S(2)}) copy-start(bf16[2,384,128]{2,1,0:T(8,128)(2,1)} %shard_map.92.rest_3_) | copy-start | bytes 589828
  11.8 7.6 %copy-start.7 = (s32[16,2]{0,1:T(2,128)S(1)}, s32[16,2]{0,1:T(2,128)}, u32[]{:S(2)}) copy-start(s32[16,2]{0,1:T(2,128)} %param.11) | copy-start | bytes 388
  17.3 2.1 %collective-permute-start.4 = (bf16[4,384,128]{2,1,0:T(8,128)(2,1)S(1)}, bf16[4,384,128]{2,1,0:T(8,128)(2,1)S(1)}, u32[]{:S(2)}, u32[]{:S(2)}) collective-permute-start(bf16[4,384,128]{2,1,0:T(8,128)(2,1)S(1)} %shard_map.95.rest_4_), channel_id=1, source_target_pairs={{0,1},{1,0},{2,3},{3,2},{4,5},{5,4},{6,7},{7,6},{8,9},{9,8},{10,11... | collective-permute-start | bytes 1179656 | tf_op jit(solution)/shard_map/ppermute | solution.py:309
  17.4 2.0 %collective-permute-start.5 = (bf16[2,384,128]{2,1,0:T(8,128)(2,1)S(1)}, bf16[2,384,128]{2,1,0:T(8,128)(2,1)S(1)}, u32[]{:S(2)}, u32[]{:S(2)}) collective-permute-start(bf16[2,384,128]{2,1,0:T(8,128)(2,1)S(1)} %shard_map.96.rest_5_), channel_id=1, source_target_pairs={{0,1},{1,0},{2,3},{3,2},{4,5},{5,4},{6,7},{7,6},{8,9},{9,8},{10,11... | collective-permute-start | bytes 589832 | tf_op jit(solution)/shard_map/ppermute | solution.py:309
  22.2 6.1 %collective-permute-start.8 = (bf16[9,16,128]{2,1,0:T(8,128)(2,1)S(1)}, bf16[9,16,128]{2,1,0:T(8,128)(2,1)S(1)}, u32[]{:S(2)}, u32[]{:S(2)}) collective-permute-start(bf16[9,16,128]{2,1,0:T(8,128)(2,1)S(1)} %get-tuple-element.29), channel_id=1, source_target_pairs={{0,24},{8,16},{16,8},{24,0},{1,25},{9,17},{17,9},{25,1},{2,26},{10... | collective-permute-start | bytes 110600 | tf_op jit(solution)/shard_map/ppermute | solution.py:309
  25.9 4.9 %collective-permute-start.7 = (bf16[9,16,128]{2,1,0:T(8,128)(2,1)S(1)}, bf16[9,16,128]{2,1,0:T(8,128)(2,1)S(1)}, u32[]{:S(2)}, u32[]{:S(2)}) collective-permute-start(bf16[9,16,128]{2,1,0:T(8,128)(2,1)S(1)} %get-tuple-element.29), channel_id=1, source_target_pairs={{0,16},{8,24},{16,0},{24,8},{1,17},{9,25},{17,1},{25,9},{2,18},{10... | collective-permute-start | bytes 110600 | tf_op jit(solution)/shard_map/ppermute | solution.py:309
  25.9 4.9 %collective-permute-start.6 = (bf16[9,16,128]{2,1,0:T(8,128)(2,1)S(1)}, bf16[9,16,128]{2,1,0:T(8,128)(2,1)S(1)}, u32[]{:S(2)}, u32[]{:S(2)}) collective-permute-start(bf16[9,16,128]{2,1,0:T(8,128)(2,1)S(1)} %get-tuple-element.29), channel_id=1, source_target_pairs={{0,8},{8,0},{16,24},{24,16},{1,9},{9,1},{17,25},{25,17},{2,10},{10... | collective-permute-start | bytes 110600 | tf_op jit(solution)/shard_map/ppermute | solution.py:309
  32.5 5.8 %collective-permute-start.11 = (bf16[8,16,128]{2,1,0:T(8,128)(2,1)S(1)}, bf16[8,16,128]{2,1,0:T(8,128)(2,1)S(1)}, u32[]{:S(2)}, u32[]{:S(2)}) collective-permute-start(bf16[8,16,128]{2,1,0:T(8,128)(2,1)S(1)} %get-tuple-element.32), channel_id=1, source_target_pairs={{0,24},{8,16},{16,8},{24,0},{1,25},{9,17},{17,9},{25,1},{2,26},{10... | collective-permute-start | bytes 98312 | tf_op jit(solution)/shard_map/ppermute | solution.py:309
  34.2 4.9 %collective-permute-start.10 = (bf16[8,16,128]{2,1,0:T(8,128)(2,1)S(1)}, bf16[8,16,128]{2,1,0:T(8,128)(2,1)S(1)}, u32[]{:S(2)}, u32[]{:S(2)}) collective-permute-start(bf16[8,16,128]{2,1,0:T(8,128)(2,1)S(1)} %get-tuple-element.32), channel_id=1, source_target_pairs={{0,16},{8,24},{16,0},{24,8},{1,17},{9,25},{17,1},{25,9},{2,18},{10... | collective-permute-start | bytes 98312 | tf_op jit(solution)/shard_map/ppermute | solution.py:309
  34.6 4.5 %collective-permute-start.9 = (bf16[8,16,128]{2,1,0:T(8,128)(2,1)S(1)}, bf16[8,16,128]{2,1,0:T(8,128)(2,1)S(1)}, u32[]{:S(2)}, u32[]{:S(2)}) collective-permute-start(bf16[8,16,128]{2,1,0:T(8,128)(2,1)S(1)} %get-tuple-element.32), channel_id=1, source_target_pairs={{0,8},{8,0},{16,24},{24,16},{1,9},{9,1},{17,25},{25,17},{2,10},{10... | collective-permute-start | bytes 98312 | tf_op jit(solution)/shard_map/ppermute | solution.py:309

commit v20 on v16

--- a/solution.py
+++ b/solution.py
@@ -217,7 +217,7 @@
 
 def adjoint_kernel(dims, hops, active_ref, states_ref, through_ref, inverse_ref, *rest):
     days, blocks, size, probes = dims
-    adjoint_ref, message_ref, inbox, enter, starts = rest[hops:]
+    adjoint_ref, message_ref, inbox, enter, starts, stored = rest[hops:]
     pairs = adjoint_ref.shape[0]
     collect(rest[:hops], inbox)
     active = active_ref[...]
@@ -225,12 +225,13 @@
         enter[pair] = carry
     for block in range(blocks):
         through = through_ref[block]
-        stored = [
-            (states_ref[block, pl.ds(pair * days, days), :] + through * enter[pair, pl.ds(block, 1), :])
-            .astype(jnp.bfloat16)
-            for pair in range(pairs)
-        ]
-        adjoint = jnp.dot(jnp.concatenate(stored, axis=0), inverse_ref[block], preferred_element_type=jnp.float32)
+        for pair in range(pairs):
+            rows = pl.ds(pair * days, days)
+            state = states_ref[block, rows, :] + through * enter[pair, pl.ds(block, 1), :]
+            stored[block, rows, :] = state.astype(jnp.bfloat16)
+    for block in range(blocks):
+        through = through_ref[block]
+        adjoint = jnp.dot(stored[block], inverse_ref[block], preferred_element_type=jnp.float32)
         for pair in range(pairs):
             tile = active * adjoint[pair * days : (pair + 1) * days]
             adjoint_ref[pair, pl.ds(block, days, stride=blocks), :] = tile
@@ -391,7 +392,7 @@
     adjoint, message = call(
         functools.partial(adjoint_kernel, dims, hops),
         [big, ((pairs, blocks, LANES), bf16)],
-        [inbox, values, values], 10**10, 10**7, 0, active, states, through, inverse, *ends,
+        [inbox, values, values, pltpu.VMEM(by_block, bf16)], 10**10, 10**7, 0, active, states, through, inverse, *ends,
     )
     starts = exchange(message)
     (partial,) = call(

time: 39.5 us -> 39.6 us (level)
  no operation moved by 1% of the time
where the time goes in v20:
time: 39.6 us; the launch traced here: 39.4 us
  Pallas kernels  16.8 us (42%)
  starting transfers between devices  13.7 us (35%)
  waiting for transfers between devices  6.7 us (17%)
  local copies, waits for them, and re-layouts  1.44 us (4%)
  between operations  0.82 us (2%)
    pallas_call x11, Pallas kernels, call(): pl.pallas_call(kernel, out_shape=[jax.ShapeDtypeStruct(shape, kind) for s...  16.8 us
    ppermute x11, starting transfers between devices, crossed(): lax.ppermute(block, axis, [(i, i ^ bits) for i in range(lax.axis_size(axi...  13.7 us
    ppermute x11, waiting for transfers between devices, crossed(): lax.ppermute(block, axis, [(i, i ^ bits) for i in range(lax.axis_size(axi...  6.7 us
    unnamed x16, local copies, waits for them, and re-layouts  1.44 us
  transfers between devices with their start and end apart: 11, of which 7 were waited for; matrix products, arithmetic and copies ran while one was open for 0% of the time, Pallas kernels for 20%

profile of v20, /device:TPU:0, one launch (start us, length us, event | category | flops | bytes accessed | tf_op | source)
XLA Modules:
  0.0 39.4 jit_solution(2528780270668436117)
XLA Ops:
  0.0 0.0 copy-start.4
  0.0 0.0 copy-start.5
  0.0 0.0 copy-start.6
  0.0 2.8 %shard_map.94.refs_0_ = bf16[2,384,128]{2,1,0:T(8,128)(2,1)} custom-call(s32[1,2]{1,0:T(1,128)} %shared_hbm.1, bf16[48,16,1024]{2,1,0:T(8,128)(2,1)} %z_hbm.1), custom_call_target="tpu_custom_call" | custom-call | flops 1000000000 | bytes 4000000 | tf_op jit(solution)/shard_map/pallas_call | solution.py:295
  2.8 4.0 %collective-permute-start.2 = (bf16[2,384,128]{2,1,0:T(8,128)(2,1)}, bf16[2,384,128]{2,1,0:T(8,128)(2,1)S(1)}, u32[]{:S(2)}, u32[]{:S(2)}) collective-permute-start(bf16[2,384,128]{2,1,0:T(8,128)(2,1)} %shard_map.94.refs_0_), channel_id=1, source_target_pairs={{0,6},{1,7},{2,4},{3,5},{4,2},{5,3},{6,0},{7,1},{8,14},{9,15},{10,... | collective-permute-start | bytes 589832 | tf_op jit(solution)/shard_map/ppermute | solution.py:307
  6.8 0.5 %collective-permute-start.1 = (bf16[2,384,128]{2,1,0:T(8,128)(2,1)}, bf16[2,384,128]{2,1,0:T(8,128)(2,1)S(1)}, u32[]{:S(2)}, u32[]{:S(2)}) collective-permute-start(bf16[2,384,128]{2,1,0:T(8,128)(2,1)} %shard_map.94.refs_0_), channel_id=1, source_target_pairs={{0,4},{1,5},{2,6},{3,7},{4,0},{5,1},{6,2},{7,3},{8,12},{9,13},{10,... | collective-permute-start | bytes 589832 | tf_op jit(solution)/shard_map/ppermute | solution.py:307
  7.3 0.1 collective-permute-start
  7.4 0.0 copy-start.2
  7.4 1.4 %copy-done.2 = bf16[48,16,1024]{2,1,0:T(8,128)(2,1)S(1)} copy-done((bf16[48,16,1024]{2,1,0:T(8,128)(2,1)S(1)}, bf16[48,16,1024]{2,1,0:T(8,128)(2,1)}, u32[]{:S(2)}) %copy-start.2) | copy-done | bytes 1572888
  8.8 0.0 copy-start.3
  8.8 2.9 %shard_map.92 = (bf16[8,768,128]{2,1,0:T(8,128)(2,1)S(1)}, bf16[16,384,128]{2,1,0:T(8,128)(2,1)S(1)}) custom-call(bf16[48,16,1024]{2,1,0:T(8,128)(2,1)S(1)} %copy-done.2), custom_call_target="tpu_custom_call" | custom-call | flops 10000000000 | bytes 10000000 | tf_op jit(solution)/shard_map/pallas_call | solution.py:295
  11.7 0.0 copy-done.4
  11.7 0.0 copy-done.5
  11.8 0.0 copy-done.6
  11.8 0.0 copy-done.3
  11.8 0.0 copy-start.1
  11.8 2.4 %shard_map.93 = (f32[16,384,128]{2,1,0:T(8,128)S(1)}, bf16[16,128,256]{2,1,0:T(8,128)(2,1)S(1)}, bf16[16,128,128]{2,1,0:T(8,128)(2,1)S(1)}) custom-call(s32[4,16]{1,0:T(4,128)S(1)} %bitcast.2, bf16[16,384,128]{2,1,0:T(8,128)(2,1)S(1)} %get-tuple-element.20.turned_ref, bf16[16,4,64,64]{3,2,1,0:T(8,128)(2,1)S(1)} %copy-done.3, ...), custom_call_target="tpu_custom_call" | custom-call | flops 10000000000 | bytes 10000000 | tf_op jit(solution)/shard_map/pallas_call | solution.py:295
  14.2 0.0 copy-start
  14.2 0.0 copy-start.7
  14.2 0.0 collective-permute-done.2.refs_1_.refs_2_.rest_2_
  14.2 0.0 copy-done.1
  14.3 0.1 collective-permute-start.3
  14.4 1.7 %collective-permute-done.1.refs_0_.rest_1_ = bf16[2,384,128]{2,1,0:T(8,128)(2,1)S(1)} collective-permute-done((bf16[2,384,128]{2,1,0:T(8,128)(2,1)}, bf16[2,384,128]{2,1,0:T(8,128)(2,1)S(1)}, u32[]{:S(2)}, u32[]{:S(2)}) %collective-permute-start.1) | collective-permute-done | bytes 196640 | tf_op jit(solution)/shard_map/ppermute | solution.py:307
  16.1 0.3 collective-permute-done.refs_1_.rest_0_
  16.4 0.1 collective-permute-start.4
  17.1 0.0 copy-done
  17.2 0.5 %shard_map.91 = (f32[768,128]{1,0:T(8,128)S(1)}, bf16[16,128]{1,0:T(8,128)(2,1)S(1)}, f32[16,48,128]{2,1,0:T(8,128)S(1)}, f32[16,48,128]{2,1,0:T(8,128)S(1)}, f32[48,128]{1,0:T(8,128)S(1)}) custom-call(s32[1]{0:T(128)S(6)} %copy.10.days_ref, f32[48,1024]{1,0:T(8,128)S(1)} %copy-done), custom_call_target="tpu_custom_call" | custom-call | flops 1000000 | bytes 100000 | tf_op jit(solution)/shard_map/pallas_call | solution.py:295
  17.7 0.6 %collective-permute-done.4.rest_6_ = bf16[4,384,128]{2,1,0:T(8,128)(2,1)S(1)} collective-permute-done((bf16[4,384,128]{2,1,0:T(8,128)(2,1)S(1)}, bf16[4,384,128]{2,1,0:T(8,128)(2,1)S(1)}, u32[]{:S(2)}, u32[]{:S(2)}) %collective-permute-start.4) | collective-permute-done | bytes 393248 | tf_op jit(solution)/shard_map/ppermute | solution.py:307
  18.2 0.0 collective-permute-done.3.rest_5_
  18.2 0.0 copy-done.7
  18.2 2.8 %shard_map.97 = (f32[8,768,128]{2,1,0:T(8,128)S(1)}, bf16[9,16,128]{2,1,0:T(8,128)(2,1)S(1)}) custom-call(s32[2,16]{1,0:T(2,128)S(1)} %bitcast.3, f32[48,128]{1,0:T(8,128)S(1)} %get-tuple-element.19.active_ref, f32[16,384,128]{2,1,0:T(8,128)S(1)} %get-tuple-element.21.running_ref, bf16[16,128,256]{2,1,0:T(8,128)(2,1)S(1)} %get-tuple-element.22.weight_ref, ...), custom_call_target="tpu_custom_call" | custom-call | flops 10000000000 | bytes 10000000 | tf_op jit(solution)/shard_map/pallas_call | solution.py:295
  21.0 3.7 %collective-permute-start.7 = (bf16[9,16,128]{2,1,0:T(8,128)(2,1)S(1)}, bf16[9,16,128]{2,1,0:T(8,128)(2,1)S(1)}, u32[]{:S(2)}, u32[]{:S(2)}) collective-permute-start(bf16[9,16,128]{2,1,0:T(8,128)(2,1)S(1)} %get-tuple-element.29), channel_id=1, source_target_pairs={{0,24},{8,16},{16,8},{24,0},{1,25},{9,17},{17,9},{25,1},{2,26},{10... | collective-permute-start | bytes 110600 | tf_op jit(solution)/shard_map/ppermute | solution.py:307
  24.7 0.0 collective-permute-start.6
  24.7 0.8 %collective-permute-start.5 = (bf16[9,16,128]{2,1,0:T(8,128)(2,1)S(1)}, bf16[9,16,128]{2,1,0:T(8,128)(2,1)S(1)}, u32[]{:S(2)}, u32[]{:S(2)}) collective-permute-start(bf16[9,16,128]{2,1,0:T(8,128)(2,1)S(1)} %get-tuple-element.29), channel_id=1, source_target_pairs={{0,8},{8,0},{16,24},{24,16},{1,9},{9,1},{17,25},{25,17},{2,10},{10... | collective-permute-start | bytes 110600 | tf_op jit(solution)/shard_map/ppermute | solution.py:307
  25.5 1.7 %shard_map.98.states_ref = f32[16,384,128]{2,1,0:T(8,128)S(1)} custom-call(f32[8,768,128]{2,1,0:T(8,128)S(1)} %get-tuple-element.26.forcing_ref, f32[768,128]{1,0:T(8,128)S(1)} %get-tuple-element.27.retain_ref), custom_call_target="tpu_custom_call" | custom-call | flops 1000000000 | bytes 1000000 | tf_op jit(solution)/shard_map/pallas_call | solution.py:295
  27.2 0.0 collective-permute-done.7.rest_2_.rest_5_
  27.2 2.4 %collective-permute-done.6.rest_1_.rest_4_ = bf16[9,16,128]{2,1,0:T(8,128)(2,1)S(1)} collective-permute-done((bf16[9,16,128]{2,1,0:T(8,128)(2,1)S(1)}, bf16[9,16,128]{2,1,0:T(8,128)(2,1)S(1)}, u32[]{:S(2)}, u32[]{:S(2)}) %collective-permute-start.6) | collective-permute-done | bytes 36896 | tf_op jit(solution)/shard_map/ppermute | solution.py:307
  29.6 0.0 collective-permute-done.5.rest_0_.rest_3_
  29.6 1.8 %shard_map.99 = (f32[8,768,128]{2,1,0:T(8,128)S(1)}, bf16[8,16,128]{2,1,0:T(8,128)(2,1)S(1)}) custom-call(f32[48,128]{1,0:T(8,128)S(1)} %get-tuple-element.19.active_ref, f32[16,384,128]{2,1,0:T(8,128)S(1)} %shard_map.98.states_ref, f32[16,48,128]{2,1,0:T(8,128)S(1)} %get-tuple-element.28.through_ref, ...), custom_call_target="tpu_custom_call" | custom-call | flops 10000000000 | bytes 10000000 | tf_op jit(solution)/shard_map/pallas_call | solution.py:295
  31.3 1.7 %collective-permute-start.10 = (bf16[8,16,128]{2,1,0:T(8,128)(2,1)S(1)}, bf16[8,16,128]{2,1,0:T(8,128)(2,1)S(1)}, u32[]{:S(2)}, u32[]{:S(2)}) collective-permute-start(bf16[8,16,128]{2,1,0:T(8,128)(2,1)S(1)} %get-tuple-element.32), channel_id=1, source_target_pairs={{0,24},{8,16},{16,8},{24,0},{1,25},{9,17},{17,9},{25,1},{2,26},{10... | collective-permute-start | bytes 98312 | tf_op jit(solution)/shard_map/ppermute | solution.py:307
  33.0 0.5 %collective-permute-start.9 = (bf16[8,16,128]{2,1,0:T(8,128)(2,1)S(1)}, bf16[8,16,128]{2,1,0:T(8,128)(2,1)S(1)}, u32[]{:S(2)}, u32[]{:S(2)}) collective-permute-start(bf16[8,16,128]{2,1,0:T(8,128)(2,1)S(1)} %get-tuple-element.32), channel_id=1, source_target_pairs={{0,16},{8,24},{16,0},{24,8},{1,17},{9,25},{17,1},{25,9},{2,18},{10... | collective-permute-start | bytes 98312 | tf_op jit(solution)/shard_map/ppermute | solution.py:307
  33.5 2.3 %collective-permute-start.8 = (bf16[8,16,128]{2,1,0:T(8,128)(2,1)S(1)}, bf16[8,16,128]{2,1,0:T(8,128)(2,1)S(1)}, u32[]{:S(2)}, u32[]{:S(2)}) collective-permute-start(bf16[8,16,128]{2,1,0:T(8,128)(2,1)S(1)} %get-tuple-element.32), channel_id=1, source_target_pairs={{0,8},{8,0},{16,24},{24,16},{1,9},{9,1},{17,25},{25,17},{2,10},{10... | collective-permute-start | bytes 98312 | tf_op jit(solution)/shard_map/ppermute | solution.py:307
  35.8 0.5 %shard_map.100.partial_ref = f32[768,128]{1,0:T(8,128)S(1)} custom-call(f32[8,768,128]{2,1,0:T(8,128)S(1)} %get-tuple-element.30.adjoint_ref, f32[768,128]{1,0:T(8,128)S(1)} %get-tuple-element.27.retain_ref, bf16[8,768,128]{2,1,0:T(8,128)(2,1)S(1)} %get-tuple-element.31.moved_ref), custom_call_target="tpu_custom_call" | custom-call | flops 1000000000 | bytes 1000000 | tf_op jit(solution)/shard_map/pallas_call | solution.py:295
  36.3 0.8 %collective-permute-done.10.rest_2_ = bf16[8,16,128]{2,1,0:T(8,128)(2,1)S(1)} collective-permute-done((bf16[8,16,128]{2,1,0:T(8,128)(2,1)S(1)}, bf16[8,16,128]{2,1,0:T(8,128)(2,1)S(1)}, u32[]{:S(2)}, u32[]{:S(2)}) %collective-permute-start.10) | collective-permute-done | bytes 32800 | tf_op jit(solution)/shard_map/ppermute | solution.py:307
  37.1 0.8 %collective-permute-done.9.rest_1_ = bf16[8,16,128]{2,1,0:T(8,128)(2,1)S(1)} collective-permute-done((bf16[8,16,128]{2,1,0:T(8,128)(2,1)S(1)}, bf16[8,16,128]{2,1,0:T(8,128)(2,1)S(1)}, u32[]{:S(2)}, u32[]{:S(2)}) %collective-permute-start.9) | collective-permute-done | bytes 32800 | tf_op jit(solution)/shard_map/ppermute | solution.py:307
  38.0 0.1 collective-permute-done.8.rest_0_
  38.0 1.4 %shard_map.101 = f32[48,1024]{1,0:T(8,128)} custom-call(f32[768,128]{1,0:T(8,128)S(1)} %shard_map.100.partial_ref, f32[768,128]{1,0:T(8,128)S(1)} %get-tuple-element.27.retain_ref, bf16[8,768,128]{2,1,0:T(8,128)(2,1)S(1)} %get-tuple-element.31.moved_ref, bf16[8,16,128]{2,1,0:T(8,128)(2,1)S(1)} %collective-permute-done.8.rest_0_, ...), custom_call_target="tpu_custom_call" | custom-call | flops 10000000000 | bytes 10000000 | tf_op jit(solution)/shard_map/pallas_call | solution.py:295
  (2 shorter events, 0.1 us)
Async XLA Ops:
  0.0 11.7 %copy-start.4 = (bf16[16,2,64,64]{3,2,1,0:T(8,128)(2,1)S(1)}, bf16[16,2,64,64]{3,2,1,0:T(8,128)(2,1)}, u32[]{:S(2)}) copy-start(bf16[16,2,64,64]{3,2,1,0:T(8,128)(2,1)} %remote_weight_ref.1) | copy-start | bytes 786436
  0.0 11.7 %copy-start.5 = (bf16[16,64,64]{2,1,0:T(8,128)(2,1)S(1)}, bf16[16,64,64]{2,1,0:T(8,128)(2,1)}, u32[]{:S(2)}) copy-start(bf16[16,64,64]{2,1,0:T(8,128)(2,1)} %inverse_ref.1) | copy-start | bytes 393220
  0.0 11.8 %copy-start.6 = (s32[16,4]{0,1:T(4,128)S(1)}, s32[16,4]{0,1:T(4,128)}, u32[]{:S(2)}) copy-start(s32[16,4]{0,1:T(4,128)} %param.10) | copy-start | bytes 772
  2.8 11.4 %collective-permute-start.2 = (bf16[2,384,128]{2,1,0:T(8,128)(2,1)}, bf16[2,384,128]{2,1,0:T(8,128)(2,1)S(1)}, u32[]{:S(2)}, u32[]{:S(2)}) collective-permute-start(bf16[2,384,128]{2,1,0:T(8,128)(2,1)} %shard_map.94.refs_0_), channel_id=1, source_target_pairs={{0,6},{1,7},{2,4},{3,5},{4,2},{5,3},{6,0},{7,1},{8,14},{9,15},{10,... | collective-permute-start | bytes 589832 | tf_op jit(solution)/shard_map/ppermute | solution.py:307
  6.8 9.3 %collective-permute-start.1 = (bf16[2,384,128]{2,1,0:T(8,128)(2,1)}, bf16[2,384,128]{2,1,0:T(8,128)(2,1)S(1)}, u32[]{:S(2)}, u32[]{:S(2)}) collective-permute-start(bf16[2,384,128]{2,1,0:T(8,128)(2,1)} %shard_map.94.refs_0_), channel_id=1, source_target_pairs={{0,4},{1,5},{2,6},{3,7},{4,0},{5,1},{6,2},{7,3},{8,12},{9,13},{10,... | collective-permute-start | bytes 589832 | tf_op jit(solution)/shard_map/ppermute | solution.py:307
  7.3 9.1 %collective-permute-start = (bf16[2,384,128]{2,1,0:T(8,128)(2,1)}, bf16[2,384,128]{2,1,0:T(8,128)(2,1)S(1)}, u32[]{:S(2)}, u32[]{:S(2)}) collective-permute-start(bf16[2,384,128]{2,1,0:T(8,128)(2,1)} %shard_map.94.refs_0_), channel_id=1, source_target_pairs={{0,2},{1,3},{2,0},{3,1},{4,6},{5,7},{6,4},{7,5},{8,10},{9,11},{10,... | collective-permute-start | bytes 589832 | tf_op jit(solution)/shard_map/ppermute | solution.py:307
  7.4 1.4 %copy-start.2 = (bf16[48,16,1024]{2,1,0:T(8,128)(2,1)S(1)}, bf16[48,16,1024]{2,1,0:T(8,128)(2,1)}, u32[]{:S(2)}) copy-start(bf16[48,16,1024]{2,1,0:T(8,128)(2,1)} %z_hbm.1) | copy-start | bytes 4718596
  8.8 2.9 %copy-start.3 = (bf16[16,4,64,64]{3,2,1,0:T(8,128)(2,1)S(1)}, bf16[16,4,64,64]{3,2,1,0:T(8,128)(2,1)}, u32[]{:S(2)}) copy-start(bf16[16,4,64,64]{3,2,1,0:T(8,128)(2,1)} %weight_ref.1) | copy-start | bytes 1572868
  11.8 2.5 %copy-start.1 = (bf16[2,384,128]{2,1,0:T(8,128)(2,1)S(1)}, bf16[2,384,128]{2,1,0:T(8,128)(2,1)}, u32[]{:S(2)}) copy-start(bf16[2,384,128]{2,1,0:T(8,128)(2,1)} %shard_map.94.refs_0_) | copy-start | bytes 589828
  14.2 2.9 %copy-start = (f32[48,1024]{1,0:T(8,128)S(1)}, f32[48,1024]{1,0:T(8,128)}, u32[]{:S(2)}) copy-start(f32[48,1024]{1,0:T(8,128)} %retention_ref.1) | copy-start | bytes 589828
  14.2 4.0 %copy-start.7 = (s32[16,2]{0,1:T(2,128)S(1)}, s32[16,2]{0,1:T(2,128)}, u32[]{:S(2)}) copy-start(s32[16,2]{0,1:T(2,128)} %param.11) | copy-start | bytes 388
  14.3 3.9 %collective-permute-start.3 = (bf16[6,384,128]{2,1,0:T(8,128)(2,1)S(1)}, bf16[6,384,128]{2,1,0:T(8,128)(2,1)S(1)}, u32[]{:S(2)}, u32[]{:S(2)}) collective-permute-start(bf16[6,384,128]{2,1,0:T(8,128)(2,1)S(1)} %shard_map.95.rest_3_), channel_id=1, source_target_pairs={{0,1},{1,0},{2,3},{3,2},{4,5},{5,4},{6,7},{7,6},{8,9},{9,8},{10,11... | collective-permute-start | bytes 1769480 | tf_op jit(solution)/shard_map/ppermute | solution.py:307
  16.4 1.8 %collective-permute-start.4 = (bf16[4,384,128]{2,1,0:T(8,128)(2,1)S(1)}, bf16[4,384,128]{2,1,0:T(8,128)(2,1)S(1)}, u32[]{:S(2)}, u32[]{:S(2)}) collective-permute-start(bf16[4,384,128]{2,1,0:T(8,128)(2,1)S(1)} %shard_map.96.rest_4_), channel_id=1, source_target_pairs={{0,1},{1,0},{2,3},{3,2},{4,5},{5,4},{6,7},{7,6},{8,9},{9,8},{10,11... | collective-permute-start | bytes 1179656 | tf_op jit(solution)/shard_map/ppermute | solution.py:307
  21.0 6.1 %collective-permute-start.7 = (bf16[9,16,128]{2,1,0:T(8,128)(2,1)S(1)}, bf16[9,16,128]{2,1,0:T(8,128)(2,1)S(1)}, u32[]{:S(2)}, u32[]{:S(2)}) collective-permute-start(bf16[9,16,128]{2,1,0:T(8,128)(2,1)S(1)} %get-tuple-element.29), channel_id=1, source_target_pairs={{0,24},{8,16},{16,8},{24,0},{1,25},{9,17},{17,9},{25,1},{2,26},{10... | collective-permute-start | bytes 110600 | tf_op jit(solution)/shard_map/ppermute | solution.py:307
  24.7 4.9 %collective-permute-start.6 = (bf16[9,16,128]{2,1,0:T(8,128)(2,1)S(1)}, bf16[9,16,128]{2,1,0:T(8,128)(2,1)S(1)}, u32[]{:S(2)}, u32[]{:S(2)}) collective-permute-start(bf16[9,16,128]{2,1,0:T(8,128)(2,1)S(1)} %get-tuple-element.29), channel_id=1, source_target_pairs={{0,16},{8,24},{16,0},{24,8},{1,17},{9,25},{17,1},{25,9},{2,18},{10... | collective-permute-start | bytes 110600 | tf_op jit(solution)/shard_map/ppermute | solution.py:307
  24.7 4.9 %collective-permute-start.5 = (bf16[9,16,128]{2,1,0:T(8,128)(2,1)S(1)}, bf16[9,16,128]{2,1,0:T(8,128)(2,1)S(1)}, u32[]{:S(2)}, u32[]{:S(2)}) collective-permute-start(bf16[9,16,128]{2,1,0:T(8,128)(2,1)S(1)} %get-tuple-element.29), channel_id=1, source_target_pairs={{0,8},{8,0},{16,24},{24,16},{1,9},{9,1},{17,25},{25,17},{2,10},{10... | collective-permute-start | bytes 110600 | tf_op jit(solution)/shard_map/ppermute | solution.py:307
  31.3 5.8 %collective-permute-start.10 = (bf16[8,16,128]{2,1,0:T(8,128)(2,1)S(1)}, bf16[8,16,128]{2,1,0:T(8,128)(2,1)S(1)}, u32[]{:S(2)}, u32[]{:S(2)}) collective-permute-start(bf16[8,16,128]{2,1,0:T(8,128)(2,1)S(1)} %get-tuple-element.32), channel_id=1, source_target_pairs={{0,24},{8,16},{16,8},{24,0},{1,25},{9,17},{17,9},{25,1},{2,26},{10... | collective-permute-start | bytes 98312 | tf_op jit(solution)/shard_map/ppermute | solution.py:307
  33.0 4.9 %collective-permute-start.9 = (bf16[8,16,128]{2,1,0:T(8,128)(2,1)S(1)}, bf16[8,16,128]{2,1,0:T(8,128)(2,1)S(1)}, u32[]{:S(2)}, u32[]{:S(2)}) collective-permute-start(bf16[8,16,128]{2,1,0:T(8,128)(2,1)S(1)} %get-tuple-element.32), channel_id=1, source_target_pairs={{0,16},{8,24},{16,0},{24,8},{1,17},{9,25},{17,1},{25,9},{2,18},{10... | collective-permute-start | bytes 98312 | tf_op jit(solution)/shard_map/ppermute | solution.py:307
  33.5 4.5 %collective-permute-start.8 = (bf16[8,16,128]{2,1,0:T(8,128)(2,1)S(1)}, bf16[8,16,128]{2,1,0:T(8,128)(2,1)S(1)}, u32[]{:S(2)}, u32[]{:S(2)}) collective-permute-start(bf16[8,16,128]{2,1,0:T(8,128)(2,1)S(1)} %get-tuple-element.32), channel_id=1, source_target_pairs={{0,8},{8,0},{16,24},{24,16},{1,9},{9,1},{17,25},{25,17},{2,10},{10... | collective-permute-start | bytes 98312 | tf_op jit(solution)/shard_map/ppermute | solution.py:307
